TPU v7x, 32 devices: a whole 2x2x4 slice. The times are simulated.
32 devices in a mesh: wide: 16 (over z, y, x), narrow: 2 (over core).
Axes of the slice: x: 2, y: 2, z: 4, core: 2. Of those that a mesh axis runs over, the one named last changes fastest.
Arguments:
- context: bfloat16 [4096, 3072], P('wide', 'narrow'), may hold values from -6 to 6
- out_weight: bfloat16 [3072, 6144], P('wide', 'narrow'), may hold values from -0.109375 to 0.109375
- residual: bfloat16 [4096, 6144], P('wide', 'narrow'), may hold values from -180 to 180
- ln_gain: bfloat16 [6144], P('narrow'), may hold values from 0.5 to 1.5
- side_down: bfloat16 [6144, 768], P('narrow', 'wide'), may hold values from -0.078125 to 0.078125
- f_weight: bfloat16 [384, 384], replicated, may hold values from -0.3125 to 0.3125
- g_weight: bfloat16 [384, 384], replicated, may hold values from -0.3125 to 0.3125
- targets: float32 [4096, 768], P(('wide', 'narrow')), may hold values from -18 to 18
Outputs:
- side_out: float32 [4096, 768], P(('wide', 'narrow'))
- f_grad: float32 [384, 384], replicated
- g_grad: float32 [384, 384], replicated
All inputs are finite; a program needn't handle non-finite values.
Results may differ from a plain program's by a relative error of at most 0.00035.
The roundings to bfloat16 on the way count: a program that leaves them out, or rounds other values in their place, can miss the bound.
Values may be sent and summed in bfloat16 or wider, within the bound.
No kernel may reach another device: no remote copies, remote signals or barrier semaphores. Data moves between devices by JAX's collectives and lax.ppermute only.
A program may use at most 64 MiB of HBM per device.

v0:
```python
import jax
import jax.numpy as jnp
from jax import lax
from jax.sharding import PartitionSpec as P


def coupling(values, weight):
    return jax.nn.gelu(jnp.dot(values, weight, precision=lax.Precision.HIGHEST))


def per_device(context, out_weight, residual, ln_gain, side_down, f_weight, g_weight, targets):
    full_weight = lax.all_gather(out_weight, "wide", axis=0, tiled=True)
    whole = lax.all_gather(context, "narrow", axis=1, tiled=True)
    attn_sum = jnp.dot(whole, full_weight, preferred_element_type=jnp.float32)
    stream = (residual.astype(jnp.float32) + attn_sum).astype(jnp.bfloat16)
    stream_value = stream.astype(jnp.float32)
    row_sum = jnp.sum(stream_value, axis=1)
    row_squares = jnp.sum(stream_value * stream_value, axis=1)
    scaled = (stream_value * ln_gain.astype(jnp.float32)[None, :]).astype(jnp.bfloat16)
    down_full = lax.all_gather(side_down, "wide", axis=1, tiled=True)
    gain_part = jnp.dot(ln_gain[None, :], down_full, preferred_element_type=jnp.float32)[0]
    local_rows = targets.shape[0]
    sums_all, squares_all, gain_map = lax.psum((row_sum, row_squares, gain_part), "narrow")
    offset = lax.axis_index("narrow") * local_rows
    token_sum = lax.dynamic_slice_in_dim(sums_all, offset, local_rows, 0)
    token_squares = lax.dynamic_slice_in_dim(squares_all, offset, local_rows, 0)
    projected = lax.psum_scatter(
        jnp.dot(scaled, down_full, preferred_element_type=jnp.float32),
        "narrow",
        scatter_dimension=0,
        tiled=True,
    )
    features = stream.shape[1] * lax.axis_size("narrow")
    mean = token_sum / features
    spread = token_squares / features - mean * mean
    side_in = (projected - mean[:, None] * gain_map[None, :]) / jnp.sqrt(spread + 1e-06)[:, None]
    half = side_in.shape[1] // 2
    f_w = f_weight.astype(jnp.float32)
    g_w = g_weight.astype(jnp.float32)
    first = side_in[:, :half]
    second = side_in[:, half:]
    upper = first + coupling(second, f_w)
    g_value, g_pull = jax.vjp(coupling, upper, g_w)
    lower = second + g_value
    side_out = jnp.concatenate([upper, lower], axis=1)
    all_tokens = local_rows * lax.axis_size("wide") * lax.axis_size("narrow")
    misfit = (side_out - targets) / all_tokens
    upper_back, g_local = g_pull(misfit[:, half:])
    rebuilt = lower - g_value
    upper_total = misfit[:, :half] + upper_back
    f_value, f_pull = jax.vjp(coupling, rebuilt, f_w)
    f_local = f_pull(upper_total)[1]
    f_total, g_total = lax.psum((f_local, g_local), ("wide", "narrow"))
    return (side_out, f_total, g_total)


def solution(mesh):
    in_specs = (
        P("wide", "narrow"),
        P("wide", "narrow"),
        P("wide", "narrow"),
        P("narrow"),
        P("narrow", "wide"),
        P(),
        P(),
        P(("wide", "narrow"), None),
    )
    out_specs = (P(("wide", "narrow"), None), P(), P())
    return jax.shard_map(
        per_device, mesh=mesh, in_specs=in_specs, out_specs=out_specs, check_vma=False
    )
```

profile of v0, /device:TPU:0, one launch (start us, length us, event | category | flops | bytes accessed | tf_op | source)
XLA Modules:
  0.0 480.8 jit_solution(12004028516498116592)
XLA Ops:
  7.2 0.0 copy-start
  7.2 0.0 all-gather.4.cloned.1.call-start
  7.2 0.7 all-gather.4.cloned.1.call-update
  7.9 0.0 all-gather.6.cloned.1.call-start
  8.0 0.7 all-gather.6.cloned.1.call-update
  8.7 0.0 all-gather.8.cloned.1.call-start
  8.7 0.7 all-gather.8.cloned.1.call-update
  9.4 0.0 reduce-scatter.2.cloned.1.call-start
  9.4 0.7 convert_element_type.20
  10.1 12.0 %all-gather.4.cloned.1.call-done = bf16[256,3072]{1,0:T(8,128)(2,1)} async-done(((bf16[256,1536]{1,0:T(8,128)(2,1)}), bf16[256,3072]{1,0:T(8,128)(2,1)}) %all-gather.4.cloned.1.call-update) | async-done | bytes 1572880 | tf_op jit(solution)/shard_map/all_gather | solution.py:13
  22.1 215.5 %all-gather.6.cloned.1.call-done = bf16[3072,3072]{1,0:T(8,128)(2,1)} async-done(((bf16[192,3072]{1,0:T(8,128)(2,1)}), bf16[3072,3072]{1,0:T(8,128)(2,1)}) %all-gather.6.cloned.1.call-update) | async-done | bytes 18874384 | tf_op jit(solution)/shard_map/all_gather | solution.py:12
  237.6 10.0 %convert_reduce_fusion = (f32[256]{0:T(256)S(1)}, f32[256]{0:T(256)S(1)}, bf16[256,3072]{1,0:T(8,128)(2,1)S(1)}) fusion(bf16[256,3072]{1,0:T(8,128)(2,1)} %all-gather.4.cloned.1.call-done, bf16[3072,3072]{1,0:T(8,128)(2,1)} %all-gather.6.cloned.1.call-done, bf16[256,3072]{1,0:T(8,128)(2,1)} %param.10), kind=kOutput, calls=%fused_computation.1 | convolution fusion | flops 4837343232 | bytes 23595008 | tf_op jit(solution)/shard_map/dot_general | solution.py:14
  247.6 71.5 %all-gather.8.cloned.1.call-done = bf16[3072,768]{0,1:T(8,128)(2,1)} async-done(((bf16[3072,48]{0,1:T(8,128)(2,1)}), bf16[3072,768]{0,1:T(8,128)(2,1)}) %all-gather.8.cloned.1.call-update) | async-done | bytes 4718608 | tf_op jit(solution)/shard_map/all_gather | solution.py:20
  319.1 0.0 copy-start.3
  319.1 4.7 fusion.3
  323.7 0.0 copy-start.2
  323.7 0.0 reduce-scatter.2.cloned.1.call-update
  323.8 0.0 all-reduce.4.cloned.1.call-start
  323.8 0.0 copy-done.3
  323.8 0.0 copy-start.1
  323.8 3.7 convolution_reduce_fusion
  327.6 2.5 all-reduce.1
  330.1 0.1 dynamic-slice_multiply_fusion
  330.2 0.6 reduce-scatter.2.cloned.1.call-done
  330.8 1.1 subtract_divide_fusion
  331.9 0.0 copy-done.2
  331.9 0.4 fusion.27
  332.3 0.0 copy-done
  332.3 0.4 slice_add_fusion
  332.7 0.0 copy-done.1
  332.7 0.8 subtract_multiply_fusion
  333.5 1.6 fusion.60
  335.1 0.5 convolution_add_fusion.1
  335.6 0.4 fusion.58
  336.0 1.6 fusion.18
  337.6 0.0 all-reduce.4.cloned.1.call-update
  337.6 132.8 %all-reduce.4.cloned.1.call-done = (f32[384,384]{1,0:T(8,128)}, f32[384,384]{1,0:T(8,128)}) async-done(((f32[384,384]{1,0:T(8,128)}, f32[384,384]{1,0:T(8,128)}), (f32[384,384]{1,0:T(8,128)}, f32[384,384]{1,0:T(8,128)})) %all-reduce.4.cloned.1.call-update) | async-done | bytes 1179664 | tf_op jit(solution)/shard_map/psum | solution.py:53
  470.4 1.9 copy.13
  472.3 1.9 copy.14
  (1 shorter events, 0.0 us)
Async XLA Ops:
  7.2 325.1 %copy-start = (bf16[384,384]{1,0:T(8,128)(2,1)S(1)}, bf16[384,384]{1,0:T(8,128)(2,1)}, u32[]{:S(2)}) copy-start(bf16[384,384]{1,0:T(8,128)(2,1)} %param.14) | copy-start | bytes 884740
  7.2 14.9 %all-gather.4.cloned.1.call-start = ((), (), s32[]{:S(2)}) async-start(), calls=%async_computation.1 | async-start | bytes 2359296 | tf_op jit(solution)/shard_map/all_gather | solution.py:13
  7.9 229.7 %all-gather.6.cloned.1.call-start = ((), (), s32[]{:S(2)}) async-start(), calls=%async_computation.2 | async-start | bytes 20054016 | tf_op jit(solution)/shard_map/all_gather | solution.py:12
  8.7 310.4 %all-gather.8.cloned.1.call-start = ((), (), s32[]{:S(2)}) async-start(), calls=%async_computation.3 | async-start | bytes 5013504 | tf_op jit(solution)/shard_map/all_gather | solution.py:20
  9.4 321.4 %reduce-scatter.2.cloned.1.call-start = ((), (), s32[]{:S(2)}) async-start(), calls=%async_computation.4 | async-start | bytes 1179648 | tf_op jit(solution)/shard_map/reduce_scatter | solution.py:27
  319.1 4.7 copy-start.3
  323.7 8.2 %copy-start.2 = (bf16[384,384]{1,0:T(8,128)(2,1)S(1)}, bf16[384,384]{1,0:T(8,128)(2,1)}, u32[]{:S(2)}) copy-start(bf16[384,384]{1,0:T(8,128)(2,1)} %param.13) | copy-start | bytes 884740
  323.8 146.7 %all-reduce.4.cloned.1.call-start = ((), (), s32[]{:S(2)}) async-start(), calls=%async_computation.5 | async-start | bytes 2359296 | tf_op jit(solution)/shard_map/psum | solution.py:53
  323.8 8.9 %copy-start.1 = (f32[128,768]{1,0:T(8,128)S(1)}, f32[128,768]{1,0:T(8,128)}, u32[]{:S(2)}) copy-start(f32[128,768]{1,0:T(8,128)} %param.15) | copy-start | bytes 1179652
Sparse Core Ops, SparseCore 0:
  9.6 12.4 all-gather.3
  24.9 212.6 all-gather.5
  240.4 78.6 all-gather.7
  323.9 6.8 reduce-scatter.1
  337.8 132.5 all-reduce.3
where the time goes:
time: 481 us
  waiting for transfers between devices  434 us (90%)
  matrix products  23.2 us (5%)
  between operations  13.9 us (3%)
    all_gather x1, waiting for transfers between devices, per_device(): full_weight = lax.all_gather(out_weight, 'wide', axis=0, tiled=True)  215 us
    psum x1, waiting for transfers between devices, per_device(): f_total, g_total = lax.psum((f_local, g_local), ('wide', 'narrow'))  133 us
    all_gather x1, waiting for transfers between devices, per_device(): down_full = lax.all_gather(side_down, 'wide', axis=1, tiled=True)  71.5 us
    all_gather x1, waiting for transfers between devices, per_device(): whole = lax.all_gather(context, 'narrow', axis=1, tiled=True)  12 us
    dot_general x1, matrix products, per_device(): attn_sum = jnp.dot(whole, full_weight, preferred_element_type=jnp.float32)  9.98 us
  transfers between devices with their start and end apart: 5, of which 5 were waited for; matrix products, arithmetic and copies ran while one was open for 3% of the time, Pallas kernels for 0%

commit v1 on v0

v1 whole, which is shorter than its diff:
```python
import functools

import jax
import jax.numpy as jnp
import numpy as np
from jax import lax
from jax.sharding import PartitionSpec as P

HIGH = lax.Precision.HIGH
F32 = jnp.float32
BF16 = jnp.bfloat16


def coupling(values, weight):
    return jax.nn.gelu(jnp.dot(values, weight, precision=HIGH))


def slot_table(planes):
    order = [sorted(range(planes), key=lambda p: (abs(p - at), p)) for at in range(planes)]
    place = [[row.index(p) for p in range(planes)] for row in order]
    return order, place


def per_device(group, wides, narrows, context, out_weight, residual, ln_gain, side_down, f_weight, g_weight, targets):
    planes = wides // group
    wide, core = lax.axis_index("wide"), lax.axis_index("narrow")
    plane, member = wide // group, wide % group
    order, place = slot_table(planes)
    short = planes <= 4
    if not short:
        order = place = [list(range(planes))] * planes

    def to_member(value, s):
        pairs = [(i, i - i % group + (i % group ^ s)) for i in range(wides)]
        return lax.ppermute(value, "wide", pairs) if s else value

    def to_core(value, t):
        return lax.ppermute(value, "narrow", [(i, i ^ t) for i in range(narrows)]) if t else value

    def along(value):
        if not short:
            lines = [[p * group + m for p in range(planes)] for m in range(group)]
            return list(lax.all_gather(value, "wide", axis_index_groups=lines))
        up, down = [value], [value]
        for _ in range(planes - 1):
            up.append(lax.ppermute(up[-1], "wide", [(i, i + group) for i in range(wides - group)]))
            down.append(lax.ppermute(down[-1], "wide", [(i + group, i) for i in range(wides - group)]))
        slots = [value]
        for j in range(1, planes):
            found, which, table = [], {}, []
            for at in range(planes):
                step = at - order[at][j]
                if step not in which:
                    which[step] = len(found)
                    found.append(up[step] if step > 0 else down[-step])
                table.append(which[step])
            at = jnp.asarray(np.array(table, np.int32))[plane]
            choice = found[0]
            for i in range(1, len(found)):
                choice = jnp.where(at == i, found[i], choice)
            slots.append(choice)
        return slots

    def block(value, index, size, axis):
        return lax.dynamic_slice_in_dim(value, index * size, size, axis)

    slot_plane = jnp.asarray(np.array(order, np.int32))[plane]
    features = out_weight.shape[1] // group
    rows = out_weight.shape[0]
    tokens = context.shape[0]
    members = range(group)

    pieces = [to_member(block(out_weight, member ^ s, features, 1), s) for s in members]
    lines = [along(piece) for piece in pieces]
    downs = [to_member(block(side_down.T, member ^ s, features, 1), s) for s in members]
    columns = downs[0].shape[0]
    down_plane = jnp.zeros((group * columns, features), BF16)
    for s in members:
        down_plane = lax.dynamic_update_slice_in_dim(down_plane, downs[s], (member ^ s) * columns, 0)
    down_slots = along(down_plane)

    part = jnp.concatenate([to_member(context, s) for s in members], axis=0)
    parts = [to_core(part, t) for t in range(narrows)]
    stay = jnp.concatenate([to_member(block(residual, member ^ s, features, 1), s) for s in members], axis=0)

    weight = jnp.zeros((wides * rows, features), BF16)
    for j in range(planes):
        for s in members:
            at = (slot_plane[j] * group + (member ^ s)) * rows
            weight = lax.dynamic_update_slice_in_dim(weight, lines[s][j], at, 0)
    attn_sum = jnp.zeros((), F32)
    for t in range(narrows):
        attn_sum = attn_sum + jnp.dot(
            parts[t], block(weight, core ^ t, part.shape[1], 0), preferred_element_type=F32
        )
    stream = (stay.astype(F32) + attn_sum).astype(BF16)
    stream_value = stream.astype(F32)
    gain = block(ln_gain, member, features, 0)
    scaled = (stream_value * gain.astype(F32)[None, :]).astype(BF16)

    local = tokens // narrows
    stats = jnp.stack([jnp.sum(stream_value, axis=1), jnp.sum(stream_value * stream_value, axis=1)])
    stats = stats.reshape(2, group, narrows, local)

    def sum_cores(pick):
        total = pick(core)
        for t in range(1, narrows):
            total = total + to_core(pick(core ^ t), t)
        return total

    def sum_members(pick):
        total = pick(0)
        for s in range(1, group):
            total = total + to_member(pick(s), s)
        return total

    stats = sum_cores(lambda k: lax.dynamic_index_in_dim(stats, k, 2, keepdims=False))
    stats = sum_members(lambda s: stats[:, s])

    gain_rows = jnp.broadcast_to(gain[None, :], (8, features))
    dims = (((1,), (1,)), ((), ()))

    def project(down):
        value = lax.dot_general(scaled, down, dims, preferred_element_type=F32)
        gain_part = lax.dot_general(gain_rows, down, dims, preferred_element_type=F32)
        value = value.reshape(group, narrows, local, value.shape[1])

        def pick(k):
            mine = lax.dynamic_index_in_dim(value, k, 1, keepdims=False)
            return jnp.concatenate([mine.reshape(group * local, -1), gain_part], axis=0)

        summed = sum_cores(pick)
        tail = summed[group * local :]
        return sum_members(lambda s: jnp.concatenate([summed[s * local : (s + 1) * local], tail], axis=0))

    if short:
        projected = [project(down) for down in down_slots]
    else:
        projected = jnp.split(project(jnp.concatenate(down_slots, axis=0)), planes, axis=1)
    ordered = []
    for p in range(planes):
        at = jnp.asarray(np.array([row[p] for row in place], np.int32))[plane]
        choice = projected[0]
        for j in range(1, planes):
            choice = jnp.where(at == j, projected[j], choice)
        ordered.append(choice)
    ordered = jnp.concatenate(ordered, axis=1)
    gain_map = ordered[local]
    projected = ordered[:local]

    width = out_weight.shape[1] * narrows
    mean = stats[0] / width
    spread = stats[1] / width - mean * mean
    side_in = (projected - mean[:, None] * gain_map[None, :]) / jnp.sqrt(spread + 1e-06)[:, None]
    half = side_in.shape[1] // 2
    f_w, g_w = f_weight.astype(F32), g_weight.astype(F32)
    first, second = side_in[:, :half], side_in[:, half:]
    f_value, f_pull = jax.vjp(coupling, second, f_w)
    upper = first + f_value
    g_value, g_pull = jax.vjp(coupling, upper, g_w)
    lower = second + g_value
    side_out = jnp.concatenate([upper, lower], axis=1)
    misfit = (side_out - targets) / (local * wides * narrows)
    upper_back, g_local = g_pull(misfit[:, half:])
    f_local = f_pull(misfit[:, :half] + upper_back)[1]

    if (2 * half) % (wides * narrows * 8):
        f_total, g_total = lax.psum((f_local, g_local), ("wide", "narrow"))
        return side_out, f_total, g_total

    grads = jnp.concatenate([f_local, g_local], axis=0)
    share = 2 * half // narrows
    grads = sum_cores(lambda k: block(grads, k, share, 0))
    share = share // group
    part = grads
    grads = sum_members(lambda s: block(part, member ^ s, share, 0))
    share = share // planes

    def shift(value, k):
        return lax.ppermute(value, "wide", [(i, (i + k * group) % wides) for i in range(wides)])

    part = grads
    grads = block(part, plane, share, 0)
    for k in range(1, planes):
        grads = grads + shift(block(part, (plane + k) % planes, share, 0), k)
    whole = jnp.zeros((planes * share, half), F32)
    for k in range(planes):
        piece = shift(grads, k) if k else grads
        whole = lax.dynamic_update_slice_in_dim(whole, piece, (plane - k) % planes * share, 0)
    share = share * planes
    part, whole = whole, jnp.zeros((group * share, half), F32)
    for s in members:
        whole = lax.dynamic_update_slice_in_dim(whole, to_member(part, s), (member ^ s) * share, 0)
    share = share * group
    part, whole = whole, jnp.zeros((narrows * share, half), F32)
    for t in range(narrows):
        whole = lax.dynamic_update_slice_in_dim(whole, to_core(part, t), (core ^ t) * share, 0)
    return side_out, whole[:half], whole[half:]


def solution(mesh):
    wides, narrows = mesh.shape["wide"], mesh.shape["narrow"]
    group = 4 if wides % 4 == 0 else 1
    in_specs = (
        P("wide", "narrow"),
        P("wide", "narrow"),
        P("wide", "narrow"),
        P("narrow"),
        P("narrow", "wide"),
        P(),
        P(),
        P(("wide", "narrow"), None),
    )
    out_specs = (P(("wide", "narrow"), None), P(), P())
    return jax.shard_map(
        functools.partial(per_device, group, wides, narrows),
        mesh=mesh,
        in_specs=in_specs,
        out_specs=out_specs,
        check_vma=False,
    )
```

time: 481 us -> 302 us (0.63)
  waiting for transfers between devices: 434 us -> 52.9 us
  starting transfers between devices: 0.19 us -> 143 us
  local copies, waits for them, and re-layouts: 3.86 us -> 50.6 us
  other arithmetic: 2.71 us -> 19.8 us
    all_gather x3 -> x0, waiting for transfers between devices: 299 us -> none  [the longest x1 215 us: per_device(): full_weight = lax.all_gather(out_weight, 'wide', axis=0, tiled=True)]
    ppermute x0 -> x77, starting transfers between devices: none -> 143 us  [the longest x15 70 us: along(): lax.ppermute(up[-1], 'wide', [(i, i + group) for i in range(wides - group)])]
    psum x1 -> x0, waiting for transfers between devices: 133 us -> none  [per_device(): f_total, g_total = lax.psum((f_local, g_local), ('wide', 'narrow'))]
    ppermute x0 -> x77, waiting for transfers between devices: none -> 52.9 us  [the longest x33 42.2 us: to_member(): return lax.ppermute(value, 'wide', pairs) if s else value]
    dynamic_slice x0 -> x18, local copies, waits for them, and re-layouts: none -> 14.6 us  [the longest x6 8.14 us: pick(): mine = lax.dynamic_index_in_dim(value, k, 1, keepdims=False)]
    dynamic_update_slice x0 -> x13, other arithmetic: none -> 12.8 us  [the longest x12 12.8 us: per_device(): weight = lax.dynamic_update_slice_in_dim(weight, lines[s][j], at, 0)]
    unnamed x11 -> x93, local copies, waits for them, and re-layouts: 3.86 us -> 10.3 us
    dynamic_update_slice x0 -> x16, local copies, waits for them, and re-layouts: none -> 5.24 us  [the longest x3 4.15 us: per_device(): weight = lax.dynamic_update_slice_in_dim(weight, lines[s][j], at, 0)]
  transfers between devices with their start and end apart: 5 -> 77, of which waited for: 5 -> 29; matrix products, arithmetic and copies ran while one was open for 3% -> 21% of each run, Pallas kernels for 0% -> 0%
where the time goes in v1:
time: 302 us; the launch traced here: 300 us
  starting transfers between devices  143 us (47%)
  waiting for transfers between devices  52.9 us (18%)
  local copies, waits for them, and re-layouts  50.6 us (17%)
  other arithmetic  19.8 us (7%)
  matrix products  19.1 us (6%)
  between operations  14.6 us (5%)
    ppermute x15, starting transfers between devices, along(): lax.ppermute(up[-1], 'wide', [(i, i + group) for i in range(wides - group)])  70 us
    ppermute x33, waiting for transfers between devices, to_member(): return lax.ppermute(value, 'wide', pairs) if s else value  42.2 us
    ppermute x33, starting transfers between devices, to_member(): return lax.ppermute(value, 'wide', pairs) if s else value  41.5 us
    ppermute x15, starting transfers between devices, along(): lax.ppermute(down[-1], 'wide', [(i + group, i) for i in range(wides - gro...  19.5 us
    dynamic_update_slice x12, other arithmetic, per_device(): weight = lax.dynamic_update_slice_in_dim(weight, lines[s][j], at, 0)  12.8 us
    dot_general x2, matrix products, per_device(): jnp.dot(parts[t], block(weight, core ^ t, part.shape[1], 0), preferred_el...  11 us
    ppermute x6, starting transfers between devices, shift(): lax.ppermute(value, 'wide', [(i, (i + k * group) % wides) for i in range(...  10.9 us
    unnamed x93, local copies, waits for them, and re-layouts  10.3 us
  transfers between devices with their start and end apart: 77, of which 29 were waited for; matrix products, arithmetic and copies ran while one was open for 21% of the time, Pallas kernels for 0%

profile of v1, /device:TPU:0, one launch (start us, length us, event | category | flops | bytes accessed | tf_op | source)
XLA Modules:
  0.0 300.2 jit_solution(5341092103635744062)
XLA Ops:
  2.9 2.5 broadcast_in_dim.24
  7.8 6.3 %collective-permute-start.9 = (bf16[192,768]{1,0:T(8,128)(2,1)}, bf16[192,768]{1,0:T(8,128)(2,1)}, u32[]{:S(2)}, u32[]{:S(2)}) collective-permute-start(bf16[192,768]{1,0:T(8,128)(2,1)} %get-tuple-element.27), channel_id=1, source_target_pairs={{0,8},{2,10},{4,12},{6,14},{8,16},{10,18},{12,20},{14,22},{16,24},... | collective-permute-start | bytes 884744 | tf_op jit(solution)/shard_map/ppermute | solution.py:46
  14.1 1.9 collective-permute-start.6
  16.0 1.5 collective-permute-start.7
  34.2 2.1 constant_dynamic-update-slice_fusion.20
  42.6 4.3 %collective-permute-done.35 = bf16[48,768]{1,0:T(8,128)(2,1)S(1)} collective-permute-done((bf16[48,768]{1,0:T(8,128)(2,1)S(1)}, bf16[48,768]{1,0:T(8,128)(2,1)S(1)}, u32[]{:S(2)}, u32[]{:S(2)}) %collective-permute-start.35) | collective-permute-done | bytes 73760 | tf_op jit(solution)/shard_map/ppermute | solution.py:35
  48.3 4.2 %collective-permute-done.36 = bf16[48,768]{1,0:T(8,128)(2,1)S(1)} collective-permute-done((bf16[48,768]{1,0:T(8,128)(2,1)S(1)}, bf16[48,768]{1,0:T(8,128)(2,1)S(1)}, u32[]{:S(2)}, u32[]{:S(2)}) %collective-permute-start.36) | collective-permute-done | bytes 73760 | tf_op jit(solution)/shard_map/ppermute | solution.py:35
  52.6 1.4 collective-permute-start.8
  55.0 2.9 collective-permute-start.37
  57.9 1.7 constant_dynamic-update-slice_fusion.15
  60.1 1.7 constant_dynamic-update-slice_fusion.14
  65.4 4.7 %collective-permute-start.11 = (bf16[192,768]{1,0:T(8,128)(2,1)}, bf16[192,768]{1,0:T(8,128)(2,1)S(1)}, u32[]{:S(2)}, u32[]{:S(2)}) collective-permute-start(bf16[192,768]{1,0:T(8,128)(2,1)} %collective-permute-done.6), channel_id=1, source_target_pairs={{0,8},{2,10},{4,12},{6,14},{8,16},{10,18},{12,20},{14,22},{16,24},... | collective-permute-start | bytes 884744 | tf_op jit(solution)/shard_map/ppermute | solution.py:46
  71.5 1.8 select_dynamic-update-slice_fusion.11
  73.3 2.5 collective-permute-start.5
  76.8 4.5 %collective-permute-start.13 = (bf16[192,768]{1,0:T(8,128)(2,1)}, bf16[192,768]{1,0:T(8,128)(2,1)S(1)}, u32[]{:S(2)}, u32[]{:S(2)}) collective-permute-start(bf16[192,768]{1,0:T(8,128)(2,1)} %collective-permute-done.7), channel_id=1, source_target_pairs={{0,8},{2,10},{4,12},{6,14},{8,16},{10,18},{12,20},{14,22},{16,24},... | collective-permute-start | bytes 884744 | tf_op jit(solution)/shard_map/ppermute | solution.py:46
  83.4 4.6 %collective-permute-start.15 = (bf16[192,768]{1,0:T(8,128)(2,1)S(1)}, bf16[192,768]{1,0:T(8,128)(2,1)S(1)}, u32[]{:S(2)}, u32[]{:S(2)}) collective-permute-start(bf16[192,768]{1,0:T(8,128)(2,1)S(1)} %collective-permute-done.8), channel_id=1, source_target_pairs={{0,8},{2,10},{4,12},{6,14},{8,16},{10,18},{12,20},{14,22},{16,24},... | collective-permute-start | bytes 884744 | tf_op jit(solution)/shard_map/ppermute | solution.py:46
  87.9 2.1 constant_dynamic-update-slice_fusion.19
  90.0 5.5 %collective-permute-done.4 = bf16[256,1536]{1,0:T(8,128)(2,1)} collective-permute-done((bf16[256,1536]{1,0:T(8,128)(2,1)S(1)}, bf16[256,1536]{1,0:T(8,128)(2,1)}, u32[]{:S(2)}, u32[]{:S(2)}) %collective-permute-start.4) | collective-permute-done | bytes 786464 | tf_op jit(solution)/shard_map/ppermute | solution.py:35
  96.8 2.1 constant_dynamic-update-slice_fusion.18
  98.9 5.0 %collective-permute-start.17 = (bf16[192,768]{1,0:T(8,128)(2,1)}, bf16[192,768]{1,0:T(8,128)(2,1)S(1)}, u32[]{:S(2)}, u32[]{:S(2)}) collective-permute-start(bf16[192,768]{1,0:T(8,128)(2,1)} %collective-permute-done.9), channel_id=1, source_target_pairs={{0,8},{2,10},{4,12},{6,14},{8,16},{10,18},{12,20},{14,22},{16,24},... | collective-permute-start | bytes 884744 | tf_op jit(solution)/shard_map/ppermute | solution.py:46
  105.2 2.1 constant_dynamic-update-slice_fusion.17
  107.3 4.6 %collective-permute-start.38 = (bf16[192,768]{1,0:T(8,128)(2,1)S(1)}, bf16[192,768]{1,0:T(8,128)(2,1)S(1)}, u32[]{:S(2)}, u32[]{:S(2)}) collective-permute-start(bf16[192,768]{1,0:T(8,128)(2,1)S(1)} %collective-permute-done.37), channel_id=1, source_target_pairs={{0,8},{2,10},{4,12},{6,14},{8,16},{10,18},{12,20},{14,22},{16,24},... | collective-permute-start | bytes 884744 | tf_op jit(solution)/shard_map/ppermute | solution.py:46
  114.1 4.5 %collective-permute-start.19 = (bf16[192,768]{1,0:T(8,128)(2,1)S(1)}, bf16[192,768]{1,0:T(8,128)(2,1)S(1)}, u32[]{:S(2)}, u32[]{:S(2)}) collective-permute-start(bf16[192,768]{1,0:T(8,128)(2,1)S(1)} %collective-permute-done.11), channel_id=1, source_target_pairs={{0,8},{2,10},{4,12},{6,14},{8,16},{10,18},{12,20},{14,22},{16,24},... | collective-permute-start | bytes 884744 | tf_op jit(solution)/shard_map/ppermute | solution.py:46
  120.7 4.7 %collective-permute-start.21 = (bf16[192,768]{1,0:T(8,128)(2,1)S(1)}, bf16[192,768]{1,0:T(8,128)(2,1)S(1)}, u32[]{:S(2)}, u32[]{:S(2)}) collective-permute-start(bf16[192,768]{1,0:T(8,128)(2,1)S(1)} %collective-permute-done.13), channel_id=1, source_target_pairs={{0,8},{2,10},{4,12},{6,14},{8,16},{10,18},{12,20},{14,22},{16,24},... | collective-permute-start | bytes 884744 | tf_op jit(solution)/shard_map/ppermute | solution.py:46
  127.6 5.5 %collective-permute-start.23 = (bf16[192,768]{1,0:T(8,128)(2,1)S(1)}, bf16[192,768]{1,0:T(8,128)(2,1)S(1)}, u32[]{:S(2)}, u32[]{:S(2)}) collective-permute-start(bf16[192,768]{1,0:T(8,128)(2,1)S(1)} %collective-permute-done.15), channel_id=1, source_target_pairs={{0,8},{2,10},{4,12},{6,14},{8,16},{10,18},{12,20},{14,22},{16,24},... | collective-permute-start | bytes 884744 | tf_op jit(solution)/shard_map/ppermute | solution.py:46
  135.2 4.6 %collective-permute-start.25 = (bf16[192,768]{1,0:T(8,128)(2,1)S(1)}, bf16[192,768]{1,0:T(8,128)(2,1)S(1)}, u32[]{:S(2)}, u32[]{:S(2)}) collective-permute-start(bf16[192,768]{1,0:T(8,128)(2,1)S(1)} %collective-permute-done.17), channel_id=1, source_target_pairs={{0,8},{2,10},{4,12},{6,14},{8,16},{10,18},{12,20},{14,22},{16,24},... | collective-permute-start | bytes 884744 | tf_op jit(solution)/shard_map/ppermute | solution.py:46
  142.0 4.6 %collective-permute-start.39 = (bf16[192,768]{1,0:T(8,128)(2,1)S(1)}, bf16[192,768]{1,0:T(8,128)(2,1)S(1)}, u32[]{:S(2)}, u32[]{:S(2)}) collective-permute-start(bf16[192,768]{1,0:T(8,128)(2,1)S(1)} %collective-permute-done.38), channel_id=1, source_target_pairs={{0,8},{2,10},{4,12},{6,14},{8,16},{10,18},{12,20},{14,22},{16,24},... | collective-permute-start | bytes 884744 | tf_op jit(solution)/shard_map/ppermute | solution.py:46
  148.7 4.6 %collective-permute-start.27 = (bf16[192,768]{1,0:T(8,128)(2,1)S(1)}, bf16[192,768]{1,0:T(8,128)(2,1)S(1)}, u32[]{:S(2)}, u32[]{:S(2)}) collective-permute-start(bf16[192,768]{1,0:T(8,128)(2,1)S(1)} %collective-permute-done.19), channel_id=1, source_target_pairs={{0,8},{2,10},{4,12},{6,14},{8,16},{10,18},{12,20},{14,22},{16,24},... | collective-permute-start | bytes 884744 | tf_op jit(solution)/shard_map/ppermute | solution.py:46
  155.4 4.6 %collective-permute-start.29 = (bf16[192,768]{1,0:T(8,128)(2,1)S(1)}, bf16[192,768]{1,0:T(8,128)(2,1)S(1)}, u32[]{:S(2)}, u32[]{:S(2)}) collective-permute-start(bf16[192,768]{1,0:T(8,128)(2,1)S(1)} %collective-permute-done.21), channel_id=1, source_target_pairs={{0,8},{2,10},{4,12},{6,14},{8,16},{10,18},{12,20},{14,22},{16,24},... | collective-permute-start | bytes 884744 | tf_op jit(solution)/shard_map/ppermute | solution.py:46
  163.0 1.4 copy.75
  164.4 1.4 copy.78
  165.9 4.6 %collective-permute-start.31 = (bf16[192,768]{1,0:T(8,128)(2,1)S(1)}, bf16[192,768]{1,0:T(8,128)(2,1)S(1)}, u32[]{:S(2)}, u32[]{:S(2)}) collective-permute-start(bf16[192,768]{1,0:T(8,128)(2,1)S(1)} %collective-permute-done.23), channel_id=1, source_target_pairs={{0,8},{2,10},{4,12},{6,14},{8,16},{10,18},{12,20},{14,22},{16,24},... | collective-permute-start | bytes 884744 | tf_op jit(solution)/shard_map/ppermute | solution.py:46
  170.5 1.5 collective-permute-start.32
  171.9 1.8 select_dynamic-update-slice_fusion.2
  173.8 1.5 collective-permute-start
  175.3 1.5 collective-permute-start.1
  176.8 1.8 select_dynamic-update-slice_fusion.1
  180.0 5.5 %fusion.2 = f32[1024,768]{0,1:T(8,128)S(1)} fusion(bf16[1024,1536]{1,0:T(8,128)(2,1)} %collective-permute-done.33, bf16[3072,768]{1,0:T(8,128)(2,1)} %select_dynamic-update-slice_fusion, s32[]{:T(128)S(6)} %select_n.541), kind=kOutput, calls=%fused_computation.6 | convolution fusion | flops 2415919104 | bytes 8650756 | tf_op jit(solution)/shard_map/dot_general | solution.py:93
  185.9 5.6 %collective-permute-done.1 = bf16[256,768]{0,1:T(8,128)(2,1)S(1)} collective-permute-done((bf16[256,768]{0,1:T(8,128)(2,1)}, bf16[256,768]{0,1:T(8,128)(2,1)S(1)}, u32[]{:S(2)}, u32[]{:S(2)}) %collective-permute-start.1) | collective-permute-done | bytes 393248 | tf_op jit(solution)/shard_map/ppermute | solution.py:35
  191.5 5.5 %convert_reduce_fusion = (f32[1024]{0:T(1024)}, f32[1024]{0:T(1024)}, bf16[1024,768]{0,1:T(8,128)(2,1)S(1)}) fusion(f32[1024,768]{0,1:T(8,128)S(1)} %fusion.2, bf16[1024,1536]{1,0:T(8,128)(2,1)S(1)} %copy-done.23, bf16[3072,768]{1,0:T(8,128)(2,1)} %select_dynamic-update-slice_fusion, s32[]{:T(128)S(6)} %select_n.540, ...), kind=kOutput, calls=%fused_computation.1 | convolution fusion | flops 2427713536 | bytes 11804676 | tf_op jit(solution)/shard_map/dot_general | solution.py:93
  197.7 1.5 fusion.85
  199.1 1.5 fusion.88
  201.3 1.8 reshape.181
  203.2 3.3 %constant_dynamic-slice_fusion.11 = (f32[4,1,128,192]{2,1,0,3:T(1,128)}, f32[4,128,192]{1,0,2:T(4,128)S(1)}, f32[4,128,192]{1,0,2:T(4,128)S(1)}, f32[4,1,128,192]{2,1,0,3:T(1,128)}) fusion(f32[4,2,128,192]{2,1,0,3:T(2,128)S(1)} %reshape.181, s32[]{:T(128)S(6)} %select_n.552, s32[]{:T(128)S(6)} %select_n.553, f32[4,2,128,192]{2,1,0,3:T(2,128)S(1)} %reshape.178), kind=kLoop, calls=%fused_computation.150 | loop fusion | bytes 3145736 | tf_op jit(solution)/shard_map/jit(dynamic_index_in_dim)/dynamic_slice | solution.py:129
  210.7 3.1 %constant_dynamic-slice_fusion.9 = (f32[4,1,128,192]{2,1,0,3:T(1,128)}, f32[4,128,192]{1,0,2:T(4,128)S(1)}, f32[4,128,192]{1,0,2:T(4,128)S(1)}, f32[4,1,128,192]{2,1,0,3:T(1,128)}) fusion(f32[4,2,128,192]{2,1,0,3:T(2,128)S(1)} %reshape.187, s32[]{:T(128)S(6)} %select_n.552, s32[]{:T(128)S(6)} %select_n.553, f32[4,2,128,192]{2,1,0,3:T(2,128)S(1)} %reshape.184), kind=kLoop, calls=%fused_computation.148 | loop fusion | bytes 3145736 | tf_op jit(solution)/shard_map/jit(dynamic_index_in_dim)/dynamic_slice | solution.py:129
  217.2 1.5 collective-permute-start.62
  230.3 1.5 collective-permute-start.46
  237.6 1.7 collective-permute-start.52
  239.4 1.5 collective-permute-start.53
  243.5 1.8 collective-permute-start.56
  250.5 2.3 collective-permute-done.56
  253.2 2.4 collective-permute-done.58
  259.6 2.0 collective-permute-done.63
  265.3 3.2 %collective-permute-done.64 = f32[96,384]{1,0:T(8,128)S(1)} collective-permute-done((f32[96,384]{1,0:T(8,128)S(1)}, f32[96,384]{1,0:T(8,128)S(1)}, u32[]{:S(2)}, u32[]{:S(2)}) %collective-permute-start.64) | collective-permute-done | bytes 147488 | tf_op jit(solution)/shard_map/ppermute | solution.py:35
  268.5 3.1 %collective-permute-done.65 = f32[96,384]{1,0:T(8,128)S(1)} collective-permute-done((f32[96,384]{1,0:T(8,128)S(1)}, f32[96,384]{1,0:T(8,128)S(1)}, u32[]{:S(2)}, u32[]{:S(2)}) %collective-permute-start.65) | collective-permute-done | bytes 147488 | tf_op jit(solution)/shard_map/ppermute | solution.py:35
  271.6 1.5 collective-permute-start.67
  273.1 4.3 %collective-permute-start.68 = (f32[24,384]{1,0:T(8,128)S(1)}, f32[24,384]{1,0:T(8,128)S(1)}, u32[]{:S(2)}, u32[]{:S(2)}) collective-permute-start(f32[24,384]{1,0:T(8,128)S(1)} %get-tuple-element.62), channel_id=1, source_target_pairs={{0,16},{2,18},{4,20},{6,22},{8,24},{10,26},{12,28},{14,30},{16,0},... | collective-permute-start | bytes 110600 | tf_op jit(solution)/shard_map/ppermute | solution.py:180
  279.5 1.9 collective-permute-done.69
  281.6 3.5 %collective-permute-start.71 = (f32[24,384]{1,0:T(8,128)S(1)}, f32[24,384]{1,0:T(8,128)S(1)}, u32[]{:S(2)}, u32[]{:S(2)}) collective-permute-start(f32[24,384]{1,0:T(8,128)S(1)} %get-tuple-element.6), channel_id=1, source_target_pairs={{0,16},{2,18},{4,20},{6,22},{8,24},{10,26},{12,28},{14,30},{16,0},... | collective-permute-start | bytes 110600 | tf_op jit(solution)/shard_map/ppermute | solution.py:180
  285.3 2.0 collective-permute-done.70
  291.0 1.6 collective-permute-start.75
  292.7 1.6 collective-permute-done.73
  295.3 1.7 collective-permute-done.75
  297.3 1.8 collective-permute-done.76
  (306 shorter events, 98.4 us)
Async XLA Ops:
  6.5 57.7 %collective-permute-start.10 = (bf16[192,768]{1,0:T(8,128)(2,1)}, bf16[192,768]{1,0:T(8,128)(2,1)}, u32[]{:S(2)}, u32[]{:S(2)}) collective-permute-start(bf16[192,768]{1,0:T(8,128)(2,1)} %get-tuple-element.27), channel_id=1, source_target_pairs={{8,0},{10,2},{12,4},{14,6},{16,8},{18,10},{20,12},{22,14},{24,16},... | collective-permute-start | bytes 884744 | tf_op jit(solution)/shard_map/ppermute | solution.py:47
  7.8 57.6 %collective-permute-start.9 = (bf16[192,768]{1,0:T(8,128)(2,1)}, bf16[192,768]{1,0:T(8,128)(2,1)}, u32[]{:S(2)}, u32[]{:S(2)}) collective-permute-start(bf16[192,768]{1,0:T(8,128)(2,1)} %get-tuple-element.27), channel_id=1, source_target_pairs={{0,8},{2,10},{4,12},{6,14},{8,16},{10,18},{12,20},{14,22},{16,24},... | collective-permute-start | bytes 884744 | tf_op jit(solution)/shard_map/ppermute | solution.py:46
  14.1 40.9 %collective-permute-start.6 = (bf16[192,768]{1,0:T(8,128)(2,1)}, bf16[192,768]{1,0:T(8,128)(2,1)}, u32[]{:S(2)}, u32[]{:S(2)}) collective-permute-start(bf16[192,768]{1,0:T(8,128)(2,1)} %get-tuple-element.25), channel_id=1, source_target_pairs={{0,2},{2,0},{4,6},{6,4},{8,10},{10,8},{12,14},{14,12},{16,18},{18,... | collective-permute-start | bytes 884744 | tf_op jit(solution)/shard_map/ppermute | solution.py:35
  16.0 43.6 %collective-permute-start.7 = (bf16[192,768]{1,0:T(8,128)(2,1)}, bf16[192,768]{1,0:T(8,128)(2,1)}, u32[]{:S(2)}, u32[]{:S(2)}) collective-permute-start(bf16[192,768]{1,0:T(8,128)(2,1)} %get-tuple-element.28), channel_id=1, source_target_pairs={{0,4},{2,6},{4,0},{6,2},{8,12},{10,14},{12,8},{14,10},{16,20},{18,... | collective-permute-start | bytes 884744 | tf_op jit(solution)/shard_map/ppermute | solution.py:35
  18.3 24.2 %collective-permute-start.34 = (bf16[48,768]{1,0:T(8,128)(2,1)}, bf16[48,768]{1,0:T(8,128)(2,1)S(1)}, u32[]{:S(2)}, u32[]{:S(2)}) collective-permute-start(bf16[48,768]{1,0:T(8,128)(2,1)} %get-tuple-element.58), channel_id=1, source_target_pairs={{0,2},{2,0},{4,6},{6,4},{8,10},{10,8},{12,14},{14,12},{16,18},{18,... | collective-permute-start | bytes 221192 | tf_op jit(solution)/shard_map/ppermute | solution.py:35
  52.6 9.6 %collective-permute-start.8 = (bf16[192,768]{1,0:T(8,128)(2,1)S(1)}, bf16[192,768]{1,0:T(8,128)(2,1)S(1)}, u32[]{:S(2)}, u32[]{:S(2)}) collective-permute-start(bf16[192,768]{1,0:T(8,128)(2,1)S(1)} %copy-done.18), channel_id=1, source_target_pairs={{0,6},{2,4},{4,2},{6,0},{8,14},{10,12},{12,10},{14,8},{16,22},{18,... | collective-permute-start | bytes 884744 | tf_op jit(solution)/shard_map/ppermute | solution.py:35
  55.0 15.2 %collective-permute-start.37 = (bf16[192,768]{1,0:T(8,128)(2,1)S(1)}, bf16[192,768]{1,0:T(8,128)(2,1)S(1)}, u32[]{:S(2)}, u32[]{:S(2)}) collective-permute-start(bf16[192,768]{1,0:T(8,128)(2,1)S(1)} %constant_dynamic-update-slice_fusion.10), channel_id=1, source_target_pairs={{0,8},{2,10},{4,12},{6,14},{8,16},{10,18},{12,20},{14,22},{16,24},... | collective-permute-start | bytes 884744 | tf_op jit(solution)/shard_map/ppermute | solution.py:46
  59.6 23.8 %collective-permute-start.3 = (bf16[256,1536]{1,0:T(8,128)(2,1)S(1)}, bf16[256,1536]{1,0:T(8,128)(2,1)}, u32[]{:S(2)}, u32[]{:S(2)}) collective-permute-start(bf16[256,1536]{1,0:T(8,128)(2,1)S(1)} %copy-done.11), channel_id=1, source_target_pairs={{0,2},{2,0},{4,6},{6,4},{8,10},{10,8},{12,14},{14,12},{16,18},{18,... | collective-permute-start | bytes 2359304 | tf_op jit(solution)/shard_map/ppermute | solution.py:35
  62.2 11.1 %collective-permute-start.40 = (bf16[192,768]{1,0:T(8,128)(2,1)S(1)}, bf16[192,768]{1,0:T(8,128)(2,1)S(1)}, u32[]{:S(2)}, u32[]{:S(2)}) collective-permute-start(bf16[192,768]{1,0:T(8,128)(2,1)S(1)} %constant_dynamic-update-slice_fusion.10), channel_id=1, source_target_pairs={{8,0},{10,2},{12,4},{14,6},{16,8},{18,10},{20,12},{22,14},{24,16},... | collective-permute-start | bytes 884744 | tf_op jit(solution)/shard_map/ppermute | solution.py:47
  64.2 31.3 %collective-permute-start.4 = (bf16[256,1536]{1,0:T(8,128)(2,1)S(1)}, bf16[256,1536]{1,0:T(8,128)(2,1)}, u32[]{:S(2)}, u32[]{:S(2)}) collective-permute-start(bf16[256,1536]{1,0:T(8,128)(2,1)S(1)} %copy-done.11), channel_id=1, source_target_pairs={{0,4},{2,6},{4,0},{6,2},{8,12},{10,14},{12,8},{14,10},{16,20},{18,... | collective-permute-start | bytes 2359304 | tf_op jit(solution)/shard_map/ppermute | solution.py:35
  65.4 11.4 %collective-permute-start.11 = (bf16[192,768]{1,0:T(8,128)(2,1)}, bf16[192,768]{1,0:T(8,128)(2,1)S(1)}, u32[]{:S(2)}, u32[]{:S(2)}) collective-permute-start(bf16[192,768]{1,0:T(8,128)(2,1)} %collective-permute-done.6), channel_id=1, source_target_pairs={{0,8},{2,10},{4,12},{6,14},{8,16},{10,18},{12,20},{14,22},{16,24},... | collective-permute-start | bytes 884744 | tf_op jit(solution)/shard_map/ppermute | solution.py:46
  70.2 11.1 %collective-permute-start.12 = (bf16[192,768]{1,0:T(8,128)(2,1)}, bf16[192,768]{1,0:T(8,128)(2,1)S(1)}, u32[]{:S(2)}, u32[]{:S(2)}) collective-permute-start(bf16[192,768]{1,0:T(8,128)(2,1)} %collective-permute-done.6), channel_id=1, source_target_pairs={{8,0},{10,2},{12,4},{14,6},{16,8},{18,10},{20,12},{22,14},{24,16},... | collective-permute-start | bytes 884744 | tf_op jit(solution)/shard_map/ppermute | solution.py:47
  73.3 30.6 %collective-permute-start.5 = (bf16[256,1536]{1,0:T(8,128)(2,1)S(1)}, bf16[256,1536]{1,0:T(8,128)(2,1)}, u32[]{:S(2)}, u32[]{:S(2)}) collective-permute-start(bf16[256,1536]{1,0:T(8,128)(2,1)S(1)} %copy-done.11), channel_id=1, source_target_pairs={{0,6},{2,4},{4,2},{6,0},{8,14},{10,12},{12,10},{14,8},{16,22},{18,... | collective-permute-start | bytes 2359304 | tf_op jit(solution)/shard_map/ppermute | solution.py:35
  76.8 22.1 %collective-permute-start.13 = (bf16[192,768]{1,0:T(8,128)(2,1)}, bf16[192,768]{1,0:T(8,128)(2,1)S(1)}, u32[]{:S(2)}, u32[]{:S(2)}) collective-permute-start(bf16[192,768]{1,0:T(8,128)(2,1)} %collective-permute-done.7), channel_id=1, source_target_pairs={{0,8},{2,10},{4,12},{6,14},{8,16},{10,18},{12,20},{14,22},{16,24},... | collective-permute-start | bytes 884744 | tf_op jit(solution)/shard_map/ppermute | solution.py:46
  81.3 26.0 %collective-permute-start.14 = (bf16[192,768]{1,0:T(8,128)(2,1)}, bf16[192,768]{1,0:T(8,128)(2,1)S(1)}, u32[]{:S(2)}, u32[]{:S(2)}) collective-permute-start(bf16[192,768]{1,0:T(8,128)(2,1)} %collective-permute-done.7), channel_id=1, source_target_pairs={{8,0},{10,2},{12,4},{14,6},{16,8},{18,10},{20,12},{22,14},{24,16},... | collective-permute-start | bytes 884744 | tf_op jit(solution)/shard_map/ppermute | solution.py:47
  83.4 28.5 %collective-permute-start.15 = (bf16[192,768]{1,0:T(8,128)(2,1)S(1)}, bf16[192,768]{1,0:T(8,128)(2,1)S(1)}, u32[]{:S(2)}, u32[]{:S(2)}) collective-permute-start(bf16[192,768]{1,0:T(8,128)(2,1)S(1)} %collective-permute-done.8), channel_id=1, source_target_pairs={{0,8},{2,10},{4,12},{6,14},{8,16},{10,18},{12,20},{14,22},{16,24},... | collective-permute-start | bytes 884744 | tf_op jit(solution)/shard_map/ppermute | solution.py:46
  95.5 17.6 %collective-permute-start.16 = (bf16[192,768]{1,0:T(8,128)(2,1)S(1)}, bf16[192,768]{1,0:T(8,128)(2,1)S(1)}, u32[]{:S(2)}, u32[]{:S(2)}) collective-permute-start(bf16[192,768]{1,0:T(8,128)(2,1)S(1)} %collective-permute-done.8), channel_id=1, source_target_pairs={{8,0},{10,2},{12,4},{14,6},{16,8},{18,10},{20,12},{22,14},{24,16},... | collective-permute-start | bytes 884744 | tf_op jit(solution)/shard_map/ppermute | solution.py:47
  98.9 15.2 %collective-permute-start.17 = (bf16[192,768]{1,0:T(8,128)(2,1)}, bf16[192,768]{1,0:T(8,128)(2,1)S(1)}, u32[]{:S(2)}, u32[]{:S(2)}) collective-permute-start(bf16[192,768]{1,0:T(8,128)(2,1)} %collective-permute-done.9), channel_id=1, source_target_pairs={{0,8},{2,10},{4,12},{6,14},{8,16},{10,18},{12,20},{14,22},{16,24},... | collective-permute-start | bytes 884744 | tf_op jit(solution)/shard_map/ppermute | solution.py:46
  103.9 14.7 %collective-permute-start.18 = (bf16[192,768]{1,0:T(8,128)(2,1)}, bf16[192,768]{1,0:T(8,128)(2,1)S(1)}, u32[]{:S(2)}, u32[]{:S(2)}) collective-permute-start(bf16[192,768]{1,0:T(8,128)(2,1)} %collective-permute-done.10), channel_id=1, source_target_pairs={{8,0},{10,2},{12,4},{14,6},{16,8},{18,10},{20,12},{22,14},{24,16},... | collective-permute-start | bytes 884744 | tf_op jit(solution)/shard_map/ppermute | solution.py:47
  107.3 13.4 %collective-permute-start.38 = (bf16[192,768]{1,0:T(8,128)(2,1)S(1)}, bf16[192,768]{1,0:T(8,128)(2,1)S(1)}, u32[]{:S(2)}, u32[]{:S(2)}) collective-permute-start(bf16[192,768]{1,0:T(8,128)(2,1)S(1)} %collective-permute-done.37), channel_id=1, source_target_pairs={{0,8},{2,10},{4,12},{6,14},{8,16},{10,18},{12,20},{14,22},{16,24},... | collective-permute-start | bytes 884744 | tf_op jit(solution)/shard_map/ppermute | solution.py:46
  111.9 13.6 %collective-permute-start.41 = (bf16[192,768]{1,0:T(8,128)(2,1)S(1)}, bf16[192,768]{1,0:T(8,128)(2,1)S(1)}, u32[]{:S(2)}, u32[]{:S(2)}) collective-permute-start(bf16[192,768]{1,0:T(8,128)(2,1)S(1)} %collective-permute-done.40), channel_id=1, source_target_pairs={{8,0},{10,2},{12,4},{14,6},{16,8},{18,10},{20,12},{22,14},{24,16},... | collective-permute-start | bytes 884744 | tf_op jit(solution)/shard_map/ppermute | solution.py:47
  113.2 66.8 %collective-permute-start.33 = (bf16[1024,1536]{1,0:T(8,128)(2,1)}, bf16[1024,1536]{1,0:T(8,128)(2,1)}, u32[]{:S(2)}, u32[]{:S(2)}) collective-permute-start(bf16[1024,1536]{1,0:T(8,128)(2,1)} %constant_dynamic-update-slice_fusion.17), channel_id=1, source_target_pairs={{0,1},{1,0},{2,3},{3,2},{4,5},{5,4},{6,7},{7,6},{8,9},{9,8},{10,11... | collective-permute-start | bytes 9437192 | tf_op jit(solution)/shard_map/ppermute | solution.py:38
  114.1 13.5 %collective-permute-start.19 = (bf16[192,768]{1,0:T(8,128)(2,1)S(1)}, bf16[192,768]{1,0:T(8,128)(2,1)S(1)}, u32[]{:S(2)}, u32[]{:S(2)}) collective-permute-start(bf16[192,768]{1,0:T(8,128)(2,1)S(1)} %collective-permute-done.11), channel_id=1, source_target_pairs={{0,8},{2,10},{4,12},{6,14},{8,16},{10,18},{12,20},{14,22},{16,24},... | collective-permute-start | bytes 884744 | tf_op jit(solution)/shard_map/ppermute | solution.py:46
  118.6 14.5 %collective-permute-start.20 = (bf16[192,768]{1,0:T(8,128)(2,1)S(1)}, bf16[192,768]{1,0:T(8,128)(2,1)S(1)}, u32[]{:S(2)}, u32[]{:S(2)}) collective-permute-start(bf16[192,768]{1,0:T(8,128)(2,1)S(1)} %collective-permute-done.12), channel_id=1, source_target_pairs={{8,0},{10,2},{12,4},{14,6},{16,8},{18,10},{20,12},{22,14},{24,16},... | collective-permute-start | bytes 884744 | tf_op jit(solution)/shard_map/ppermute | solution.py:47
  120.7 14.5 %collective-permute-start.21 = (bf16[192,768]{1,0:T(8,128)(2,1)S(1)}, bf16[192,768]{1,0:T(8,128)(2,1)S(1)}, u32[]{:S(2)}, u32[]{:S(2)}) collective-permute-start(bf16[192,768]{1,0:T(8,128)(2,1)S(1)} %collective-permute-done.13), channel_id=1, source_target_pairs={{0,8},{2,10},{4,12},{6,14},{8,16},{10,18},{12,20},{14,22},{16,24},... | collective-permute-start | bytes 884744 | tf_op jit(solution)/shard_map/ppermute | solution.py:46
  125.4 14.4 %collective-permute-start.22 = (bf16[192,768]{1,0:T(8,128)(2,1)S(1)}, bf16[192,768]{1,0:T(8,128)(2,1)S(1)}, u32[]{:S(2)}, u32[]{:S(2)}) collective-permute-start(bf16[192,768]{1,0:T(8,128)(2,1)S(1)} %collective-permute-done.14), channel_id=1, source_target_pairs={{8,0},{10,2},{12,4},{14,6},{16,8},{18,10},{20,12},{22,14},{24,16},... | collective-permute-start | bytes 884744 | tf_op jit(solution)/shard_map/ppermute | solution.py:47
  127.6 14.4 %collective-permute-start.23 = (bf16[192,768]{1,0:T(8,128)(2,1)S(1)}, bf16[192,768]{1,0:T(8,128)(2,1)S(1)}, u32[]{:S(2)}, u32[]{:S(2)}) collective-permute-start(bf16[192,768]{1,0:T(8,128)(2,1)S(1)} %collective-permute-done.15), channel_id=1, source_target_pairs={{0,8},{2,10},{4,12},{6,14},{8,16},{10,18},{12,20},{14,22},{16,24},... | collective-permute-start | bytes 884744 | tf_op jit(solution)/shard_map/ppermute | solution.py:46
  133.1 13.4 %collective-permute-start.24 = (bf16[192,768]{1,0:T(8,128)(2,1)S(1)}, bf16[192,768]{1,0:T(8,128)(2,1)S(1)}, u32[]{:S(2)}, u32[]{:S(2)}) collective-permute-start(bf16[192,768]{1,0:T(8,128)(2,1)S(1)} %collective-permute-done.16), channel_id=1, source_target_pairs={{8,0},{10,2},{12,4},{14,6},{16,8},{18,10},{20,12},{22,14},{24,16},... | collective-permute-start | bytes 884744 | tf_op jit(solution)/shard_map/ppermute | solution.py:47
  135.2 13.4 %collective-permute-start.25 = (bf16[192,768]{1,0:T(8,128)(2,1)S(1)}, bf16[192,768]{1,0:T(8,128)(2,1)S(1)}, u32[]{:S(2)}, u32[]{:S(2)}) collective-permute-start(bf16[192,768]{1,0:T(8,128)(2,1)S(1)} %collective-permute-done.17), channel_id=1, source_target_pairs={{0,8},{2,10},{4,12},{6,14},{8,16},{10,18},{12,20},{14,22},{16,24},... | collective-permute-start | bytes 884744 | tf_op jit(solution)/shard_map/ppermute | solution.py:46
  139.8 13.4 %collective-permute-start.26 = (bf16[192,768]{1,0:T(8,128)(2,1)S(1)}, bf16[192,768]{1,0:T(8,128)(2,1)S(1)}, u32[]{:S(2)}, u32[]{:S(2)}) collective-permute-start(bf16[192,768]{1,0:T(8,128)(2,1)S(1)} %collective-permute-done.18), channel_id=1, source_target_pairs={{8,0},{10,2},{12,4},{14,6},{16,8},{18,10},{20,12},{22,14},{24,16},... | collective-permute-start | bytes 884744 | tf_op jit(solution)/shard_map/ppermute | solution.py:47
  142.0 13.4 %collective-permute-start.39 = (bf16[192,768]{1,0:T(8,128)(2,1)S(1)}, bf16[192,768]{1,0:T(8,128)(2,1)S(1)}, u32[]{:S(2)}, u32[]{:S(2)}) collective-permute-start(bf16[192,768]{1,0:T(8,128)(2,1)S(1)} %collective-permute-done.38), channel_id=1, source_target_pairs={{0,8},{2,10},{4,12},{6,14},{8,16},{10,18},{12,20},{14,22},{16,24},... | collective-permute-start | bytes 884744 | tf_op jit(solution)/shard_map/ppermute | solution.py:46
  146.5 13.4 %collective-permute-start.42 = (bf16[192,768]{1,0:T(8,128)(2,1)S(1)}, bf16[192,768]{1,0:T(8,128)(2,1)S(1)}, u32[]{:S(2)}, u32[]{:S(2)}) collective-permute-start(bf16[192,768]{1,0:T(8,128)(2,1)S(1)} %collective-permute-done.41), channel_id=1, source_target_pairs={{8,0},{10,2},{12,4},{14,6},{16,8},{18,10},{20,12},{22,14},{24,16},... | collective-permute-start | bytes 884744 | tf_op jit(solution)/shard_map/ppermute | solution.py:47
  148.7 17.2 %collective-permute-start.27 = (bf16[192,768]{1,0:T(8,128)(2,1)S(1)}, bf16[192,768]{1,0:T(8,128)(2,1)S(1)}, u32[]{:S(2)}, u32[]{:S(2)}) collective-permute-start(bf16[192,768]{1,0:T(8,128)(2,1)S(1)} %collective-permute-done.19), channel_id=1, source_target_pairs={{0,8},{2,10},{4,12},{6,14},{8,16},{10,18},{12,20},{14,22},{16,24},... | collective-permute-start | bytes 884744 | tf_op jit(solution)/shard_map/ppermute | solution.py:46
  153.2 17.2 %collective-permute-start.28 = (bf16[192,768]{1,0:T(8,128)(2,1)S(1)}, bf16[192,768]{1,0:T(8,128)(2,1)}, u32[]{:S(2)}, u32[]{:S(2)}) collective-permute-start(bf16[192,768]{1,0:T(8,128)(2,1)S(1)} %collective-permute-done.20), channel_id=1, source_target_pairs={{8,0},{10,2},{12,4},{14,6},{16,8},{18,10},{20,12},{22,14},{24,16},... | collective-permute-start | bytes 884744 | tf_op jit(solution)/shard_map/ppermute | solution.py:47
  155.4 18.4 %collective-permute-start.29 = (bf16[192,768]{1,0:T(8,128)(2,1)S(1)}, bf16[192,768]{1,0:T(8,128)(2,1)S(1)}, u32[]{:S(2)}, u32[]{:S(2)}) collective-permute-start(bf16[192,768]{1,0:T(8,128)(2,1)S(1)} %collective-permute-done.21), channel_id=1, source_target_pairs={{0,8},{2,10},{4,12},{6,14},{8,16},{10,18},{12,20},{14,22},{16,24},... | collective-permute-start | bytes 884744 | tf_op jit(solution)/shard_map/ppermute | solution.py:46
  160.0 15.4 %collective-permute-start.30 = (bf16[192,768]{1,0:T(8,128)(2,1)S(1)}, bf16[192,768]{1,0:T(8,128)(2,1)}, u32[]{:S(2)}, u32[]{:S(2)}) collective-permute-start(bf16[192,768]{1,0:T(8,128)(2,1)S(1)} %collective-permute-done.22), channel_id=1, source_target_pairs={{8,0},{10,2},{12,4},{14,6},{16,8},{18,10},{20,12},{22,14},{24,16},... | collective-permute-start | bytes 884744 | tf_op jit(solution)/shard_map/ppermute | solution.py:47
  165.9 12.7 %collective-permute-start.31 = (bf16[192,768]{1,0:T(8,128)(2,1)S(1)}, bf16[192,768]{1,0:T(8,128)(2,1)S(1)}, u32[]{:S(2)}, u32[]{:S(2)}) collective-permute-start(bf16[192,768]{1,0:T(8,128)(2,1)S(1)} %collective-permute-done.23), channel_id=1, source_target_pairs={{0,8},{2,10},{4,12},{6,14},{8,16},{10,18},{12,20},{14,22},{16,24},... | collective-permute-start | bytes 884744 | tf_op jit(solution)/shard_map/ppermute | solution.py:46
  170.5 8.6 %collective-permute-start.32 = (bf16[192,768]{1,0:T(8,128)(2,1)S(1)}, bf16[192,768]{1,0:T(8,128)(2,1)S(1)}, u32[]{:S(2)}, u32[]{:S(2)}) collective-permute-start(bf16[192,768]{1,0:T(8,128)(2,1)S(1)} %collective-permute-done.24), channel_id=1, source_target_pairs={{8,0},{10,2},{12,4},{14,6},{16,8},{18,10},{20,12},{22,14},{24,16},... | collective-permute-start | bytes 884744 | tf_op jit(solution)/shard_map/ppermute | solution.py:47
  173.8 12.1 %collective-permute-start = (bf16[256,768]{0,1:T(8,128)(2,1)}, bf16[256,768]{0,1:T(8,128)(2,1)S(1)}, u32[]{:S(2)}, u32[]{:S(2)}) collective-permute-start(bf16[256,768]{0,1:T(8,128)(2,1)} %copy.90), channel_id=1, source_target_pairs={{0,2},{2,0},{4,6},{6,4},{8,10},{10,8},{12,14},{14,12},{16,18},{18,... | collective-permute-start | bytes 1179656 | tf_op jit(solution)/shard_map/ppermute | solution.py:35
  175.3 16.2 %collective-permute-start.1 = (bf16[256,768]{0,1:T(8,128)(2,1)}, bf16[256,768]{0,1:T(8,128)(2,1)S(1)}, u32[]{:S(2)}, u32[]{:S(2)}) collective-permute-start(bf16[256,768]{0,1:T(8,128)(2,1)} %copy.91), channel_id=1, source_target_pairs={{0,4},{2,6},{4,0},{6,2},{8,12},{10,14},{12,8},{14,10},{16,20},{18,... | collective-permute-start | bytes 1179656 | tf_op jit(solution)/shard_map/ppermute | solution.py:35
  178.6 12.9 %collective-permute-start.2 = (bf16[256,768]{0,1:T(8,128)(2,1)}, bf16[256,768]{0,1:T(8,128)(2,1)S(1)}, u32[]{:S(2)}, u32[]{:S(2)}) collective-permute-start(bf16[256,768]{0,1:T(8,128)(2,1)} %copy.92), channel_id=1, source_target_pairs={{0,6},{2,4},{4,2},{6,0},{8,14},{10,12},{12,10},{14,8},{16,22},{18,... | collective-permute-start | bytes 1179656 | tf_op jit(solution)/shard_map/ppermute | solution.py:35
  207.3 14.7 %collective-permute-start.43 = (f32[520,192]{0,1:T(8,128)}, f32[520,192]{0,1:T(8,128)}, u32[]{:S(2)}, u32[]{:S(2)}) collective-permute-start(f32[520,192]{0,1:T(8,128)} %pad_maximum_fusion), channel_id=1, source_target_pairs={{0,1},{1,0},{2,3},{3,2},{4,5},{5,4},{6,7},{7,6},{8,9},{9,8},{10,11... | collective-permute-start | bytes 1198088 | tf_op jit(solution)/shard_map/ppermute | solution.py:38
  208.2 15.8 %collective-permute-start.47 = (f32[520,192]{0,1:T(8,128)}, f32[520,192]{0,1:T(8,128)}, u32[]{:S(2)}, u32[]{:S(2)}) collective-permute-start(f32[520,192]{0,1:T(8,128)} %pad_maximum_fusion.1), channel_id=1, source_target_pairs={{0,1},{1,0},{2,3},{3,2},{4,5},{5,4},{6,7},{7,6},{8,9},{9,8},{10,11... | collective-permute-start | bytes 1198088 | tf_op jit(solution)/shard_map/ppermute | solution.py:38
  215.1 6.2 %collective-permute-start.60 = (f32[2,128]{1,0:T(2,128)S(1)}, f32[2,128]{1,0:T(2,128)S(1)}, u32[]{:S(2)}, u32[]{:S(2)}) collective-permute-start(f32[2,128]{1,0:T(2,128)S(1)} %bitcast.119), channel_id=1, source_target_pairs={{0,2},{2,0},{4,6},{6,4},{8,10},{10,8},{12,14},{14,12},{16,18},{18,... | collective-permute-start | bytes 3080 | tf_op jit(solution)/shard_map/ppermute | solution.py:35
  228.3 6.6 %collective-permute-start.44 = (f32[136,192]{1,0:T(8,128)S(1)}, f32[136,192]{1,0:T(8,128)S(1)}, u32[]{:S(2)}, u32[]{:S(2)}) collective-permute-start(f32[136,192]{1,0:T(8,128)S(1)} %get-tuple-element.65), channel_id=1, source_target_pairs={{0,2},{2,0},{4,6},{6,4},{8,10},{10,8},{12,14},{14,12},{16,18},{18,... | collective-permute-start | bytes 313352 | tf_op jit(solution)/shard_map/ppermute | solution.py:35
  229.3 8.3 %collective-permute-start.45 = (f32[136,192]{1,0:T(8,128)S(1)}, f32[136,192]{1,0:T(8,128)S(1)}, u32[]{:S(2)}, u32[]{:S(2)}) collective-permute-start(f32[136,192]{1,0:T(8,128)S(1)} %get-tuple-element.66), channel_id=1, source_target_pairs={{0,4},{2,6},{4,0},{6,2},{8,12},{10,14},{12,8},{14,10},{16,20},{18,... | collective-permute-start | bytes 313352 | tf_op jit(solution)/shard_map/ppermute | solution.py:35
  230.3 9.0 %collective-permute-start.46 = (f32[136,192]{1,0:T(8,128)S(1)}, f32[136,192]{1,0:T(8,128)S(1)}, u32[]{:S(2)}, u32[]{:S(2)}) collective-permute-start(f32[136,192]{1,0:T(8,128)S(1)} %copy-done.24), channel_id=1, source_target_pairs={{0,6},{2,4},{4,2},{6,0},{8,14},{10,12},{12,10},{14,8},{16,22},{18,... | collective-permute-start | bytes 313352 | tf_op jit(solution)/shard_map/ppermute | solution.py:35
  231.8 9.0 %collective-permute-start.48 = (f32[136,192]{1,0:T(8,128)S(1)}, f32[136,192]{1,0:T(8,128)S(1)}, u32[]{:S(2)}, u32[]{:S(2)}) collective-permute-start(f32[136,192]{1,0:T(8,128)S(1)} %get-tuple-element.67), channel_id=1, source_target_pairs={{0,2},{2,0},{4,6},{6,4},{8,10},{10,8},{12,14},{14,12},{16,18},{18,... | collective-permute-start | bytes 313352 | tf_op jit(solution)/shard_map/ppermute | solution.py:35
  232.8 10.7 %collective-permute-start.49 = (f32[136,192]{1,0:T(8,128)S(1)}, f32[136,192]{1,0:T(8,128)S(1)}, u32[]{:S(2)}, u32[]{:S(2)}) collective-permute-start(f32[136,192]{1,0:T(8,128)S(1)} %get-tuple-element.68), channel_id=1, source_target_pairs={{0,4},{2,6},{4,0},{6,2},{8,12},{10,14},{12,8},{14,10},{16,20},{18,... | collective-permute-start | bytes 313352 | tf_op jit(solution)/shard_map/ppermute | solution.py:35
  234.8 10.5 %collective-permute-start.50 = (f32[136,192]{1,0:T(8,128)S(1)}, f32[136,192]{1,0:T(8,128)S(1)}, u32[]{:S(2)}, u32[]{:S(2)}) collective-permute-start(f32[136,192]{1,0:T(8,128)S(1)} %concatenate.118), channel_id=1, source_target_pairs={{0,6},{2,4},{4,2},{6,0},{8,14},{10,12},{12,10},{14,8},{16,22},{18,... | collective-permute-start | bytes 313352 | tf_op jit(solution)/shard_map/ppermute | solution.py:35
  237.6 9.3 %collective-permute-start.52 = (f32[136,192]{1,0:T(8,128)S(1)}, f32[136,192]{1,0:T(8,128)S(1)}, u32[]{:S(2)}, u32[]{:S(2)}) collective-permute-start(f32[136,192]{1,0:T(8,128)S(1)} %get-tuple-element.69), channel_id=1, source_target_pairs={{0,2},{2,0},{4,6},{6,4},{8,10},{10,8},{12,14},{14,12},{16,18},{18,... | collective-permute-start | bytes 313352 | tf_op jit(solution)/shard_map/ppermute | solution.py:35
  239.4 10.1 %collective-permute-start.53 = (f32[136,192]{1,0:T(8,128)S(1)}, f32[136,192]{1,0:T(8,128)S(1)}, u32[]{:S(2)}, u32[]{:S(2)}) collective-permute-start(f32[136,192]{1,0:T(8,128)S(1)} %get-tuple-element.70), channel_id=1, source_target_pairs={{0,4},{2,6},{4,0},{6,2},{8,12},{10,14},{12,8},{14,10},{16,20},{18,... | collective-permute-start | bytes 313352 | tf_op jit(solution)/shard_map/ppermute | solution.py:35
  240.9 9.7 %collective-permute-start.54 = (f32[136,192]{1,0:T(8,128)S(1)}, f32[136,192]{1,0:T(8,128)S(1)}, u32[]{:S(2)}, u32[]{:S(2)}) collective-permute-start(f32[136,192]{1,0:T(8,128)S(1)} %concatenate.119), channel_id=1, source_target_pairs={{0,6},{2,4},{4,2},{6,0},{8,14},{10,12},{12,10},{14,8},{16,22},{18,... | collective-permute-start | bytes 313352 | tf_op jit(solution)/shard_map/ppermute | solution.py:35
  243.5 9.4 %collective-permute-start.56 = (f32[136,192]{1,0:T(8,128)S(1)}, f32[136,192]{1,0:T(8,128)S(1)}, u32[]{:S(2)}, u32[]{:S(2)}) collective-permute-start(f32[136,192]{1,0:T(8,128)S(1)} %get-tuple-element.71), channel_id=1, source_target_pairs={{0,2},{2,0},{4,6},{6,4},{8,10},{10,8},{12,14},{14,12},{16,18},{18,... | collective-permute-start | bytes 313352 | tf_op jit(solution)/shard_map/ppermute | solution.py:35
  245.3 7.9 %collective-permute-start.57 = (f32[136,192]{1,0:T(8,128)S(1)}, f32[136,192]{1,0:T(8,128)S(1)}, u32[]{:S(2)}, u32[]{:S(2)}) collective-permute-start(f32[136,192]{1,0:T(8,128)S(1)} %get-tuple-element.72), channel_id=1, source_target_pairs={{0,4},{2,6},{4,0},{6,2},{8,12},{10,14},{12,8},{14,10},{16,20},{18,... | collective-permute-start | bytes 313352 | tf_op jit(solution)/shard_map/ppermute | solution.py:35
  246.9 8.8 %collective-permute-start.58 = (f32[136,192]{1,0:T(8,128)S(1)}, f32[136,192]{1,0:T(8,128)S(1)}, u32[]{:S(2)}, u32[]{:S(2)}) collective-permute-start(f32[136,192]{1,0:T(8,128)S(1)} %concatenate.120), channel_id=1, source_target_pairs={{0,6},{2,4},{4,2},{6,0},{8,14},{10,12},{12,10},{14,8},{16,22},{18,... | collective-permute-start | bytes 313352 | tf_op jit(solution)/shard_map/ppermute | solution.py:35
  261.8 6.8 %collective-permute-start.64 = (f32[96,384]{1,0:T(8,128)S(1)}, f32[96,384]{1,0:T(8,128)S(1)}, u32[]{:S(2)}, u32[]{:S(2)}) collective-permute-start(f32[96,384]{1,0:T(8,128)S(1)} %get-tuple-element.37), channel_id=1, source_target_pairs={{0,2},{2,0},{4,6},{6,4},{8,10},{10,8},{12,14},{14,12},{16,18},{18,... | collective-permute-start | bytes 442376 | tf_op jit(solution)/shard_map/ppermute | solution.py:35
  262.8 8.8 %collective-permute-start.65 = (f32[96,384]{1,0:T(8,128)S(1)}, f32[96,384]{1,0:T(8,128)S(1)}, u32[]{:S(2)}, u32[]{:S(2)}) collective-permute-start(f32[96,384]{1,0:T(8,128)S(1)} %get-tuple-element.39), channel_id=1, source_target_pairs={{0,4},{2,6},{4,0},{6,2},{8,12},{10,14},{12,8},{14,10},{16,20},{18,... | collective-permute-start | bytes 442376 | tf_op jit(solution)/shard_map/ppermute | solution.py:35
  264.0 7.6 %collective-permute-start.66 = (f32[96,384]{1,0:T(8,128)S(1)}, f32[96,384]{1,0:T(8,128)S(1)}, u32[]{:S(2)}, u32[]{:S(2)}) collective-permute-start(f32[96,384]{1,0:T(8,128)S(1)} %get-tuple-element.38), channel_id=1, source_target_pairs={{0,6},{2,4},{4,2},{6,0},{8,14},{10,12},{12,10},{14,8},{16,22},{18,... | collective-permute-start | bytes 442376 | tf_op jit(solution)/shard_map/ppermute | solution.py:35
  271.6 7.4 %collective-permute-start.67 = (f32[24,384]{1,0:T(8,128)S(1)}, f32[24,384]{1,0:T(8,128)S(1)}, u32[]{:S(2)}, u32[]{:S(2)}) collective-permute-start(f32[24,384]{1,0:T(8,128)S(1)} %get-tuple-element.60), channel_id=1, source_target_pairs={{0,8},{2,10},{4,12},{6,14},{8,16},{10,18},{12,20},{14,22},{16,24},... | collective-permute-start | bytes 110600 | tf_op jit(solution)/shard_map/ppermute | solution.py:180
  273.1 6.3 %collective-permute-start.68 = (f32[24,384]{1,0:T(8,128)S(1)}, f32[24,384]{1,0:T(8,128)S(1)}, u32[]{:S(2)}, u32[]{:S(2)}) collective-permute-start(f32[24,384]{1,0:T(8,128)S(1)} %get-tuple-element.62), channel_id=1, source_target_pairs={{0,16},{2,18},{4,20},{6,22},{8,24},{10,26},{12,28},{14,30},{16,0},... | collective-permute-start | bytes 110600 | tf_op jit(solution)/shard_map/ppermute | solution.py:180
  281.4 5.9 %collective-permute-start.70 = (f32[24,384]{1,0:T(8,128)S(1)}, f32[24,384]{1,0:T(8,128)S(1)}, u32[]{:S(2)}, u32[]{:S(2)}) collective-permute-start(f32[24,384]{1,0:T(8,128)S(1)} %get-tuple-element.6), channel_id=1, source_target_pairs={{0,8},{2,10},{4,12},{6,14},{8,16},{10,18},{12,20},{14,22},{16,24},... | collective-permute-start | bytes 110600 | tf_op jit(solution)/shard_map/ppermute | solution.py:180
  281.6 6.2 %collective-permute-start.71 = (f32[24,384]{1,0:T(8,128)S(1)}, f32[24,384]{1,0:T(8,128)S(1)}, u32[]{:S(2)}, u32[]{:S(2)}) collective-permute-start(f32[24,384]{1,0:T(8,128)S(1)} %get-tuple-element.6), channel_id=1, source_target_pairs={{0,16},{2,18},{4,20},{6,22},{8,24},{10,26},{12,28},{14,30},{16,0},... | collective-permute-start | bytes 110600 | tf_op jit(solution)/shard_map/ppermute | solution.py:180
  291.0 6.0 %collective-permute-start.75 = (f32[96,384]{1,0:T(8,128)S(1)}, f32[96,384]{1,0:T(8,128)S(1)}, u32[]{:S(2)}, u32[]{:S(2)}) collective-permute-start(f32[96,384]{1,0:T(8,128)S(1)} %constant_dynamic-update-slice_fusion.6), channel_id=1, source_target_pairs={{0,6},{2,4},{4,2},{6,0},{8,14},{10,12},{12,10},{14,8},{16,22},{18,... | collective-permute-start | bytes 442376 | tf_op jit(solution)/shard_map/ppermute | solution.py:35
  (54 other events, 898.8 us)

commit v2 on v1

v2 whole, which is shorter than its diff:
```python
import functools

import jax
import jax.numpy as jnp
from jax import lax
from jax.experimental import pallas as pl
from jax.experimental.pallas import tpu as pltpu
from jax.sharding import PartitionSpec as P

HIGH = lax.Precision.HIGH
F32 = jnp.float32
BF16 = jnp.bfloat16


def coupling(values, weight):
    return jax.nn.gelu(jnp.dot(values, weight, precision=HIGH))


def attend_kernel(group, planes, count, *refs):
    mine_ref, other_ref, *refs = refs
    stay_refs, refs = refs[:group], refs[group:]
    gain_ref, *refs = refs
    flow_refs, (scaled_ref, stats_ref, weight, sems) = refs[:-4], refs[-4:]
    own, up, down = flow_refs[:2], flow_refs[2 : 2 * planes], flow_refs[2 * planes :]
    wide, core = lax.axis_index("wide"), lax.axis_index("narrow")
    plane, member = wide // group, wide % group
    rows = own[0].shape[0]

    def copies(at, p):
        if at == p:
            first, rest = own
        else:
            first, rest = (up if at > p else down)[2 * (abs(at - p) - 1) :][:2]
        out = []
        for s in range(group):
            source = rest.at[pl.ds((s - 1) * rows, rows)] if s else first
            target = pl.multiple_of((p * group + (member ^ s)) * rows, 64)
            out.append(pltpu.make_async_copy(source, weight.at[pl.ds(target, rows)], sems.at[p, s]))
        return out

    for at in range(planes):

        @pl.when((pl.program_id(0) == 0) & (plane == at))
        def _():
            everything = [copy for p in range(planes) for copy in copies(at, p)]
            for copy in everything:
                copy.start()
            for copy in everything:
                copy.wait()

    heads = mine_ref.shape[2]
    local = mine_ref.shape[1]
    gain = gain_ref[...].astype(F32)
    for h in range(0, group, 2):
        lhs = mine_ref[h : h + 2].reshape(2 * local, heads)
        rhs = other_ref[h : h + 2].reshape(2 * local, heads)
        at = pl.multiple_of(core * heads, 128)
        total = jnp.dot(lhs, weight[pl.ds(at, heads)], preferred_element_type=F32)
        at = pl.multiple_of((1 - core) * heads, 128)
        total += jnp.dot(rhs, weight[pl.ds(at, heads)], preferred_element_type=F32)
        stay = jnp.concatenate([stay_refs[h][...], stay_refs[h + 1][...]], axis=0)
        stream = (stay.astype(F32) + total).astype(BF16).astype(F32)
        scaled_ref[0, h * local : (h + 2) * local] = (stream * gain).astype(BF16)
        sums = jnp.sum(stream, axis=1, keepdims=True)
        squares = jnp.sum(stream * stream, axis=1, keepdims=True)
        lane = lax.broadcasted_iota(jnp.int32, (2 * local, 128), 1)
        both = jnp.where(lane == 0, sums, jnp.where(lane == 1, squares, 0.0))
        stats_ref[:, h * local : (h + 2) * local] = both.T[:8]
    scaled_ref[0, group * local :] = jnp.broadcast_to(gain_ref[...], (16, count))


def attend(mine, other, stay, gain, own, up, down):
    group, tokens, heads = mine.shape
    local = tokens // 2
    count = gain.shape[1]
    planes = len(up) + 1
    flow = [*own] + [v for pair in up for v in pair] + [v for pair in down for v in pair]
    whole = pl.BlockSpec(memory_space=pl.ANY)
    part = pl.BlockSpec((group, local, heads), lambda i: (0, i, 0))
    work = group * tokens * heads * 2 * count
    return pl.pallas_call(
        functools.partial(attend_kernel, group, planes, count),
        grid=(2,),
        in_specs=[part, part]
        + [pl.BlockSpec((local, count), lambda i: (i, 0))] * group
        + [pl.BlockSpec((1, count), lambda i: (0, 0))]
        + [whole] * len(flow),
        out_specs=[
            pl.BlockSpec((1, group * local + 16, count), lambda i: (i, 0, 0)),
            pl.BlockSpec((8, group * local), lambda i: (0, i)),
        ],
        out_shape=[
            jax.ShapeDtypeStruct((2, group * local + 16, count), BF16),
            jax.ShapeDtypeStruct((8, group * tokens), F32),
        ],
        scratch_shapes=[
            pltpu.VMEM((2 * heads, count), BF16),
            pltpu.SemaphoreType.DMA((planes, group)),
        ],
        compiler_params=pltpu.CompilerParams(vmem_limit_bytes=60 << 20),
        cost_estimate=pl.CostEstimate(flops=2 * work, bytes_accessed=14 << 20, transcendentals=0),
    )(mine, other, *stay, gain, *flow)


def project_kernel(group, planes, *refs):
    scaled_ref, stats_ref, *refs = refs
    flow_refs, (out_ref, down, sems) = refs[:-3], refs[-3:]
    own, up, lower = flow_refs[0], flow_refs[1:planes], flow_refs[planes:]
    plane, core = lax.axis_index("wide") // group, lax.axis_index("narrow")
    rows = own.shape[0]

    def copies(at):
        out = []
        for p in range(planes):
            source = own if at == p else (up if at > p else lower)[abs(at - p) - 1]
            out.append(pltpu.make_async_copy(source, down.at[pl.ds(p * rows, rows)], sems.at[p]))
        return out

    for at in range(planes):

        @pl.when(plane == at)
        def _():
            for copy in copies(at):
                copy.start()
            for copy in copies(at):
                copy.wait()

    local = (scaled_ref.shape[1] - 16) // group
    span = local + 8
    dims = (((1,), (1,)), ((), ()))
    gain = lax.dot_general(
        scaled_ref[0, group * local : group * local + 16], down[...], dims, preferred_element_type=F32
    )
    for t in range(2):
        k = core if t == 0 else 1 - core
        at = pl.multiple_of(k * (group * local), 128)
        value = lax.dot_general(scaled_ref[k, : group * local], down[...], dims, preferred_element_type=F32)
        sums = stats_ref[:, pl.ds(at, group * local)]
        for s in range(group):
            out_ref[t, s * span : s * span + local] = value[s * local : (s + 1) * local]
            out_ref[t, s * span + local : (s + 1) * span] = gain[:8]
            out_ref[t, s * span + local + 1 : s * span + local + 3, :local] = sums[:2, s * local : (s + 1) * local]


def project(group, scaled, stats, own, up, down):
    planes = len(up) + 1
    rows, features = own.shape
    local = (scaled.shape[1] - 16) // group
    count = planes * rows
    whole = pl.BlockSpec(memory_space=pl.ANY)
    inside = pl.BlockSpec(memory_space=pltpu.VMEM)
    return pl.pallas_call(
        functools.partial(project_kernel, group, planes),
        in_specs=[inside, inside] + [whole] * (2 * planes - 1),
        out_specs=inside,
        out_shape=jax.ShapeDtypeStruct((2, group * (local + 8), count), F32),
        scratch_shapes=[pltpu.VMEM((count, features), BF16), pltpu.SemaphoreType.DMA((planes,))],
        compiler_params=pltpu.CompilerParams(vmem_limit_bytes=40 << 20),
        cost_estimate=pl.CostEstimate(
            flops=4 * group * local * features * count, bytes_accessed=8 << 20, transcendentals=0
        ),
    )(scaled, stats, own, *up, *down)


def per_device(group, wides, narrows, context, out_weight, residual, ln_gain, side_down, f_weight, g_weight, targets):
    planes = wides // group
    wide, core = lax.axis_index("wide"), lax.axis_index("narrow")
    plane, member = wide // group, wide % group
    short = planes == 4 and narrows == 2
    features = out_weight.shape[1] // group
    rows = out_weight.shape[0]
    tokens = context.shape[0]
    local = tokens // narrows
    members = range(group)
    cores = range(narrows)

    def to_member(value, s):
        pairs = [(i, i - i % group + (i % group ^ s)) for i in range(wides)]
        return lax.ppermute(value, "wide", pairs) if s else value

    def to_core(value, t):
        return lax.ppermute(value, "narrow", [(i, i ^ t) for i in range(narrows)]) if t else value

    def block(value, index, size, axis):
        return lax.dynamic_slice_in_dim(value, index * size, size, axis)

    def step_up(value, k):
        pairs = [(i, i + group) for i in range((k - 1) * group, wides - group)]
        return lax.ppermute(value, "wide", pairs)

    def step_down(value, k):
        pairs = [(i + group, i) for i in range(wides - k * group)]
        return lax.ppermute(value, "wide", pairs)

    def sum_cores(pick):
        total = pick(core)
        for t in range(1, narrows):
            total = total + to_core(pick(core ^ t), t)
        return total

    def sum_members(pick):
        total = pick(0)
        for s in range(1, group):
            total = total + to_member(pick(s), s)
        return total

    own = [block(out_weight, member ^ s, features, 1) for s in members]
    down_own = [block(side_down.T, member ^ s, features, 1) for s in members]
    stay_own = [block(residual, member ^ s, features, 1) for s in members]
    gain = block(ln_gain, member, features, 0)[None, :]
    columns = down_own[0].shape[0]
    side_rows = group * local

    def in_plane(downs):
        value = jnp.zeros((group * columns, features), BF16)
        for s in members:
            value = lax.dynamic_update_slice_in_dim(value, downs[s], (member ^ s) * columns, 0)
        return value

    if short:
        up, down = [[v] for v in own[:1]], [[v] for v in own[:1]]

        def pass_on(i, k):
            up[i].append(step_up(up[i][-1], k))
            down[i].append(step_down(down[i][-1], k))

        pass_on(0, 1)
        pass_on(0, 2)
        pieces = [to_member(own[s], s) for s in members]
        rest = jnp.concatenate(pieces[1:], axis=0)

        rest, context, down_own, up, down = lax.optimization_barrier((rest, context, down_own, up, down))
        up.append([rest])
        down.append([rest])
        pass_on(1, 1)
        pass_on(0, 3)
        arrived = [context, to_member(context, 1), to_member(context, 2)]
        down_plane = in_plane([to_member(down_own[s], s) for s in members])

        state = (down_plane, arrived, stay_own, up, down)
        down_plane, arrived, stay_own, up, down = lax.optimization_barrier(state)
        up.append([down_plane])
        down.append([down_plane])
        pass_on(1, 2)
        pass_on(2, 1)
        arrived.append(to_member(arrived[0], 3))
        stay = [stay_own[0], None, None, to_member(stay_own[3], 3)]
        part = jnp.concatenate(arrived, axis=0)

        part, stay_own, up, down = lax.optimization_barrier((part, stay_own, up, down))
        pass_on(1, 3)
        pass_on(2, 2)
        stay[1], stay[2] = to_member(stay_own[1], 1), to_member(stay_own[2], 2)
        mine, other = [v.reshape(group, tokens, -1) for v in (part, to_core(part, 1))]

        mine, other, stay, up, down = lax.optimization_barrier((mine, other, stay, up, down))
        pass_on(2, 3)
        pairs = [list(zip(v[0][1:], v[1][1:])) for v in (up, down)]
        scaled, stats = attend(mine, other, stay, gain, [own[0], rest], *pairs)
        both = project(group, scaled, stats, down_plane, up[2][1:], down[2][1:])
        summed = both[0] + to_core(both[1], 1)
        span = local + 8
        projected = summed[:span]
        for s in range(1, group):
            projected = projected + to_member(summed[s * span : (s + 1) * span], s)
        stats = projected[local + 1 : local + 3, :local]
    else:
        pieces = [to_member(own[s], s) for s in members]
        down_plane = in_plane([to_member(down_own[s], s) for s in members])
        arrived = [to_member(context, s) for s in members]
        stay = [to_member(stay_own[s], s) for s in members]
        parts = [to_core(jnp.concatenate(arrived, axis=0), t) for t in cores]
        lines = [[p * group + m for p in range(planes)] for m in range(group)]
        chunk = jnp.zeros((group * rows, features), BF16)
        for s in members:
            chunk = lax.dynamic_update_slice_in_dim(chunk, pieces[s], (member ^ s) * rows, 0)
        weight = lax.all_gather(chunk, "wide", axis_index_groups=lines, tiled=True)
        all_down = lax.all_gather(down_plane, "wide", axis_index_groups=lines, tiled=True)

        def by_core(value):
            value = value.reshape(group, narrows, local, -1)
            return value.swapaxes(0, 1).reshape(group * tokens, -1)

        heads = context.shape[1]
        attn_sum = jnp.zeros((), F32)
        for t in cores:
            share = block(weight, core ^ t, heads, 0)
            attn_sum = attn_sum + jnp.dot(parts[t], share, preferred_element_type=F32)
        stream = (jnp.concatenate(stay, axis=0).astype(F32) + attn_sum).astype(BF16)
        stream = by_core(stream).astype(F32)
        scaled = (stream * gain.astype(F32)).astype(BF16).reshape(narrows, side_rows, features)
        gains = jnp.broadcast_to(gain[None], (narrows, 8, features))
        scaled = jnp.concatenate([scaled, gains], axis=1)
        stats = jnp.stack([jnp.sum(stream, axis=1), jnp.sum(stream * stream, axis=1)])
        stats_own = stats.reshape(2, narrows, group, local)

        def share_of_core(k):
            lhs = lax.dynamic_index_in_dim(scaled, k, 0, keepdims=False)
            return lax.dot_general(lhs, all_down, (((1,), (1,)), ((), ())), preferred_element_type=F32)

        summed = sum_cores(share_of_core)
        tail = summed[side_rows:]
        projected = sum_members(
            lambda s: jnp.concatenate([summed[s * local : (s + 1) * local], tail], axis=0)
        )
        summed_stats = sum_cores(lambda k: lax.dynamic_index_in_dim(stats_own, k, 1, keepdims=False))
        stats = sum_members(lambda s: summed_stats[:, s])
    projected, gain_map = projected[:local], projected[local]

    width = out_weight.shape[1] * narrows
    mean = stats[0] / width
    spread = stats[1] / width - mean * mean
    side_in = (projected - mean[:, None] * gain_map[None, :]) / jnp.sqrt(spread + 1e-06)[:, None]
    half = side_in.shape[1] // 2
    f_w, g_w = f_weight.astype(F32), g_weight.astype(F32)
    first, second = side_in[:, :half], side_in[:, half:]
    f_value, f_pull = jax.vjp(coupling, second, f_w)
    upper = first + f_value
    g_value, g_pull = jax.vjp(coupling, upper, g_w)
    lower = second + g_value
    side_out = jnp.concatenate([upper, lower], axis=1)
    misfit = (side_out - targets) / (local * wides * narrows)
    upper_back, g_local = g_pull(misfit[:, half:])
    f_local = f_pull(misfit[:, :half] + upper_back)[1]

    if (2 * half) % (wides * narrows * 8):
        f_total, g_total = lax.psum((f_local, g_local), ("wide", "narrow"))
        return side_out, f_total, g_total

    grads = jnp.concatenate([f_local, g_local], axis=0)
    share = 2 * half // narrows
    grads = sum_cores(lambda k: block(grads, k, share, 0))
    share = share // group
    part = grads
    grads = sum_members(lambda s: block(part, member ^ s, share, 0))
    share = share // planes

    def shift(value, k):
        return lax.ppermute(value, "wide", [(i, (i + k * group) % wides) for i in range(wides)])

    part = grads
    grads = block(part, plane, share, 0)
    for k in range(1, planes):
        grads = grads + shift(block(part, (plane + k) % planes, share, 0), k)
    whole = jnp.zeros((planes * share, half), F32)
    for k in range(planes):
        piece = shift(grads, k) if k else grads
        whole = lax.dynamic_update_slice_in_dim(whole, piece, (plane - k) % planes * share, 0)
    share = share * planes
    part, whole = whole, jnp.zeros((group * share, half), F32)
    for s in members:
        whole = lax.dynamic_update_slice_in_dim(whole, to_member(part, s), (member ^ s) * share, 0)
    share = share * group
    part, whole = whole, jnp.zeros((narrows * share, half), F32)
    for t in range(narrows):
        whole = lax.dynamic_update_slice_in_dim(whole, to_core(part, t), (core ^ t) * share, 0)
    return side_out, whole[:half], whole[half:]


def solution(mesh):
    wides, narrows = mesh.shape["wide"], mesh.shape["narrow"]
    group = 4 if wides % 4 == 0 else 1
    in_specs = (
        P("wide", "narrow"),
        P("wide", "narrow"),
        P("wide", "narrow"),
        P("narrow"),
        P("narrow", "wide"),
        P(),
        P(),
        P(("wide", "narrow"), None),
    )
    out_specs = (P(("wide", "narrow"), None), P(), P())
    return jax.shard_map(
        functools.partial(per_device, group, wides, narrows),
        mesh=mesh,
        in_specs=in_specs,
        out_specs=out_specs,
        check_vma=False,
    )
```

time: 302 us -> 229 us (0.76)
  waiting for transfers between devices: 52.9 us -> 127 us
  starting transfers between devices: 143 us -> 70.8 us
  local copies, waits for them, and re-layouts: 50.6 us -> 9.43 us
  matrix products: 19.1 us -> 2.06 us
  other arithmetic: 19.8 us -> 4.73 us
  Pallas kernels: 0 us -> 13.6 us
  between operations: 14.6 us -> 1.43 us
    ppermute x30 -> x18, starting transfers between devices: 89.5 us -> 31.3 us  [the longest x9 19.7 us: step_up(): return lax.ppermute(value, 'wide', pairs)]
    ppermute x30 -> x18, waiting for transfers between devices: 0.08 us -> 42.7 us  [the longest x9 41.3 us: step_down(): return lax.ppermute(value, 'wide', pairs)]
    ppermute x33 -> x21, waiting for transfers between devices: 42.2 us -> 71.2 us  [to_member(): return lax.ppermute(value, 'wide', pairs) if s else value]
    dot_general x10 -> x0, matrix products: 17.1 us -> none  [the longest x2 11 us: per_device(): jnp.dot(parts[t], block(weight, core ^ t, part.shape[1], 0), preferred_el...]
    pallas_call x0 -> x2, Pallas kernels: none -> 13.6 us  [the longest x1 11.4 us: attend(): pl.pallas_call(functools.partial(attend_kernel, group, planes, count), gr...]
    dynamic_update_slice x12 -> x0, other arithmetic: 12.8 us -> none  [per_device(): weight = lax.dynamic_update_slice_in_dim(weight, lines[s][j], at, 0)]
    ppermute x33 -> x21, starting transfers between devices: 41.5 us -> 29 us  [to_member(): return lax.ppermute(value, 'wide', pairs) if s else value]
    dynamic_slice x13 -> x0, local copies, waits for them, and re-layouts: 12.5 us -> none  [the longest x6 8.14 us: pick(): mine = lax.dynamic_index_in_dim(value, k, 1, keepdims=False)]
  transfers between devices with their start and end apart: 77 -> 49, of which waited for: 29 -> 28; matrix products, arithmetic and copies ran while one was open for 21% -> 2% of each run, Pallas kernels for 0% -> 5%
where the time goes in v2:
time: 229 us
  waiting for transfers between devices  127 us (55%)
  starting transfers between devices  70.8 us (31%)
  Pallas kernels  13.6 us (6%)
  local copies, waits for them, and re-layouts  9.43 us (4%)
  other arithmetic  4.73 us (2%)
    ppermute x21, waiting for transfers between devices, to_member(): return lax.ppermute(value, 'wide', pairs) if s else value  71.2 us
    ppermute x9, waiting for transfers between devices, step_down(): return lax.ppermute(value, 'wide', pairs)  41.3 us
    ppermute x21, starting transfers between devices, to_member(): return lax.ppermute(value, 'wide', pairs) if s else value  29 us
    ppermute x9, starting transfers between devices, step_up(): return lax.ppermute(value, 'wide', pairs)  19.7 us
    ppermute x9, starting transfers between devices, step_down(): return lax.ppermute(value, 'wide', pairs)  11.6 us
    pallas_call x1, Pallas kernels, attend(): pl.pallas_call(functools.partial(attend_kernel, group, planes, count), gr...  11.4 us
    ppermute x6, starting transfers between devices, shift(): lax.ppermute(value, 'wide', [(i, (i + k * group) % wides) for i in range(...  10.1 us
    ppermute x4, waiting for transfers between devices, to_core(): lax.ppermute(value, 'narrow', [(i, i ^ t) for i in range(narrows)])  7.35 us
  transfers between devices with their start and end apart: 49, of which 28 were waited for; matrix products, arithmetic and copies ran while one was open for 2% of the time, Pallas kernels for 5%

profile of v2, /device:TPU:0, one launch (start us, length us, event | category | flops | bytes accessed | tf_op | source)
XLA Modules:
  0.0 228.7 jit_solution(118331275923930915)
XLA Ops:
  0.7 1.4 constant_dynamic-slice_fusion.10
  2.1 5.1 %collective-permute-start.3 = (bf16[192,768]{1,0:T(8,128)(2,1)S(1)}, bf16[192,768]{1,0:T(8,128)(2,1)S(1)}, u32[]{:S(2)}, u32[]{:S(2)}) collective-permute-start(bf16[192,768]{1,0:T(8,128)(2,1)S(1)} %get-tuple-element.146.refs_7_), channel_id=1, source_target_pairs={{0,8},{2,10},{4,12},{6,14},{8,16},{10,18},{12,20},{14,22},{16,24},... | collective-permute-start | bytes 884744 | tf_op jit(solution)/shard_map/ppermute | solution.py:189
  7.2 1.3 collective-permute-start.5
  8.5 1.6 collective-permute-start
  10.1 1.5 collective-permute-start.1
  12.1 1.4 collective-permute-done.3.refs_9_
  13.4 1.4 collective-permute-start.4
  14.8 2.8 %collective-permute-done.5.refs_15_ = bf16[192,768]{1,0:T(8,128)(2,1)S(1)} collective-permute-done((bf16[192,768]{1,0:T(8,128)(2,1)S(1)}, bf16[192,768]{1,0:T(8,128)(2,1)S(1)}, u32[]{:S(2)}, u32[]{:S(2)}) %collective-permute-start.5) | collective-permute-done | bytes 294944 | tf_op jit(solution)/shard_map/ppermute | solution.py:193
  17.6 1.3 collective-permute-start.6
  18.9 5.6 %collective-permute-done.1 = bf16[192,768]{1,0:T(8,128)(2,1)S(1)} collective-permute-done((bf16[192,768]{1,0:T(8,128)(2,1)S(1)}, bf16[192,768]{1,0:T(8,128)(2,1)S(1)}, u32[]{:S(2)}, u32[]{:S(2)}) %collective-permute-start.1) | collective-permute-done | bytes 294944 | tf_op jit(solution)/shard_map/ppermute | solution.py:179
  24.6 3.2 %collective-permute-done.6.refs_17_ = bf16[192,768]{1,0:T(8,128)(2,1)S(1)} collective-permute-done((bf16[192,768]{1,0:T(8,128)(2,1)S(1)}, bf16[192,768]{1,0:T(8,128)(2,1)S(1)}, u32[]{:S(2)}, u32[]{:S(2)}) %collective-permute-start.6) | collective-permute-done | bytes 294944 | tf_op jit(solution)/shard_map/ppermute | solution.py:193
  27.9 4.6 %collective-permute-start.13 = (bf16[576,768]{1,0:T(8,128)(2,1)S(1)}, bf16[576,768]{1,0:T(8,128)(2,1)}, u32[]{:S(2)}, u32[]{:S(2)}) collective-permute-start(bf16[576,768]{1,0:T(8,128)(2,1)S(1)} %pad_maximum_fusion.1.refs_8_), channel_id=1, source_target_pairs={{0,8},{2,10},{4,12},{6,14},{8,16},{10,18},{12,20},{14,22},{16,24},... | collective-permute-start | bytes 2654216 | tf_op jit(solution)/shard_map/ppermute | solution.py:189
  32.4 1.3 collective-permute-start.15
  33.7 1.6 collective-permute-start.7
  35.8 1.5 collective-permute-start.11
  37.3 1.7 collective-permute-done.7
  39.0 1.5 collective-permute-start.8
  40.5 13.7 %collective-permute-done.8 = bf16[48,768]{1,0:T(8,128)(2,1)S(1)} collective-permute-done((bf16[48,768]{1,0:T(8,128)(2,1)S(1)}, bf16[48,768]{1,0:T(8,128)(2,1)S(1)}, u32[]{:S(2)}, u32[]{:S(2)}) %collective-permute-start.8) | collective-permute-done | bytes 73760 | tf_op jit(solution)/shard_map/ppermute | solution.py:179
  54.2 3.0 %collective-permute-start.9 = (bf16[48,768]{1,0:T(8,128)(2,1)S(1)}, bf16[48,768]{1,0:T(8,128)(2,1)S(1)}, u32[]{:S(2)}, u32[]{:S(2)}) collective-permute-start(bf16[48,768]{1,0:T(8,128)(2,1)S(1)} %get-tuple-element.71), channel_id=1, source_target_pairs={{0,6},{2,4},{4,2},{6,0},{8,14},{10,12},{12,10},{14,8},{16,22},{18,... | collective-permute-start | bytes 221192 | tf_op jit(solution)/shard_map/ppermute | solution.py:179
  57.2 2.3 %collective-permute-done.9 = bf16[48,768]{1,0:T(8,128)(2,1)S(1)} collective-permute-done((bf16[48,768]{1,0:T(8,128)(2,1)S(1)}, bf16[48,768]{1,0:T(8,128)(2,1)S(1)}, u32[]{:S(2)}, u32[]{:S(2)}) %collective-permute-start.9) | collective-permute-done | bytes 73760 | tf_op jit(solution)/shard_map/ppermute | solution.py:179
  59.6 1.4 collective-permute-start.12
  61.9 1.3 collective-permute-start.14
  63.3 7.3 %collective-permute-done.14.refs_19_ = bf16[192,768]{1,0:T(8,128)(2,1)S(1)} collective-permute-done((bf16[192,768]{1,0:T(8,128)(2,1)S(1)}, bf16[192,768]{1,0:T(8,128)(2,1)S(1)}, u32[]{:S(2)}, u32[]{:S(2)}) %collective-permute-start.14) | collective-permute-done | bytes 294944 | tf_op jit(solution)/shard_map/ppermute | solution.py:193
  70.6 3.8 %collective-permute-start.16 = (bf16[256,1536]{1,0:T(8,128)(2,1)}, bf16[256,1536]{1,0:T(8,128)(2,1)S(1)}, u32[]{:S(2)}, u32[]{:S(2)}) collective-permute-start(bf16[256,1536]{1,0:T(8,128)(2,1)} %param.8), channel_id=1, source_target_pairs={{0,6},{2,4},{4,2},{6,0},{8,14},{10,12},{12,10},{14,8},{16,22},{18,... | collective-permute-start | bytes 2359304 | tf_op jit(solution)/shard_map/ppermute | solution.py:179
  75.1 1.3 collective-permute-start.19
  76.4 4.6 %collective-permute-start.18 = (bf16[192,768]{1,0:T(8,128)(2,1)S(1)}, bf16[192,768]{1,0:T(8,128)(2,1)S(1)}, u32[]{:S(2)}, u32[]{:S(2)}) collective-permute-start(bf16[192,768]{1,0:T(8,128)(2,1)S(1)} %constant_dynamic-update-slice_fusion.10.refs_2_), channel_id=1, source_target_pairs={{0,8},{2,10},{4,12},{6,14},{8,16},{10,18},{12,20},{14,22},{16,24},... | collective-permute-start | bytes 884744 | tf_op jit(solution)/shard_map/ppermute | solution.py:189
  81.0 1.3 collective-permute-start.20
  82.3 2.8 %collective-permute-done.16 = bf16[256,1536]{1,0:T(8,128)(2,1)S(1)} collective-permute-done((bf16[256,1536]{1,0:T(8,128)(2,1)}, bf16[256,1536]{1,0:T(8,128)(2,1)S(1)}, u32[]{:S(2)}, u32[]{:S(2)}) %collective-permute-start.16) | collective-permute-done | bytes 786464 | tf_op jit(solution)/shard_map/ppermute | solution.py:179
  85.1 1.7 pad_maximum_fusion
  86.9 10.2 %collective-permute-done.20.refs_6_ = bf16[192,768]{1,0:T(8,128)(2,1)S(1)} collective-permute-done((bf16[192,768]{1,0:T(8,128)(2,1)S(1)}, bf16[192,768]{1,0:T(8,128)(2,1)S(1)}, u32[]{:S(2)}, u32[]{:S(2)}) %collective-permute-start.20) | collective-permute-done | bytes 294944 | tf_op jit(solution)/shard_map/ppermute | solution.py:193
  97.2 1.7 collective-permute-start.24
  99.6 1.3 collective-permute-start.27
  101.6 8.0 %collective-permute-done.24.refs_5_ = bf16[256,768]{1,0:T(8,128)(2,1)S(1)} collective-permute-done((bf16[256,768]{1,0:T(8,128)(2,1)S(1)}, bf16[256,768]{1,0:T(8,128)(2,1)S(1)}, u32[]{:S(2)}, u32[]{:S(2)}) %collective-permute-start.24) | collective-permute-done | bytes 393248 | tf_op jit(solution)/shard_map/ppermute | solution.py:179
  109.6 1.3 collective-permute-start.28
  111.7 17.9 %collective-permute-done.28.refs_7_ = bf16[192,768]{1,0:T(8,128)(2,1)S(1)} collective-permute-done((bf16[192,768]{1,0:T(8,128)(2,1)S(1)}, bf16[192,768]{1,0:T(8,128)(2,1)S(1)}, u32[]{:S(2)}, u32[]{:S(2)}) %collective-permute-start.28) | collective-permute-done | bytes 294944 | tf_op jit(solution)/shard_map/ppermute | solution.py:193
  131.4 8.5 %collective-permute-done.23.refs_4_ = bf16[256,768]{1,0:T(8,128)(2,1)S(1)} collective-permute-done((bf16[256,768]{1,0:T(8,128)(2,1)S(1)}, bf16[256,768]{1,0:T(8,128)(2,1)S(1)}, u32[]{:S(2)}, u32[]{:S(2)}) %collective-permute-start.23) | collective-permute-done | bytes 393248 | tf_op jit(solution)/shard_map/ppermute | solution.py:179
  142.3 1.3 collective-permute-start.30
  143.6 11.4 %shard_map.103 = (bf16[2,528,768]{2,1,0:T(8,128)(2,1)}, f32[8,1024]{1,0:T(8,128)}) custom-call(bf16[4,256,1536]{2,1,0:T(8,128)(2,1)} %bitcast.31, bf16[4,256,1536]{2,1,0:T(8,128)(2,1)} %bitcast.32, bf16[256,768]{1,0:T(8,128)(2,1)} %get-tuple-element.111.refs_2_, bf16[256,768]{1,0:T(8,128)(2,1)} %copy-done.16, bf16[256,768]{1,0:T(8,128)(2,1)} %copy-done.17, ...), custom_call_target="tpu_custom_call" | custom-call | flops 4831838208 | bytes 14680064 | tf_op jit(solution)/shard_map/pallas_call | solution.py:81
  155.1 1.4 copy-done.1
  157.3 2.2 shard_map.104
  159.7 3.5 %collective-permute-done.31 = f32[544,768]{1,0:T(8,128)S(1)} collective-permute-done((f32[544,768]{1,0:T(8,128)S(1)}, f32[544,768]{1,0:T(8,128)S(1)}, u32[]{:S(2)}, u32[]{:S(2)}) %collective-permute-start.31) | collective-permute-done | bytes 1671200 | tf_op jit(solution)/shard_map/ppermute | solution.py:182
  164.1 1.3 collective-permute-start.33
  165.4 1.6 collective-permute-start.34
  167.1 9.1 %collective-permute-done.32 = f32[136,768]{1,0:T(8,128)} collective-permute-done((f32[136,768]{1,0:T(8,128)S(1)}, f32[136,768]{1,0:T(8,128)}, u32[]{:S(2)}, u32[]{:S(2)}) %collective-permute-start.32) | collective-permute-done | bytes 417824 | tf_op jit(solution)/shard_map/ppermute | solution.py:179
  176.2 8.4 %collective-permute-done.33 = f32[136,768]{1,0:T(8,128)} collective-permute-done((f32[136,768]{1,0:T(8,128)S(1)}, f32[136,768]{1,0:T(8,128)}, u32[]{:S(2)}, u32[]{:S(2)}) %collective-permute-start.33) | collective-permute-done | bytes 417824 | tf_op jit(solution)/shard_map/ppermute | solution.py:179
  184.6 1.3 fusion.5
  189.5 2.0 collective-permute-done.35
  191.7 1.6 collective-permute-start.36
  193.7 1.5 collective-permute-start.38
  195.2 3.1 %collective-permute-done.36 = f32[96,384]{1,0:T(8,128)S(1)} collective-permute-done((f32[96,384]{1,0:T(8,128)S(1)}, f32[96,384]{1,0:T(8,128)S(1)}, u32[]{:S(2)}, u32[]{:S(2)}) %collective-permute-start.36) | collective-permute-done | bytes 147488 | tf_op jit(solution)/shard_map/ppermute | solution.py:179
  198.3 3.7 %collective-permute-done.37 = f32[96,384]{1,0:T(8,128)S(1)} collective-permute-done((f32[96,384]{1,0:T(8,128)S(1)}, f32[96,384]{1,0:T(8,128)S(1)}, u32[]{:S(2)}, u32[]{:S(2)}) %collective-permute-start.37) | collective-permute-done | bytes 147488 | tf_op jit(solution)/shard_map/ppermute | solution.py:179
  202.1 2.7 %collective-permute-start.39 = (f32[24,384]{1,0:T(8,128)S(1)}, f32[24,384]{1,0:T(8,128)S(1)}, u32[]{:S(2)}, u32[]{:S(2)}) collective-permute-start(f32[24,384]{1,0:T(8,128)S(1)} %get-tuple-element.157), channel_id=1, source_target_pairs={{0,8},{2,10},{4,12},{6,14},{8,16},{10,18},{12,20},{14,22},{16,24},... | collective-permute-start | bytes 110600 | tf_op jit(solution)/shard_map/ppermute | solution.py:339
  204.8 2.4 %collective-permute-start.41 = (f32[24,384]{1,0:T(8,128)S(1)}, f32[24,384]{1,0:T(8,128)S(1)}, u32[]{:S(2)}, u32[]{:S(2)}) collective-permute-start(f32[24,384]{1,0:T(8,128)S(1)} %get-tuple-element.158), channel_id=1, source_target_pairs={{0,24},{2,26},{4,28},{6,30},{8,0},{10,2},{12,4},{14,6},{16,8},{18,... | collective-permute-start | bytes 110600 | tf_op jit(solution)/shard_map/ppermute | solution.py:339
  207.9 1.7 collective-permute-done.40
  209.7 1.0 collective-permute-start.42
  210.7 3.0 %collective-permute-start.43 = (f32[24,384]{1,0:T(8,128)S(1)}, f32[24,384]{1,0:T(8,128)S(1)}, u32[]{:S(2)}, u32[]{:S(2)}) collective-permute-start(f32[24,384]{1,0:T(8,128)S(1)} %get-tuple-element.134), channel_id=1, source_target_pairs={{0,16},{2,18},{4,20},{6,22},{8,24},{10,26},{12,28},{14,30},{16,0},... | collective-permute-start | bytes 110600 | tf_op jit(solution)/shard_map/ppermute | solution.py:339
  213.7 0.9 collective-permute-start.44
  215.9 1.8 collective-permute-done.44
  218.2 1.2 collective-permute-start.46
  219.4 1.8 collective-permute-start.47
  221.3 1.6 collective-permute-done.45
  223.4 2.1 collective-permute-done.47
  225.7 1.9 collective-permute-done.48
  227.6 1.1 fusion.55
  (127 shorter events, 18.7 us)
Async XLA Ops:
  0.6 185.8 %copy-start = (bf16[384,384]{1,0:T(8,128)(2,1)S(1)}, bf16[384,384]{1,0:T(8,128)(2,1)}, u32[]{:S(2)}) copy-start(bf16[384,384]{1,0:T(8,128)(2,1)} %param.14) | copy-start | bytes 884740
  0.6 18.2 %copy-start.8 = (bf16[3072,48]{0,1:T(8,128)(2,1)S(1)}, bf16[3072,48]{0,1:T(8,128)(2,1)}, u32[]{:S(2)}) copy-start(bf16[3072,48]{0,1:T(8,128)(2,1)} %param.12) | copy-start | bytes 884740
  2.1 59.8 %copy-start.9 = (bf16[192,768]{1,0:T(8,128)(2,1)}, bf16[192,768]{1,0:T(8,128)(2,1)S(1)}, u32[]{:S(2)}) copy-start(bf16[192,768]{1,0:T(8,128)(2,1)S(1)} %get-tuple-element.146.refs_7_) | copy-start | bytes 884740
  2.1 58.8 %copy-start.4 = (bf16[256,3072]{1,0:T(8,128)(2,1)S(1)}, bf16[256,3072]{1,0:T(8,128)(2,1)}, u32[]{:S(2)}) copy-start(bf16[256,3072]{1,0:T(8,128)(2,1)} %param.10) | copy-start | bytes 4718596
  2.1 11.3 %collective-permute-start.3 = (bf16[192,768]{1,0:T(8,128)(2,1)S(1)}, bf16[192,768]{1,0:T(8,128)(2,1)S(1)}, u32[]{:S(2)}, u32[]{:S(2)}) collective-permute-start(bf16[192,768]{1,0:T(8,128)(2,1)S(1)} %get-tuple-element.146.refs_7_), channel_id=1, source_target_pairs={{0,8},{2,10},{4,12},{6,14},{8,16},{10,18},{12,20},{14,22},{16,24},... | collective-permute-start | bytes 884744 | tf_op jit(solution)/shard_map/ppermute | solution.py:189
  7.2 10.4 %collective-permute-start.5 = (bf16[192,768]{1,0:T(8,128)(2,1)S(1)}, bf16[192,768]{1,0:T(8,128)(2,1)S(1)}, u32[]{:S(2)}, u32[]{:S(2)}) collective-permute-start(bf16[192,768]{1,0:T(8,128)(2,1)S(1)} %get-tuple-element.146.refs_7_), channel_id=1, source_target_pairs={{8,0},{10,2},{12,4},{14,6},{16,8},{18,10},{20,12},{22,14},{24,16},... | collective-permute-start | bytes 884744 | tf_op jit(solution)/shard_map/ppermute | solution.py:193
  8.5 10.4 %collective-permute-start = (bf16[192,768]{1,0:T(8,128)(2,1)S(1)}, bf16[192,768]{1,0:T(8,128)(2,1)S(1)}, u32[]{:S(2)}, u32[]{:S(2)}) collective-permute-start(bf16[192,768]{1,0:T(8,128)(2,1)S(1)} %get-tuple-element.148), channel_id=1, source_target_pairs={{0,2},{2,0},{4,6},{6,4},{8,10},{10,8},{12,14},{14,12},{16,18},{18,... | collective-permute-start | bytes 884744 | tf_op jit(solution)/shard_map/ppermute | solution.py:179
  10.1 14.5 %collective-permute-start.1 = (bf16[192,768]{1,0:T(8,128)(2,1)S(1)}, bf16[192,768]{1,0:T(8,128)(2,1)S(1)}, u32[]{:S(2)}, u32[]{:S(2)}) collective-permute-start(bf16[192,768]{1,0:T(8,128)(2,1)S(1)} %get-tuple-element.147), channel_id=1, source_target_pairs={{0,4},{2,6},{4,0},{6,2},{8,12},{10,14},{12,8},{14,10},{16,20},{18,... | collective-permute-start | bytes 884744 | tf_op jit(solution)/shard_map/ppermute | solution.py:179
  11.6 13.0 %collective-permute-start.2 = (bf16[192,768]{1,0:T(8,128)(2,1)S(1)}, bf16[192,768]{1,0:T(8,128)(2,1)S(1)}, u32[]{:S(2)}, u32[]{:S(2)}) collective-permute-start(bf16[192,768]{1,0:T(8,128)(2,1)S(1)} %get-tuple-element.149), channel_id=1, source_target_pairs={{0,6},{2,4},{4,2},{6,0},{8,14},{10,12},{12,10},{14,8},{16,22},{18,... | collective-permute-start | bytes 884744 | tf_op jit(solution)/shard_map/ppermute | solution.py:179
  13.4 46.1 %copy-start.18 = (bf16[192,768]{1,0:T(8,128)(2,1)}, bf16[192,768]{1,0:T(8,128)(2,1)S(1)}, u32[]{:S(2)}) copy-start(bf16[192,768]{1,0:T(8,128)(2,1)S(1)} %collective-permute-done.3.refs_9_) | copy-start | bytes 884740
  13.4 11.2 %collective-permute-start.4 = (bf16[192,768]{1,0:T(8,128)(2,1)S(1)}, bf16[192,768]{1,0:T(8,128)(2,1)}, u32[]{:S(2)}, u32[]{:S(2)}) collective-permute-start(bf16[192,768]{1,0:T(8,128)(2,1)S(1)} %collective-permute-done.3.refs_9_), channel_id=1, source_target_pairs={{8,16},{10,18},{12,20},{14,22},{16,24},{18,26},{20,28},{22,30},{9,... | collective-permute-start | bytes 884744 | tf_op jit(solution)/shard_map/ppermute | solution.py:189
  17.6 42.0 %copy-start.19 = (bf16[192,768]{1,0:T(8,128)(2,1)}, bf16[192,768]{1,0:T(8,128)(2,1)S(1)}, u32[]{:S(2)}) copy-start(bf16[192,768]{1,0:T(8,128)(2,1)S(1)} %collective-permute-done.5.refs_15_) | copy-start | bytes 884740
  17.6 10.3 %collective-permute-start.6 = (bf16[192,768]{1,0:T(8,128)(2,1)S(1)}, bf16[192,768]{1,0:T(8,128)(2,1)S(1)}, u32[]{:S(2)}, u32[]{:S(2)}) collective-permute-start(bf16[192,768]{1,0:T(8,128)(2,1)S(1)} %collective-permute-done.5.refs_15_), channel_id=1, source_target_pairs={{8,0},{10,2},{12,4},{14,6},{16,8},{18,10},{20,12},{22,14},{9,1},{1... | collective-permute-start | bytes 884744 | tf_op jit(solution)/shard_map/ppermute | solution.py:193
  24.6 37.3 %copy-start.5 = (bf16[576,768]{1,0:T(8,128)(2,1)}, bf16[576,768]{1,0:T(8,128)(2,1)S(1)}, u32[]{:S(2)}) copy-start(bf16[576,768]{1,0:T(8,128)(2,1)S(1)} %pad_maximum_fusion.1.refs_8_) | copy-start | bytes 2654212
  27.9 31.7 %copy-start.20 = (bf16[192,768]{1,0:T(8,128)(2,1)}, bf16[192,768]{1,0:T(8,128)(2,1)S(1)}, u32[]{:S(2)}) copy-start(bf16[192,768]{1,0:T(8,128)(2,1)S(1)} %collective-permute-done.6.refs_17_) | copy-start | bytes 884740
  27.9 42.7 %collective-permute-start.13 = (bf16[576,768]{1,0:T(8,128)(2,1)S(1)}, bf16[576,768]{1,0:T(8,128)(2,1)}, u32[]{:S(2)}, u32[]{:S(2)}) collective-permute-start(bf16[576,768]{1,0:T(8,128)(2,1)S(1)} %pad_maximum_fusion.1.refs_8_), channel_id=1, source_target_pairs={{0,8},{2,10},{4,12},{6,14},{8,16},{10,18},{12,20},{14,22},{16,24},... | collective-permute-start | bytes 2654216 | tf_op jit(solution)/shard_map/ppermute | solution.py:189
  32.4 38.1 %collective-permute-start.15 = (bf16[576,768]{1,0:T(8,128)(2,1)S(1)}, bf16[576,768]{1,0:T(8,128)(2,1)}, u32[]{:S(2)}, u32[]{:S(2)}) collective-permute-start(bf16[576,768]{1,0:T(8,128)(2,1)S(1)} %pad_maximum_fusion.1.refs_8_), channel_id=1, source_target_pairs={{8,0},{10,2},{12,4},{14,6},{16,8},{18,10},{20,12},{22,14},{24,16},... | collective-permute-start | bytes 2654216 | tf_op jit(solution)/shard_map/ppermute | solution.py:193
  33.7 5.3 %collective-permute-start.7 = (bf16[48,768]{1,0:T(8,128)(2,1)S(1)}, bf16[48,768]{1,0:T(8,128)(2,1)S(1)}, u32[]{:S(2)}, u32[]{:S(2)}) collective-permute-start(bf16[48,768]{1,0:T(8,128)(2,1)S(1)} %get-tuple-element.69), channel_id=1, source_target_pairs={{0,2},{2,0},{4,6},{6,4},{8,10},{10,8},{12,14},{14,12},{16,18},{18,... | collective-permute-start | bytes 221192 | tf_op jit(solution)/shard_map/ppermute | solution.py:179
  35.3 35.3 %collective-permute-start.10 = (bf16[256,1536]{1,0:T(8,128)(2,1)}, bf16[256,1536]{1,0:T(8,128)(2,1)}, u32[]{:S(2)}, u32[]{:S(2)}) collective-permute-start(bf16[256,1536]{1,0:T(8,128)(2,1)} %param.8), channel_id=1, source_target_pairs={{0,2},{2,0},{4,6},{6,4},{8,10},{10,8},{12,14},{14,12},{16,18},{18,... | collective-permute-start | bytes 2359304 | tf_op jit(solution)/shard_map/ppermute | solution.py:179
  35.8 34.7 %collective-permute-start.11 = (bf16[256,1536]{1,0:T(8,128)(2,1)}, bf16[256,1536]{1,0:T(8,128)(2,1)}, u32[]{:S(2)}, u32[]{:S(2)}) collective-permute-start(bf16[256,1536]{1,0:T(8,128)(2,1)} %param.8), channel_id=1, source_target_pairs={{0,4},{2,6},{4,0},{6,2},{8,12},{10,14},{12,8},{14,10},{16,20},{18,... | collective-permute-start | bytes 2359304 | tf_op jit(solution)/shard_map/ppermute | solution.py:179
  39.0 15.2 %collective-permute-start.8 = (bf16[48,768]{1,0:T(8,128)(2,1)S(1)}, bf16[48,768]{1,0:T(8,128)(2,1)S(1)}, u32[]{:S(2)}, u32[]{:S(2)}) collective-permute-start(bf16[48,768]{1,0:T(8,128)(2,1)S(1)} %get-tuple-element.70), channel_id=1, source_target_pairs={{0,4},{2,6},{4,0},{6,2},{8,12},{10,14},{12,8},{14,10},{16,20},{18,... | collective-permute-start | bytes 221192 | tf_op jit(solution)/shard_map/ppermute | solution.py:179
  54.2 5.3 %collective-permute-start.9 = (bf16[48,768]{1,0:T(8,128)(2,1)S(1)}, bf16[48,768]{1,0:T(8,128)(2,1)S(1)}, u32[]{:S(2)}, u32[]{:S(2)}) collective-permute-start(bf16[48,768]{1,0:T(8,128)(2,1)S(1)} %get-tuple-element.71), channel_id=1, source_target_pairs={{0,6},{2,4},{4,2},{6,0},{8,14},{10,12},{12,10},{14,8},{16,22},{18,... | collective-permute-start | bytes 221192 | tf_op jit(solution)/shard_map/ppermute | solution.py:179
  59.6 2.4 %collective-permute-start.12 = (bf16[192,768]{1,0:T(8,128)(2,1)}, bf16[192,768]{1,0:T(8,128)(2,1)}, u32[]{:S(2)}, u32[]{:S(2)}) collective-permute-start(bf16[192,768]{1,0:T(8,128)(2,1)} %collective-permute-done.4.refs_11_), channel_id=1, source_target_pairs={{16,24},{18,26},{20,28},{22,30},{17,25},{19,27},{21,29},{23,31}} | collective-permute-start | bytes 884744 | tf_op jit(solution)/shard_map/ppermute | solution.py:189
  61.9 8.6 %collective-permute-start.14 = (bf16[192,768]{1,0:T(8,128)(2,1)S(1)}, bf16[192,768]{1,0:T(8,128)(2,1)S(1)}, u32[]{:S(2)}, u32[]{:S(2)}) collective-permute-start(bf16[192,768]{1,0:T(8,128)(2,1)S(1)} %copy-done.21), channel_id=1, source_target_pairs={{8,0},{10,2},{12,4},{14,6},{9,1},{11,3},{13,5},{15,7}} | collective-permute-start | bytes 884744 | tf_op jit(solution)/shard_map/ppermute | solution.py:193
  70.5 16.3 %copy-start.22 = (bf16[192,768]{1,0:T(8,128)(2,1)}, bf16[192,768]{1,0:T(8,128)(2,1)S(1)}, u32[]{:S(2)}) copy-start(bf16[192,768]{1,0:T(8,128)(2,1)S(1)} %collective-permute-done.14.refs_19_) | copy-start | bytes 884740
  70.6 14.5 %collective-permute-start.16 = (bf16[256,1536]{1,0:T(8,128)(2,1)}, bf16[256,1536]{1,0:T(8,128)(2,1)S(1)}, u32[]{:S(2)}, u32[]{:S(2)}) collective-permute-start(bf16[256,1536]{1,0:T(8,128)(2,1)} %param.8), channel_id=1, source_target_pairs={{0,6},{2,4},{4,2},{6,0},{8,14},{10,12},{12,10},{14,8},{16,22},{18,... | collective-permute-start | bytes 2359304 | tf_op jit(solution)/shard_map/ppermute | solution.py:179
  74.4 22.7 %collective-permute-start.17 = (bf16[576,768]{1,0:T(8,128)(2,1)}, bf16[576,768]{1,0:T(8,128)(2,1)S(1)}, u32[]{:S(2)}, u32[]{:S(2)}) collective-permute-start(bf16[576,768]{1,0:T(8,128)(2,1)} %collective-permute-done.13.refs_10_), channel_id=1, source_target_pairs={{8,16},{10,18},{12,20},{14,22},{16,24},{18,26},{20,28},{22,30},{9,... | collective-permute-start | bytes 2654216 | tf_op jit(solution)/shard_map/ppermute | solution.py:189
  75.1 22.0 %collective-permute-start.19 = (bf16[576,768]{1,0:T(8,128)(2,1)}, bf16[576,768]{1,0:T(8,128)(2,1)S(1)}, u32[]{:S(2)}, u32[]{:S(2)}) collective-permute-start(bf16[576,768]{1,0:T(8,128)(2,1)} %collective-permute-done.15.refs_16_), channel_id=1, source_target_pairs={{8,0},{10,2},{12,4},{14,6},{16,8},{18,10},{20,12},{22,14},{9,1},{1... | collective-permute-start | bytes 2654216 | tf_op jit(solution)/shard_map/ppermute | solution.py:193
  76.4 10.5 %collective-permute-start.18 = (bf16[192,768]{1,0:T(8,128)(2,1)S(1)}, bf16[192,768]{1,0:T(8,128)(2,1)S(1)}, u32[]{:S(2)}, u32[]{:S(2)}) collective-permute-start(bf16[192,768]{1,0:T(8,128)(2,1)S(1)} %constant_dynamic-update-slice_fusion.10.refs_2_), channel_id=1, source_target_pairs={{0,8},{2,10},{4,12},{6,14},{8,16},{10,18},{12,20},{14,22},{16,24},... | collective-permute-start | bytes 884744 | tf_op jit(solution)/shard_map/ppermute | solution.py:189
  81.0 16.1 %collective-permute-start.20 = (bf16[192,768]{1,0:T(8,128)(2,1)S(1)}, bf16[192,768]{1,0:T(8,128)(2,1)S(1)}, u32[]{:S(2)}, u32[]{:S(2)}) collective-permute-start(bf16[192,768]{1,0:T(8,128)(2,1)S(1)} %constant_dynamic-update-slice_fusion.10.refs_2_), channel_id=1, source_target_pairs={{8,0},{10,2},{12,4},{14,6},{16,8},{18,10},{20,12},{22,14},{24,16},... | collective-permute-start | bytes 884744 | tf_op jit(solution)/shard_map/ppermute | solution.py:193
  86.8 53.8 %copy-start.3 = (bf16[1024,1536]{1,0:T(8,128)(2,1)}, bf16[1024,1536]{1,0:T(8,128)(2,1)S(1)}, u32[]{:S(2)}) copy-start(bf16[1024,1536]{1,0:T(8,128)(2,1)S(1)} %pad_maximum_fusion) | copy-start | bytes 9437188
  97.1 46.5 %copy-start.11 = (bf16[576,768]{1,0:T(8,128)(2,1)}, bf16[576,768]{1,0:T(8,128)(2,1)S(1)}, u32[]{:S(2)}) copy-start(bf16[576,768]{1,0:T(8,128)(2,1)S(1)} %collective-permute-done.17.refs_12_) | copy-start | bytes 2654212
  97.1 44.2 %copy-start.12 = (bf16[576,768]{1,0:T(8,128)(2,1)}, bf16[576,768]{1,0:T(8,128)(2,1)S(1)}, u32[]{:S(2)}) copy-start(bf16[576,768]{1,0:T(8,128)(2,1)S(1)} %collective-permute-done.19.refs_18_) | copy-start | bytes 2654212
  97.1 42.8 %collective-permute-start.21 = (bf16[1024,1536]{1,0:T(8,128)(2,1)S(1)}, bf16[1024,1536]{1,0:T(8,128)(2,1)S(1)}, u32[]{:S(2)}, u32[]{:S(2)}) collective-permute-start(bf16[1024,1536]{1,0:T(8,128)(2,1)S(1)} %pad_maximum_fusion), channel_id=1, source_target_pairs={{0,1},{1,0},{2,3},{3,2},{4,5},{5,4},{6,7},{7,6},{8,9},{9,8},{10,11... | collective-permute-start | bytes 9437192 | tf_op jit(solution)/shard_map/ppermute | solution.py:182
  97.2 12.4 %collective-permute-start.24 = (bf16[256,768]{1,0:T(8,128)(2,1)S(1)}, bf16[256,768]{1,0:T(8,128)(2,1)S(1)}, u32[]{:S(2)}, u32[]{:S(2)}) collective-permute-start(bf16[256,768]{1,0:T(8,128)(2,1)S(1)} %get-tuple-element.84), channel_id=1, source_target_pairs={{0,6},{2,4},{4,2},{6,0},{8,14},{10,12},{12,10},{14,8},{16,22},{18,... | collective-permute-start | bytes 1179656 | tf_op jit(solution)/shard_map/ppermute | solution.py:179
  98.9 41.0 %collective-permute-start.25 = (bf16[576,768]{1,0:T(8,128)(2,1)S(1)}, bf16[576,768]{1,0:T(8,128)(2,1)S(1)}, u32[]{:S(2)}, u32[]{:S(2)}) collective-permute-start(bf16[576,768]{1,0:T(8,128)(2,1)S(1)} %collective-permute-done.17.refs_12_), channel_id=1, source_target_pairs={{16,24},{18,26},{20,28},{22,30},{17,25},{19,27},{21,29},{23,31}} | collective-permute-start | bytes 2654216 | tf_op jit(solution)/shard_map/ppermute | solution.py:189
  99.6 40.3 %collective-permute-start.27 = (bf16[576,768]{1,0:T(8,128)(2,1)S(1)}, bf16[576,768]{1,0:T(8,128)(2,1)S(1)}, u32[]{:S(2)}, u32[]{:S(2)}) collective-permute-start(bf16[576,768]{1,0:T(8,128)(2,1)S(1)} %collective-permute-done.19.refs_18_), channel_id=1, source_target_pairs={{8,0},{10,2},{12,4},{14,6},{9,1},{11,3},{13,5},{15,7}} | collective-permute-start | bytes 2654216 | tf_op jit(solution)/shard_map/ppermute | solution.py:193
  100.9 10.0 %collective-permute-start.26 = (bf16[192,768]{1,0:T(8,128)(2,1)S(1)}, bf16[192,768]{1,0:T(8,128)(2,1)S(1)}, u32[]{:S(2)}, u32[]{:S(2)}) collective-permute-start(bf16[192,768]{1,0:T(8,128)(2,1)S(1)} %collective-permute-done.18.refs_3_), channel_id=1, source_target_pairs={{8,16},{10,18},{12,20},{14,22},{16,24},{18,26},{20,28},{22,30},{9,... | collective-permute-start | bytes 884744 | tf_op jit(solution)/shard_map/ppermute | solution.py:189
  109.6 34.0 %copy-start.15 = (bf16[256,768]{1,0:T(8,128)(2,1)}, bf16[256,768]{1,0:T(8,128)(2,1)S(1)}, u32[]{:S(2)}) copy-start(bf16[256,768]{1,0:T(8,128)(2,1)S(1)} %collective-permute-done.24.refs_5_) | copy-start | bytes 1179652
  109.6 19.9 %collective-permute-start.28 = (bf16[192,768]{1,0:T(8,128)(2,1)S(1)}, bf16[192,768]{1,0:T(8,128)(2,1)S(1)}, u32[]{:S(2)}, u32[]{:S(2)}) collective-permute-start(bf16[192,768]{1,0:T(8,128)(2,1)S(1)} %collective-permute-done.20.refs_6_), channel_id=1, source_target_pairs={{8,0},{10,2},{12,4},{14,6},{16,8},{18,10},{20,12},{22,14},{9,1},{1... | collective-permute-start | bytes 884744 | tf_op jit(solution)/shard_map/ppermute | solution.py:193
  110.9 20.5 %collective-permute-start.22 = (bf16[256,768]{1,0:T(8,128)(2,1)S(1)}, bf16[256,768]{1,0:T(8,128)(2,1)S(1)}, u32[]{:S(2)}, u32[]{:S(2)}) collective-permute-start(bf16[256,768]{1,0:T(8,128)(2,1)S(1)} %get-tuple-element.95), channel_id=1, source_target_pairs={{0,2},{2,0},{4,6},{6,4},{8,10},{10,8},{12,14},{14,12},{16,18},{18,... | collective-permute-start | bytes 1179656 | tf_op jit(solution)/shard_map/ppermute | solution.py:179
  129.6 10.4 %collective-permute-start.23 = (bf16[256,768]{1,0:T(8,128)(2,1)S(1)}, bf16[256,768]{1,0:T(8,128)(2,1)S(1)}, u32[]{:S(2)}, u32[]{:S(2)}) collective-permute-start(bf16[256,768]{1,0:T(8,128)(2,1)S(1)} %get-tuple-element.96), channel_id=1, source_target_pairs={{0,4},{2,6},{4,0},{6,2},{8,12},{10,14},{12,8},{14,10},{16,20},{18,... | collective-permute-start | bytes 1179656 | tf_op jit(solution)/shard_map/ppermute | solution.py:179
  131.4 9.9 %copy-start.16 = (bf16[256,768]{1,0:T(8,128)(2,1)}, bf16[256,768]{1,0:T(8,128)(2,1)S(1)}, u32[]{:S(2)}) copy-start(bf16[256,768]{1,0:T(8,128)(2,1)S(1)} %collective-permute-done.22.refs_3_) | copy-start | bytes 1179652
  140.7 14.4 %collective-permute-start.29 = (bf16[192,768]{1,0:T(8,128)(2,1)S(1)}, bf16[192,768]{1,0:T(8,128)(2,1)S(1)}, u32[]{:S(2)}, u32[]{:S(2)}) collective-permute-start(bf16[192,768]{1,0:T(8,128)(2,1)S(1)} %collective-permute-done.26.refs_4_), channel_id=1, source_target_pairs={{16,24},{18,26},{20,28},{22,30},{17,25},{19,27},{21,29},{23,31}} | collective-permute-start | bytes 884744 | tf_op jit(solution)/shard_map/ppermute | solution.py:189
  142.3 12.7 %collective-permute-start.30 = (bf16[192,768]{1,0:T(8,128)(2,1)S(1)}, bf16[192,768]{1,0:T(8,128)(2,1)S(1)}, u32[]{:S(2)}, u32[]{:S(2)}) collective-permute-start(bf16[192,768]{1,0:T(8,128)(2,1)S(1)} %collective-permute-done.28.refs_7_), channel_id=1, source_target_pairs={{8,0},{10,2},{12,4},{14,6},{9,1},{11,3},{13,5},{15,7}} | collective-permute-start | bytes 884744 | tf_op jit(solution)/shard_map/ppermute | solution.py:193
  159.6 3.6 %collective-permute-start.31 = (f32[544,768]{1,0:T(8,128)S(1)}, f32[544,768]{1,0:T(8,128)S(1)}, u32[]{:S(2)}, u32[]{:S(2)}) collective-permute-start(f32[544,768]{1,0:T(8,128)S(1)} %slice_bitcast_fusion), channel_id=1, source_target_pairs={{0,1},{1,0},{2,3},{3,2},{4,5},{5,4},{6,7},{7,6},{8,9},{9,8},{10,11... | collective-permute-start | bytes 5013512 | tf_op jit(solution)/shard_map/ppermute | solution.py:182
  163.5 22.6 %copy-start.7 = (bf16[384,384]{1,0:T(8,128)(2,1)S(1)}, bf16[384,384]{1,0:T(8,128)(2,1)}, u32[]{:S(2)}) copy-start(bf16[384,384]{1,0:T(8,128)(2,1)} %param.13) | copy-start | bytes 884740
  163.5 12.7 %collective-permute-start.32 = (f32[136,768]{1,0:T(8,128)S(1)}, f32[136,768]{1,0:T(8,128)}, u32[]{:S(2)}, u32[]{:S(2)}) collective-permute-start(f32[136,768]{1,0:T(8,128)S(1)} %get-tuple-element.137), channel_id=1, source_target_pairs={{0,2},{2,0},{4,6},{6,4},{8,10},{10,8},{12,14},{14,12},{16,18},{18,... | collective-permute-start | bytes 1253384 | tf_op jit(solution)/shard_map/ppermute | solution.py:179
  164.1 20.5 %collective-permute-start.33 = (f32[136,768]{1,0:T(8,128)S(1)}, f32[136,768]{1,0:T(8,128)}, u32[]{:S(2)}, u32[]{:S(2)}) collective-permute-start(f32[136,768]{1,0:T(8,128)S(1)} %get-tuple-element.139), channel_id=1, source_target_pairs={{0,4},{2,6},{4,0},{6,2},{8,12},{10,14},{12,8},{14,10},{16,20},{18,... | collective-permute-start | bytes 1253384 | tf_op jit(solution)/shard_map/ppermute | solution.py:179
  165.4 19.2 %collective-permute-start.34 = (f32[136,768]{1,0:T(8,128)S(1)}, f32[136,768]{1,0:T(8,128)}, u32[]{:S(2)}, u32[]{:S(2)}) collective-permute-start(f32[136,768]{1,0:T(8,128)S(1)} %get-tuple-element.138), channel_id=1, source_target_pairs={{0,6},{2,4},{4,2},{6,0},{8,14},{10,12},{12,10},{14,8},{16,22},{18,... | collective-permute-start | bytes 1253384 | tf_op jit(solution)/shard_map/ppermute | solution.py:179
  189.4 2.1 collective-permute-start.35
  191.7 6.7 %collective-permute-start.36 = (f32[96,384]{1,0:T(8,128)S(1)}, f32[96,384]{1,0:T(8,128)S(1)}, u32[]{:S(2)}, u32[]{:S(2)}) collective-permute-start(f32[96,384]{1,0:T(8,128)S(1)} %get-tuple-element.150), channel_id=1, source_target_pairs={{0,2},{2,0},{4,6},{6,4},{8,10},{10,8},{12,14},{14,12},{16,18},{18,... | collective-permute-start | bytes 442376 | tf_op jit(solution)/shard_map/ppermute | solution.py:179
  193.2 8.8 %collective-permute-start.37 = (f32[96,384]{1,0:T(8,128)S(1)}, f32[96,384]{1,0:T(8,128)S(1)}, u32[]{:S(2)}, u32[]{:S(2)}) collective-permute-start(f32[96,384]{1,0:T(8,128)S(1)} %get-tuple-element.152), channel_id=1, source_target_pairs={{0,4},{2,6},{4,0},{6,2},{8,12},{10,14},{12,8},{14,10},{16,20},{18,... | collective-permute-start | bytes 442376 | tf_op jit(solution)/shard_map/ppermute | solution.py:179
  193.7 8.3 %collective-permute-start.38 = (f32[96,384]{1,0:T(8,128)S(1)}, f32[96,384]{1,0:T(8,128)S(1)}, u32[]{:S(2)}, u32[]{:S(2)}) collective-permute-start(f32[96,384]{1,0:T(8,128)S(1)} %get-tuple-element.151), channel_id=1, source_target_pairs={{0,6},{2,4},{4,2},{6,0},{8,14},{10,12},{12,10},{14,8},{16,22},{18,... | collective-permute-start | bytes 442376 | tf_op jit(solution)/shard_map/ppermute | solution.py:179
  202.1 5.9 %collective-permute-start.39 = (f32[24,384]{1,0:T(8,128)S(1)}, f32[24,384]{1,0:T(8,128)S(1)}, u32[]{:S(2)}, u32[]{:S(2)}) collective-permute-start(f32[24,384]{1,0:T(8,128)S(1)} %get-tuple-element.157), channel_id=1, source_target_pairs={{0,8},{2,10},{4,12},{6,14},{8,16},{10,18},{12,20},{14,22},{16,24},... | collective-permute-start | bytes 110600 | tf_op jit(solution)/shard_map/ppermute | solution.py:339
  204.8 4.9 %collective-permute-start.40 = (f32[24,384]{1,0:T(8,128)S(1)}, f32[24,384]{1,0:T(8,128)S(1)}, u32[]{:S(2)}, u32[]{:S(2)}) collective-permute-start(f32[24,384]{1,0:T(8,128)S(1)} %get-tuple-element.159), channel_id=1, source_target_pairs={{0,16},{2,18},{4,20},{6,22},{8,24},{10,26},{12,28},{14,30},{16,0},... | collective-permute-start | bytes 110600 | tf_op jit(solution)/shard_map/ppermute | solution.py:339
  204.8 4.9 %collective-permute-start.41 = (f32[24,384]{1,0:T(8,128)S(1)}, f32[24,384]{1,0:T(8,128)S(1)}, u32[]{:S(2)}, u32[]{:S(2)}) collective-permute-start(f32[24,384]{1,0:T(8,128)S(1)} %get-tuple-element.158), channel_id=1, source_target_pairs={{0,24},{2,26},{4,28},{6,30},{8,0},{10,2},{12,4},{14,6},{16,8},{18,... | collective-permute-start | bytes 110600 | tf_op jit(solution)/shard_map/ppermute | solution.py:339
  209.7 5.8 %collective-permute-start.42 = (f32[24,384]{1,0:T(8,128)S(1)}, f32[24,384]{1,0:T(8,128)S(1)}, u32[]{:S(2)}, u32[]{:S(2)}) collective-permute-start(f32[24,384]{1,0:T(8,128)S(1)} %get-tuple-element.134), channel_id=1, source_target_pairs={{0,8},{2,10},{4,12},{6,14},{8,16},{10,18},{12,20},{14,22},{16,24},... | collective-permute-start | bytes 110600 | tf_op jit(solution)/shard_map/ppermute | solution.py:339
  210.7 5.2 %collective-permute-start.43 = (f32[24,384]{1,0:T(8,128)S(1)}, f32[24,384]{1,0:T(8,128)S(1)}, u32[]{:S(2)}, u32[]{:S(2)}) collective-permute-start(f32[24,384]{1,0:T(8,128)S(1)} %get-tuple-element.134), channel_id=1, source_target_pairs={{0,16},{2,18},{4,20},{6,22},{8,24},{10,26},{12,28},{14,30},{16,0},... | collective-permute-start | bytes 110600 | tf_op jit(solution)/shard_map/ppermute | solution.py:339
  213.7 4.0 %collective-permute-start.44 = (f32[24,384]{1,0:T(8,128)S(1)}, f32[24,384]{1,0:T(8,128)S(1)}, u32[]{:S(2)}, u32[]{:S(2)}) collective-permute-start(f32[24,384]{1,0:T(8,128)S(1)} %get-tuple-element.134), channel_id=1, source_target_pairs={{0,24},{2,26},{4,28},{6,30},{8,0},{10,2},{12,4},{14,6},{16,8},{18,... | collective-permute-start | bytes 110600 | tf_op jit(solution)/shard_map/ppermute | solution.py:339
  217.7 5.1 %collective-permute-start.45 = (f32[96,384]{1,0:T(8,128)S(1)}, f32[96,384]{1,0:T(8,128)S(1)}, u32[]{:S(2)}, u32[]{:S(2)}) collective-permute-start(f32[96,384]{1,0:T(8,128)S(1)} %constant_dynamic-update-slice_fusion.6), channel_id=1, source_target_pairs={{0,2},{2,0},{4,6},{6,4},{8,10},{10,8},{12,14},{14,12},{16,18},{18,... | collective-permute-start | bytes 442376 | tf_op jit(solution)/shard_map/ppermute | solution.py:179
  218.2 5.1 %collective-permute-start.46 = (f32[96,384]{1,0:T(8,128)S(1)}, f32[96,384]{1,0:T(8,128)S(1)}, u32[]{:S(2)}, u32[]{:S(2)}) collective-permute-start(f32[96,384]{1,0:T(8,128)S(1)} %constant_dynamic-update-slice_fusion.6), channel_id=1, source_target_pairs={{0,4},{2,6},{4,0},{6,2},{8,12},{10,14},{12,8},{14,10},{16,20},{18,... | collective-permute-start | bytes 442376 | tf_op jit(solution)/shard_map/ppermute | solution.py:179
  219.4 6.0 %collective-permute-start.47 = (f32[96,384]{1,0:T(8,128)S(1)}, f32[96,384]{1,0:T(8,128)S(1)}, u32[]{:S(2)}, u32[]{:S(2)}) collective-permute-start(f32[96,384]{1,0:T(8,128)S(1)} %constant_dynamic-update-slice_fusion.6), channel_id=1, source_target_pairs={{0,6},{2,4},{4,2},{6,0},{8,14},{10,12},{12,10},{14,8},{16,22},{18,... | collective-permute-start | bytes 442376 | tf_op jit(solution)/shard_map/ppermute | solution.py:179
  225.5 2.1 collective-permute-start.48
  (8 other events, 10.2 us)

commit v3 on v2

--- a/solution.py
+++ b/solution.py
@@ -10,47 +10,59 @@
 HIGH = lax.Precision.HIGH
 F32 = jnp.float32
 BF16 = jnp.bfloat16
+GROUP = 4
 
 
 def coupling(values, weight):
     return jax.nn.gelu(jnp.dot(values, weight, precision=HIGH))
 
 
-def attend_kernel(group, planes, count, *refs):
-    mine_ref, other_ref, *refs = refs
-    stay_refs, refs = refs[:group], refs[group:]
-    gain_ref, *refs = refs
-    flow_refs, (scaled_ref, stats_ref, weight, sems) = refs[:-4], refs[-4:]
-    own, up, down = flow_refs[:2], flow_refs[2 : 2 * planes], flow_refs[2 * planes :]
+def place():
     wide, core = lax.axis_index("wide"), lax.axis_index("narrow")
-    plane, member = wide // group, wide % group
-    rows = own[0].shape[0]
-
-    def copies(at, p):
-        if at == p:
-            first, rest = own
-        else:
-            first, rest = (up if at > p else down)[2 * (abs(at - p) - 1) :][:2]
-        out = []
-        for s in range(group):
-            source = rest.at[pl.ds((s - 1) * rows, rows)] if s else first
-            target = pl.multiple_of((p * group + (member ^ s)) * rows, 64)
-            out.append(pltpu.make_async_copy(source, weight.at[pl.ds(target, rows)], sems.at[p, s]))
-        return out
+    return wide // GROUP, wide % GROUP, core
+
+
+def part_of(flow, at, p):
+    steps = (len(flow) // 2 - 2) // 2
+    step = abs(at - p)
+    if step > steps:
+        return flow[2:4]
+    if not step:
+        return flow[:2]
+    first = 4 + 2 * (step - 1) + (0 if at > p else 2 * steps)
+    return flow[first : first + 2]
+
+
+def share_of(pair, s, start, count, span):
+    at = start + (s - 1) * span if s else start
+    return pair[1 if s else 0].at[pl.ds(at, count)]
+
+
+def attend_kernel(rows, planes, *refs):
+    mine_ref, other_ref, *flow, out_ref, weight, sems = refs
+    plane, member, core = place()
+    span = flow[0].shape[0]
+    steps = (len(flow) // 2 - 2) // 2
 
     for at in range(planes):
 
         @pl.when((pl.program_id(0) == 0) & (plane == at))
         def _():
-            everything = [copy for p in range(planes) for copy in copies(at, p)]
-            for copy in everything:
+            copies = []
+            for p in range(planes):
+                if abs(at - p) > steps:
+                    weight[p * GROUP * rows : (p + 1) * GROUP * rows] = jnp.zeros((GROUP * rows, weight.shape[1]), BF16)
+                    continue
+                for s in range(GROUP):
+                    target = pl.multiple_of((p * GROUP + (member ^ s)) * rows, 64)
+                    source = share_of(part_of(flow, at, p), s, 0, rows, span)
+                    copies.append(pltpu.make_async_copy(source, weight.at[pl.ds(target, rows)], sems.at[p, s]))
+            for copy in copies:
                 copy.start()
-            for copy in everything:
+            for copy in copies:
                 copy.wait()
 
-    heads = mine_ref.shape[2]
-    local = mine_ref.shape[1]
-    gain = gain_ref[...].astype(F32)
+    group, local, heads = mine_ref.shape
     for h in range(0, group, 2):
         lhs = mine_ref[h : h + 2].reshape(2 * local, heads)
         rhs = other_ref[h : h + 2].reshape(2 * local, heads)
@@ -58,115 +70,129 @@
         total = jnp.dot(lhs, weight[pl.ds(at, heads)], preferred_element_type=F32)
         at = pl.multiple_of((1 - core) * heads, 128)
         total += jnp.dot(rhs, weight[pl.ds(at, heads)], preferred_element_type=F32)
-        stay = jnp.concatenate([stay_refs[h][...], stay_refs[h + 1][...]], axis=0)
-        stream = (stay.astype(F32) + total).astype(BF16).astype(F32)
-        scaled_ref[0, h * local : (h + 2) * local] = (stream * gain).astype(BF16)
-        sums = jnp.sum(stream, axis=1, keepdims=True)
-        squares = jnp.sum(stream * stream, axis=1, keepdims=True)
-        lane = lax.broadcasted_iota(jnp.int32, (2 * local, 128), 1)
-        both = jnp.where(lane == 0, sums, jnp.where(lane == 1, squares, 0.0))
-        stats_ref[:, h * local : (h + 2) * local] = both.T[:8]
-    scaled_ref[0, group * local :] = jnp.broadcast_to(gain_ref[...], (16, count))
-
-
-def attend(mine, other, stay, gain, own, up, down):
+        out_ref[h * local : (h + 2) * local] = total
+
+
+def attend(rows, planes, mine, other, flow):
     group, tokens, heads = mine.shape
-    local = tokens // 2
-    count = gain.shape[1]
-    planes = len(up) + 1
-    flow = [*own] + [v for pair in up for v in pair] + [v for pair in down for v in pair]
-    whole = pl.BlockSpec(memory_space=pl.ANY)
-    part = pl.BlockSpec((group, local, heads), lambda i: (0, i, 0))
-    work = group * tokens * heads * 2 * count
+    count = flow[0].shape[1]
+    part = pl.BlockSpec((group, tokens // 2, heads), lambda i: (0, i, 0))
     return pl.pallas_call(
-        functools.partial(attend_kernel, group, planes, count),
+        functools.partial(attend_kernel, rows, planes),
         grid=(2,),
-        in_specs=[part, part]
-        + [pl.BlockSpec((local, count), lambda i: (i, 0))] * group
-        + [pl.BlockSpec((1, count), lambda i: (0, 0))]
-        + [whole] * len(flow),
-        out_specs=[
-            pl.BlockSpec((1, group * local + 16, count), lambda i: (i, 0, 0)),
-            pl.BlockSpec((8, group * local), lambda i: (0, i)),
-        ],
-        out_shape=[
-            jax.ShapeDtypeStruct((2, group * local + 16, count), BF16),
-            jax.ShapeDtypeStruct((8, group * tokens), F32),
-        ],
-        scratch_shapes=[
-            pltpu.VMEM((2 * heads, count), BF16),
-            pltpu.SemaphoreType.DMA((planes, group)),
-        ],
-        compiler_params=pltpu.CompilerParams(vmem_limit_bytes=60 << 20),
-        cost_estimate=pl.CostEstimate(flops=2 * work, bytes_accessed=14 << 20, transcendentals=0),
-    )(mine, other, *stay, gain, *flow)
-
-
-def project_kernel(group, planes, *refs):
-    scaled_ref, stats_ref, *refs = refs
-    flow_refs, (out_ref, down, sems) = refs[:-3], refs[-3:]
-    own, up, lower = flow_refs[0], flow_refs[1:planes], flow_refs[planes:]
-    plane, core = lax.axis_index("wide") // group, lax.axis_index("narrow")
-    rows = own.shape[0]
-
-    def copies(at):
+        in_specs=[part, part] + [pl.BlockSpec(memory_space=pl.ANY)] * len(flow),
+        out_specs=pl.BlockSpec((group * tokens // 2, count), lambda i: (i, 0)),
+        out_shape=jax.ShapeDtypeStruct((group * tokens, count), F32),
+        scratch_shapes=[pltpu.VMEM((2 * heads, count), BF16), pltpu.SemaphoreType.DMA((planes, group))],
+        compiler_params=pltpu.CompilerParams(vmem_limit_bytes=40 << 20),
+        cost_estimate=pl.CostEstimate(
+            flops=4 * group * tokens * heads * count, bytes_accessed=16 << 20, transcendentals=0
+        ),
+    )(mine, other, *flow)
+
+
+def finish_kernel(rows, planes, *refs):
+    total_ref, far_ref, gain_ref, *refs = refs
+    stay_refs, (*flow, out_ref, weight, down, scaled, sums, sems, down_sems) = refs[:GROUP], refs[GROUP:]
+    plane, member, core = place()
+    span = flow[0].shape[0]
+    columns = span - rows
+
+    def far_copies():
+        out = []
+        for s in range(GROUP):
+            target = pl.multiple_of((member ^ s) * rows, 64)
+            source = share_of(flow[2:4], s, 0, rows, span)
+            out.append(pltpu.make_async_copy(source, weight.at[pl.ds(target, rows)], sems.at[s]))
+        return out
+
+    def down_copies(at):
         out = []
         for p in range(planes):
-            source = own if at == p else (up if at > p else lower)[abs(at - p) - 1]
-            out.append(pltpu.make_async_copy(source, down.at[pl.ds(p * rows, rows)], sems.at[p]))
+            for s in range(GROUP):
+                target = pl.multiple_of((p * GROUP + (member ^ s)) * columns, 16)
+                source = share_of(part_of(flow, at, p), s, rows, columns, span)
+                out.append(pltpu.make_async_copy(source, down.at[pl.ds(target, columns)], down_sems.at[p, s]))
         return out
 
+    far = far_copies()
+    for copy in far:
+        copy.start()
     for at in range(planes):
 
         @pl.when(plane == at)
         def _():
-            for copy in copies(at):
+            copies = down_copies(at)
+            for copy in copies:
                 copy.start()
-            for copy in copies(at):
+            for copy in copies:
                 copy.wait()
 
-    local = (scaled_ref.shape[1] - 16) // group
-    span = local + 8
+    for copy in far:
+        copy.wait()
+    local = stay_refs[0].shape[0] // 2
+    half = GROUP * local
+    gain = gain_ref[...].astype(F32)
+    for i in range(2):
+        for h in range(0, GROUP, 2):
+            at = i * half + h * local
+            lhs = jnp.concatenate([far_ref[h + g, i * local : (i + 1) * local] for g in range(2)], axis=0)
+            total = total_ref[at : at + 2 * local] + jnp.dot(lhs, weight[...], preferred_element_type=F32)
+            stay = jnp.concatenate([stay_refs[h + g][i * local : (i + 1) * local] for g in range(2)], axis=0)
+            stream = (stay.astype(F32) + total).astype(BF16).astype(F32)
+            scaled[at : at + 2 * local] = (stream * gain).astype(BF16)
+            row_sum = jnp.sum(stream, axis=1, keepdims=True)
+            squares = jnp.sum(stream * stream, axis=1, keepdims=True)
+            lane = lax.broadcasted_iota(jnp.int32, (2 * local, 128), 1)
+            both = jnp.where(lane == 0, row_sum, jnp.where(lane == 1, squares, 0.0))
+            sums[:, at : at + 2 * local] = both.T[:8]
+
     dims = (((1,), (1,)), ((), ()))
-    gain = lax.dot_general(
-        scaled_ref[0, group * local : group * local + 16], down[...], dims, preferred_element_type=F32
-    )
+    gains = jnp.broadcast_to(gain_ref[...], (16, gain_ref.shape[1]))
+    gains = lax.dot_general(gains, down[...], dims, preferred_element_type=F32)
+    line = local + 8
     for t in range(2):
         k = core if t == 0 else 1 - core
-        at = pl.multiple_of(k * (group * local), 128)
-        value = lax.dot_general(scaled_ref[k, : group * local], down[...], dims, preferred_element_type=F32)
-        sums = stats_ref[:, pl.ds(at, group * local)]
-        for s in range(group):
-            out_ref[t, s * span : s * span + local] = value[s * local : (s + 1) * local]
-            out_ref[t, s * span + local : (s + 1) * span] = gain[:8]
-            out_ref[t, s * span + local + 1 : s * span + local + 3, :local] = sums[:2, s * local : (s + 1) * local]
-
-
-def project(group, scaled, stats, own, up, down):
-    planes = len(up) + 1
-    rows, features = own.shape
-    local = (scaled.shape[1] - 16) // group
-    count = planes * rows
-    whole = pl.BlockSpec(memory_space=pl.ANY)
+        at = pl.multiple_of(k * half, 128)
+        value = lax.dot_general(scaled[pl.ds(at, half)], down[...], dims, preferred_element_type=F32)
+        stats = sums[:, pl.ds(at, half)]
+        for s in range(GROUP):
+            out_ref[t, s * line : s * line + local] = value[s * local : (s + 1) * local]
+            out_ref[t, s * line + local : (s + 1) * line] = gains[:8]
+            out_ref[t, s * line + local + 1 : s * line + local + 3, :local] = stats[:2, s * local : (s + 1) * local]
+
+
+def finish(rows, planes, total, far, gain, stay, flow):
+    count = total.shape[1]
+    tokens = total.shape[0]
+    span = flow[0].shape[0]
+    out = (span - rows) * GROUP * planes
     inside = pl.BlockSpec(memory_space=pltpu.VMEM)
     return pl.pallas_call(
-        functools.partial(project_kernel, group, planes),
-        in_specs=[inside, inside] + [whole] * (2 * planes - 1),
+        functools.partial(finish_kernel, rows, planes),
+        in_specs=[inside] * (3 + GROUP) + [pl.BlockSpec(memory_space=pl.ANY)] * len(flow),
         out_specs=inside,
-        out_shape=jax.ShapeDtypeStruct((2, group * (local + 8), count), F32),
-        scratch_shapes=[pltpu.VMEM((count, features), BF16), pltpu.SemaphoreType.DMA((planes,))],
+        out_shape=jax.ShapeDtypeStruct((2, tokens // 2 + 8 * GROUP, out), F32),
+        scratch_shapes=[
+            pltpu.VMEM((GROUP * rows, count), BF16),
+            pltpu.VMEM((out, count), BF16),
+            pltpu.VMEM((tokens, count), BF16),
+            pltpu.VMEM((8, tokens), F32),
+            pltpu.SemaphoreType.DMA((GROUP,)),
+            pltpu.SemaphoreType.DMA((planes, GROUP)),
+        ],
         compiler_params=pltpu.CompilerParams(vmem_limit_bytes=40 << 20),
         cost_estimate=pl.CostEstimate(
-            flops=4 * group * local * features * count, bytes_accessed=8 << 20, transcendentals=0
+            flops=2 * tokens * count * (GROUP * rows + out), bytes_accessed=16 << 20, transcendentals=0
         ),
-    )(scaled, stats, own, *up, *down)
+    )(total, far, gain, *stay, *flow)
 
 
 def per_device(group, wides, narrows, context, out_weight, residual, ln_gain, side_down, f_weight, g_weight, targets):
     planes = wides // group
     wide, core = lax.axis_index("wide"), lax.axis_index("narrow")
     plane, member = wide // group, wide % group
-    short = planes == 4 and narrows == 2
+    short = group == GROUP and planes == 4 and narrows == 2
     features = out_weight.shape[1] // group
     rows = out_weight.shape[0]
     tokens = context.shape[0]
@@ -218,46 +244,52 @@
         return value
 
     if short:
+        own = [jnp.concatenate(pair, axis=0) for pair in zip(own, down_own)]
+        boxes = [jnp.concatenate([context, value], axis=1) for value in stay_own[1:]]
         up, down = [[v] for v in own[:1]], [[v] for v in own[:1]]
+        far = []
 
         def pass_on(i, k):
             up[i].append(step_up(up[i][-1], k))
             down[i].append(step_down(down[i][-1], k))
 
+        def pass_last(i):
+            middle = planes // 2 * group
+            pairs = [(j, j + group) for j in range(wides - 2 * group, wides - group)]
+            pairs += [(j + group, j) for j in range(group)]
+            far.append(lax.ppermute(jnp.where(wide >= middle, up[i][-1], down[i][-1]), "wide", pairs))
+
         pass_on(0, 1)
         pass_on(0, 2)
-        pieces = [to_member(own[s], s) for s in members]
-        rest = jnp.concatenate(pieces[1:], axis=0)
-
-        rest, context, down_own, up, down = lax.optimization_barrier((rest, context, down_own, up, down))
+        pieces = [to_member(own[s], s) for s in range(1, group)]
+        rest = jnp.concatenate(pieces, axis=0)
+
+        rest, boxes, up, down = lax.optimization_barrier((rest, boxes, up, down))
         up.append([rest])
         down.append([rest])
         pass_on(1, 1)
-        pass_on(0, 3)
-        arrived = [context, to_member(context, 1), to_member(context, 2)]
-        down_plane = in_plane([to_member(down_own[s], s) for s in members])
-
-        state = (down_plane, arrived, stay_own, up, down)
-        down_plane, arrived, stay_own, up, down = lax.optimization_barrier(state)
-        up.append([down_plane])
-        down.append([down_plane])
+        pass_last(0)
+        arrived = [to_member(boxes[0], 1), to_member(boxes[1], 2)]
+
+        arrived, boxes, up, down, far = lax.optimization_barrier((arrived, boxes, up, down, far))
         pass_on(1, 2)
-        pass_on(2, 1)
-        arrived.append(to_member(arrived[0], 3))
-        stay = [stay_own[0], None, None, to_member(stay_own[3], 3)]
-        part = jnp.concatenate(arrived, axis=0)
-
-        part, stay_own, up, down = lax.optimization_barrier((part, stay_own, up, down))
-        pass_on(1, 3)
-        pass_on(2, 2)
-        stay[1], stay[2] = to_member(stay_own[1], 1), to_member(stay_own[2], 2)
+        arrived.append(to_member(boxes[2], 3))
+        heads = context.shape[1]
+        part = jnp.concatenate([context] + [v[:, :heads] for v in arrived], axis=0)
+        stay = stay_own[:1] + [v[:, heads:] for v in arrived]
+
+        part, stay, up, down, far = lax.optimization_barrier((part, stay, up, down, far))
         mine, other = [v.reshape(group, tokens, -1) for v in (part, to_core(part, 1))]
-
-        mine, other, stay, up, down = lax.optimization_barrier((mine, other, stay, up, down))
-        pass_on(2, 3)
-        pairs = [list(zip(v[0][1:], v[1][1:])) for v in (up, down)]
-        scaled, stats = attend(mine, other, stay, gain, [own[0], rest], *pairs)
-        both = project(group, scaled, stats, down_plane, up[2][1:], down[2][1:])
+        pass_last(1)
+        near = [v[i][k] for v in (up, down) for k in range(1, planes - 1) for i in range(2)]
+        flow = [own[0], rest, own[0], rest] + near
+        total = attend(rows, planes, mine, other, flow)
+        last = jnp.where(plane == 0, planes - 1, 0)
+        width = group * rows
+        last_part = jnp.where(last * width // heads == core, mine, other)
+        last_part = lax.dynamic_slice_in_dim(last_part, last * width % heads, width, 2)
+        flow = [own[0], rest, *far] + near
+        both = finish(rows, planes, total, last_part, gain, stay, flow)
         summed = both[0] + to_core(both[1], 1)
         span = local + 8
         projected = summed[:span]
@@ -359,7 +391,7 @@
 
 def solution(mesh):
     wides, narrows = mesh.shape["wide"], mesh.shape["narrow"]
-    group = 4 if wides % 4 == 0 else 1
+    group = GROUP if wides % GROUP == 0 else 1
     in_specs = (
         P("wide", "narrow"),
         P("wide", "narrow"),

time: 229 us -> 208 us (0.908)
  starting transfers between devices: 70.8 us -> 43.2 us
  waiting for transfers between devices: 127 us -> 116 us
  local copies, waits for them, and re-layouts: 9.43 us -> 16.9 us
  other arithmetic: 4.73 us -> 10 us
  Pallas kernels: 13.6 us -> 17.6 us
    ppermute x0 -> x2, waiting for transfers between devices: none -> 39 us  [pass_last(): lax.ppermute(jnp.where(wide >= middle, up[i][-1], down[i][-1]), 'wide', p...]
    ppermute x9 -> x4, waiting for transfers between devices: 41.3 us -> 6.15 us  [step_down(): return lax.ppermute(value, 'wide', pairs)]
    ppermute x21 -> x15, waiting for transfers between devices: 71.2 us -> 52.9 us  [to_member(): return lax.ppermute(value, 'wide', pairs) if s else value]
    ppermute x21 -> x15, starting transfers between devices: 29 us -> 18 us  [to_member(): return lax.ppermute(value, 'wide', pairs) if s else value]
    ppermute x9 -> x4, starting transfers between devices: 19.7 us -> 11.2 us  [step_up(): return lax.ppermute(value, 'wide', pairs)]
    ppermute x9 -> x4, starting transfers between devices: 11.6 us -> 5.14 us  [step_down(): return lax.ppermute(value, 'wide', pairs)]
    select_n x0 -> x3, other arithmetic: none -> 4.7 us  [the longest x1 3.33 us: per_device(): last_part = jnp.where(last * width // heads == core, mine, other)]
    slice x0 -> x7, local copies, waits for them, and re-layouts: none -> 4.64 us  [the longest x3 3.4 us: per_device(): stay = stay_own[:1] + [v[:, heads:] for v in arrived]]
  transfers between devices with their start and end apart: 49 -> 35, of which waited for: 28 -> 24; matrix products, arithmetic and copies ran while one was open for 2% -> 7% of each run, Pallas kernels for 5% -> 4%
where the time goes in v3:
time: 208 us
  waiting for transfers between devices  116 us (56%)
  starting transfers between devices  43.2 us (21%)
  Pallas kernels  17.6 us (8%)
  local copies, waits for them, and re-layouts  16.9 us (8%)
  other arithmetic  10 us (5%)
    ppermute x15, waiting for transfers between devices, to_member(): return lax.ppermute(value, 'wide', pairs) if s else value  52.9 us
    ppermute x2, waiting for transfers between devices, pass_last(): lax.ppermute(jnp.where(wide >= middle, up[i][-1], down[i][-1]), 'wide', p...  39 us
    ppermute x15, starting transfers between devices, to_member(): return lax.ppermute(value, 'wide', pairs) if s else value  18 us
    ppermute x4, starting transfers between devices, step_up(): return lax.ppermute(value, 'wide', pairs)  11.2 us
    ppermute x4, waiting for transfers between devices, to_core(): lax.ppermute(value, 'narrow', [(i, i ^ t) for i in range(narrows)])  9.39 us
    pallas_call x1, Pallas kernels, finish(): pl.pallas_call(functools.partial(finish_kernel, rows, planes), in_specs=[...  8.97 us
    pallas_call x1, Pallas kernels, attend(): pl.pallas_call(functools.partial(attend_kernel, rows, planes), grid=(2,),...  8.64 us
    ppermute x6, waiting for transfers between devices, shift(): lax.ppermute(value, 'wide', [(i, (i + k * group) % wides) for i in range(...  7.15 us
  transfers between devices with their start and end apart: 35, of which 24 were waited for; matrix products, arithmetic and copies ran while one was open for 7% of the time, Pallas kernels for 4%

profile of v3, /device:TPU:0, one launch (start us, length us, event | category | flops | bytes accessed | tf_op | source)
XLA Modules:
  0.0 207.5 jit_solution(16540680791042847611)
XLA Ops:
  0.7 1.1 dynamic-slice_bitcast_fusion
  1.7 1.3 constant_dynamic-slice_fusion.7
  3.1 5.1 %collective-permute-start.3 = (bf16[240,768]{1,0:T(8,128)(2,1)S(1)}, bf16[240,768]{1,0:T(8,128)(2,1)S(1)}, u32[]{:S(2)}, u32[]{:S(2)}) collective-permute-start(bf16[240,768]{1,0:T(8,128)(2,1)S(1)} %pad_maximum_fusion.9.refs_2_.refs_4_.refs_7_), channel_id=1, source_target_pairs={{0,8},{2,10},{4,12},{6,14},{8,16},{10,18},{12,20},{14,22},{16,24},... | collective-permute-start | bytes 1105928 | tf_op jit(solution)/shard_map/ppermute | solution.py:215
  8.2 1.3 collective-permute-start.5
  9.6 2.5 %collective-permute-start.2 = (bf16[240,768]{1,0:T(8,128)(2,1)S(1)}, bf16[240,768]{1,0:T(8,128)(2,1)S(1)}, u32[]{:S(2)}, u32[]{:S(2)}) collective-permute-start(bf16[240,768]{1,0:T(8,128)(2,1)S(1)} %pad_maximum_fusion.8), channel_id=1, source_target_pairs={{0,6},{2,4},{4,2},{6,0},{8,14},{10,12},{12,10},{14,8},{16,22},{18,... | collective-permute-start | bytes 1105928 | tf_op jit(solution)/shard_map/ppermute | solution.py:205
  13.3 0.9 constant_dynamic-slice_fusion.6
  14.2 1.8 collective-permute-done.3.refs_6_.refs_11_
  16.7 3.5 %collective-permute-done.5.refs_10_.refs_15_ = bf16[240,768]{1,0:T(8,128)(2,1)S(1)} collective-permute-done((bf16[240,768]{1,0:T(8,128)(2,1)S(1)}, bf16[240,768]{1,0:T(8,128)(2,1)S(1)}, u32[]{:S(2)}, u32[]{:S(2)}) %collective-permute-start.5) | collective-permute-done | bytes 368672 | tf_op jit(solution)/shard_map/ppermute | solution.py:219
  20.2 1.3 collective-permute-start.6
  21.5 2.0 pad_maximum_fusion.1
  23.5 5.0 %collective-permute-done.1 = bf16[240,768]{1,0:T(8,128)(2,1)S(1)} collective-permute-done((bf16[240,768]{1,0:T(8,128)(2,1)S(1)}, bf16[240,768]{1,0:T(8,128)(2,1)S(1)}, u32[]{:S(2)}, u32[]{:S(2)}) %collective-permute-start.1) | collective-permute-done | bytes 368672 | tf_op jit(solution)/shard_map/ppermute | solution.py:205
  28.7 2.7 %collective-permute-done.6.refs_12_.refs_17_ = bf16[240,768]{1,0:T(8,128)(2,1)S(1)} collective-permute-done((bf16[240,768]{1,0:T(8,128)(2,1)S(1)}, bf16[240,768]{1,0:T(8,128)(2,1)S(1)}, u32[]{:S(2)}, u32[]{:S(2)}) %collective-permute-start.6) | collective-permute-done | bytes 368672 | tf_op jit(solution)/shard_map/ppermute | solution.py:219
  31.4 1.5 collective-permute-start.7
  32.9 1.5 collective-permute-start.8
  34.4 4.7 %collective-permute-start.9 = (bf16[720,768]{1,0:T(8,128)(2,1)S(1)}, bf16[720,768]{1,0:T(8,128)(2,1)}, u32[]{:S(2)}, u32[]{:S(2)}) collective-permute-start(bf16[720,768]{1,0:T(8,128)(2,1)S(1)} %pad_maximum_fusion.4.refs_3_.refs_5_.refs_8_), channel_id=1, source_target_pairs={{0,8},{2,10},{4,12},{6,14},{8,16},{10,18},{12,20},{14,22},{16,24},... | collective-permute-start | bytes 3317768 | tf_op jit(solution)/shard_map/ppermute | solution.py:215
  39.1 1.3 collective-permute-start.10
  40.5 1.3 collective-permute-start.11
  41.8 30.4 %collective-permute-done.11.refs_9_ = bf16[240,768]{1,0:T(8,128)(2,1)S(1)} collective-permute-done((bf16[240,768]{1,0:T(8,128)(2,1)S(1)}, bf16[240,768]{1,0:T(8,128)(2,1)S(1)}, u32[]{:S(2)}, u32[]{:S(2)}) %collective-permute-start.11) | collective-permute-done | bytes 368672 | tf_op jit(solution)/shard_map/ppermute | solution.py:260
  74.3 1.3 collective-permute-start.14
  75.6 0.8 slice.72.refs_4_
  76.4 1.2 slice.70
  77.6 1.8 slice.73.refs_5_
  79.5 18.6 %collective-permute-done.12 = bf16[256,2304]{1,0:T(8,128)(2,1)S(1)} collective-permute-done((bf16[256,2304]{1,0:T(8,128)(2,1)}, bf16[256,2304]{1,0:T(8,128)(2,1)S(1)}, u32[]{:S(2)}, u32[]{:S(2)}) %collective-permute-start.12) | collective-permute-done | bytes 1179680 | tf_op jit(solution)/shard_map/ppermute | solution.py:205
  98.1 0.8 slice.92.refs_6_
  99.2 1.3 broadcast_select_fusion
  100.9 1.3 collective-permute-start.16
  103.0 2.0 collective-permute-done.15
  105.1 3.3 %dynamic-slice_select_fusion.refs_1_ = bf16[4,256,768]{2,1,0:T(8,128)(2,1)S(1)} fusion(bf16[4,256,1536]{2,1,0:T(8,128)(2,1)} %bitcast.5.refs_1_, s32[]{:T(128)S(6)} %select_n.164, bf16[4,256,1536]{2,1,0:T(8,128)(2,1)S(1)} %bitcast.31, pred[]{:T(512)S(6)} %eq.18), kind=kLoop, calls=%fused_computation.4 | loop fusion | flops 786432 | bytes 4718597 | tf_op jit(solution)/shard_map/jit(_where)/select_n | solution.py:289
  108.5 1.0 copy-done.19
  109.4 1.0 copy-done.21
  110.4 8.6 %shard_map.103.refs_0_ = f32[1024,768]{1,0:T(8,128)S(1)} custom-call(bf16[4,256,1536]{2,1,0:T(8,128)(2,1)S(1)} %bitcast.32, bf16[4,256,1536]{2,1,0:T(8,128)(2,1)} %bitcast.5.refs_1_, bf16[240,768]{1,0:T(8,128)(2,1)S(1)} %copy-done.9, bf16[720,768]{1,0:T(8,128)(2,1)S(1)} %copy-done.2, bf16[240,768]{1,0:T(8,128)(2,1)S(1)} %copy-done.9, ...), custom_call_target="tpu_custom_call" | custom-call | flops 4831838208 | bytes 16777216 | tf_op jit(solution)/shard_map/pallas_call | solution.py:80
  119.1 1.7 copy-done.3
  120.8 8.6 %collective-permute-done.16.refs_10_ = bf16[720,768]{1,0:T(8,128)(2,1)} collective-permute-done((bf16[720,768]{1,0:T(8,128)(2,1)}, bf16[720,768]{1,0:T(8,128)(2,1)}, u32[]{:S(2)}, u32[]{:S(2)}) %collective-permute-start.16) | collective-permute-done | bytes 1105952 | tf_op jit(solution)/shard_map/ppermute | solution.py:260
  129.4 9.0 %shard_map.104 = f32[2,544,768]{2,1,0:T(8,128)} custom-call(f32[1024,768]{1,0:T(8,128)} %copy-done.3, bf16[4,256,768]{2,1,0:T(8,128)(2,1)S(1)} %dynamic-slice_select_fusion.refs_1_, bf16[1,768]{1,0:T(2,128)(2,1)S(1)} %broadcast_in_dim.14.refs_2_, bf16[256,768]{1,0:T(8,128)(2,1)S(1)} %copy-done.17, bf16[256,768]{1,0:T(8,128)(2,1)S(1)} %copy-done.14, ...), custom_call_target="tpu_custom_call" | custom-call | flops 2415919104 | bytes 16777216 | tf_op jit(solution)/shard_map/pallas_call | solution.py:171
  138.4 1.7 slice_bitcast_fusion
  140.2 3.5 %collective-permute-done.17 = f32[544,768]{1,0:T(8,128)S(1)} collective-permute-done((f32[544,768]{1,0:T(8,128)S(1)}, f32[544,768]{1,0:T(8,128)S(1)}, u32[]{:S(2)}, u32[]{:S(2)}) %collective-permute-start.17) | collective-permute-done | bytes 1671200 | tf_op jit(solution)/shard_map/ppermute | solution.py:208
  144.0 1.7 collective-permute-start.20
  145.7 0.8 collective-permute-start.19
  146.5 1.1 collective-permute-start.18
  147.6 10.0 %collective-permute-done.20 = f32[136,768]{1,0:T(8,128)} collective-permute-done((f32[136,768]{1,0:T(8,128)S(1)}, f32[136,768]{1,0:T(8,128)}, u32[]{:S(2)}, u32[]{:S(2)}) %collective-permute-start.20) | collective-permute-done | bytes 417824 | tf_op jit(solution)/shard_map/ppermute | solution.py:205
  157.6 8.1 %collective-permute-done.19 = f32[136,768]{1,0:T(8,128)} collective-permute-done((f32[136,768]{1,0:T(8,128)S(1)}, f32[136,768]{1,0:T(8,128)}, u32[]{:S(2)}, u32[]{:S(2)}) %collective-permute-start.19) | collective-permute-done | bytes 417824 | tf_op jit(solution)/shard_map/ppermute | solution.py:205
  165.7 1.3 fusion.5
  168.1 0.8 subtract_multiply_fusion
  170.6 2.0 collective-permute-done.21
  172.9 1.7 collective-permute-start.24
  174.5 0.8 collective-permute-start.23
  175.3 1.1 collective-permute-start.22
  176.4 4.1 %collective-permute-done.24 = f32[96,384]{1,0:T(8,128)S(1)} collective-permute-done((f32[96,384]{1,0:T(8,128)S(1)}, f32[96,384]{1,0:T(8,128)S(1)}, u32[]{:S(2)}, u32[]{:S(2)}) %collective-permute-start.24) | collective-permute-done | bytes 147488 | tf_op jit(solution)/shard_map/ppermute | solution.py:205
  180.6 2.3 %collective-permute-done.23 = f32[96,384]{1,0:T(8,128)S(1)} collective-permute-done((f32[96,384]{1,0:T(8,128)S(1)}, f32[96,384]{1,0:T(8,128)S(1)}, u32[]{:S(2)}, u32[]{:S(2)}) %collective-permute-start.23) | collective-permute-done | bytes 147488 | tf_op jit(solution)/shard_map/ppermute | solution.py:205
  183.6 1.4 collective-permute-start.25
  185.0 2.3 %collective-permute-done.27 = f32[24,384]{1,0:T(8,128)S(1)} collective-permute-done((f32[24,384]{1,0:T(8,128)S(1)}, f32[24,384]{1,0:T(8,128)S(1)}, u32[]{:S(2)}, u32[]{:S(2)}) %collective-permute-start.27) | collective-permute-done | bytes 36896 | tf_op jit(solution)/shard_map/ppermute | solution.py:371
  187.3 1.5 collective-permute-done.26
  188.9 0.8 collective-permute-done.25
  190.0 2.0 collective-permute-start.29
  192.0 1.6 collective-permute-start.30
  193.6 1.9 collective-permute-done.28
  196.1 1.2 collective-permute-start.31
  197.3 1.0 collective-permute-start.32
  198.3 1.3 collective-permute-start.33
  199.7 1.6 collective-permute-done.31
  201.3 1.2 collective-permute-done.32
  202.5 1.8 collective-permute-done.33
  204.6 1.8 collective-permute-done.34
  206.5 1.1 fusion.55
  (125 shorter events, 11.0 us)
Async XLA Ops:
  0.6 167.0 %copy-start = (bf16[384,384]{1,0:T(8,128)(2,1)S(1)}, bf16[384,384]{1,0:T(8,128)(2,1)}, u32[]{:S(2)}) copy-start(bf16[384,384]{1,0:T(8,128)(2,1)} %param.14) | copy-start | bytes 884740
  3.1 10.2 %copy-start.28 = (bf16[256,3072]{1,0:T(8,128)(2,1)S(1)}, bf16[256,3072]{1,0:T(8,128)(2,1)}, u32[]{:S(2)}) copy-start(bf16[256,3072]{1,0:T(8,128)(2,1)} %param.10) | copy-start | bytes 4718596
  3.1 11.1 %copy-start.8 = (bf16[240,768]{1,0:T(8,128)(2,1)}, bf16[240,768]{1,0:T(8,128)(2,1)S(1)}, u32[]{:S(2)}) copy-start(bf16[240,768]{1,0:T(8,128)(2,1)S(1)} %pad_maximum_fusion.9.refs_2_.refs_4_.refs_7_) | copy-start | bytes 1105924
  3.1 12.9 %collective-permute-start.3 = (bf16[240,768]{1,0:T(8,128)(2,1)S(1)}, bf16[240,768]{1,0:T(8,128)(2,1)S(1)}, u32[]{:S(2)}, u32[]{:S(2)}) collective-permute-start(bf16[240,768]{1,0:T(8,128)(2,1)S(1)} %pad_maximum_fusion.9.refs_2_.refs_4_.refs_7_), channel_id=1, source_target_pairs={{0,8},{2,10},{4,12},{6,14},{8,16},{10,18},{12,20},{14,22},{16,24},... | collective-permute-start | bytes 1105928 | tf_op jit(solution)/shard_map/ppermute | solution.py:215
  8.2 11.9 %collective-permute-start.5 = (bf16[240,768]{1,0:T(8,128)(2,1)S(1)}, bf16[240,768]{1,0:T(8,128)(2,1)S(1)}, u32[]{:S(2)}, u32[]{:S(2)}) collective-permute-start(bf16[240,768]{1,0:T(8,128)(2,1)S(1)} %pad_maximum_fusion.9.refs_2_.refs_4_.refs_7_), channel_id=1, source_target_pairs={{8,0},{10,2},{12,4},{14,6},{16,8},{18,10},{20,12},{22,14},{24,16},... | collective-permute-start | bytes 1105928 | tf_op jit(solution)/shard_map/ppermute | solution.py:219
  9.6 13.9 %collective-permute-start.2 = (bf16[240,768]{1,0:T(8,128)(2,1)S(1)}, bf16[240,768]{1,0:T(8,128)(2,1)S(1)}, u32[]{:S(2)}, u32[]{:S(2)}) collective-permute-start(bf16[240,768]{1,0:T(8,128)(2,1)S(1)} %pad_maximum_fusion.8), channel_id=1, source_target_pairs={{0,6},{2,4},{4,2},{6,0},{8,14},{10,12},{12,10},{14,8},{16,22},{18,... | collective-permute-start | bytes 1105928 | tf_op jit(solution)/shard_map/ppermute | solution.py:205
  12.1 16.4 %collective-permute-start.1 = (bf16[240,768]{1,0:T(8,128)(2,1)S(1)}, bf16[240,768]{1,0:T(8,128)(2,1)S(1)}, u32[]{:S(2)}, u32[]{:S(2)}) collective-permute-start(bf16[240,768]{1,0:T(8,128)(2,1)S(1)} %pad_maximum_fusion.7), channel_id=1, source_target_pairs={{0,4},{2,6},{4,0},{6,2},{8,12},{10,14},{12,8},{14,10},{16,20},{18,... | collective-permute-start | bytes 1105928 | tf_op jit(solution)/shard_map/ppermute | solution.py:205
  12.7 8.8 %copy-start.26 = (bf16[256,1536]{1,0:T(8,128)(2,1)S(1)}, bf16[256,1536]{1,0:T(8,128)(2,1)}, u32[]{:S(2)}) copy-start(bf16[256,1536]{1,0:T(8,128)(2,1)} %param.8) | copy-start | bytes 2359300
  12.7 15.9 %collective-permute-start = (bf16[240,768]{1,0:T(8,128)(2,1)S(1)}, bf16[240,768]{1,0:T(8,128)(2,1)S(1)}, u32[]{:S(2)}, u32[]{:S(2)}) collective-permute-start(bf16[240,768]{1,0:T(8,128)(2,1)S(1)} %pad_maximum_fusion.6), channel_id=1, source_target_pairs={{0,2},{2,0},{4,6},{6,4},{8,10},{10,8},{12,14},{14,12},{16,18},{18,... | collective-permute-start | bytes 1105928 | tf_op jit(solution)/shard_map/ppermute | solution.py:205
  16.0 7.4 %copy-start.18 = (bf16[240,768]{1,0:T(8,128)(2,1)}, bf16[240,768]{1,0:T(8,128)(2,1)S(1)}, u32[]{:S(2)}) copy-start(bf16[240,768]{1,0:T(8,128)(2,1)S(1)} %collective-permute-done.3.refs_6_.refs_11_) | copy-start | bytes 1105924
  16.0 12.6 %collective-permute-start.4 = (bf16[240,768]{1,0:T(8,128)(2,1)S(1)}, bf16[240,768]{1,0:T(8,128)(2,1)S(1)}, u32[]{:S(2)}, u32[]{:S(2)}) collective-permute-start(bf16[240,768]{1,0:T(8,128)(2,1)S(1)} %collective-permute-done.3.refs_6_.refs_11_), channel_id=1, source_target_pairs={{8,16},{10,18},{12,20},{14,22},{16,24},{18,26},{20,28},{22,30},{9,... | collective-permute-start | bytes 1105928 | tf_op jit(solution)/shard_map/ppermute | solution.py:215
  20.2 3.3 %copy-start.20 = (bf16[240,768]{1,0:T(8,128)(2,1)}, bf16[240,768]{1,0:T(8,128)(2,1)S(1)}, u32[]{:S(2)}) copy-start(bf16[240,768]{1,0:T(8,128)(2,1)S(1)} %collective-permute-done.5.refs_10_.refs_15_) | copy-start | bytes 1105924
  20.2 11.2 %collective-permute-start.6 = (bf16[240,768]{1,0:T(8,128)(2,1)S(1)}, bf16[240,768]{1,0:T(8,128)(2,1)S(1)}, u32[]{:S(2)}, u32[]{:S(2)}) collective-permute-start(bf16[240,768]{1,0:T(8,128)(2,1)S(1)} %collective-permute-done.5.refs_10_.refs_15_), channel_id=1, source_target_pairs={{8,0},{10,2},{12,4},{14,6},{16,8},{18,10},{20,12},{22,14},{9,1},{1... | collective-permute-start | bytes 1105928 | tf_op jit(solution)/shard_map/ppermute | solution.py:219
  28.6 47.8 %copy-start.1 = (bf16[720,768]{1,0:T(8,128)(2,1)}, bf16[720,768]{1,0:T(8,128)(2,1)S(1)}, u32[]{:S(2)}) copy-start(bf16[720,768]{1,0:T(8,128)(2,1)S(1)} %pad_maximum_fusion.4.refs_3_.refs_5_.refs_8_) | copy-start | bytes 3317764
  28.7 47.7 %copy-start.10 = (bf16[240,768]{1,0:T(8,128)(2,1)}, bf16[240,768]{1,0:T(8,128)(2,1)S(1)}, u32[]{:S(2)}) copy-start(bf16[240,768]{1,0:T(8,128)(2,1)S(1)} %collective-permute-done.4.refs_8_.refs_13_) | copy-start | bytes 1105924
  31.4 45.0 %copy-start.12 = (bf16[240,768]{1,0:T(8,128)(2,1)}, bf16[240,768]{1,0:T(8,128)(2,1)S(1)}, u32[]{:S(2)}) copy-start(bf16[240,768]{1,0:T(8,128)(2,1)S(1)} %collective-permute-done.6.refs_12_.refs_17_) | copy-start | bytes 1105924
  31.4 41.5 %collective-permute-start.7 = (bf16[256,2304]{1,0:T(8,128)(2,1)}, bf16[256,2304]{1,0:T(8,128)(2,1)S(1)}, u32[]{:S(2)}, u32[]{:S(2)}) collective-permute-start(bf16[256,2304]{1,0:T(8,128)(2,1)} %get-tuple-element.35), channel_id=1, source_target_pairs={{0,2},{2,0},{4,6},{6,4},{8,10},{10,8},{12,14},{14,12},{16,18},{18,... | collective-permute-start | bytes 3538952 | tf_op jit(solution)/shard_map/ppermute | solution.py:205
  32.9 40.0 %collective-permute-start.8 = (bf16[256,2304]{1,0:T(8,128)(2,1)}, bf16[256,2304]{1,0:T(8,128)(2,1)}, u32[]{:S(2)}, u32[]{:S(2)}) collective-permute-start(bf16[256,2304]{1,0:T(8,128)(2,1)} %get-tuple-element.36), channel_id=1, source_target_pairs={{0,4},{2,6},{4,0},{6,2},{8,12},{10,14},{12,8},{14,10},{16,20},{18,... | collective-permute-start | bytes 3538952 | tf_op jit(solution)/shard_map/ppermute | solution.py:205
  34.4 38.5 %collective-permute-start.9 = (bf16[720,768]{1,0:T(8,128)(2,1)S(1)}, bf16[720,768]{1,0:T(8,128)(2,1)}, u32[]{:S(2)}, u32[]{:S(2)}) collective-permute-start(bf16[720,768]{1,0:T(8,128)(2,1)S(1)} %pad_maximum_fusion.4.refs_3_.refs_5_.refs_8_), channel_id=1, source_target_pairs={{0,8},{2,10},{4,12},{6,14},{8,16},{10,18},{12,20},{14,22},{16,24},... | collective-permute-start | bytes 3317768 | tf_op jit(solution)/shard_map/ppermute | solution.py:215
  39.1 33.7 %collective-permute-start.10 = (bf16[720,768]{1,0:T(8,128)(2,1)S(1)}, bf16[720,768]{1,0:T(8,128)(2,1)}, u32[]{:S(2)}, u32[]{:S(2)}) collective-permute-start(bf16[720,768]{1,0:T(8,128)(2,1)S(1)} %pad_maximum_fusion.4.refs_3_.refs_5_.refs_8_), channel_id=1, source_target_pairs={{8,0},{10,2},{12,4},{14,6},{16,8},{18,10},{20,12},{22,14},{24,16},... | collective-permute-start | bytes 3317768 | tf_op jit(solution)/shard_map/ppermute | solution.py:219
  40.5 31.7 %collective-permute-start.11 = (bf16[240,768]{1,0:T(8,128)(2,1)S(1)}, bf16[240,768]{1,0:T(8,128)(2,1)S(1)}, u32[]{:S(2)}, u32[]{:S(2)}) collective-permute-start(bf16[240,768]{1,0:T(8,128)(2,1)S(1)} %broadcast_select_fusion.1), channel_id=1, source_target_pairs={{16,24},{18,26},{20,28},{22,30},{8,0},{10,2},{12,4},{14,6},{17,25}... | collective-permute-start | bytes 1105928 | tf_op jit(solution)/shard_map/ppermute | solution.py:260
  72.9 4.7 %copy-start.25 = (bf16[256,2304]{1,0:T(8,128)(2,1)}, bf16[256,2304]{1,0:T(8,128)(2,1)S(1)}, u32[]{:S(2)}) copy-start(bf16[256,2304]{1,0:T(8,128)(2,1)S(1)} %collective-permute-done.7) | copy-start | bytes 3538948
  72.9 25.2 %collective-permute-start.12 = (bf16[256,2304]{1,0:T(8,128)(2,1)}, bf16[256,2304]{1,0:T(8,128)(2,1)S(1)}, u32[]{:S(2)}, u32[]{:S(2)}) collective-permute-start(bf16[256,2304]{1,0:T(8,128)(2,1)} %get-tuple-element.45), channel_id=1, source_target_pairs={{0,6},{2,4},{4,2},{6,0},{8,14},{10,12},{12,10},{14,8},{16,22},{18,... | collective-permute-start | bytes 3538952 | tf_op jit(solution)/shard_map/ppermute | solution.py:205
  73.6 25.5 %collective-permute-start.13 = (bf16[720,768]{1,0:T(8,128)(2,1)}, bf16[720,768]{1,0:T(8,128)(2,1)S(1)}, u32[]{:S(2)}, u32[]{:S(2)}) collective-permute-start(bf16[720,768]{1,0:T(8,128)(2,1)} %collective-permute-done.9.refs_7_.refs_12_), channel_id=1, source_target_pairs={{8,16},{10,18},{12,20},{14,22},{16,24},{18,26},{20,28},{22,30},{9,... | collective-permute-start | bytes 3317768 | tf_op jit(solution)/shard_map/ppermute | solution.py:215
  74.3 24.8 %collective-permute-start.14 = (bf16[720,768]{1,0:T(8,128)(2,1)}, bf16[720,768]{1,0:T(8,128)(2,1)S(1)}, u32[]{:S(2)}, u32[]{:S(2)}) collective-permute-start(bf16[720,768]{1,0:T(8,128)(2,1)} %collective-permute-done.10.refs_11_.refs_16_), channel_id=1, source_target_pairs={{8,0},{10,2},{12,4},{14,6},{16,8},{18,10},{20,12},{22,14},{9,1},{1... | collective-permute-start | bytes 3317768 | tf_op jit(solution)/shard_map/ppermute | solution.py:219
  77.6 21.3 %copy-start.27 = (bf16[256,1536]{1,0:T(8,128)(2,1)S(1)}, bf16[256,1536]{1,0:T(8,128)(2,1)}, u32[]{:S(2)}) copy-start(bf16[256,1536]{1,0:T(8,128)(2,1)} %param.8) | copy-start | bytes 2359300
  79.5 19.4 %slice-start = ((bf16[256,2304]{1,0:T(8,128)(2,1)}), bf16[256,1536]{1,0:T(8,128)(2,1)S(1)}, s32[]{:S(2)}) async-start(bf16[256,2304]{1,0:T(8,128)(2,1)} %copy-done.25), calls=%async_computation | async-start | bytes 1572864 | tf_op jit(solution)/shard_map/slice | solution.py:278
  99.1 1.4 copy-start.4
  99.2 1.7 copy-start.6
  99.2 5.9 %collective-permute-start.15 = (bf16[1024,1536]{1,0:T(8,128)(2,1)S(1)}, bf16[1024,1536]{1,0:T(8,128)(2,1)}, u32[]{:S(2)}, u32[]{:S(2)}) collective-permute-start(bf16[1024,1536]{1,0:T(8,128)(2,1)S(1)} %pad_maximum_fusion), channel_id=1, source_target_pairs={{0,1},{1,0},{2,3},{3,2},{4,5},{5,4},{6,7},{7,6},{8,9},{9,8},{10,11... | collective-permute-start | bytes 9437192 | tf_op jit(solution)/shard_map/ppermute | solution.py:208
  100.9 28.5 %collective-permute-start.16 = (bf16[720,768]{1,0:T(8,128)(2,1)}, bf16[720,768]{1,0:T(8,128)(2,1)}, u32[]{:S(2)}, u32[]{:S(2)}) collective-permute-start(bf16[720,768]{1,0:T(8,128)(2,1)} %broadcast_select_fusion), channel_id=1, source_target_pairs={{16,24},{18,26},{20,28},{22,30},{8,0},{10,2},{12,4},{14,6},{17,25}... | collective-permute-start | bytes 3317768 | tf_op jit(solution)/shard_map/ppermute | solution.py:260
  105.0 3.4 %copy-start.2 = (bf16[720,768]{1,0:T(8,128)(2,1)S(1)}, bf16[720,768]{1,0:T(8,128)(2,1)}, u32[]{:S(2)}) copy-start(bf16[720,768]{1,0:T(8,128)(2,1)} %copy-done.1) | copy-start | bytes 3317764
  105.0 3.4 %copy-start.5 = (bf16[720,768]{1,0:T(8,128)(2,1)S(1)}, bf16[720,768]{1,0:T(8,128)(2,1)}, u32[]{:S(2)}) copy-start(bf16[720,768]{1,0:T(8,128)(2,1)} %copy-done.4) | copy-start | bytes 3317764
  105.0 3.4 %copy-start.7 = (bf16[720,768]{1,0:T(8,128)(2,1)S(1)}, bf16[720,768]{1,0:T(8,128)(2,1)}, u32[]{:S(2)}) copy-start(bf16[720,768]{1,0:T(8,128)(2,1)} %copy-done.6) | copy-start | bytes 3317764
  105.0 3.4 %copy-start.9 = (bf16[240,768]{1,0:T(8,128)(2,1)S(1)}, bf16[240,768]{1,0:T(8,128)(2,1)}, u32[]{:S(2)}) copy-start(bf16[240,768]{1,0:T(8,128)(2,1)} %copy-done.8) | copy-start | bytes 1105924
  105.0 3.4 %copy-start.11 = (bf16[240,768]{1,0:T(8,128)(2,1)S(1)}, bf16[240,768]{1,0:T(8,128)(2,1)}, u32[]{:S(2)}) copy-start(bf16[240,768]{1,0:T(8,128)(2,1)} %copy-done.10) | copy-start | bytes 1105924
  105.0 3.4 %copy-start.13 = (bf16[240,768]{1,0:T(8,128)(2,1)S(1)}, bf16[240,768]{1,0:T(8,128)(2,1)}, u32[]{:S(2)}) copy-start(bf16[240,768]{1,0:T(8,128)(2,1)} %copy-done.12) | copy-start | bytes 1105924
  110.4 19.0 %copy-start.14 = (bf16[256,768]{1,0:T(8,128)(2,1)S(1)}, bf16[256,768]{1,0:T(8,128)(2,1)}, u32[]{:S(2)}) copy-start(bf16[256,768]{1,0:T(8,128)(2,1)} %slice.72.refs_4_) | copy-start | bytes 1179652
  110.4 19.0 %copy-start.15 = (bf16[256,768]{1,0:T(8,128)(2,1)S(1)}, bf16[256,768]{1,0:T(8,128)(2,1)}, u32[]{:S(2)}) copy-start(bf16[256,768]{1,0:T(8,128)(2,1)} %slice.73.refs_5_) | copy-start | bytes 1179652
  110.4 19.0 %copy-start.16 = (bf16[256,768]{1,0:T(8,128)(2,1)S(1)}, bf16[256,768]{1,0:T(8,128)(2,1)}, u32[]{:S(2)}) copy-start(bf16[256,768]{1,0:T(8,128)(2,1)} %slice.92.refs_6_) | copy-start | bytes 1179652
  110.4 19.0 %copy-start.17 = (bf16[256,768]{1,0:T(8,128)(2,1)S(1)}, bf16[256,768]{1,0:T(8,128)(2,1)}, u32[]{:S(2)}) copy-start(bf16[256,768]{1,0:T(8,128)(2,1)} %get-tuple-element.62.refs_3_) | copy-start | bytes 1179652
  110.4 19.0 %copy-start.23 = (bf16[240,768]{1,0:T(8,128)(2,1)S(1)}, bf16[240,768]{1,0:T(8,128)(2,1)}, u32[]{:S(2)}) copy-start(bf16[240,768]{1,0:T(8,128)(2,1)} %copy-done.22) | copy-start | bytes 1105924
  119.1 1.7 copy-start.3
  138.4 5.3 %copy-start.24 = (f32[2,544,768]{2,1,0:T(8,128)S(1)}, f32[2,544,768]{2,1,0:T(8,128)}, u32[]{:S(2)}) copy-start(f32[2,544,768]{2,1,0:T(8,128)} %shard_map.104) | copy-start | bytes 10027012
  140.1 3.6 %collective-permute-start.17 = (f32[544,768]{1,0:T(8,128)S(1)}, f32[544,768]{1,0:T(8,128)S(1)}, u32[]{:S(2)}, u32[]{:S(2)}) collective-permute-start(f32[544,768]{1,0:T(8,128)S(1)} %slice_bitcast_fusion), channel_id=1, source_target_pairs={{0,1},{1,0},{2,3},{3,2},{4,5},{5,4},{6,7},{7,6},{8,9},{9,8},{10,11... | collective-permute-start | bytes 5013512 | tf_op jit(solution)/shard_map/ppermute | solution.py:208
  144.0 23.3 %copy-start.30 = (bf16[384,384]{1,0:T(8,128)(2,1)S(1)}, bf16[384,384]{1,0:T(8,128)(2,1)}, u32[]{:S(2)}) copy-start(bf16[384,384]{1,0:T(8,128)(2,1)} %param.13) | copy-start | bytes 884740
  144.0 13.6 %collective-permute-start.20 = (f32[136,768]{1,0:T(8,128)S(1)}, f32[136,768]{1,0:T(8,128)}, u32[]{:S(2)}, u32[]{:S(2)}) collective-permute-start(f32[136,768]{1,0:T(8,128)S(1)} %get-tuple-element.72), channel_id=1, source_target_pairs={{0,6},{2,4},{4,2},{6,0},{8,14},{10,12},{12,10},{14,8},{16,22},{18,... | collective-permute-start | bytes 1253384 | tf_op jit(solution)/shard_map/ppermute | solution.py:205
  145.7 20.0 %collective-permute-start.19 = (f32[136,768]{1,0:T(8,128)S(1)}, f32[136,768]{1,0:T(8,128)}, u32[]{:S(2)}, u32[]{:S(2)}) collective-permute-start(f32[136,768]{1,0:T(8,128)S(1)} %get-tuple-element.73), channel_id=1, source_target_pairs={{0,4},{2,6},{4,0},{6,2},{8,12},{10,14},{12,8},{14,10},{16,20},{18,... | collective-permute-start | bytes 1253384 | tf_op jit(solution)/shard_map/ppermute | solution.py:205
  146.5 19.2 %collective-permute-start.18 = (f32[136,768]{1,0:T(8,128)S(1)}, f32[136,768]{1,0:T(8,128)}, u32[]{:S(2)}, u32[]{:S(2)}) collective-permute-start(f32[136,768]{1,0:T(8,128)S(1)} %get-tuple-element.71), channel_id=1, source_target_pairs={{0,2},{2,0},{4,6},{6,4},{8,10},{10,8},{12,14},{14,12},{16,18},{18,... | collective-permute-start | bytes 1253384 | tf_op jit(solution)/shard_map/ppermute | solution.py:205
  167.1 1.0 copy-start.29
  170.5 2.1 collective-permute-start.21
  172.9 7.7 %collective-permute-start.24 = (f32[96,384]{1,0:T(8,128)S(1)}, f32[96,384]{1,0:T(8,128)S(1)}, u32[]{:S(2)}, u32[]{:S(2)}) collective-permute-start(f32[96,384]{1,0:T(8,128)S(1)} %get-tuple-element.88), channel_id=1, source_target_pairs={{0,6},{2,4},{4,2},{6,0},{8,14},{10,12},{12,10},{14,8},{16,22},{18,... | collective-permute-start | bytes 442376 | tf_op jit(solution)/shard_map/ppermute | solution.py:205
  174.5 8.4 %collective-permute-start.23 = (f32[96,384]{1,0:T(8,128)S(1)}, f32[96,384]{1,0:T(8,128)S(1)}, u32[]{:S(2)}, u32[]{:S(2)}) collective-permute-start(f32[96,384]{1,0:T(8,128)S(1)} %get-tuple-element.89), channel_id=1, source_target_pairs={{0,4},{2,6},{4,0},{6,2},{8,12},{10,14},{12,8},{14,10},{16,20},{18,... | collective-permute-start | bytes 442376 | tf_op jit(solution)/shard_map/ppermute | solution.py:205
  175.3 7.5 %collective-permute-start.22 = (f32[96,384]{1,0:T(8,128)S(1)}, f32[96,384]{1,0:T(8,128)S(1)}, u32[]{:S(2)}, u32[]{:S(2)}) collective-permute-start(f32[96,384]{1,0:T(8,128)S(1)} %get-tuple-element.87), channel_id=1, source_target_pairs={{0,2},{2,0},{4,6},{6,4},{8,10},{10,8},{12,14},{14,12},{16,18},{18,... | collective-permute-start | bytes 442376 | tf_op jit(solution)/shard_map/ppermute | solution.py:205
  182.9 4.4 %collective-permute-start.27 = (f32[24,384]{1,0:T(8,128)S(1)}, f32[24,384]{1,0:T(8,128)S(1)}, u32[]{:S(2)}, u32[]{:S(2)}) collective-permute-start(f32[24,384]{1,0:T(8,128)S(1)} %get-tuple-element.95), channel_id=1, source_target_pairs={{0,24},{2,26},{4,28},{6,30},{8,0},{10,2},{12,4},{14,6},{16,8},{18,... | collective-permute-start | bytes 110600 | tf_op jit(solution)/shard_map/ppermute | solution.py:371
  183.6 5.3 %collective-permute-start.26 = (f32[24,384]{1,0:T(8,128)S(1)}, f32[24,384]{1,0:T(8,128)S(1)}, u32[]{:S(2)}, u32[]{:S(2)}) collective-permute-start(f32[24,384]{1,0:T(8,128)S(1)} %get-tuple-element.96), channel_id=1, source_target_pairs={{0,16},{2,18},{4,20},{6,22},{8,24},{10,26},{12,28},{14,30},{16,0},... | collective-permute-start | bytes 110600 | tf_op jit(solution)/shard_map/ppermute | solution.py:371
  183.6 6.1 %collective-permute-start.25 = (f32[24,384]{1,0:T(8,128)S(1)}, f32[24,384]{1,0:T(8,128)S(1)}, u32[]{:S(2)}, u32[]{:S(2)}) collective-permute-start(f32[24,384]{1,0:T(8,128)S(1)} %get-tuple-element.94), channel_id=1, source_target_pairs={{0,8},{2,10},{4,12},{6,14},{8,16},{10,18},{12,20},{14,22},{16,24},... | collective-permute-start | bytes 110600 | tf_op jit(solution)/shard_map/ppermute | solution.py:371
  189.7 5.8 %collective-permute-start.28 = (f32[24,384]{1,0:T(8,128)S(1)}, f32[24,384]{1,0:T(8,128)S(1)}, u32[]{:S(2)}, u32[]{:S(2)}) collective-permute-start(f32[24,384]{1,0:T(8,128)S(1)} %get-tuple-element.68), channel_id=1, source_target_pairs={{0,8},{2,10},{4,12},{6,14},{8,16},{10,18},{12,20},{14,22},{16,24},... | collective-permute-start | bytes 110600 | tf_op jit(solution)/shard_map/ppermute | solution.py:371
  190.0 5.6 %collective-permute-start.29 = (f32[24,384]{1,0:T(8,128)S(1)}, f32[24,384]{1,0:T(8,128)S(1)}, u32[]{:S(2)}, u32[]{:S(2)}) collective-permute-start(f32[24,384]{1,0:T(8,128)S(1)} %get-tuple-element.68), channel_id=1, source_target_pairs={{0,16},{2,18},{4,20},{6,22},{8,24},{10,26},{12,28},{14,30},{16,0},... | collective-permute-start | bytes 110600 | tf_op jit(solution)/shard_map/ppermute | solution.py:371
  192.0 4.1 %collective-permute-start.30 = (f32[24,384]{1,0:T(8,128)S(1)}, f32[24,384]{1,0:T(8,128)S(1)}, u32[]{:S(2)}, u32[]{:S(2)}) collective-permute-start(f32[24,384]{1,0:T(8,128)S(1)} %get-tuple-element.68), channel_id=1, source_target_pairs={{0,24},{2,26},{4,28},{6,30},{8,0},{10,2},{12,4},{14,6},{16,8},{18,... | collective-permute-start | bytes 110600 | tf_op jit(solution)/shard_map/ppermute | solution.py:371
  196.1 5.1 %collective-permute-start.31 = (f32[96,384]{1,0:T(8,128)S(1)}, f32[96,384]{1,0:T(8,128)S(1)}, u32[]{:S(2)}, u32[]{:S(2)}) collective-permute-start(f32[96,384]{1,0:T(8,128)S(1)} %constant_dynamic-update-slice_fusion.6), channel_id=1, source_target_pairs={{0,2},{2,0},{4,6},{6,4},{8,10},{10,8},{12,14},{14,12},{16,18},{18,... | collective-permute-start | bytes 442376 | tf_op jit(solution)/shard_map/ppermute | solution.py:205
  197.3 5.1 %collective-permute-start.32 = (f32[96,384]{1,0:T(8,128)S(1)}, f32[96,384]{1,0:T(8,128)S(1)}, u32[]{:S(2)}, u32[]{:S(2)}) collective-permute-start(f32[96,384]{1,0:T(8,128)S(1)} %constant_dynamic-update-slice_fusion.6), channel_id=1, source_target_pairs={{0,4},{2,6},{4,0},{6,2},{8,12},{10,14},{12,8},{14,10},{16,20},{18,... | collective-permute-start | bytes 442376 | tf_op jit(solution)/shard_map/ppermute | solution.py:205
  198.3 6.0 %collective-permute-start.33 = (f32[96,384]{1,0:T(8,128)S(1)}, f32[96,384]{1,0:T(8,128)S(1)}, u32[]{:S(2)}, u32[]{:S(2)}) collective-permute-start(f32[96,384]{1,0:T(8,128)S(1)} %constant_dynamic-update-slice_fusion.6), channel_id=1, source_target_pairs={{0,6},{2,4},{4,2},{6,0},{8,14},{10,12},{12,10},{14,8},{16,22},{18,... | collective-permute-start | bytes 442376 | tf_op jit(solution)/shard_map/ppermute | solution.py:205
  204.3 2.1 collective-permute-start.34
  (3 other events, 2.7 us)

commit v4 on v3

--- a/solution.py
+++ b/solution.py
@@ -22,15 +22,12 @@
     return wide // GROUP, wide % GROUP, core
 
 
+ROUTES = ((0, 1, 4, 5), (1, 0, 2, 3), (3, 2, 0, 1), (5, 4, 1, 0))
+LAST = 5
+
+
 def part_of(flow, at, p):
-    steps = (len(flow) // 2 - 2) // 2
-    step = abs(at - p)
-    if step > steps:
-        return flow[2:4]
-    if not step:
-        return flow[:2]
-    first = 4 + 2 * (step - 1) + (0 if at > p else 2 * steps)
-    return flow[first : first + 2]
+    return flow[2 * ROUTES[at][p] :][:2]
 
 
 def share_of(pair, s, start, count, span):
@@ -42,7 +39,6 @@
     mine_ref, other_ref, *flow, out_ref, weight, sems = refs
     plane, member, core = place()
     span = flow[0].shape[0]
-    steps = (len(flow) // 2 - 2) // 2
 
     for at in range(planes):
 
@@ -50,7 +46,7 @@
         def _():
             copies = []
             for p in range(planes):
-                if abs(at - p) > steps:
+                if ROUTES[at][p] == LAST:
                     weight[p * GROUP * rows : (p + 1) * GROUP * rows] = jnp.zeros((GROUP * rows, weight.shape[1]), BF16)
                     continue
                 for s in range(GROUP):
@@ -93,7 +89,8 @@
 
 def finish_kernel(rows, planes, *refs):
     total_ref, far_ref, gain_ref, *refs = refs
-    stay_refs, (*flow, out_ref, weight, down, scaled, sums, sems, down_sems) = refs[:GROUP], refs[GROUP:]
+    stay_refs, refs = refs[:GROUP], refs[GROUP:]
+    *flow, keep_ref, send_ref, weight, down, scaled, sums, sems, down_sems = refs
     plane, member, core = place()
     span = flow[0].shape[0]
     columns = span - rows
@@ -102,7 +99,7 @@
         out = []
         for s in range(GROUP):
             target = pl.multiple_of((member ^ s) * rows, 64)
-            source = share_of(flow[2:4], s, 0, rows, span)
+            source = share_of(flow[2 * LAST :], s, 0, rows, span)
             out.append(pltpu.make_async_copy(source, weight.at[pl.ds(target, rows)], sems.at[s]))
         return out
 
@@ -122,11 +119,8 @@
 
         @pl.when(plane == at)
         def _():
-            copies = down_copies(at)
-            for copy in copies:
+            for copy in down_copies(at):
                 copy.start()
-            for copy in copies:
-                copy.wait()
 
     for copy in far:
         copy.wait()
@@ -147,19 +141,25 @@
             both = jnp.where(lane == 0, row_sum, jnp.where(lane == 1, squares, 0.0))
             sums[:, at : at + 2 * local] = both.T[:8]
 
+    for at in range(planes):
+
+        @pl.when(plane == at)
+        def _():
+            for copy in down_copies(at):
+                copy.wait()
+
     dims = (((1,), (1,)), ((), ()))
     gains = jnp.broadcast_to(gain_ref[...], (16, gain_ref.shape[1]))
     gains = lax.dot_general(gains, down[...], dims, preferred_element_type=F32)
     line = local + 8
-    for t in range(2):
-        k = core if t == 0 else 1 - core
+    for out_ref, k in ((send_ref, 1 - core), (keep_ref, core)):
         at = pl.multiple_of(k * half, 128)
         value = lax.dot_general(scaled[pl.ds(at, half)], down[...], dims, preferred_element_type=F32)
         stats = sums[:, pl.ds(at, half)]
         for s in range(GROUP):
-            out_ref[t, s * line : s * line + local] = value[s * local : (s + 1) * local]
-            out_ref[t, s * line + local : (s + 1) * line] = gains[:8]
-            out_ref[t, s * line + local + 1 : s * line + local + 3, :local] = stats[:2, s * local : (s + 1) * local]
+            out_ref[s * line : s * line + local] = value[s * local : (s + 1) * local]
+            out_ref[s * line + local : (s + 1) * line] = gains[:8]
+            out_ref[s * line + local + 1 : s * line + local + 3, :local] = stats[:2, s * local : (s + 1) * local]
 
 
 def finish(rows, planes, total, far, gain, stay, flow):
@@ -171,8 +171,8 @@
     return pl.pallas_call(
         functools.partial(finish_kernel, rows, planes),
         in_specs=[inside] * (3 + GROUP) + [pl.BlockSpec(memory_space=pl.ANY)] * len(flow),
-        out_specs=inside,
-        out_shape=jax.ShapeDtypeStruct((2, tokens // 2 + 8 * GROUP, out), F32),
+        out_specs=[inside, inside],
+        out_shape=[jax.ShapeDtypeStruct((tokens // 2 + 8 * GROUP, out), F32)] * 2,
         scratch_shapes=[
             pltpu.VMEM((GROUP * rows, count), BF16),
             pltpu.VMEM((out, count), BF16),
@@ -210,14 +210,6 @@
     def block(value, index, size, axis):
         return lax.dynamic_slice_in_dim(value, index * size, size, axis)
 
-    def step_up(value, k):
-        pairs = [(i, i + group) for i in range((k - 1) * group, wides - group)]
-        return lax.ppermute(value, "wide", pairs)
-
-    def step_down(value, k):
-        pairs = [(i + group, i) for i in range(wides - k * group)]
-        return lax.ppermute(value, "wide", pairs)
-
     def sum_cores(pick):
         total = pick(core)
         for t in range(1, narrows):
@@ -246,51 +238,49 @@
     if short:
         own = [jnp.concatenate(pair, axis=0) for pair in zip(own, down_own)]
         boxes = [jnp.concatenate([context, value], axis=1) for value in stay_own[1:]]
-        up, down = [[v] for v in own[:1]], [[v] for v in own[:1]]
-        far = []
-
-        def pass_on(i, k):
-            up[i].append(step_up(up[i][-1], k))
-            down[i].append(step_down(down[i][-1], k))
-
-        def pass_last(i):
-            middle = planes // 2 * group
-            pairs = [(j, j + group) for j in range(wides - 2 * group, wides - group)]
-            pairs += [(j + group, j) for j in range(group)]
-            far.append(lax.ppermute(jnp.where(wide >= middle, up[i][-1], down[i][-1]), "wide", pairs))
-
-        pass_on(0, 1)
-        pass_on(0, 2)
-        pieces = [to_member(own[s], s) for s in range(1, group)]
-        rest = jnp.concatenate(pieces, axis=0)
-
-        rest, boxes, up, down = lax.optimization_barrier((rest, boxes, up, down))
-        up.append([rest])
-        down.append([rest])
-        pass_on(1, 1)
-        pass_last(0)
+
+        def line(value, pairs):
+            pairs = [(i * group + m, j * group + m) for i, j in pairs for m in members]
+            return lax.ppermute(value, "wide", pairs)
+
+        outward, inward = [(1, 0), (2, 3)], [(1, 2), (2, 1)]
+
+        def step_one(value):
+            return line(value, outward + [(0, 1), (3, 2)]), line(value, inward)
+
+        def step_two(first, second):
+            return line(first, inward), line(second, outward)
+
+        own_one = step_one(own[0])
+        own_two = step_two(*own_one)
+        rest = jnp.concatenate([to_member(own[s], s) for s in range(1, group)], axis=0)
+
+        rest, boxes, own_two = lax.optimization_barrier((rest, boxes, own_two))
+        rest_one = step_one(rest)
+        own_last = line(own_two[0], outward)
         arrived = [to_member(boxes[0], 1), to_member(boxes[1], 2)]
 
-        arrived, boxes, up, down, far = lax.optimization_barrier((arrived, boxes, up, down, far))
-        pass_on(1, 2)
+        arrived, boxes, rest_one, own_last = lax.optimization_barrier((arrived, boxes, rest_one, own_last))
+        rest_two = step_two(*rest_one)
         arrived.append(to_member(boxes[2], 3))
+
+        arrived, rest_two = lax.optimization_barrier((arrived, rest_two))
+        rest_last = line(rest_two[0], outward)
         heads = context.shape[1]
         part = jnp.concatenate([context] + [v[:, :heads] for v in arrived], axis=0)
         stay = stay_own[:1] + [v[:, heads:] for v in arrived]
-
-        part, stay, up, down, far = lax.optimization_barrier((part, stay, up, down, far))
         mine, other = [v.reshape(group, tokens, -1) for v in (part, to_core(part, 1))]
-        pass_last(1)
-        near = [v[i][k] for v in (up, down) for k in range(1, planes - 1) for i in range(2)]
-        flow = [own[0], rest, own[0], rest] + near
+        flow = [own[0], rest]
+        for pair in zip(own_one + own_two, rest_one + rest_two):
+            flow += pair
         total = attend(rows, planes, mine, other, flow)
         last = jnp.where(plane == 0, planes - 1, 0)
         width = group * rows
         last_part = jnp.where(last * width // heads == core, mine, other)
         last_part = lax.dynamic_slice_in_dim(last_part, last * width % heads, width, 2)
-        flow = [own[0], rest, *far] + near
-        both = finish(rows, planes, total, last_part, gain, stay, flow)
-        summed = both[0] + to_core(both[1], 1)
+        flow += [own_last, rest_last]
+        keep, send = finish(rows, planes, total, last_part, gain, stay, flow)
+        summed = keep + to_core(send, 1)
         span = local + 8
         projected = summed[:span]
         for s in range(1, group):

time: 208 us -> 203 us (0.976)
  other arithmetic: 10 us -> 6.94 us
    ppermute x10, waiting for transfers between devices: 46.9 us -> 66 us  [line(): return lax.ppermute(value, 'wide', pairs)]
    ppermute x15, waiting for transfers between devices: 52.9 us -> 38.4 us  [to_member(): return lax.ppermute(value, 'wide', pairs) if s else value]
    ppermute x10, starting transfers between devices: 18.9 us -> 14.4 us  [line(): return lax.ppermute(value, 'wide', pairs)]
    unnamed x62, local copies, waits for them, and re-layouts: 4.9 us -> 7.99 us
    ppermute x6, starting transfers between devices: 5.96 us -> 8.11 us  [shift(): lax.ppermute(value, 'wide', [(i, (i + k * group) % wides) for i in range(...]
  transfers between devices with their start and end apart: 35 -> 35, of which waited for: 24 -> 22; matrix products, arithmetic and copies ran while one was open for 7% -> 4% of each run, Pallas kernels for 4% -> 4%
where the time goes in v4:
time: 203 us
  waiting for transfers between devices  118 us (58%)
  starting transfers between devices  41.6 us (20%)
  Pallas kernels  16.3 us (8%)
  local copies, waits for them, and re-layouts  16.1 us (8%)
  other arithmetic  6.94 us (3%)
  matrix products  2.06 us (1%)
    ppermute x10, waiting for transfers between devices, line(): return lax.ppermute(value, 'wide', pairs)  66 us
    ppermute x15, waiting for transfers between devices, to_member(): return lax.ppermute(value, 'wide', pairs) if s else value  38.4 us
    ppermute x15, starting transfers between devices, to_member(): return lax.ppermute(value, 'wide', pairs) if s else value  18.8 us
    ppermute x10, starting transfers between devices, line(): return lax.ppermute(value, 'wide', pairs)  14.4 us
    pallas_call x1, Pallas kernels, finish(): pl.pallas_call(functools.partial(finish_kernel, rows, planes), in_specs=[...  8.29 us
    ppermute x6, starting transfers between devices, shift(): lax.ppermute(value, 'wide', [(i, (i + k * group) % wides) for i in range(...  8.11 us
    unnamed x62, local copies, waits for them, and re-layouts  7.99 us
    pallas_call x1, Pallas kernels, attend(): pl.pallas_call(functools.partial(attend_kernel, rows, planes), grid=(2,),...  7.98 us
  transfers between devices with their start and end apart: 35, of which 22 were waited for; matrix products, arithmetic and copies ran while one was open for 4% of the time, Pallas kernels for 4%

profile of v4, /device:TPU:0, one launch (start us, length us, event | category | flops | bytes accessed | tf_op | source)
XLA Modules:
  0.0 202.9 jit_solution(12700161497097050424)
XLA Ops:
  0.7 1.4 constant_dynamic-slice_fusion.7
  2.2 3.1 %collective-permute-start.3 = (bf16[240,768]{1,0:T(8,128)(2,1)S(1)}, bf16[240,768]{1,0:T(8,128)(2,1)S(1)}, u32[]{:S(2)}, u32[]{:S(2)}) collective-permute-start(bf16[240,768]{1,0:T(8,128)(2,1)S(1)} %pad_maximum_fusion.9.refs_2_.refs_7_), channel_id=1, source_target_pairs={{8,0},{10,2},{12,4},{14,6},{16,24},{18,26},{20,28},{22,30},{0,8},{... | collective-permute-start | bytes 1105928 | tf_op jit(solution)/shard_map/ppermute | solution.py:244
  6.0 1.6 collective-permute-start
  7.6 1.6 collective-permute-start.1
  9.8 0.9 constant_dynamic-slice_fusion.6
  10.7 3.2 %collective-permute-done.3.refs_4_.refs_9_ = bf16[240,768]{1,0:T(8,128)(2,1)S(1)} collective-permute-done((bf16[240,768]{1,0:T(8,128)(2,1)S(1)}, bf16[240,768]{1,0:T(8,128)(2,1)S(1)}, u32[]{:S(2)}, u32[]{:S(2)}) %collective-permute-start.3) | collective-permute-done | bytes 368672 | tf_op jit(solution)/shard_map/ppermute | solution.py:244
  14.6 1.3 collective-permute-start.6
  16.2 1.4 collective-permute-done
  17.6 7.7 %collective-permute-done.1 = bf16[240,768]{1,0:T(8,128)(2,1)S(1)} collective-permute-done((bf16[240,768]{1,0:T(8,128)(2,1)S(1)}, bf16[240,768]{1,0:T(8,128)(2,1)S(1)}, u32[]{:S(2)}, u32[]{:S(2)}) %collective-permute-start.1) | collective-permute-done | bytes 368672 | tf_op jit(solution)/shard_map/ppermute | solution.py:205
  25.4 2.4 %collective-permute-done.6.refs_10_.refs_15_ = bf16[240,768]{1,0:T(8,128)(2,1)S(1)} collective-permute-done((bf16[240,768]{1,0:T(8,128)(2,1)S(1)}, bf16[240,768]{1,0:T(8,128)(2,1)S(1)}, u32[]{:S(2)}, u32[]{:S(2)}) %collective-permute-start.6) | collective-permute-done | bytes 368672 | tf_op jit(solution)/shard_map/ppermute | solution.py:244
  27.8 0.7 copy-done.19
  28.6 1.5 collective-permute-start.7
  30.1 1.5 collective-permute-start.8
  31.6 0.7 collective-permute-start.10
  32.3 2.3 %collective-permute-start.9 = (bf16[720,768]{1,0:T(8,128)(2,1)S(1)}, bf16[720,768]{1,0:T(8,128)(2,1)S(1)}, u32[]{:S(2)}, u32[]{:S(2)}) collective-permute-start(bf16[720,768]{1,0:T(8,128)(2,1)S(1)} %pad_maximum_fusion.4.refs_3_.refs_8_), channel_id=1, source_target_pairs={{8,0},{10,2},{12,4},{14,6},{16,24},{18,26},{20,28},{22,30},{0,8},{... | collective-permute-start | bytes 3317768 | tf_op jit(solution)/shard_map/ppermute | solution.py:244
  34.7 1.3 collective-permute-start.11
  36.0 0.7 copy-done.17
  36.7 27.9 %collective-permute-done.11.refs_17_ = bf16[240,768]{1,0:T(8,128)(2,1)S(1)} collective-permute-done((bf16[240,768]{1,0:T(8,128)(2,1)S(1)}, bf16[240,768]{1,0:T(8,128)(2,1)S(1)}, u32[]{:S(2)}, u32[]{:S(2)}) %collective-permute-start.11) | collective-permute-done | bytes 368672 | tf_op jit(solution)/shard_map/ppermute | solution.py:244
  64.6 0.8 copy-done.21
  65.4 1.6 collective-permute-start.12
  66.9 1.8 collective-permute-start.13
  68.7 1.0 copy-done.9
  69.7 1.3 collective-permute-start.14
  71.0 1.1 copy-done.7
  72.0 22.4 %collective-permute-done.14.refs_11_.refs_16_ = bf16[720,768]{1,0:T(8,128)(2,1)S(1)} collective-permute-done((bf16[720,768]{1,0:T(8,128)(2,1)S(1)}, bf16[720,768]{1,0:T(8,128)(2,1)S(1)}, u32[]{:S(2)}, u32[]{:S(2)}) %collective-permute-start.14) | collective-permute-done | bytes 1105952 | tf_op jit(solution)/shard_map/ppermute | solution.py:244
  94.4 1.0 copy-done.11
  95.6 0.9 copy-done.27
  96.8 1.3 collective-permute-start.16
  98.2 0.8 dynamic_slice.84
  98.9 1.0 slice.66.refs_4_
  100.0 1.1 slice.67.refs_5_
  101.1 1.1 slice.68.refs_6_
  102.6 3.3 %dynamic-slice_select_fusion.refs_1_ = bf16[4,256,768]{2,1,0:T(8,128)(2,1)S(1)} fusion(bf16[4,256,1536]{2,1,0:T(8,128)(2,1)} %bitcast.5.refs_1_, s32[]{:T(128)S(6)} %select_n.146, bf16[4,256,1536]{2,1,0:T(8,128)(2,1)S(1)} %bitcast.25, pred[]{:T(512)S(6)} %eq.18), kind=kLoop, calls=%fused_computation.1 | loop fusion | flops 786432 | bytes 4718597 | tf_op jit(solution)/shard_map/jit(_where)/select_n | solution.py:279
  106.1 8.0 %shard_map.103.refs_0_ = f32[1024,768]{1,0:T(8,128)S(1)} custom-call(bf16[4,256,1536]{2,1,0:T(8,128)(2,1)S(1)} %bitcast.26, bf16[4,256,1536]{2,1,0:T(8,128)(2,1)} %bitcast.5.refs_1_, bf16[240,768]{1,0:T(8,128)(2,1)S(1)} %copy-done.6, bf16[720,768]{1,0:T(8,128)(2,1)S(1)} %copy-done.2, bf16[240,768]{1,0:T(8,128)(2,1)S(1)} %copy-done.14, ...), custom_call_target="tpu_custom_call" | custom-call | flops 4831838208 | bytes 16777216 | tf_op jit(solution)/shard_map/pallas_call | solution.py:76
  114.1 1.6 copy-done.3
  115.7 10.1 %collective-permute-done.16.refs_18_ = bf16[720,768]{1,0:T(8,128)(2,1)} collective-permute-done((bf16[720,768]{1,0:T(8,128)(2,1)}, bf16[720,768]{1,0:T(8,128)(2,1)}, u32[]{:S(2)}, u32[]{:S(2)}) %collective-permute-start.16) | collective-permute-done | bytes 1105952 | tf_op jit(solution)/shard_map/ppermute | solution.py:244
  125.8 8.3 %shard_map.104 = (f32[544,768]{1,0:T(8,128)S(1)}, f32[544,768]{1,0:T(8,128)}) custom-call(f32[1024,768]{1,0:T(8,128)} %copy-done.3, bf16[4,256,768]{2,1,0:T(8,128)(2,1)S(1)} %dynamic-slice_select_fusion.refs_1_, bf16[1,768]{1,0:T(2,128)(2,1)S(1)} %broadcast_in_dim.14.refs_2_, bf16[256,768]{1,0:T(8,128)(2,1)S(1)} %copy-done.4, ...), custom_call_target="tpu_custom_call" | custom-call | flops 2415919104 | bytes 16777216 | tf_op jit(solution)/shard_map/pallas_call | solution.py:171
  134.2 3.7 %collective-permute-done.17 = f32[544,768]{1,0:T(8,128)S(1)} collective-permute-done((f32[544,768]{1,0:T(8,128)}, f32[544,768]{1,0:T(8,128)S(1)}, u32[]{:S(2)}, u32[]{:S(2)}) %collective-permute-start.17) | collective-permute-done | bytes 1671200 | tf_op jit(solution)/shard_map/ppermute | solution.py:208
  138.3 1.8 collective-permute-start.18
  140.3 1.5 collective-permute-start.20
  141.8 9.1 %collective-permute-done.18 = f32[136,768]{1,0:T(8,128)} collective-permute-done((f32[136,768]{1,0:T(8,128)S(1)}, f32[136,768]{1,0:T(8,128)}, u32[]{:S(2)}, u32[]{:S(2)}) %collective-permute-start.18) | collective-permute-done | bytes 417824 | tf_op jit(solution)/shard_map/ppermute | solution.py:205
  150.9 9.6 %collective-permute-done.19 = f32[136,768]{1,0:T(8,128)} collective-permute-done((f32[136,768]{1,0:T(8,128)S(1)}, f32[136,768]{1,0:T(8,128)}, u32[]{:S(2)}, u32[]{:S(2)}) %collective-permute-start.19) | collective-permute-done | bytes 417824 | tf_op jit(solution)/shard_map/ppermute | solution.py:205
  160.5 1.3 fusion.4
  162.9 0.8 subtract_multiply_fusion
  165.4 2.0 collective-permute-done.21
  168.1 1.4 collective-permute-start.23
  169.5 1.8 collective-permute-start.24
  171.2 3.2 %collective-permute-done.22 = f32[96,384]{1,0:T(8,128)S(1)} collective-permute-done((f32[96,384]{1,0:T(8,128)S(1)}, f32[96,384]{1,0:T(8,128)S(1)}, u32[]{:S(2)}, u32[]{:S(2)}) %collective-permute-start.22) | collective-permute-done | bytes 147488 | tf_op jit(solution)/shard_map/ppermute | solution.py:205
  174.4 2.4 %collective-permute-done.23 = f32[96,384]{1,0:T(8,128)S(1)} collective-permute-done((f32[96,384]{1,0:T(8,128)S(1)}, f32[96,384]{1,0:T(8,128)S(1)}, u32[]{:S(2)}, u32[]{:S(2)}) %collective-permute-start.23) | collective-permute-done | bytes 147488 | tf_op jit(solution)/shard_map/ppermute | solution.py:205
  177.0 2.7 %collective-permute-start.26 = (f32[24,384]{1,0:T(8,128)S(1)}, f32[24,384]{1,0:T(8,128)S(1)}, u32[]{:S(2)}, u32[]{:S(2)}) collective-permute-start(f32[24,384]{1,0:T(8,128)S(1)} %get-tuple-element.70), channel_id=1, source_target_pairs={{0,16},{2,18},{4,20},{6,22},{8,24},{10,26},{12,28},{14,30},{16,0},... | collective-permute-start | bytes 110600 | tf_op jit(solution)/shard_map/ppermute | solution.py:361
  179.7 1.1 collective-permute-start.27
  180.8 1.9 collective-permute-done.25
  182.7 0.9 collective-permute-done.27
  183.7 1.7 collective-permute-start.28
  185.4 1.9 collective-permute-start.29
  187.9 1.6 collective-permute-done.28
  189.5 0.8 collective-permute-done.29
  190.3 1.0 collective-permute-done.30
  191.3 1.7 collective-permute-start.31
  193.2 1.5 collective-permute-start.33
  194.8 1.6 collective-permute-done.31
  196.4 3.2 %collective-permute-done.32 = f32[96,384]{1,0:T(8,128)S(1)} collective-permute-done((f32[96,384]{1,0:T(8,128)S(1)}, f32[96,384]{1,0:T(8,128)S(1)}, u32[]{:S(2)}, u32[]{:S(2)}) %collective-permute-start.32) | collective-permute-done | bytes 147488 | tf_op jit(solution)/shard_map/ppermute | solution.py:205
  199.9 1.8 collective-permute-done.34
  201.8 1.1 fusion.54
  (121 shorter events, 8.5 us)
Async XLA Ops:
  0.6 161.8 %copy-start = (bf16[384,384]{1,0:T(8,128)(2,1)S(1)}, bf16[384,384]{1,0:T(8,128)(2,1)}, u32[]{:S(2)}) copy-start(bf16[384,384]{1,0:T(8,128)(2,1)} %param.14) | copy-start | bytes 884740
  0.6 1.4 copy-start.30
  2.1 7.6 %copy-start.24 = (bf16[256,3072]{1,0:T(8,128)(2,1)S(1)}, bf16[256,3072]{1,0:T(8,128)(2,1)}, u32[]{:S(2)}) copy-start(bf16[256,3072]{1,0:T(8,128)(2,1)} %param.10) | copy-start | bytes 4718596
  2.2 8.5 %copy-start.5 = (bf16[240,768]{1,0:T(8,128)(2,1)}, bf16[240,768]{1,0:T(8,128)(2,1)S(1)}, u32[]{:S(2)}) copy-start(bf16[240,768]{1,0:T(8,128)(2,1)S(1)} %pad_maximum_fusion.9.refs_2_.refs_7_) | copy-start | bytes 1105924
  2.2 11.7 %collective-permute-start.3 = (bf16[240,768]{1,0:T(8,128)(2,1)S(1)}, bf16[240,768]{1,0:T(8,128)(2,1)S(1)}, u32[]{:S(2)}, u32[]{:S(2)}) collective-permute-start(bf16[240,768]{1,0:T(8,128)(2,1)S(1)} %pad_maximum_fusion.9.refs_2_.refs_7_), channel_id=1, source_target_pairs={{8,0},{10,2},{12,4},{14,6},{16,24},{18,26},{20,28},{22,30},{0,8},{... | collective-permute-start | bytes 1105928 | tf_op jit(solution)/shard_map/ppermute | solution.py:244
  5.3 9.3 %collective-permute-start.5 = (bf16[240,768]{1,0:T(8,128)(2,1)S(1)}, bf16[240,768]{1,0:T(8,128)(2,1)S(1)}, u32[]{:S(2)}, u32[]{:S(2)}) collective-permute-start(bf16[240,768]{1,0:T(8,128)(2,1)S(1)} %pad_maximum_fusion.9.refs_2_.refs_7_), channel_id=1, source_target_pairs={{8,16},{10,18},{12,20},{14,22},{16,8},{18,10},{20,12},{22,14},{9,1... | collective-permute-start | bytes 1105928 | tf_op jit(solution)/shard_map/ppermute | solution.py:244
  6.0 11.6 %collective-permute-start = (bf16[240,768]{1,0:T(8,128)(2,1)S(1)}, bf16[240,768]{1,0:T(8,128)(2,1)S(1)}, u32[]{:S(2)}, u32[]{:S(2)}) collective-permute-start(bf16[240,768]{1,0:T(8,128)(2,1)S(1)} %pad_maximum_fusion.6), channel_id=1, source_target_pairs={{0,2},{2,0},{4,6},{6,4},{8,10},{10,8},{12,14},{14,12},{16,18},{18,... | collective-permute-start | bytes 1105928 | tf_op jit(solution)/shard_map/ppermute | solution.py:205
  7.6 17.7 %collective-permute-start.1 = (bf16[240,768]{1,0:T(8,128)(2,1)S(1)}, bf16[240,768]{1,0:T(8,128)(2,1)S(1)}, u32[]{:S(2)}, u32[]{:S(2)}) collective-permute-start(bf16[240,768]{1,0:T(8,128)(2,1)S(1)} %pad_maximum_fusion.7), channel_id=1, source_target_pairs={{0,4},{2,6},{4,0},{6,2},{8,12},{10,14},{12,8},{14,10},{16,20},{18,... | collective-permute-start | bytes 1105928 | tf_op jit(solution)/shard_map/ppermute | solution.py:205
  9.2 6.7 %copy-start.23 = (bf16[256,1536]{1,0:T(8,128)(2,1)S(1)}, bf16[256,1536]{1,0:T(8,128)(2,1)}, u32[]{:S(2)}) copy-start(bf16[256,1536]{1,0:T(8,128)(2,1)} %param.8) | copy-start | bytes 2359300
  9.2 16.1 %collective-permute-start.2 = (bf16[240,768]{1,0:T(8,128)(2,1)S(1)}, bf16[240,768]{1,0:T(8,128)(2,1)S(1)}, u32[]{:S(2)}, u32[]{:S(2)}) collective-permute-start(bf16[240,768]{1,0:T(8,128)(2,1)S(1)} %pad_maximum_fusion.8), channel_id=1, source_target_pairs={{0,6},{2,4},{4,2},{6,0},{8,14},{10,12},{12,10},{14,8},{16,22},{18,... | collective-permute-start | bytes 1105928 | tf_op jit(solution)/shard_map/ppermute | solution.py:205
  13.9 2.3 %copy-start.13 = (bf16[240,768]{1,0:T(8,128)(2,1)}, bf16[240,768]{1,0:T(8,128)(2,1)S(1)}, u32[]{:S(2)}) copy-start(bf16[240,768]{1,0:T(8,128)(2,1)S(1)} %collective-permute-done.3.refs_4_.refs_9_) | copy-start | bytes 1105924
  13.9 11.5 %collective-permute-start.4 = (bf16[240,768]{1,0:T(8,128)(2,1)S(1)}, bf16[240,768]{1,0:T(8,128)(2,1)S(1)}, u32[]{:S(2)}, u32[]{:S(2)}) collective-permute-start(bf16[240,768]{1,0:T(8,128)(2,1)S(1)} %collective-permute-done.3.refs_4_.refs_9_), channel_id=1, source_target_pairs={{8,16},{10,18},{12,20},{14,22},{16,8},{18,10},{20,12},{22,14},{9,1... | collective-permute-start | bytes 1105928 | tf_op jit(solution)/shard_map/ppermute | solution.py:244
  14.6 1.6 copy-start.15
  14.6 13.3 %collective-permute-start.6 = (bf16[240,768]{1,0:T(8,128)(2,1)S(1)}, bf16[240,768]{1,0:T(8,128)(2,1)S(1)}, u32[]{:S(2)}, u32[]{:S(2)}) collective-permute-start(bf16[240,768]{1,0:T(8,128)(2,1)S(1)} %collective-permute-done.5.refs_6_.refs_11_), channel_id=1, source_target_pairs={{8,0},{10,2},{12,4},{14,6},{16,24},{18,26},{20,28},{22,30},{9,1},{... | collective-permute-start | bytes 1105928 | tf_op jit(solution)/shard_map/ppermute | solution.py:244
  25.4 70.1 %copy-start.1 = (bf16[720,768]{1,0:T(8,128)(2,1)}, bf16[720,768]{1,0:T(8,128)(2,1)S(1)}, u32[]{:S(2)}) copy-start(bf16[720,768]{1,0:T(8,128)(2,1)S(1)} %pad_maximum_fusion.4.refs_3_.refs_8_) | copy-start | bytes 3317764
  28.6 36.7 %collective-permute-start.7 = (bf16[256,2304]{1,0:T(8,128)(2,1)S(1)}, bf16[256,2304]{1,0:T(8,128)(2,1)S(1)}, u32[]{:S(2)}, u32[]{:S(2)}) collective-permute-start(bf16[256,2304]{1,0:T(8,128)(2,1)S(1)} %get-tuple-element.22), channel_id=1, source_target_pairs={{0,2},{2,0},{4,6},{6,4},{8,10},{10,8},{12,14},{14,12},{16,18},{18,... | collective-permute-start | bytes 3538952 | tf_op jit(solution)/shard_map/ppermute | solution.py:205
  30.1 35.3 %collective-permute-start.8 = (bf16[256,2304]{1,0:T(8,128)(2,1)S(1)}, bf16[256,2304]{1,0:T(8,128)(2,1)S(1)}, u32[]{:S(2)}, u32[]{:S(2)}) collective-permute-start(bf16[256,2304]{1,0:T(8,128)(2,1)S(1)} %get-tuple-element.23), channel_id=1, source_target_pairs={{0,4},{2,6},{4,0},{6,2},{8,12},{10,14},{12,8},{14,10},{16,20},{18,... | collective-permute-start | bytes 3538952 | tf_op jit(solution)/shard_map/ppermute | solution.py:205
  31.6 33.7 %collective-permute-start.10 = (bf16[720,768]{1,0:T(8,128)(2,1)S(1)}, bf16[720,768]{1,0:T(8,128)(2,1)S(1)}, u32[]{:S(2)}, u32[]{:S(2)}) collective-permute-start(bf16[720,768]{1,0:T(8,128)(2,1)S(1)} %pad_maximum_fusion.4.refs_3_.refs_8_), channel_id=1, source_target_pairs={{8,16},{10,18},{12,20},{14,22},{16,8},{18,10},{20,12},{22,14},{9,1... | collective-permute-start | bytes 3317768 | tf_op jit(solution)/shard_map/ppermute | solution.py:244
  32.3 33.0 %collective-permute-start.9 = (bf16[720,768]{1,0:T(8,128)(2,1)S(1)}, bf16[720,768]{1,0:T(8,128)(2,1)S(1)}, u32[]{:S(2)}, u32[]{:S(2)}) collective-permute-start(bf16[720,768]{1,0:T(8,128)(2,1)S(1)} %pad_maximum_fusion.4.refs_3_.refs_8_), channel_id=1, source_target_pairs={{8,0},{10,2},{12,4},{14,6},{16,24},{18,26},{20,28},{22,30},{0,8},{... | collective-permute-start | bytes 3317768 | tf_op jit(solution)/shard_map/ppermute | solution.py:244
  34.7 29.9 %collective-permute-start.11 = (bf16[240,768]{1,0:T(8,128)(2,1)S(1)}, bf16[240,768]{1,0:T(8,128)(2,1)S(1)}, u32[]{:S(2)}, u32[]{:S(2)}) collective-permute-start(bf16[240,768]{1,0:T(8,128)(2,1)S(1)} %collective-permute-done.4.refs_8_.refs_13_), channel_id=1, source_target_pairs={{8,0},{10,2},{12,4},{14,6},{16,24},{18,26},{20,28},{22,30},{9,1},{... | collective-permute-start | bytes 1105928 | tf_op jit(solution)/shard_map/ppermute | solution.py:244
  64.6 0.8 copy-start.21
  65.3 30.1 %copy-start.25 = (bf16[256,2304]{1,0:T(8,128)(2,1)}, bf16[256,2304]{1,0:T(8,128)(2,1)S(1)}, u32[]{:S(2)}) copy-start(bf16[256,2304]{1,0:T(8,128)(2,1)S(1)} %collective-permute-done.7) | copy-start | bytes 3538948
  65.4 30.1 %copy-start.26 = (bf16[256,2304]{1,0:T(8,128)(2,1)}, bf16[256,2304]{1,0:T(8,128)(2,1)S(1)}, u32[]{:S(2)}) copy-start(bf16[256,2304]{1,0:T(8,128)(2,1)S(1)} %collective-permute-done.8) | copy-start | bytes 3538948
  65.4 30.0 %collective-permute-start.12 = (bf16[256,2304]{1,0:T(8,128)(2,1)S(1)}, bf16[256,2304]{1,0:T(8,128)(2,1)S(1)}, u32[]{:S(2)}, u32[]{:S(2)}) collective-permute-start(bf16[256,2304]{1,0:T(8,128)(2,1)S(1)} %get-tuple-element.29), channel_id=1, source_target_pairs={{0,6},{2,4},{4,2},{6,0},{8,14},{10,12},{12,10},{14,8},{16,22},{18,... | collective-permute-start | bytes 3538952 | tf_op jit(solution)/shard_map/ppermute | solution.py:205
  66.9 5.1 %collective-permute-start.13 = (bf16[720,768]{1,0:T(8,128)(2,1)S(1)}, bf16[720,768]{1,0:T(8,128)(2,1)}, u32[]{:S(2)}, u32[]{:S(2)}) collective-permute-start(bf16[720,768]{1,0:T(8,128)(2,1)S(1)} %collective-permute-done.9.refs_5_.refs_10_), channel_id=1, source_target_pairs={{8,16},{10,18},{12,20},{14,22},{16,8},{18,10},{20,12},{22,14},{9,1... | collective-permute-start | bytes 3317768 | tf_op jit(solution)/shard_map/ppermute | solution.py:244
  68.7 1.0 copy-start.9
  69.7 24.8 %collective-permute-start.14 = (bf16[720,768]{1,0:T(8,128)(2,1)S(1)}, bf16[720,768]{1,0:T(8,128)(2,1)S(1)}, u32[]{:S(2)}, u32[]{:S(2)}) collective-permute-start(bf16[720,768]{1,0:T(8,128)(2,1)S(1)} %collective-permute-done.10.refs_7_.refs_12_), channel_id=1, source_target_pairs={{8,0},{10,2},{12,4},{14,6},{16,24},{18,26},{20,28},{22,30},{9,1},{... | collective-permute-start | bytes 3317768 | tf_op jit(solution)/shard_map/ppermute | solution.py:244
  71.0 1.1 copy-start.7
  94.4 1.0 copy-start.11
  95.4 1.0 copy-start.27
  96.7 5.9 %collective-permute-start.15 = (bf16[1024,1536]{1,0:T(8,128)(2,1)S(1)}, bf16[1024,1536]{1,0:T(8,128)(2,1)}, u32[]{:S(2)}, u32[]{:S(2)}) collective-permute-start(bf16[1024,1536]{1,0:T(8,128)(2,1)S(1)} %pad_maximum_fusion), channel_id=1, source_target_pairs={{0,1},{1,0},{2,3},{3,2},{4,5},{5,4},{6,7},{7,6},{8,9},{9,8},{10,11... | collective-permute-start | bytes 9437192 | tf_op jit(solution)/shard_map/ppermute | solution.py:208
  96.8 29.0 %collective-permute-start.16 = (bf16[720,768]{1,0:T(8,128)(2,1)}, bf16[720,768]{1,0:T(8,128)(2,1)}, u32[]{:S(2)}, u32[]{:S(2)}) collective-permute-start(bf16[720,768]{1,0:T(8,128)(2,1)} %collective-permute-done.13.refs_9_.refs_14_), channel_id=1, source_target_pairs={{8,0},{10,2},{12,4},{14,6},{16,24},{18,26},{20,28},{22,30},{9,1},{... | collective-permute-start | bytes 3317768 | tf_op jit(solution)/shard_map/ppermute | solution.py:244
  100.0 6.0 %copy-start.16 = (bf16[240,768]{1,0:T(8,128)(2,1)S(1)}, bf16[240,768]{1,0:T(8,128)(2,1)}, u32[]{:S(2)}) copy-start(bf16[240,768]{1,0:T(8,128)(2,1)} %copy-done.15) | copy-start | bytes 1105924
  100.0 6.0 %copy-start.18 = (bf16[240,768]{1,0:T(8,128)(2,1)S(1)}, bf16[240,768]{1,0:T(8,128)(2,1)}, u32[]{:S(2)}) copy-start(bf16[240,768]{1,0:T(8,128)(2,1)} %copy-done.17) | copy-start | bytes 1105924
  100.0 6.0 %copy-start.20 = (bf16[240,768]{1,0:T(8,128)(2,1)S(1)}, bf16[240,768]{1,0:T(8,128)(2,1)}, u32[]{:S(2)}) copy-start(bf16[240,768]{1,0:T(8,128)(2,1)} %copy-done.19) | copy-start | bytes 1105924
  101.1 4.9 %copy-start.12 = (bf16[720,768]{1,0:T(8,128)(2,1)S(1)}, bf16[720,768]{1,0:T(8,128)(2,1)}, u32[]{:S(2)}) copy-start(bf16[720,768]{1,0:T(8,128)(2,1)} %copy-done.11) | copy-start | bytes 3317764
  102.6 3.4 %copy-start.2 = (bf16[720,768]{1,0:T(8,128)(2,1)S(1)}, bf16[720,768]{1,0:T(8,128)(2,1)}, u32[]{:S(2)}) copy-start(bf16[720,768]{1,0:T(8,128)(2,1)} %copy-done.1) | copy-start | bytes 3317764
  102.6 3.4 %copy-start.6 = (bf16[240,768]{1,0:T(8,128)(2,1)S(1)}, bf16[240,768]{1,0:T(8,128)(2,1)}, u32[]{:S(2)}) copy-start(bf16[240,768]{1,0:T(8,128)(2,1)} %copy-done.5) | copy-start | bytes 1105924
  102.6 3.4 %copy-start.8 = (bf16[720,768]{1,0:T(8,128)(2,1)S(1)}, bf16[720,768]{1,0:T(8,128)(2,1)}, u32[]{:S(2)}) copy-start(bf16[720,768]{1,0:T(8,128)(2,1)} %copy-done.7) | copy-start | bytes 3317764
  102.6 3.4 %copy-start.10 = (bf16[720,768]{1,0:T(8,128)(2,1)S(1)}, bf16[720,768]{1,0:T(8,128)(2,1)}, u32[]{:S(2)}) copy-start(bf16[720,768]{1,0:T(8,128)(2,1)} %copy-done.9) | copy-start | bytes 3317764
  102.6 3.4 %copy-start.14 = (bf16[240,768]{1,0:T(8,128)(2,1)S(1)}, bf16[240,768]{1,0:T(8,128)(2,1)}, u32[]{:S(2)}) copy-start(bf16[240,768]{1,0:T(8,128)(2,1)} %copy-done.13) | copy-start | bytes 1105924
  106.0 19.8 %copy-start.4 = (bf16[256,768]{1,0:T(8,128)(2,1)S(1)}, bf16[256,768]{1,0:T(8,128)(2,1)}, u32[]{:S(2)}) copy-start(bf16[256,768]{1,0:T(8,128)(2,1)} %get-tuple-element.48.refs_3_) | copy-start | bytes 1179652
  106.1 19.8 %copy-start.22 = (bf16[240,768]{1,0:T(8,128)(2,1)S(1)}, bf16[240,768]{1,0:T(8,128)(2,1)}, u32[]{:S(2)}) copy-start(bf16[240,768]{1,0:T(8,128)(2,1)} %copy-done.21) | copy-start | bytes 1105924
  114.1 1.6 copy-start.3
  134.1 3.8 %collective-permute-start.17 = (f32[544,768]{1,0:T(8,128)}, f32[544,768]{1,0:T(8,128)S(1)}, u32[]{:S(2)}, u32[]{:S(2)}) collective-permute-start(f32[544,768]{1,0:T(8,128)} %get-tuple-element.40), channel_id=1, source_target_pairs={{0,1},{1,0},{2,3},{3,2},{4,5},{5,4},{6,7},{7,6},{8,9},{9,8},{10,11... | collective-permute-start | bytes 5013512 | tf_op jit(solution)/shard_map/ppermute | solution.py:208
  138.2 23.8 %copy-start.29 = (bf16[384,384]{1,0:T(8,128)(2,1)S(1)}, bf16[384,384]{1,0:T(8,128)(2,1)}, u32[]{:S(2)}) copy-start(bf16[384,384]{1,0:T(8,128)(2,1)} %param.13) | copy-start | bytes 884740
  138.3 12.7 %collective-permute-start.18 = (f32[136,768]{1,0:T(8,128)S(1)}, f32[136,768]{1,0:T(8,128)}, u32[]{:S(2)}, u32[]{:S(2)}) collective-permute-start(f32[136,768]{1,0:T(8,128)S(1)} %get-tuple-element.45), channel_id=1, source_target_pairs={{0,2},{2,0},{4,6},{6,4},{8,10},{10,8},{12,14},{14,12},{16,18},{18,... | collective-permute-start | bytes 1253384 | tf_op jit(solution)/shard_map/ppermute | solution.py:205
  140.1 20.5 %collective-permute-start.19 = (f32[136,768]{1,0:T(8,128)S(1)}, f32[136,768]{1,0:T(8,128)}, u32[]{:S(2)}, u32[]{:S(2)}) collective-permute-start(f32[136,768]{1,0:T(8,128)S(1)} %get-tuple-element.47), channel_id=1, source_target_pairs={{0,4},{2,6},{4,0},{6,2},{8,12},{10,14},{12,8},{14,10},{16,20},{18,... | collective-permute-start | bytes 1253384 | tf_op jit(solution)/shard_map/ppermute | solution.py:205
  140.3 20.3 %collective-permute-start.20 = (f32[136,768]{1,0:T(8,128)S(1)}, f32[136,768]{1,0:T(8,128)}, u32[]{:S(2)}, u32[]{:S(2)}) collective-permute-start(f32[136,768]{1,0:T(8,128)S(1)} %get-tuple-element.46), channel_id=1, source_target_pairs={{0,6},{2,4},{4,2},{6,0},{8,14},{10,12},{12,10},{14,8},{16,22},{18,... | collective-permute-start | bytes 1253384 | tf_op jit(solution)/shard_map/ppermute | solution.py:205
  161.9 1.0 copy-start.28
  165.3 2.1 %collective-permute-start.21 = (f32[384,384]{1,0:T(8,128)S(1)}, f32[384,384]{1,0:T(8,128)S(1)}, u32[]{:S(2)}, u32[]{:S(2)}) collective-permute-start(f32[384,384]{1,0:T(8,128)S(1)} %fusion), channel_id=1, source_target_pairs={{0,1},{1,0},{2,3},{3,2},{4,5},{5,4},{6,7},{7,6},{8,9},{9,8},{10,11... | collective-permute-start | bytes 1769480 | tf_op jit(solution)/shard_map/ppermute | solution.py:208
  167.7 6.8 %collective-permute-start.22 = (f32[96,384]{1,0:T(8,128)S(1)}, f32[96,384]{1,0:T(8,128)S(1)}, u32[]{:S(2)}, u32[]{:S(2)}) collective-permute-start(f32[96,384]{1,0:T(8,128)S(1)} %get-tuple-element.61), channel_id=1, source_target_pairs={{0,2},{2,0},{4,6},{6,4},{8,10},{10,8},{12,14},{14,12},{16,18},{18,... | collective-permute-start | bytes 442376 | tf_op jit(solution)/shard_map/ppermute | solution.py:205
  168.1 8.8 %collective-permute-start.23 = (f32[96,384]{1,0:T(8,128)S(1)}, f32[96,384]{1,0:T(8,128)S(1)}, u32[]{:S(2)}, u32[]{:S(2)}) collective-permute-start(f32[96,384]{1,0:T(8,128)S(1)} %get-tuple-element.63), channel_id=1, source_target_pairs={{0,4},{2,6},{4,0},{6,2},{8,12},{10,14},{12,8},{14,10},{16,20},{18,... | collective-permute-start | bytes 442376 | tf_op jit(solution)/shard_map/ppermute | solution.py:205
  169.5 7.4 %collective-permute-start.24 = (f32[96,384]{1,0:T(8,128)S(1)}, f32[96,384]{1,0:T(8,128)S(1)}, u32[]{:S(2)}, u32[]{:S(2)}) collective-permute-start(f32[96,384]{1,0:T(8,128)S(1)} %get-tuple-element.62), channel_id=1, source_target_pairs={{0,6},{2,4},{4,2},{6,0},{8,14},{10,12},{12,10},{14,8},{16,22},{18,... | collective-permute-start | bytes 442376 | tf_op jit(solution)/shard_map/ppermute | solution.py:205
  176.9 5.8 %collective-permute-start.25 = (f32[24,384]{1,0:T(8,128)S(1)}, f32[24,384]{1,0:T(8,128)S(1)}, u32[]{:S(2)}, u32[]{:S(2)}) collective-permute-start(f32[24,384]{1,0:T(8,128)S(1)} %get-tuple-element.68), channel_id=1, source_target_pairs={{0,8},{2,10},{4,12},{6,14},{8,16},{10,18},{12,20},{14,22},{16,24},... | collective-permute-start | bytes 110600 | tf_op jit(solution)/shard_map/ppermute | solution.py:361
  177.0 5.7 %collective-permute-start.26 = (f32[24,384]{1,0:T(8,128)S(1)}, f32[24,384]{1,0:T(8,128)S(1)}, u32[]{:S(2)}, u32[]{:S(2)}) collective-permute-start(f32[24,384]{1,0:T(8,128)S(1)} %get-tuple-element.70), channel_id=1, source_target_pairs={{0,16},{2,18},{4,20},{6,22},{8,24},{10,26},{12,28},{14,30},{16,0},... | collective-permute-start | bytes 110600 | tf_op jit(solution)/shard_map/ppermute | solution.py:361
  179.7 4.0 %collective-permute-start.27 = (f32[24,384]{1,0:T(8,128)S(1)}, f32[24,384]{1,0:T(8,128)S(1)}, u32[]{:S(2)}, u32[]{:S(2)}) collective-permute-start(f32[24,384]{1,0:T(8,128)S(1)} %get-tuple-element.69), channel_id=1, source_target_pairs={{0,24},{2,26},{4,28},{6,30},{8,0},{10,2},{12,4},{14,6},{16,8},{18,... | collective-permute-start | bytes 110600 | tf_op jit(solution)/shard_map/ppermute | solution.py:361
  183.7 5.8 %collective-permute-start.28 = (f32[24,384]{1,0:T(8,128)S(1)}, f32[24,384]{1,0:T(8,128)S(1)}, u32[]{:S(2)}, u32[]{:S(2)}) collective-permute-start(f32[24,384]{1,0:T(8,128)S(1)} %get-tuple-element.42), channel_id=1, source_target_pairs={{0,8},{2,10},{4,12},{6,14},{8,16},{10,18},{12,20},{14,22},{16,24},... | collective-permute-start | bytes 110600 | tf_op jit(solution)/shard_map/ppermute | solution.py:361
  185.4 4.9 %collective-permute-start.29 = (f32[24,384]{1,0:T(8,128)S(1)}, f32[24,384]{1,0:T(8,128)S(1)}, u32[]{:S(2)}, u32[]{:S(2)}) collective-permute-start(f32[24,384]{1,0:T(8,128)S(1)} %get-tuple-element.42), channel_id=1, source_target_pairs={{0,16},{2,18},{4,20},{6,22},{8,24},{10,26},{12,28},{14,30},{16,0},... | collective-permute-start | bytes 110600 | tf_op jit(solution)/shard_map/ppermute | solution.py:361
  187.3 4.0 %collective-permute-start.30 = (f32[24,384]{1,0:T(8,128)S(1)}, f32[24,384]{1,0:T(8,128)S(1)}, u32[]{:S(2)}, u32[]{:S(2)}) collective-permute-start(f32[24,384]{1,0:T(8,128)S(1)} %get-tuple-element.42), channel_id=1, source_target_pairs={{0,24},{2,26},{4,28},{6,30},{8,0},{10,2},{12,4},{14,6},{16,8},{18,... | collective-permute-start | bytes 110600 | tf_op jit(solution)/shard_map/ppermute | solution.py:361
  191.3 5.1 %collective-permute-start.31 = (f32[96,384]{1,0:T(8,128)S(1)}, f32[96,384]{1,0:T(8,128)S(1)}, u32[]{:S(2)}, u32[]{:S(2)}) collective-permute-start(f32[96,384]{1,0:T(8,128)S(1)} %constant_dynamic-update-slice_fusion.6), channel_id=1, source_target_pairs={{0,2},{2,0},{4,6},{6,4},{8,10},{10,8},{12,14},{14,12},{16,18},{18,... | collective-permute-start | bytes 442376 | tf_op jit(solution)/shard_map/ppermute | solution.py:205
  192.9 6.7 %collective-permute-start.32 = (f32[96,384]{1,0:T(8,128)S(1)}, f32[96,384]{1,0:T(8,128)S(1)}, u32[]{:S(2)}, u32[]{:S(2)}) collective-permute-start(f32[96,384]{1,0:T(8,128)S(1)} %constant_dynamic-update-slice_fusion.6), channel_id=1, source_target_pairs={{0,4},{2,6},{4,0},{6,2},{8,12},{10,14},{12,8},{14,10},{16,20},{18,... | collective-permute-start | bytes 442376 | tf_op jit(solution)/shard_map/ppermute | solution.py:205
  193.2 6.5 %collective-permute-start.33 = (f32[96,384]{1,0:T(8,128)S(1)}, f32[96,384]{1,0:T(8,128)S(1)}, u32[]{:S(2)}, u32[]{:S(2)}) collective-permute-start(f32[96,384]{1,0:T(8,128)S(1)} %constant_dynamic-update-slice_fusion.6), channel_id=1, source_target_pairs={{0,6},{2,4},{4,2},{6,0},{8,14},{10,12},{12,10},{14,8},{16,22},{18,... | collective-permute-start | bytes 442376 | tf_op jit(solution)/shard_map/ppermute | solution.py:205
  199.7 2.1 %collective-permute-start.34 = (f32[384,384]{1,0:T(8,128)S(1)}, f32[384,384]{1,0:T(8,128)S(1)}, u32[]{:S(2)}, u32[]{:S(2)}) collective-permute-start(f32[384,384]{1,0:T(8,128)S(1)} %constant_dynamic-update-slice_fusion.2), channel_id=1, source_target_pairs={{0,1},{1,0},{2,3},{3,2},{4,5},{5,4},{6,7},{7,6},{8,9},{9,8},{10,11... | collective-permute-start | bytes 1769480 | tf_op jit(solution)/shard_map/ppermute | solution.py:208
  (2 other events, 1.5 us)

commit v5 on v4

--- a/solution.py
+++ b/solution.py
@@ -36,7 +36,8 @@
 
 
 def attend_kernel(rows, planes, *refs):
-    mine_ref, other_ref, *flow, out_ref, weight, sems = refs
+    mine_ref, other_ref, *refs = refs
+    stay_refs, (*flow, out_ref, weight, sems) = refs[:GROUP], refs[GROUP:]
     plane, member, core = place()
     span = flow[0].shape[0]
 
@@ -66,17 +67,21 @@
         total = jnp.dot(lhs, weight[pl.ds(at, heads)], preferred_element_type=F32)
         at = pl.multiple_of((1 - core) * heads, 128)
         total += jnp.dot(rhs, weight[pl.ds(at, heads)], preferred_element_type=F32)
-        out_ref[h * local : (h + 2) * local] = total
-
-
-def attend(rows, planes, mine, other, flow):
+        for g in range(2):
+            stay = stay_refs[h + g][...].astype(F32)
+            out_ref[(h + g) * local : (h + g + 1) * local] = stay + total[g * local : (g + 1) * local]
+
+
+def attend(rows, planes, mine, other, stay, flow):
     group, tokens, heads = mine.shape
     count = flow[0].shape[1]
     part = pl.BlockSpec((group, tokens // 2, heads), lambda i: (0, i, 0))
     return pl.pallas_call(
         functools.partial(attend_kernel, rows, planes),
         grid=(2,),
-        in_specs=[part, part] + [pl.BlockSpec(memory_space=pl.ANY)] * len(flow),
+        in_specs=[part, part]
+        + [pl.BlockSpec((tokens // 2, count), lambda i: (i, 0))] * group
+        + [pl.BlockSpec(memory_space=pl.ANY)] * len(flow),
         out_specs=pl.BlockSpec((group * tokens // 2, count), lambda i: (i, 0)),
         out_shape=jax.ShapeDtypeStruct((group * tokens, count), F32),
         scratch_shapes=[pltpu.VMEM((2 * heads, count), BF16), pltpu.SemaphoreType.DMA((planes, group))],
@@ -84,13 +89,11 @@
         cost_estimate=pl.CostEstimate(
             flops=4 * group * tokens * heads * count, bytes_accessed=16 << 20, transcendentals=0
         ),
-    )(mine, other, *flow)
+    )(mine, other, *stay, *flow)
 
 
 def finish_kernel(rows, planes, *refs):
-    total_ref, far_ref, gain_ref, *refs = refs
-    stay_refs, refs = refs[:GROUP], refs[GROUP:]
-    *flow, keep_ref, send_ref, weight, down, scaled, sums, sems, down_sems = refs
+    total_ref, far_ref, gain_ref, *flow, keep_ref, send_ref, weight, down, sems, down_sems = refs
     plane, member, core = place()
     span = flow[0].shape[0]
     columns = span - rows
@@ -124,45 +127,41 @@
 
     for copy in far:
         copy.wait()
-    local = stay_refs[0].shape[0] // 2
-    half = GROUP * local
     gain = gain_ref[...].astype(F32)
-    for i in range(2):
+    half = total_ref.shape[0] // 2
+    local = half // GROUP
+    line = local + 8
+    dims = (((1,), (1,)), ((), ()))
+    gains = None
+    for out_ref, k in ((send_ref, 1 - core), (keep_ref, core)):
         for h in range(0, GROUP, 2):
-            at = i * half + h * local
-            lhs = jnp.concatenate([far_ref[h + g, i * local : (i + 1) * local] for g in range(2)], axis=0)
-            total = total_ref[at : at + 2 * local] + jnp.dot(lhs, weight[...], preferred_element_type=F32)
-            stay = jnp.concatenate([stay_refs[h + g][i * local : (i + 1) * local] for g in range(2)], axis=0)
-            stream = (stay.astype(F32) + total).astype(BF16).astype(F32)
-            scaled[at : at + 2 * local] = (stream * gain).astype(BF16)
+            own_rows = pl.ds(pl.multiple_of(k * half + h * local, 128), 2 * local)
+            total = total_ref[own_rows] + jnp.dot(far_ref[own_rows], weight[...], preferred_element_type=F32)
+            stream = total.astype(BF16).astype(F32)
             row_sum = jnp.sum(stream, axis=1, keepdims=True)
             squares = jnp.sum(stream * stream, axis=1, keepdims=True)
             lane = lax.broadcasted_iota(jnp.int32, (2 * local, 128), 1)
-            both = jnp.where(lane == 0, row_sum, jnp.where(lane == 1, squares, 0.0))
-            sums[:, at : at + 2 * local] = both.T[:8]
-
-    for at in range(planes):
-
-        @pl.when(plane == at)
-        def _():
-            for copy in down_copies(at):
-                copy.wait()
-
-    dims = (((1,), (1,)), ((), ()))
-    gains = jnp.broadcast_to(gain_ref[...], (16, gain_ref.shape[1]))
-    gains = lax.dot_general(gains, down[...], dims, preferred_element_type=F32)
-    line = local + 8
-    for out_ref, k in ((send_ref, 1 - core), (keep_ref, core)):
-        at = pl.multiple_of(k * half, 128)
-        value = lax.dot_general(scaled[pl.ds(at, half)], down[...], dims, preferred_element_type=F32)
-        stats = sums[:, pl.ds(at, half)]
-        for s in range(GROUP):
-            out_ref[s * line : s * line + local] = value[s * local : (s + 1) * local]
-            out_ref[s * line + local : (s + 1) * line] = gains[:8]
-            out_ref[s * line + local + 1 : s * line + local + 3, :local] = stats[:2, s * local : (s + 1) * local]
-
-
-def finish(rows, planes, total, far, gain, stay, flow):
+            both = jnp.where(lane == 0, row_sum, jnp.where(lane == 1, squares, 0.0)).T
+            if gains is None:
+                for at in range(planes):
+
+                    @pl.when(plane == at)
+                    def _():
+                        for copy in down_copies(at):
+                            copy.wait()
+
+                gains = jnp.broadcast_to(gain_ref[...], (16, gain_ref.shape[1]))
+                gains = lax.dot_general(gains, down[...], dims, preferred_element_type=F32)[:8]
+            scaled = (stream * gain).astype(BF16)
+            value = lax.dot_general(scaled, down[...], dims, preferred_element_type=F32)
+            for g in range(2):
+                at = (h + g) * line
+                out_ref[at : at + local] = value[g * local : (g + 1) * local]
+                out_ref[at + local : at + line] = gains
+                out_ref[at + local + 1 : at + local + 3, :local] = both[:2, g * local : (g + 1) * local]
+
+
+def finish(rows, planes, total, far, gain, flow):
     count = total.shape[1]
     tokens = total.shape[0]
     span = flow[0].shape[0]
@@ -170,14 +169,12 @@
     inside = pl.BlockSpec(memory_space=pltpu.VMEM)
     return pl.pallas_call(
         functools.partial(finish_kernel, rows, planes),
-        in_specs=[inside] * (3 + GROUP) + [pl.BlockSpec(memory_space=pl.ANY)] * len(flow),
+        in_specs=[inside] * 3 + [pl.BlockSpec(memory_space=pl.ANY)] * len(flow),
         out_specs=[inside, inside],
         out_shape=[jax.ShapeDtypeStruct((tokens // 2 + 8 * GROUP, out), F32)] * 2,
         scratch_shapes=[
             pltpu.VMEM((GROUP * rows, count), BF16),
             pltpu.VMEM((out, count), BF16),
-            pltpu.VMEM((tokens, count), BF16),
-            pltpu.VMEM((8, tokens), F32),
             pltpu.SemaphoreType.DMA((GROUP,)),
             pltpu.SemaphoreType.DMA((planes, GROUP)),
         ],
@@ -185,7 +182,84 @@
         cost_estimate=pl.CostEstimate(
             flops=2 * tokens * count * (GROUP * rows + out), bytes_accessed=16 << 20, transcendentals=0
         ),
-    )(total, far, gain, *stay, *flow)
+    )(total, far, gain, *flow)
+
+
+def split(value):
+    high = value.astype(BF16)
+    return high, (value - high.astype(F32)).astype(BF16)
+
+
+def times(value, weight, turned=False):
+    count = value.shape[0]
+    dims = (((1,), (1 if turned else 0,)), ((), ()))
+    both = lax.dot_general(jnp.concatenate(split(value), axis=0), weight, dims, preferred_element_type=F32)
+    return both[:count] + both[count:]
+
+
+def outer(left, right):
+    (left, left_low), (right, right_low) = split(left), split(right)
+    left = jnp.concatenate([left, left, left_low], axis=0)
+    right = jnp.concatenate([right, right_low, right], axis=0)
+    return lax.dot_general(left, right, (((0,), (0,)), ((), ())), preferred_element_type=F32)
+
+
+def gelu_and_slope(v):
+    scale = 0.7978845608028654
+    t = jnp.tanh(scale * (v + 0.044715 * (v * v * v)))
+    slope = 0.5 * (1.0 + t) + 0.5 * v * (1.0 - t * t) * (scale * (1.0 + 3.0 * 0.044715 * (v * v)))
+    return 0.5 * v * (1.0 + t), slope
+
+
+def side_kernel(width, all_tokens, *refs):
+    *part_refs, f_ref, g_ref, target_ref, out_ref, keep_ref, send_ref = refs
+    local, features = out_ref.shape
+    half = features // 2
+    total = part_refs[0][...]
+    for ref in part_refs[1:]:
+        total = total + ref[...]
+    tail = total[local:]
+    stats = jnp.concatenate([tail[:, :local]] * (local // 8), axis=0).T
+    mean = stats[:, 1:2] / width
+    spread = stats[:, 2:3] / width - mean * mean
+    side_in = (total[:local] - mean * tail[:1]) / jnp.sqrt(spread + 1e-06)
+    first, second = side_in[:, :half], side_in[:, half:]
+    f_w, g_w = f_ref[...], g_ref[...]
+    f_value, f_slope = gelu_and_slope(times(second, f_w))
+    upper = first + f_value
+    g_value, g_slope = gelu_and_slope(times(upper, g_w))
+    lower = second + g_value
+    out_ref[:, :half] = upper
+    out_ref[:, half:] = lower
+    g_back = (lower - target_ref[:, half:]) / all_tokens * g_slope
+    upper_back = (upper - target_ref[:, :half]) / all_tokens + times(g_back, g_w, turned=True)
+    g_grad = outer(upper, g_back)
+    f_grad = outer(second, upper_back * f_slope)
+    core = lax.axis_index("narrow")
+
+    @pl.when(core == 0)
+    def _():
+        keep_ref[...] = f_grad
+        send_ref[...] = g_grad
+
+    @pl.when(core != 0)
+    def _():
+        keep_ref[...] = g_grad
+        send_ref[...] = f_grad
+
+
+def side_block(width, all_tokens, parts, f_weight, g_weight, targets):
+    inside = pl.BlockSpec(memory_space=pltpu.VMEM)
+    grad = jax.ShapeDtypeStruct(f_weight.shape, F32)
+    work = targets.shape[0] * f_weight.size
+    return pl.pallas_call(
+        functools.partial(side_kernel, width, all_tokens),
+        in_specs=[inside] * (len(parts) + 3),
+        out_specs=[inside] * 3,
+        out_shape=[jax.ShapeDtypeStruct(targets.shape, F32), grad, grad],
+        compiler_params=pltpu.CompilerParams(vmem_limit_bytes=24 << 20),
+        cost_estimate=pl.CostEstimate(flops=24 * work, bytes_accessed=5 << 20, transcendentals=2 * targets.size),
+    )(*parts, f_weight, g_weight, targets)
 
 
 def per_device(group, wides, narrows, context, out_weight, residual, ln_gain, side_down, f_weight, g_weight, targets):
@@ -273,19 +347,22 @@
         flow = [own[0], rest]
         for pair in zip(own_one + own_two, rest_one + rest_two):
             flow += pair
-        total = attend(rows, planes, mine, other, flow)
+        total = attend(rows, planes, mine, other, stay, flow)
         last = jnp.where(plane == 0, planes - 1, 0)
         width = group * rows
         last_part = jnp.where(last * width // heads == core, mine, other)
         last_part = lax.dynamic_slice_in_dim(last_part, last * width % heads, width, 2)
+        last_part = last_part.reshape(group, narrows, local, width).swapaxes(0, 1).reshape(-1, width)
         flow += [own_last, rest_last]
-        keep, send = finish(rows, planes, total, last_part, gain, stay, flow)
+        keep, send = finish(rows, planes, total, last_part, gain, flow)
         summed = keep + to_core(send, 1)
         span = local + 8
-        projected = summed[:span]
-        for s in range(1, group):
-            projected = projected + to_member(summed[s * span : (s + 1) * span], s)
-        stats = projected[local + 1 : local + 3, :local]
+        pieces = [summed[:span]]
+        pieces += [to_member(summed[s * span : (s + 1) * span], s) for s in range(1, group)]
+        width = out_weight.shape[1] * narrows
+        all_tokens = local * wides * narrows
+        side_out, keep, send = side_block(width, all_tokens, pieces, f_weight, g_weight, targets)
+        grads = keep + to_core(send, 1)
     else:
         pieces = [to_member(own[s], s) for s in members]
         down_plane = in_plane([to_member(down_own[s], s) for s in members])
@@ -327,32 +404,28 @@
         )
         summed_stats = sum_cores(lambda k: lax.dynamic_index_in_dim(stats_own, k, 1, keepdims=False))
         stats = sum_members(lambda s: summed_stats[:, s])
-    projected, gain_map = projected[:local], projected[local]
-
-    width = out_weight.shape[1] * narrows
-    mean = stats[0] / width
-    spread = stats[1] / width - mean * mean
-    side_in = (projected - mean[:, None] * gain_map[None, :]) / jnp.sqrt(spread + 1e-06)[:, None]
-    half = side_in.shape[1] // 2
-    f_w, g_w = f_weight.astype(F32), g_weight.astype(F32)
-    first, second = side_in[:, :half], side_in[:, half:]
-    f_value, f_pull = jax.vjp(coupling, second, f_w)
-    upper = first + f_value
-    g_value, g_pull = jax.vjp(coupling, upper, g_w)
-    lower = second + g_value
-    side_out = jnp.concatenate([upper, lower], axis=1)
-    misfit = (side_out - targets) / (local * wides * narrows)
-    upper_back, g_local = g_pull(misfit[:, half:])
-    f_local = f_pull(misfit[:, :half] + upper_back)[1]
-
-    if (2 * half) % (wides * narrows * 8):
+        projected, gain_map = projected[:local], projected[local]
+
+        width = out_weight.shape[1] * narrows
+        mean = stats[0] / width
+        spread = stats[1] / width - mean * mean
+        side_in = (projected - mean[:, None] * gain_map[None, :]) / jnp.sqrt(spread + 1e-06)[:, None]
+        half = side_in.shape[1] // 2
+        f_w, g_w = f_weight.astype(F32), g_weight.astype(F32)
+        first, second = side_in[:, :half], side_in[:, half:]
+        f_value, f_pull = jax.vjp(coupling, second, f_w)
+        upper = first + f_value
+        g_value, g_pull = jax.vjp(coupling, upper, g_w)
+        lower = second + g_value
+        side_out = jnp.concatenate([upper, lower], axis=1)
+        misfit = (side_out - targets) / (local * wides * narrows)
+        upper_back, g_local = g_pull(misfit[:, half:])
+        f_local = f_pull(misfit[:, :half] + upper_back)[1]
         f_total, g_total = lax.psum((f_local, g_local), ("wide", "narrow"))
         return side_out, f_total, g_total
 
-    grads = jnp.concatenate([f_local, g_local], axis=0)
-    share = 2 * half // narrows
-    grads = sum_cores(lambda k: block(grads, k, share, 0))
-    share = share // group
+    half = grads.shape[1]
+    share = grads.shape[0] // group
     part = grads
     grads = sum_members(lambda s: block(part, member ^ s, share, 0))
     share = share // planes
@@ -372,11 +445,8 @@
     part, whole = whole, jnp.zeros((group * share, half), F32)
     for s in members:
         whole = lax.dynamic_update_slice_in_dim(whole, to_member(part, s), (member ^ s) * share, 0)
-    share = share * group
-    part, whole = whole, jnp.zeros((narrows * share, half), F32)
-    for t in range(narrows):
-        whole = lax.dynamic_update_slice_in_dim(whole, to_core(part, t), (core ^ t) * share, 0)
-    return side_out, whole[:half], whole[half:]
+    other = to_core(whole, 1)
+    return side_out, jnp.where(core == 0, whole, other), jnp.where(core == 0, other, whole)
 
 
 def solution(mesh):

time: 203 us -> 201 us (level)
  starting transfers between devices: 41.6 us -> 37.8 us
  waiting for transfers between devices: 118 us -> 121 us
  matrix products: 2.06 us -> 0 us
    pallas_call x0 -> x1, Pallas kernels: none -> 2.36 us  [side_block(): pl.pallas_call(functools.partial(side_kernel, width, all_tokens), in_spec...]
    ppermute x6, starting transfers between devices: 8.11 us -> 5.96 us  [shift(): lax.ppermute(value, 'wide', [(i, (i + k * group) % wides) for i in range(...]
    dot_general x5 -> x0, matrix products: 2.06 us -> none  [coupling(): return jax.nn.gelu(jnp.dot(values, weight, precision=HIGH))]
    unnamed x62 -> x48, local copies, waits for them, and re-layouts: 7.99 us -> 7.41 us
  transfers between devices with their start and end apart: 35 -> 35, of which waited for: 22 -> 24; matrix products, arithmetic and copies ran while one was open for 4% -> 4% of each run, Pallas kernels for 4% -> 4%
where the time goes in v5:
time: 201 us; the launch traced here: 200 us
  waiting for transfers between devices  121 us (60%)
  starting transfers between devices  37.8 us (19%)
  Pallas kernels  17.9 us (9%)
  local copies, waits for them, and re-layouts  15.1 us (8%)
  other arithmetic  7.39 us (4%)
    ppermute x10, waiting for transfers between devices, line(): return lax.ppermute(value, 'wide', pairs)  66.8 us
    ppermute x15, waiting for transfers between devices, to_member(): return lax.ppermute(value, 'wide', pairs) if s else value  38.2 us
    ppermute x15, starting transfers between devices, to_member(): return lax.ppermute(value, 'wide', pairs) if s else value  19 us
    ppermute x10, starting transfers between devices, line(): return lax.ppermute(value, 'wide', pairs)  12.6 us
    ppermute x4, waiting for transfers between devices, to_core(): lax.ppermute(value, 'narrow', [(i, i ^ t) for i in range(narrows)])  8.33 us
    pallas_call x1, Pallas kernels, attend(): pl.pallas_call(functools.partial(attend_kernel, rows, planes), grid=(2,),...  8.31 us
    unnamed x48, local copies, waits for them, and re-layouts  7.41 us
    pallas_call x1, Pallas kernels, finish(): pl.pallas_call(functools.partial(finish_kernel, rows, planes), in_specs=[...  7.24 us
  transfers between devices with their start and end apart: 35, of which 24 were waited for; matrix products, arithmetic and copies ran while one was open for 4% of the time, Pallas kernels for 4%

profile of v5, /device:TPU:0, one launch (start us, length us, event | category | flops | bytes accessed | tf_op | source)
XLA Modules:
  0.0 199.9 jit_solution(16867554494889006445)
XLA Ops:
  0.7 1.0 dynamic-slice_bitcast_fusion
  1.7 1.3 constant_dynamic-slice_fusion.7
  3.1 3.1 %collective-permute-start.3 = (bf16[240,768]{1,0:T(8,128)(2,1)S(1)}, bf16[240,768]{1,0:T(8,128)(2,1)S(1)}, u32[]{:S(2)}, u32[]{:S(2)}) collective-permute-start(bf16[240,768]{1,0:T(8,128)(2,1)S(1)} %pad_maximum_fusion.8.refs_6_.refs_3_), channel_id=1, source_target_pairs={{8,0},{10,2},{12,4},{14,6},{16,24},{18,26},{20,28},{22,30},{0,8},{... | collective-permute-start | bytes 1105928 | tf_op jit(solution)/shard_map/ppermute | solution.py:318
  6.2 0.7 collective-permute-start.5
  6.9 2.5 %collective-permute-start.2 = (bf16[240,768]{1,0:T(8,128)(2,1)S(1)}, bf16[240,768]{1,0:T(8,128)(2,1)S(1)}, u32[]{:S(2)}, u32[]{:S(2)}) collective-permute-start(bf16[240,768]{1,0:T(8,128)(2,1)S(1)} %pad_maximum_fusion.7), channel_id=1, source_target_pairs={{0,6},{2,4},{4,2},{6,0},{8,14},{10,12},{12,10},{14,8},{16,22},{18,... | collective-permute-start | bytes 1105928 | tf_op jit(solution)/shard_map/ppermute | solution.py:279
  10.6 0.9 constant_dynamic-slice_fusion.6
  11.5 3.2 %collective-permute-done.3.refs_8_.refs_5_ = bf16[240,768]{1,0:T(8,128)(2,1)S(1)} collective-permute-done((bf16[240,768]{1,0:T(8,128)(2,1)S(1)}, bf16[240,768]{1,0:T(8,128)(2,1)S(1)}, u32[]{:S(2)}, u32[]{:S(2)}) %collective-permute-start.3) | collective-permute-done | bytes 368672 | tf_op jit(solution)/shard_map/ppermute | solution.py:318
  14.8 0.7 collective-permute-start.4
  15.5 1.3 collective-permute-start.6
  17.0 2.4 %collective-permute-done.2 = bf16[240,768]{1,0:T(8,128)(2,1)S(1)} collective-permute-done((bf16[240,768]{1,0:T(8,128)(2,1)S(1)}, bf16[240,768]{1,0:T(8,128)(2,1)S(1)}, u32[]{:S(2)}, u32[]{:S(2)}) %collective-permute-start.2) | collective-permute-done | bytes 368672 | tf_op jit(solution)/shard_map/ppermute | solution.py:279
  19.4 6.4 %collective-permute-done.1 = bf16[240,768]{1,0:T(8,128)(2,1)S(1)} collective-permute-done((bf16[240,768]{1,0:T(8,128)(2,1)S(1)}, bf16[240,768]{1,0:T(8,128)(2,1)S(1)}, u32[]{:S(2)}, u32[]{:S(2)}) %collective-permute-start.1) | collective-permute-done | bytes 368672 | tf_op jit(solution)/shard_map/ppermute | solution.py:279
  26.0 2.7 %collective-permute-done.6.refs_14_.refs_11_ = bf16[240,768]{1,0:T(8,128)(2,1)S(1)} collective-permute-done((bf16[240,768]{1,0:T(8,128)(2,1)S(1)}, bf16[240,768]{1,0:T(8,128)(2,1)S(1)}, u32[]{:S(2)}, u32[]{:S(2)}) %collective-permute-start.6) | collective-permute-done | bytes 368672 | tf_op jit(solution)/shard_map/ppermute | solution.py:318
  28.7 0.7 copy-done.12
  29.5 1.5 collective-permute-start.7
  31.0 1.5 collective-permute-start.8
  32.5 0.7 collective-permute-start.9
  33.1 0.7 collective-permute-start.10
  33.9 1.3 collective-permute-start.11
  35.2 0.7 copy-done.10
  35.9 28.5 %collective-permute-done.11.refs_13_ = bf16[240,768]{1,0:T(8,128)(2,1)S(1)} collective-permute-done((bf16[240,768]{1,0:T(8,128)(2,1)S(1)}, bf16[240,768]{1,0:T(8,128)(2,1)S(1)}, u32[]{:S(2)}, u32[]{:S(2)}) %collective-permute-start.11) | collective-permute-done | bytes 368672 | tf_op jit(solution)/shard_map/ppermute | solution.py:318
  64.5 0.7 copy-done.15
  65.2 1.8 collective-permute-start.12
  67.0 1.7 collective-permute-start.13
  68.7 1.3 collective-permute-start.14
  70.0 24.7 %collective-permute-done.14.refs_15_.refs_12_ = bf16[720,768]{1,0:T(8,128)(2,1)S(1)} collective-permute-done((bf16[720,768]{1,0:T(8,128)(2,1)S(1)}, bf16[720,768]{1,0:T(8,128)(2,1)S(1)}, u32[]{:S(2)}, u32[]{:S(2)}) %collective-permute-start.14) | collective-permute-done | bytes 1105952 | tf_op jit(solution)/shard_map/ppermute | solution.py:318
  94.6 1.0 copy-done.1
  95.7 0.9 copy-done.23
  96.7 1.8 pad_maximum_fusion
  98.5 1.3 collective-permute-start.16
  99.9 0.8 dynamic_slice.79
  100.6 1.0 slice.33.refs_3_
  101.7 1.0 slice.34.refs_4_
  102.7 1.0 slice.35.refs_5_
  103.7 0.8 collective-permute-done.15
  104.5 3.6 %dynamic-slice_select_fusion = bf16[4,256,768]{2,1,0:T(8,128)(2,1)S(1)} fusion(bf16[4,256,1536]{2,1,0:T(8,128)(2,1)} %bitcast.5.refs_1_, s32[]{:T(128)S(6)} %select_n.150, bf16[4,256,1536]{2,1,0:T(8,128)(2,1)} %bitcast.4.refs_0_, pred[]{:T(512)S(6)} %eq.22), kind=kLoop, calls=%fused_computation.1 | loop fusion | flops 786432 | bytes 4718597 | tf_op jit(solution)/shard_map/jit(_where)/select_n | solution.py:353
  108.4 1.1 copy-done.2
  110.0 8.3 %shard_map.103.refs_0_ = f32[1024,768]{1,0:T(8,128)S(1)} custom-call(bf16[4,256,1536]{2,1,0:T(8,128)(2,1)} %bitcast.4.refs_0_, bf16[4,256,1536]{2,1,0:T(8,128)(2,1)} %bitcast.5.refs_1_, bf16[256,768]{1,0:T(8,128)(2,1)S(1)} %copy-done.5, bf16[256,768]{1,0:T(8,128)(2,1)S(1)} %slice.33.refs_3_, bf16[256,768]{1,0:T(8,128)(2,1)S(1)} %slice.34.refs_4_, ...), custom_call_target="tpu_custom_call" | custom-call | flops 4831838208 | bytes 16777216 | tf_op jit(solution)/shard_map/pallas_call | solution.py:79
  118.3 1.6 copy-done
  119.9 7.6 %collective-permute-done.16.refs_14_ = bf16[720,768]{1,0:T(8,128)(2,1)} collective-permute-done((bf16[720,768]{1,0:T(8,128)(2,1)}, bf16[720,768]{1,0:T(8,128)(2,1)}, u32[]{:S(2)}, u32[]{:S(2)}) %collective-permute-start.16) | collective-permute-done | bytes 1105952 | tf_op jit(solution)/shard_map/ppermute | solution.py:318
  127.5 7.2 %shard_map.104 = (f32[544,768]{1,0:T(8,128)S(1)}, f32[544,768]{1,0:T(8,128)S(1)}) custom-call(f32[1024,768]{1,0:T(8,128)} %copy-done, bf16[1024,768]{1,0:T(8,128)(2,1)S(1)} %bitcast.14, bf16[1,768]{1,0:T(2,128)(2,1)S(1)} %broadcast_in_dim.9.refs_2_, bf16[240,768]{1,0:T(8,128)(2,1)S(1)} %copy-done.4, bf16[720,768]{1,0:T(8,128)(2,1)S(1)} %pad_maximum_fusion.4.refs_7_.refs_4_, ...), custom_call_target="tpu_custom_call" | custom-call | flops 2415919104 | bytes 16777216 | tf_op jit(solution)/shard_map/pallas_call | solution.py:170
  134.9 3.5 %collective-permute-done.17 = f32[544,768]{1,0:T(8,128)S(1)} collective-permute-done((f32[544,768]{1,0:T(8,128)S(1)}, f32[544,768]{1,0:T(8,128)S(1)}, u32[]{:S(2)}, u32[]{:S(2)}) %collective-permute-start.17) | collective-permute-done | bytes 1671200 | tf_op jit(solution)/shard_map/ppermute | solution.py:282
  138.9 1.6 collective-permute-start.18
  140.5 1.9 collective-permute-start.20
  142.4 9.0 %collective-permute-done.18.refs_1_ = f32[136,768]{1,0:T(8,128)S(1)} collective-permute-done((f32[136,768]{1,0:T(8,128)S(1)}, f32[136,768]{1,0:T(8,128)S(1)}, u32[]{:S(2)}, u32[]{:S(2)}) %collective-permute-start.18) | collective-permute-done | bytes 417824 | tf_op jit(solution)/shard_map/ppermute | solution.py:279
  151.4 9.4 %collective-permute-done.19.refs_2_ = f32[136,768]{1,0:T(8,128)S(1)} collective-permute-done((f32[136,768]{1,0:T(8,128)S(1)}, f32[136,768]{1,0:T(8,128)S(1)}, u32[]{:S(2)}, u32[]{:S(2)}) %collective-permute-start.19) | collective-permute-done | bytes 417824 | tf_op jit(solution)/shard_map/ppermute | solution.py:279
  160.8 2.4 %shard_map.105 = (f32[128,768]{1,0:T(8,128)}, f32[384,384]{1,0:T(8,128)S(1)}, f32[384,384]{1,0:T(8,128)S(1)}) custom-call(f32[136,768]{1,0:T(8,128)S(1)} %get-tuple-element.52.refs_0_, f32[136,768]{1,0:T(8,128)S(1)} %collective-permute-done.18.refs_1_, f32[136,768]{1,0:T(8,128)S(1)} %collective-permute-done.19.refs_2_, ...), custom_call_target="tpu_custom_call" | custom-call | flops 452984832 | bytes 5242880 | tf_op jit(solution)/shard_map/pallas_call | solution.py:255
  163.2 2.0 %collective-permute-done.21 = f32[384,384]{1,0:T(8,128)S(1)} collective-permute-done((f32[384,384]{1,0:T(8,128)S(1)}, f32[384,384]{1,0:T(8,128)S(1)}, u32[]{:S(2)}, u32[]{:S(2)}) %collective-permute-start.21) | collective-permute-done | bytes 589856 | tf_op jit(solution)/shard_map/ppermute | solution.py:282
  165.3 1.6 collective-permute-start.24
  167.3 1.5 collective-permute-start.22
  168.8 4.1 %collective-permute-done.24 = f32[96,384]{1,0:T(8,128)S(1)} collective-permute-done((f32[96,384]{1,0:T(8,128)S(1)}, f32[96,384]{1,0:T(8,128)S(1)}, u32[]{:S(2)}, u32[]{:S(2)}) %collective-permute-start.24) | collective-permute-done | bytes 147488 | tf_op jit(solution)/shard_map/ppermute | solution.py:279
  173.0 2.3 %collective-permute-done.23 = f32[96,384]{1,0:T(8,128)S(1)} collective-permute-done((f32[96,384]{1,0:T(8,128)S(1)}, f32[96,384]{1,0:T(8,128)S(1)}, u32[]{:S(2)}, u32[]{:S(2)}) %collective-permute-start.23) | collective-permute-done | bytes 147488 | tf_op jit(solution)/shard_map/ppermute | solution.py:279
  176.4 1.0 collective-permute-start.25
  177.5 2.3 %collective-permute-done.27 = f32[24,384]{1,0:T(8,128)S(1)} collective-permute-done((f32[24,384]{1,0:T(8,128)S(1)}, f32[24,384]{1,0:T(8,128)S(1)}, u32[]{:S(2)}, u32[]{:S(2)}) %collective-permute-start.27) | collective-permute-done | bytes 36896 | tf_op jit(solution)/shard_map/ppermute | solution.py:434
  179.8 1.5 collective-permute-done.26
  181.3 0.9 collective-permute-done.25
  182.4 2.0 %collective-permute-start.29 = (f32[24,384]{1,0:T(8,128)S(1)}, f32[24,384]{1,0:T(8,128)S(1)}, u32[]{:S(2)}, u32[]{:S(2)}) collective-permute-start(f32[24,384]{1,0:T(8,128)S(1)} %get-tuple-element.48), channel_id=1, source_target_pairs={{0,16},{2,18},{4,20},{6,22},{8,24},{10,26},{12,28},{14,30},{16,0},... | collective-permute-start | bytes 110600 | tf_op jit(solution)/shard_map/ppermute | solution.py:434
  184.4 1.7 collective-permute-start.30
  186.1 1.9 collective-permute-done.28
  189.3 1.4 collective-permute-start.32
  190.7 1.4 collective-permute-start.33
  192.2 1.6 collective-permute-done.31
  194.4 2.3 %collective-permute-done.33 = f32[96,384]{1,0:T(8,128)S(1)} collective-permute-done((f32[96,384]{1,0:T(8,128)S(1)}, f32[96,384]{1,0:T(8,128)S(1)}, u32[]{:S(2)}, u32[]{:S(2)}) %collective-permute-start.33) | collective-permute-done | bytes 147488 | tf_op jit(solution)/shard_map/ppermute | solution.py:279
  196.8 2.0 collective-permute-done.34
  198.8 1.1 broadcast_select_fusion
  (94 shorter events, 7.1 us)
Async XLA Ops:
  3.0 7.6 %copy-start.20 = (bf16[256,3072]{1,0:T(8,128)(2,1)S(1)}, bf16[256,3072]{1,0:T(8,128)(2,1)}, u32[]{:S(2)}) copy-start(bf16[256,3072]{1,0:T(8,128)(2,1)} %param.10) | copy-start | bytes 4718596
  3.1 8.5 %copy-start.3 = (bf16[240,768]{1,0:T(8,128)(2,1)}, bf16[240,768]{1,0:T(8,128)(2,1)S(1)}, u32[]{:S(2)}) copy-start(bf16[240,768]{1,0:T(8,128)(2,1)S(1)} %pad_maximum_fusion.8.refs_6_.refs_3_) | copy-start | bytes 1105924
  3.1 11.7 %collective-permute-start.3 = (bf16[240,768]{1,0:T(8,128)(2,1)S(1)}, bf16[240,768]{1,0:T(8,128)(2,1)S(1)}, u32[]{:S(2)}, u32[]{:S(2)}) collective-permute-start(bf16[240,768]{1,0:T(8,128)(2,1)S(1)} %pad_maximum_fusion.8.refs_6_.refs_3_), channel_id=1, source_target_pairs={{8,0},{10,2},{12,4},{14,6},{16,24},{18,26},{20,28},{22,30},{0,8},{... | collective-permute-start | bytes 1105928 | tf_op jit(solution)/shard_map/ppermute | solution.py:318
  6.2 9.3 %collective-permute-start.5 = (bf16[240,768]{1,0:T(8,128)(2,1)S(1)}, bf16[240,768]{1,0:T(8,128)(2,1)S(1)}, u32[]{:S(2)}, u32[]{:S(2)}) collective-permute-start(bf16[240,768]{1,0:T(8,128)(2,1)S(1)} %pad_maximum_fusion.8.refs_6_.refs_3_), channel_id=1, source_target_pairs={{8,16},{10,18},{12,20},{14,22},{16,8},{18,10},{20,12},{22,14},{9,1... | collective-permute-start | bytes 1105928 | tf_op jit(solution)/shard_map/ppermute | solution.py:318
  6.9 12.5 %collective-permute-start.2 = (bf16[240,768]{1,0:T(8,128)(2,1)S(1)}, bf16[240,768]{1,0:T(8,128)(2,1)S(1)}, u32[]{:S(2)}, u32[]{:S(2)}) collective-permute-start(bf16[240,768]{1,0:T(8,128)(2,1)S(1)} %pad_maximum_fusion.7), channel_id=1, source_target_pairs={{0,6},{2,4},{4,2},{6,0},{8,14},{10,12},{12,10},{14,8},{16,22},{18,... | collective-permute-start | bytes 1105928 | tf_op jit(solution)/shard_map/ppermute | solution.py:279
  9.4 16.4 %collective-permute-start.1 = (bf16[240,768]{1,0:T(8,128)(2,1)S(1)}, bf16[240,768]{1,0:T(8,128)(2,1)S(1)}, u32[]{:S(2)}, u32[]{:S(2)}) collective-permute-start(bf16[240,768]{1,0:T(8,128)(2,1)S(1)} %pad_maximum_fusion.6), channel_id=1, source_target_pairs={{0,4},{2,6},{4,0},{6,2},{8,12},{10,14},{12,8},{14,10},{16,20},{18,... | collective-permute-start | bytes 1105928 | tf_op jit(solution)/shard_map/ppermute | solution.py:279
  10.0 6.7 %copy-start.19 = (bf16[256,1536]{1,0:T(8,128)(2,1)S(1)}, bf16[256,1536]{1,0:T(8,128)(2,1)}, u32[]{:S(2)}) copy-start(bf16[256,1536]{1,0:T(8,128)(2,1)} %param.8) | copy-start | bytes 2359300
  10.0 15.9 %collective-permute-start = (bf16[240,768]{1,0:T(8,128)(2,1)S(1)}, bf16[240,768]{1,0:T(8,128)(2,1)S(1)}, u32[]{:S(2)}, u32[]{:S(2)}) collective-permute-start(bf16[240,768]{1,0:T(8,128)(2,1)S(1)} %pad_maximum_fusion.5), channel_id=1, source_target_pairs={{0,2},{2,0},{4,6},{6,4},{8,10},{10,8},{12,14},{14,12},{16,18},{18,... | collective-permute-start | bytes 1105928 | tf_op jit(solution)/shard_map/ppermute | solution.py:279
  14.8 2.3 %copy-start.6 = (bf16[240,768]{1,0:T(8,128)(2,1)}, bf16[240,768]{1,0:T(8,128)(2,1)S(1)}, u32[]{:S(2)}) copy-start(bf16[240,768]{1,0:T(8,128)(2,1)S(1)} %collective-permute-done.3.refs_8_.refs_5_) | copy-start | bytes 1105924
  14.8 11.2 %collective-permute-start.4 = (bf16[240,768]{1,0:T(8,128)(2,1)S(1)}, bf16[240,768]{1,0:T(8,128)(2,1)S(1)}, u32[]{:S(2)}, u32[]{:S(2)}) collective-permute-start(bf16[240,768]{1,0:T(8,128)(2,1)S(1)} %collective-permute-done.3.refs_8_.refs_5_), channel_id=1, source_target_pairs={{8,16},{10,18},{12,20},{14,22},{16,8},{18,10},{20,12},{22,14},{9,1... | collective-permute-start | bytes 1105928 | tf_op jit(solution)/shard_map/ppermute | solution.py:318
  15.5 1.6 copy-start.8
  15.5 13.3 %collective-permute-start.6 = (bf16[240,768]{1,0:T(8,128)(2,1)S(1)}, bf16[240,768]{1,0:T(8,128)(2,1)S(1)}, u32[]{:S(2)}, u32[]{:S(2)}) collective-permute-start(bf16[240,768]{1,0:T(8,128)(2,1)S(1)} %collective-permute-done.5.refs_10_.refs_7_), channel_id=1, source_target_pairs={{8,0},{10,2},{12,4},{14,6},{16,24},{18,26},{20,28},{22,30},{9,1},{... | collective-permute-start | bytes 1105928 | tf_op jit(solution)/shard_map/ppermute | solution.py:318
  28.7 0.7 copy-start.12
  29.5 35.7 %collective-permute-start.7 = (bf16[256,2304]{1,0:T(8,128)(2,1)S(1)}, bf16[256,2304]{1,0:T(8,128)(2,1)S(1)}, u32[]{:S(2)}, u32[]{:S(2)}) collective-permute-start(bf16[256,2304]{1,0:T(8,128)(2,1)S(1)} %get-tuple-element.25), channel_id=1, source_target_pairs={{0,2},{2,0},{4,6},{6,4},{8,10},{10,8},{12,14},{14,12},{16,18},{18,... | collective-permute-start | bytes 3538952 | tf_op jit(solution)/shard_map/ppermute | solution.py:279
  31.0 34.3 %collective-permute-start.8 = (bf16[256,2304]{1,0:T(8,128)(2,1)S(1)}, bf16[256,2304]{1,0:T(8,128)(2,1)S(1)}, u32[]{:S(2)}, u32[]{:S(2)}) collective-permute-start(bf16[256,2304]{1,0:T(8,128)(2,1)S(1)} %get-tuple-element.26), channel_id=1, source_target_pairs={{0,4},{2,6},{4,0},{6,2},{8,12},{10,14},{12,8},{14,10},{16,20},{18,... | collective-permute-start | bytes 3538952 | tf_op jit(solution)/shard_map/ppermute | solution.py:279
  32.5 32.7 %collective-permute-start.9 = (bf16[720,768]{1,0:T(8,128)(2,1)S(1)}, bf16[720,768]{1,0:T(8,128)(2,1)S(1)}, u32[]{:S(2)}, u32[]{:S(2)}) collective-permute-start(bf16[720,768]{1,0:T(8,128)(2,1)S(1)} %pad_maximum_fusion.4.refs_7_.refs_4_), channel_id=1, source_target_pairs={{8,0},{10,2},{12,4},{14,6},{16,24},{18,26},{20,28},{22,30},{0,8},{... | collective-permute-start | bytes 3317768 | tf_op jit(solution)/shard_map/ppermute | solution.py:318
  33.1 32.1 %collective-permute-start.10 = (bf16[720,768]{1,0:T(8,128)(2,1)S(1)}, bf16[720,768]{1,0:T(8,128)(2,1)S(1)}, u32[]{:S(2)}, u32[]{:S(2)}) collective-permute-start(bf16[720,768]{1,0:T(8,128)(2,1)S(1)} %pad_maximum_fusion.4.refs_7_.refs_4_), channel_id=1, source_target_pairs={{8,16},{10,18},{12,20},{14,22},{16,8},{18,10},{20,12},{22,14},{9,1... | collective-permute-start | bytes 3317768 | tf_op jit(solution)/shard_map/ppermute | solution.py:318
  33.9 30.6 %collective-permute-start.11 = (bf16[240,768]{1,0:T(8,128)(2,1)S(1)}, bf16[240,768]{1,0:T(8,128)(2,1)S(1)}, u32[]{:S(2)}, u32[]{:S(2)}) collective-permute-start(bf16[240,768]{1,0:T(8,128)(2,1)S(1)} %collective-permute-done.4.refs_12_.refs_9_), channel_id=1, source_target_pairs={{8,0},{10,2},{12,4},{14,6},{16,24},{18,26},{20,28},{22,30},{9,1},{... | collective-permute-start | bytes 1105928 | tf_op jit(solution)/shard_map/ppermute | solution.py:318
  35.2 0.8 copy-start.10
  64.5 0.7 copy-start.15
  65.2 33.3 %copy-start.21 = (bf16[256,2304]{1,0:T(8,128)(2,1)}, bf16[256,2304]{1,0:T(8,128)(2,1)S(1)}, u32[]{:S(2)}) copy-start(bf16[256,2304]{1,0:T(8,128)(2,1)S(1)} %collective-permute-done.7) | copy-start | bytes 3538948
  65.2 30.4 %copy-start.22 = (bf16[256,2304]{1,0:T(8,128)(2,1)}, bf16[256,2304]{1,0:T(8,128)(2,1)S(1)}, u32[]{:S(2)}) copy-start(bf16[256,2304]{1,0:T(8,128)(2,1)S(1)} %collective-permute-done.8) | copy-start | bytes 3538948
  65.2 30.4 %collective-permute-start.12 = (bf16[256,2304]{1,0:T(8,128)(2,1)S(1)}, bf16[256,2304]{1,0:T(8,128)(2,1)S(1)}, u32[]{:S(2)}, u32[]{:S(2)}) collective-permute-start(bf16[256,2304]{1,0:T(8,128)(2,1)S(1)} %get-tuple-element.32), channel_id=1, source_target_pairs={{0,6},{2,4},{4,2},{6,0},{8,14},{10,12},{12,10},{14,8},{16,22},{18,... | collective-permute-start | bytes 3538952 | tf_op jit(solution)/shard_map/ppermute | solution.py:279
  67.0 3.0 %collective-permute-start.13 = (bf16[720,768]{1,0:T(8,128)(2,1)S(1)}, bf16[720,768]{1,0:T(8,128)(2,1)}, u32[]{:S(2)}, u32[]{:S(2)}) collective-permute-start(bf16[720,768]{1,0:T(8,128)(2,1)S(1)} %collective-permute-done.9.refs_9_.refs_6_), channel_id=1, source_target_pairs={{8,16},{10,18},{12,20},{14,22},{16,8},{18,10},{20,12},{22,14},{9,1... | collective-permute-start | bytes 3317768 | tf_op jit(solution)/shard_map/ppermute | solution.py:318
  68.7 26.0 %collective-permute-start.14 = (bf16[720,768]{1,0:T(8,128)(2,1)S(1)}, bf16[720,768]{1,0:T(8,128)(2,1)S(1)}, u32[]{:S(2)}, u32[]{:S(2)}) collective-permute-start(bf16[720,768]{1,0:T(8,128)(2,1)S(1)} %collective-permute-done.10.refs_11_.refs_8_), channel_id=1, source_target_pairs={{8,0},{10,2},{12,4},{14,6},{16,24},{18,26},{20,28},{22,30},{9,1},{... | collective-permute-start | bytes 3317768 | tf_op jit(solution)/shard_map/ppermute | solution.py:318
  94.6 1.0 copy-start.1
  95.6 1.0 copy-start.23
  98.5 6.0 %collective-permute-start.15 = (bf16[1024,1536]{1,0:T(8,128)(2,1)}, bf16[1024,1536]{1,0:T(8,128)(2,1)}, u32[]{:S(2)}, u32[]{:S(2)}) collective-permute-start(bf16[1024,1536]{1,0:T(8,128)(2,1)} %pad_maximum_fusion), channel_id=1, source_target_pairs={{0,1},{1,0},{2,3},{3,2},{4,5},{5,4},{6,7},{7,6},{8,9},{9,8},{10,11... | collective-permute-start | bytes 9437192 | tf_op jit(solution)/shard_map/ppermute | solution.py:282
  98.5 29.0 %collective-permute-start.16 = (bf16[720,768]{1,0:T(8,128)(2,1)}, bf16[720,768]{1,0:T(8,128)(2,1)}, u32[]{:S(2)}, u32[]{:S(2)}) collective-permute-start(bf16[720,768]{1,0:T(8,128)(2,1)} %collective-permute-done.13.refs_13_.refs_10_), channel_id=1, source_target_pairs={{8,0},{10,2},{12,4},{14,6},{16,24},{18,26},{20,28},{22,30},{9,1},{... | collective-permute-start | bytes 3317768 | tf_op jit(solution)/shard_map/ppermute | solution.py:318
  104.5 3.8 %copy-start.13 = (bf16[240,768]{1,0:T(8,128)(2,1)S(1)}, bf16[240,768]{1,0:T(8,128)(2,1)}, u32[]{:S(2)}) copy-start(bf16[240,768]{1,0:T(8,128)(2,1)} %copy-done.12) | copy-start | bytes 1105924
  108.2 1.2 copy-start.2
  108.2 1.3 copy-start.4
  108.2 1.4 copy-start.5
  108.2 1.5 copy-start.7
  108.2 1.6 copy-start.9
  108.2 1.7 copy-start.11
  110.0 17.6 %copy-start.16 = (bf16[240,768]{1,0:T(8,128)(2,1)S(1)}, bf16[240,768]{1,0:T(8,128)(2,1)}, u32[]{:S(2)}) copy-start(bf16[240,768]{1,0:T(8,128)(2,1)} %copy-done.15) | copy-start | bytes 1105924
  118.3 1.6 copy-start
  134.8 3.6 %collective-permute-start.17 = (f32[544,768]{1,0:T(8,128)S(1)}, f32[544,768]{1,0:T(8,128)S(1)}, u32[]{:S(2)}, u32[]{:S(2)}) collective-permute-start(f32[544,768]{1,0:T(8,128)S(1)} %get-tuple-element.43), channel_id=1, source_target_pairs={{0,1},{1,0},{2,3},{3,2},{4,5},{5,4},{6,7},{7,6},{8,9},{9,8},{10,11... | collective-permute-start | bytes 5013512 | tf_op jit(solution)/shard_map/ppermute | solution.py:282
  138.7 22.1 %copy-start.14 = (f32[128,768]{1,0:T(8,128)S(1)}, f32[128,768]{1,0:T(8,128)}, u32[]{:S(2)}) copy-start(f32[128,768]{1,0:T(8,128)} %refs_6_.1) | copy-start | bytes 1179652
  138.7 22.1 %copy-start.17 = (bf16[384,384]{1,0:T(8,128)(2,1)S(1)}, bf16[384,384]{1,0:T(8,128)(2,1)}, u32[]{:S(2)}) copy-start(bf16[384,384]{1,0:T(8,128)(2,1)} %refs_4_.1) | copy-start | bytes 884740
  138.7 22.1 %copy-start.18 = (bf16[384,384]{1,0:T(8,128)(2,1)S(1)}, bf16[384,384]{1,0:T(8,128)(2,1)}, u32[]{:S(2)}) copy-start(bf16[384,384]{1,0:T(8,128)(2,1)} %refs_5_.1) | copy-start | bytes 884740
  138.9 12.5 %collective-permute-start.18 = (f32[136,768]{1,0:T(8,128)S(1)}, f32[136,768]{1,0:T(8,128)S(1)}, u32[]{:S(2)}, u32[]{:S(2)}) collective-permute-start(f32[136,768]{1,0:T(8,128)S(1)} %get-tuple-element.51), channel_id=1, source_target_pairs={{0,2},{2,0},{4,6},{6,4},{8,10},{10,8},{12,14},{14,12},{16,18},{18,... | collective-permute-start | bytes 1253384 | tf_op jit(solution)/shard_map/ppermute | solution.py:279
  140.4 20.4 %collective-permute-start.19 = (f32[136,768]{1,0:T(8,128)S(1)}, f32[136,768]{1,0:T(8,128)S(1)}, u32[]{:S(2)}, u32[]{:S(2)}) collective-permute-start(f32[136,768]{1,0:T(8,128)S(1)} %get-tuple-element.50), channel_id=1, source_target_pairs={{0,4},{2,6},{4,0},{6,2},{8,12},{10,14},{12,8},{14,10},{16,20},{18,... | collective-permute-start | bytes 1253384 | tf_op jit(solution)/shard_map/ppermute | solution.py:279
  140.5 20.3 %collective-permute-start.20 = (f32[136,768]{1,0:T(8,128)S(1)}, f32[136,768]{1,0:T(8,128)S(1)}, u32[]{:S(2)}, u32[]{:S(2)}) collective-permute-start(f32[136,768]{1,0:T(8,128)S(1)} %get-tuple-element.49), channel_id=1, source_target_pairs={{0,6},{2,4},{4,2},{6,0},{8,14},{10,12},{12,10},{14,8},{16,22},{18,... | collective-permute-start | bytes 1253384 | tf_op jit(solution)/shard_map/ppermute | solution.py:279
  163.2 2.0 %collective-permute-start.21 = (f32[384,384]{1,0:T(8,128)S(1)}, f32[384,384]{1,0:T(8,128)S(1)}, u32[]{:S(2)}, u32[]{:S(2)}) collective-permute-start(f32[384,384]{1,0:T(8,128)S(1)} %get-tuple-element.46), channel_id=1, source_target_pairs={{0,1},{1,0},{2,3},{3,2},{4,5},{5,4},{6,7},{7,6},{8,9},{9,8},{10,11... | collective-permute-start | bytes 1769480 | tf_op jit(solution)/shard_map/ppermute | solution.py:282
  165.3 7.7 %collective-permute-start.24 = (f32[96,384]{1,0:T(8,128)S(1)}, f32[96,384]{1,0:T(8,128)S(1)}, u32[]{:S(2)}, u32[]{:S(2)}) collective-permute-start(f32[96,384]{1,0:T(8,128)S(1)} %get-tuple-element.67), channel_id=1, source_target_pairs={{0,6},{2,4},{4,2},{6,0},{8,14},{10,12},{12,10},{14,8},{16,22},{18,... | collective-permute-start | bytes 442376 | tf_op jit(solution)/shard_map/ppermute | solution.py:279
  166.8 8.5 %collective-permute-start.23 = (f32[96,384]{1,0:T(8,128)S(1)}, f32[96,384]{1,0:T(8,128)S(1)}, u32[]{:S(2)}, u32[]{:S(2)}) collective-permute-start(f32[96,384]{1,0:T(8,128)S(1)} %get-tuple-element.68), channel_id=1, source_target_pairs={{0,4},{2,6},{4,0},{6,2},{8,12},{10,14},{12,8},{14,10},{16,20},{18,... | collective-permute-start | bytes 442376 | tf_op jit(solution)/shard_map/ppermute | solution.py:279
  167.3 8.0 %collective-permute-start.22 = (f32[96,384]{1,0:T(8,128)S(1)}, f32[96,384]{1,0:T(8,128)S(1)}, u32[]{:S(2)}, u32[]{:S(2)}) collective-permute-start(f32[96,384]{1,0:T(8,128)S(1)} %get-tuple-element.66), channel_id=1, source_target_pairs={{0,2},{2,0},{4,6},{6,4},{8,10},{10,8},{12,14},{14,12},{16,18},{18,... | collective-permute-start | bytes 442376 | tf_op jit(solution)/shard_map/ppermute | solution.py:279
  175.4 4.4 %collective-permute-start.27 = (f32[24,384]{1,0:T(8,128)S(1)}, f32[24,384]{1,0:T(8,128)S(1)}, u32[]{:S(2)}, u32[]{:S(2)}) collective-permute-start(f32[24,384]{1,0:T(8,128)S(1)} %get-tuple-element.74), channel_id=1, source_target_pairs={{0,24},{2,26},{4,28},{6,30},{8,0},{10,2},{12,4},{14,6},{16,8},{18,... | collective-permute-start | bytes 110600 | tf_op jit(solution)/shard_map/ppermute | solution.py:434
  175.8 5.5 %collective-permute-start.26 = (f32[24,384]{1,0:T(8,128)S(1)}, f32[24,384]{1,0:T(8,128)S(1)}, u32[]{:S(2)}, u32[]{:S(2)}) collective-permute-start(f32[24,384]{1,0:T(8,128)S(1)} %get-tuple-element.75), channel_id=1, source_target_pairs={{0,16},{2,18},{4,20},{6,22},{8,24},{10,26},{12,28},{14,30},{16,0},... | collective-permute-start | bytes 110600 | tf_op jit(solution)/shard_map/ppermute | solution.py:434
  176.4 5.8 %collective-permute-start.25 = (f32[24,384]{1,0:T(8,128)S(1)}, f32[24,384]{1,0:T(8,128)S(1)}, u32[]{:S(2)}, u32[]{:S(2)}) collective-permute-start(f32[24,384]{1,0:T(8,128)S(1)} %get-tuple-element.73), channel_id=1, source_target_pairs={{0,8},{2,10},{4,12},{6,14},{8,16},{10,18},{12,20},{14,22},{16,24},... | collective-permute-start | bytes 110600 | tf_op jit(solution)/shard_map/ppermute | solution.py:434
  182.2 5.8 %collective-permute-start.28 = (f32[24,384]{1,0:T(8,128)S(1)}, f32[24,384]{1,0:T(8,128)S(1)}, u32[]{:S(2)}, u32[]{:S(2)}) collective-permute-start(f32[24,384]{1,0:T(8,128)S(1)} %get-tuple-element.48), channel_id=1, source_target_pairs={{0,8},{2,10},{4,12},{6,14},{8,16},{10,18},{12,20},{14,22},{16,24},... | collective-permute-start | bytes 110600 | tf_op jit(solution)/shard_map/ppermute | solution.py:434
  182.4 5.7 %collective-permute-start.29 = (f32[24,384]{1,0:T(8,128)S(1)}, f32[24,384]{1,0:T(8,128)S(1)}, u32[]{:S(2)}, u32[]{:S(2)}) collective-permute-start(f32[24,384]{1,0:T(8,128)S(1)} %get-tuple-element.48), channel_id=1, source_target_pairs={{0,16},{2,18},{4,20},{6,22},{8,24},{10,26},{12,28},{14,30},{16,0},... | collective-permute-start | bytes 110600 | tf_op jit(solution)/shard_map/ppermute | solution.py:434
  184.4 4.2 %collective-permute-start.30 = (f32[24,384]{1,0:T(8,128)S(1)}, f32[24,384]{1,0:T(8,128)S(1)}, u32[]{:S(2)}, u32[]{:S(2)}) collective-permute-start(f32[24,384]{1,0:T(8,128)S(1)} %get-tuple-element.48), channel_id=1, source_target_pairs={{0,24},{2,26},{4,28},{6,30},{8,0},{10,2},{12,4},{14,6},{16,8},{18,... | collective-permute-start | bytes 110600 | tf_op jit(solution)/shard_map/ppermute | solution.py:434
  188.6 5.1 %collective-permute-start.31 = (f32[96,384]{1,0:T(8,128)S(1)}, f32[96,384]{1,0:T(8,128)S(1)}, u32[]{:S(2)}, u32[]{:S(2)}) collective-permute-start(f32[96,384]{1,0:T(8,128)S(1)} %constant_dynamic-update-slice_fusion.4), channel_id=1, source_target_pairs={{0,2},{2,0},{4,6},{6,4},{8,10},{10,8},{12,14},{14,12},{16,18},{18,... | collective-permute-start | bytes 442376 | tf_op jit(solution)/shard_map/ppermute | solution.py:279
  189.3 5.1 %collective-permute-start.32 = (f32[96,384]{1,0:T(8,128)S(1)}, f32[96,384]{1,0:T(8,128)S(1)}, u32[]{:S(2)}, u32[]{:S(2)}) collective-permute-start(f32[96,384]{1,0:T(8,128)S(1)} %constant_dynamic-update-slice_fusion.4), channel_id=1, source_target_pairs={{0,4},{2,6},{4,0},{6,2},{8,12},{10,14},{12,8},{14,10},{16,20},{18,... | collective-permute-start | bytes 442376 | tf_op jit(solution)/shard_map/ppermute | solution.py:279
  190.7 6.0 %collective-permute-start.33 = (f32[96,384]{1,0:T(8,128)S(1)}, f32[96,384]{1,0:T(8,128)S(1)}, u32[]{:S(2)}, u32[]{:S(2)}) collective-permute-start(f32[96,384]{1,0:T(8,128)S(1)} %constant_dynamic-update-slice_fusion.4), channel_id=1, source_target_pairs={{0,6},{2,4},{4,2},{6,0},{8,14},{10,12},{12,10},{14,8},{16,22},{18,... | collective-permute-start | bytes 442376 | tf_op jit(solution)/shard_map/ppermute | solution.py:279
  196.7 2.1 %collective-permute-start.34 = (f32[384,384]{1,0:T(8,128)S(1)}, f32[384,384]{1,0:T(8,128)S(1)}, u32[]{:S(2)}, u32[]{:S(2)}) collective-permute-start(f32[384,384]{1,0:T(8,128)S(1)} %constant_dynamic-update-slice_fusion), channel_id=1, source_target_pairs={{0,1},{1,0},{2,3},{3,2},{4,5},{5,4},{6,7},{7,6},{8,9},{9,8},{10,11... | collective-permute-start | bytes 1769480 | tf_op jit(solution)/shard_map/ppermute | solution.py:282

commit v6 on v5

--- a/solution.py
+++ b/solution.py
@@ -37,9 +37,10 @@
 
 def attend_kernel(rows, planes, *refs):
     mine_ref, other_ref, *refs = refs
-    stay_refs, (*flow, out_ref, weight, sems) = refs[:GROUP], refs[GROUP:]
+    stay_refs, (*flow, out_ref, down_ref, weight, sems, down_sems) = refs[:GROUP], refs[GROUP:]
     plane, member, core = place()
     span = flow[0].shape[0]
+    columns = span - rows
 
     for at in range(planes):
 
@@ -49,11 +50,17 @@
             for p in range(planes):
                 if ROUTES[at][p] == LAST:
                     weight[p * GROUP * rows : (p + 1) * GROUP * rows] = jnp.zeros((GROUP * rows, weight.shape[1]), BF16)
+                    ends = (p * GROUP * columns, (p + 1) * GROUP * columns)
+                    down_ref[ends[0] : ends[1]] = jnp.zeros((GROUP * columns, weight.shape[1]), BF16)
                     continue
                 for s in range(GROUP):
                     target = pl.multiple_of((p * GROUP + (member ^ s)) * rows, 64)
                     source = share_of(part_of(flow, at, p), s, 0, rows, span)
                     copies.append(pltpu.make_async_copy(source, weight.at[pl.ds(target, rows)], sems.at[p, s]))
+                    target = pl.multiple_of((p * GROUP + (member ^ s)) * columns, 16)
+                    source = share_of(part_of(flow, at, p), s, rows, columns, span)
+                    target = down_ref.at[pl.ds(target, columns)]
+                    copies.append(pltpu.make_async_copy(source, target, down_sems.at[p, s]))
             for copy in copies:
                 copy.start()
             for copy in copies:
@@ -76,16 +83,27 @@
     group, tokens, heads = mine.shape
     count = flow[0].shape[1]
     part = pl.BlockSpec((group, tokens // 2, heads), lambda i: (0, i, 0))
+    out = (flow[0].shape[0] - rows) * group * planes
     return pl.pallas_call(
         functools.partial(attend_kernel, rows, planes),
         grid=(2,),
         in_specs=[part, part]
         + [pl.BlockSpec((tokens // 2, count), lambda i: (i, 0))] * group
         + [pl.BlockSpec(memory_space=pl.ANY)] * len(flow),
-        out_specs=pl.BlockSpec((group * tokens // 2, count), lambda i: (i, 0)),
-        out_shape=jax.ShapeDtypeStruct((group * tokens, count), F32),
-        scratch_shapes=[pltpu.VMEM((2 * heads, count), BF16), pltpu.SemaphoreType.DMA((planes, group))],
-        compiler_params=pltpu.CompilerParams(vmem_limit_bytes=40 << 20),
+        out_specs=[
+            pl.BlockSpec((group * tokens // 2, count), lambda i: (i, 0)),
+            pl.BlockSpec((out, count), lambda i: (0, 0)),
+        ],
+        out_shape=[
+            jax.ShapeDtypeStruct((group * tokens, count), F32),
+            jax.ShapeDtypeStruct((out, count), BF16),
+        ],
+        scratch_shapes=[
+            pltpu.VMEM((2 * heads, count), BF16),
+            pltpu.SemaphoreType.DMA((planes, group)),
+            pltpu.SemaphoreType.DMA((planes, group)),
+        ],
+        compiler_params=pltpu.CompilerParams(vmem_limit_bytes=28 << 20),
         cost_estimate=pl.CostEstimate(
             flops=4 * group * tokens * heads * count, bytes_accessed=16 << 20, transcendentals=0
         ),
@@ -93,7 +111,7 @@
 
 
 def finish_kernel(rows, planes, *refs):
-    total_ref, far_ref, gain_ref, *flow, keep_ref, send_ref, weight, down, sems, down_sems = refs
+    total_ref, far_ref, gain_ref, near_ref, *flow, keep_ref, send_ref, weight, down, sems, down_sems, near_sem = refs
     plane, member, core = place()
     span = flow[0].shape[0]
     columns = span - rows
@@ -102,27 +120,30 @@
         out = []
         for s in range(GROUP):
             target = pl.multiple_of((member ^ s) * rows, 64)
-            source = share_of(flow[2 * LAST :], s, 0, rows, span)
+            source = share_of(flow, s, 0, rows, span)
             out.append(pltpu.make_async_copy(source, weight.at[pl.ds(target, rows)], sems.at[s]))
         return out
 
-    def down_copies(at):
+    def down_copies(p):
         out = []
-        for p in range(planes):
-            for s in range(GROUP):
-                target = pl.multiple_of((p * GROUP + (member ^ s)) * columns, 16)
-                source = share_of(part_of(flow, at, p), s, rows, columns, span)
-                out.append(pltpu.make_async_copy(source, down.at[pl.ds(target, columns)], down_sems.at[p, s]))
+        for s in range(GROUP):
+            target = pl.multiple_of((p * GROUP + (member ^ s)) * columns, 16)
+            source = share_of(flow, s, rows, columns, span)
+            out.append(pltpu.make_async_copy(source, down.at[pl.ds(target, columns)], down_sems.at[s]))
         return out
 
+    near = pltpu.make_async_copy(near_ref, down, near_sem)
+    near.start()
     far = far_copies()
     for copy in far:
         copy.start()
-    for at in range(planes):
+    near.wait()
+    ends = [(at, ROUTES[at].index(LAST)) for at in range(planes) if LAST in ROUTES[at]]
+    for at, p in ends:
 
         @pl.when(plane == at)
         def _():
-            for copy in down_copies(at):
+            for copy in down_copies(p):
                 copy.start()
 
     for copy in far:
@@ -143,11 +164,11 @@
             lane = lax.broadcasted_iota(jnp.int32, (2 * local, 128), 1)
             both = jnp.where(lane == 0, row_sum, jnp.where(lane == 1, squares, 0.0)).T
             if gains is None:
-                for at in range(planes):
+                for at, p in ends:
 
                     @pl.when(plane == at)
                     def _():
-                        for copy in down_copies(at):
+                        for copy in down_copies(p):
                             copy.wait()
 
                 gains = jnp.broadcast_to(gain_ref[...], (16, gain_ref.shape[1]))
@@ -161,7 +182,7 @@
                 out_ref[at + local + 1 : at + local + 3, :local] = both[:2, g * local : (g + 1) * local]
 
 
-def finish(rows, planes, total, far, gain, flow):
+def finish(rows, planes, total, far, gain, near, flow):
     count = total.shape[1]
     tokens = total.shape[0]
     span = flow[0].shape[0]
@@ -169,20 +190,21 @@
     inside = pl.BlockSpec(memory_space=pltpu.VMEM)
     return pl.pallas_call(
         functools.partial(finish_kernel, rows, planes),
-        in_specs=[inside] * 3 + [pl.BlockSpec(memory_space=pl.ANY)] * len(flow),
+        in_specs=[inside] * 4 + [pl.BlockSpec(memory_space=pl.ANY)] * len(flow),
         out_specs=[inside, inside],
         out_shape=[jax.ShapeDtypeStruct((tokens // 2 + 8 * GROUP, out), F32)] * 2,
         scratch_shapes=[
             pltpu.VMEM((GROUP * rows, count), BF16),
             pltpu.VMEM((out, count), BF16),
             pltpu.SemaphoreType.DMA((GROUP,)),
-            pltpu.SemaphoreType.DMA((planes, GROUP)),
+            pltpu.SemaphoreType.DMA((GROUP,)),
+            pltpu.SemaphoreType.DMA,
         ],
-        compiler_params=pltpu.CompilerParams(vmem_limit_bytes=40 << 20),
+        compiler_params=pltpu.CompilerParams(vmem_limit_bytes=20 << 20),
         cost_estimate=pl.CostEstimate(
             flops=2 * tokens * count * (GROUP * rows + out), bytes_accessed=16 << 20, transcendentals=0
         ),
-    )(total, far, gain, *flow)
+    )(total, far, gain, near, *flow)
 
 
 def split(value):
@@ -337,24 +359,26 @@
         arrived, boxes, rest_one, own_last = lax.optimization_barrier((arrived, boxes, rest_one, own_last))
         rest_two = step_two(*rest_one)
         arrived.append(to_member(boxes[2], 3))
-
-        arrived, rest_two = lax.optimization_barrier((arrived, rest_two))
+        heads = context.shape[1]
+        part = jnp.concatenate([context] + [v[:, :heads] for v in arrived[:2]] + [jnp.zeros_like(context)], axis=0)
+        stay = stay_own[:1] + [v[:, heads:] for v in arrived[:2]]
+
+        box, part, stay, rest_two = lax.optimization_barrier((arrived[2], part, stay, rest_two))
         rest_last = line(rest_two[0], outward)
-        heads = context.shape[1]
-        part = jnp.concatenate([context] + [v[:, :heads] for v in arrived], axis=0)
-        stay = stay_own[:1] + [v[:, heads:] for v in arrived]
+        part = lax.dynamic_update_slice_in_dim(part, box[:, :heads], 3 * tokens, 0)
+        stay.append(box[:, heads:])
         mine, other = [v.reshape(group, tokens, -1) for v in (part, to_core(part, 1))]
         flow = [own[0], rest]
         for pair in zip(own_one + own_two, rest_one + rest_two):
             flow += pair
-        total = attend(rows, planes, mine, other, stay, flow)
+        total, near_down = attend(rows, planes, mine, other, stay, flow)
         last = jnp.where(plane == 0, planes - 1, 0)
         width = group * rows
         last_part = jnp.where(last * width // heads == core, mine, other)
         last_part = lax.dynamic_slice_in_dim(last_part, last * width % heads, width, 2)
         last_part = last_part.reshape(group, narrows, local, width).swapaxes(0, 1).reshape(-1, width)
-        flow += [own_last, rest_last]
-        keep, send = finish(rows, planes, total, last_part, gain, flow)
+        flow = [own_last, rest_last]
+        keep, send = finish(rows, planes, total, last_part, gain, near_down, flow)
         summed = keep + to_core(send, 1)
         span = local + 8
         pieces = [summed[:span]]

time: 201 us -> 195 us (0.970)
  local copies, waits for them, and re-layouts: 15.1 us -> 10.9 us
    ppermute x10, waiting for transfers between devices: 66.8 us -> 63.5 us  [line(): return lax.ppermute(value, 'wide', pairs)]
    unnamed x48 -> x56, local copies, waits for them, and re-layouts: 7.41 us -> 4.51 us
    pallas_call x1, Pallas kernels: 7.24 us -> 4.97 us  [finish(): pl.pallas_call(functools.partial(finish_kernel, rows, planes), in_specs=[...]
    concatenate x1, other arithmetic: 1.81 us -> 3.94 us  [per_device(): jnp.concatenate([context] + [v[:, :heads] for v in arrived[:2]] + [jnp.ze...]
  transfers between devices with their start and end apart: 35 -> 35, of which waited for: 24 -> 24; matrix products, arithmetic and copies ran while one was open for 4% -> 6% of each run, Pallas kernels for 4% -> 5%
where the time goes in v6:
time: 195 us
  waiting for transfers between devices  119 us (61%)
  starting transfers between devices  37.8 us (19%)
  Pallas kernels  16.9 us (9%)
  local copies, waits for them, and re-layouts  10.9 us (6%)
  other arithmetic  9.07 us (5%)
    ppermute x10, waiting for transfers between devices, line(): return lax.ppermute(value, 'wide', pairs)  63.5 us
    ppermute x15, waiting for transfers between devices, to_member(): return lax.ppermute(value, 'wide', pairs) if s else value  38.2 us
    ppermute x15, starting transfers between devices, to_member(): return lax.ppermute(value, 'wide', pairs) if s else value  19 us
    ppermute x10, starting transfers between devices, line(): return lax.ppermute(value, 'wide', pairs)  12.7 us
    ppermute x4, waiting for transfers between devices, to_core(): lax.ppermute(value, 'narrow', [(i, i ^ t) for i in range(narrows)])  9.76 us
    pallas_call x1, Pallas kernels, attend(): pl.pallas_call(functools.partial(attend_kernel, rows, planes), grid=(2,),...  9.54 us
    ppermute x6, waiting for transfers between devices, shift(): lax.ppermute(value, 'wide', [(i, (i + k * group) % wides) for i in range(...  7.19 us
    ppermute x6, starting transfers between devices, shift(): lax.ppermute(value, 'wide', [(i, (i + k * group) % wides) for i in range(...  5.96 us
  transfers between devices with their start and end apart: 35, of which 24 were waited for; matrix products, arithmetic and copies ran while one was open for 6% of the time, Pallas kernels for 5%

profile of v6, /device:TPU:0, one launch (start us, length us, event | category | flops | bytes accessed | tf_op | source)
XLA Modules:
  0.0 194.7 jit_solution(2468259924244206555)
XLA Ops:
  0.7 1.0 dynamic-slice_bitcast_fusion
  1.7 1.3 constant_dynamic-slice_fusion.7
  3.1 3.1 %collective-permute-start.3 = (bf16[240,768]{1,0:T(8,128)(2,1)S(1)}, bf16[240,768]{1,0:T(8,128)(2,1)S(1)}, u32[]{:S(2)}, u32[]{:S(2)}) collective-permute-start(bf16[240,768]{1,0:T(8,128)(2,1)S(1)} %pad_maximum_fusion.7.refs_6_), channel_id=1, source_target_pairs={{8,0},{10,2},{12,4},{14,6},{16,24},{18,26},{20,28},{22,30},{0,8},{... | collective-permute-start | bytes 1105928 | tf_op jit(solution)/shard_map/ppermute | solution.py:340
  6.2 0.7 collective-permute-start.5
  6.9 2.5 %collective-permute-start.2 = (bf16[240,768]{1,0:T(8,128)(2,1)S(1)}, bf16[240,768]{1,0:T(8,128)(2,1)S(1)}, u32[]{:S(2)}, u32[]{:S(2)}) collective-permute-start(bf16[240,768]{1,0:T(8,128)(2,1)S(1)} %pad_maximum_fusion.6), channel_id=1, source_target_pairs={{0,6},{2,4},{4,2},{6,0},{8,14},{10,12},{12,10},{14,8},{16,22},{18,... | collective-permute-start | bytes 1105928 | tf_op jit(solution)/shard_map/ppermute | solution.py:301
  10.0 0.6 collective-permute-start
  10.6 0.9 constant_dynamic-slice_fusion.6
  11.5 3.2 %collective-permute-done.3.refs_8_ = bf16[240,768]{1,0:T(8,128)(2,1)S(1)} collective-permute-done((bf16[240,768]{1,0:T(8,128)(2,1)S(1)}, bf16[240,768]{1,0:T(8,128)(2,1)S(1)}, u32[]{:S(2)}, u32[]{:S(2)}) %collective-permute-start.3) | collective-permute-done | bytes 368672 | tf_op jit(solution)/shard_map/ppermute | solution.py:340
  14.8 0.7 collective-permute-start.4
  15.5 1.3 collective-permute-start.6
  17.0 2.4 %collective-permute-done.2 = bf16[240,768]{1,0:T(8,128)(2,1)S(1)} collective-permute-done((bf16[240,768]{1,0:T(8,128)(2,1)S(1)}, bf16[240,768]{1,0:T(8,128)(2,1)S(1)}, u32[]{:S(2)}, u32[]{:S(2)}) %collective-permute-start.2) | collective-permute-done | bytes 368672 | tf_op jit(solution)/shard_map/ppermute | solution.py:301
  19.4 6.4 %collective-permute-done.1 = bf16[240,768]{1,0:T(8,128)(2,1)S(1)} collective-permute-done((bf16[240,768]{1,0:T(8,128)(2,1)S(1)}, bf16[240,768]{1,0:T(8,128)(2,1)S(1)}, u32[]{:S(2)}, u32[]{:S(2)}) %collective-permute-start.1) | collective-permute-done | bytes 368672 | tf_op jit(solution)/shard_map/ppermute | solution.py:301
  26.0 2.7 %collective-permute-done.6.refs_14_ = bf16[240,768]{1,0:T(8,128)(2,1)S(1)} collective-permute-done((bf16[240,768]{1,0:T(8,128)(2,1)S(1)}, bf16[240,768]{1,0:T(8,128)(2,1)S(1)}, u32[]{:S(2)}, u32[]{:S(2)}) %collective-permute-start.6) | collective-permute-done | bytes 368672 | tf_op jit(solution)/shard_map/ppermute | solution.py:340
  28.7 0.7 copy-done.21
  29.5 1.5 collective-permute-start.7
  30.9 1.5 collective-permute-start.8
  32.5 0.7 collective-permute-start.9
  33.2 0.7 collective-permute-start.10
  33.9 1.3 collective-permute-start.11
  35.2 29.3 %collective-permute-done.11.refs_4_ = bf16[240,768]{1,0:T(8,128)(2,1)S(1)} collective-permute-done((bf16[240,768]{1,0:T(8,128)(2,1)S(1)}, bf16[240,768]{1,0:T(8,128)(2,1)S(1)}, u32[]{:S(2)}, u32[]{:S(2)}) %collective-permute-start.11) | collective-permute-done | bytes 368672 | tf_op jit(solution)/shard_map/ppermute | solution.py:340
  64.5 0.8 copy-done.23
  65.3 1.8 collective-permute-start.12
  67.1 1.6 collective-permute-start.13
  68.7 1.3 collective-permute-start.14
  70.2 0.8 slice.33.refs_4_
  71.0 3.9 %maximum_maximum_fusion = bf16[1024,1536]{1,0:T(8,128)(2,1)S(1)} fusion(bf16[256,1536]{1,0:T(8,128)(2,1)S(1)} %slice.31, bf16[256,1536]{1,0:T(8,128)(2,1)S(1)} %slice.30, bf16[256,1536]{1,0:T(8,128)(2,1)S(1)} %copy-done.25, bf16[1024]{0:T(1024)(128)(2,1)S(1)} %pad.3.clone), kind=kLoop, calls=%fused_computation | loop fusion | flops 12582912 | bytes 5507072 | tf_op jit(solution)/shard_map/concatenate | solution.py:363
  75.0 19.8 %collective-permute-done.14.refs_15_ = bf16[720,768]{1,0:T(8,128)(2,1)S(1)} collective-permute-done((bf16[720,768]{1,0:T(8,128)(2,1)S(1)}, bf16[720,768]{1,0:T(8,128)(2,1)S(1)}, u32[]{:S(2)}, u32[]{:S(2)}) %collective-permute-start.14) | collective-permute-done | bytes 1105952 | tf_op jit(solution)/shard_map/ppermute | solution.py:340
  94.8 0.9 copy-done.13
  96.2 1.3 collective-permute-start.16
  97.5 0.8 dynamic_slice.79
  98.3 1.0 slice.35.refs_5_
  99.3 2.2 %collective-permute-done.15 = bf16[1024,1536]{1,0:T(8,128)(2,1)} collective-permute-done((bf16[1024,1536]{1,0:T(8,128)(2,1)S(1)}, bf16[1024,1536]{1,0:T(8,128)(2,1)}, u32[]{:S(2)}, u32[]{:S(2)}) %collective-permute-start.15) | collective-permute-done | bytes 3145760 | tf_op jit(solution)/shard_map/ppermute | solution.py:304
  101.6 3.3 %dynamic-slice_select_fusion = bf16[4,256,768]{2,1,0:T(8,128)(2,1)S(1)} fusion(bf16[4,256,1536]{2,1,0:T(8,128)(2,1)} %bitcast.5.refs_1_, s32[]{:T(128)S(6)} %select_n.150, bf16[4,256,1536]{2,1,0:T(8,128)(2,1)S(1)} %bitcast.14, pred[]{:T(512)S(6)} %eq.22), kind=kLoop, calls=%fused_computation.1 | loop fusion | flops 786432 | bytes 4718597 | tf_op jit(solution)/shard_map/jit(_where)/select_n | solution.py:377
  105.1 1.0 copy-done.1
  106.7 9.5 %shard_map.103 = (f32[1024,768]{1,0:T(8,128)S(1)}, bf16[768,768]{1,0:T(8,128)(2,1)S(1)}) custom-call(bf16[4,256,1536]{2,1,0:T(8,128)(2,1)S(1)} %bitcast.15, bf16[4,256,1536]{2,1,0:T(8,128)(2,1)} %bitcast.5.refs_1_, bf16[256,768]{1,0:T(8,128)(2,1)S(1)} %copy-done.4, bf16[256,768]{1,0:T(8,128)(2,1)S(1)} %slice.32.refs_3_, bf16[256,768]{1,0:T(8,128)(2,1)S(1)} %copy-done.2, ...), custom_call_target="tpu_custom_call" | custom-call | flops 4831838208 | bytes 16777216 | tf_op jit(solution)/shard_map/pallas_call | solution.py:87
  116.2 8.5 %collective-permute-done.16.refs_5_ = bf16[720,768]{1,0:T(8,128)(2,1)} collective-permute-done((bf16[720,768]{1,0:T(8,128)(2,1)}, bf16[720,768]{1,0:T(8,128)(2,1)}, u32[]{:S(2)}, u32[]{:S(2)}) %collective-permute-start.16) | collective-permute-done | bytes 1105952 | tf_op jit(solution)/shard_map/ppermute | solution.py:340
  124.8 5.0 %shard_map.104 = (f32[544,768]{1,0:T(8,128)S(1)}, f32[544,768]{1,0:T(8,128)S(1)}) custom-call(f32[1024,768]{1,0:T(8,128)S(1)} %get-tuple-element.47.refs_0_, bf16[1024,768]{1,0:T(8,128)(2,1)S(1)} %bitcast.16, bf16[1,768]{1,0:T(2,128)(2,1)S(1)} %broadcast_in_dim.13.refs_2_, bf16[768,768]{1,0:T(8,128)(2,1)S(1)} %get-tuple-element.48.refs_3_, ...), custom_call_target="tpu_custom_call" | custom-call | flops 2415919104 | bytes 16777216 | tf_op jit(solution)/shard_map/pallas_call | solution.py:191
  129.8 3.5 %collective-permute-done.17 = f32[544,768]{1,0:T(8,128)S(1)} collective-permute-done((f32[544,768]{1,0:T(8,128)S(1)}, f32[544,768]{1,0:T(8,128)S(1)}, u32[]{:S(2)}, u32[]{:S(2)}) %collective-permute-start.17) | collective-permute-done | bytes 1671200 | tf_op jit(solution)/shard_map/ppermute | solution.py:304
  133.7 1.6 collective-permute-start.18
  135.4 1.9 collective-permute-start.20
  137.3 9.0 %collective-permute-done.18.refs_1_ = f32[136,768]{1,0:T(8,128)S(1)} collective-permute-done((f32[136,768]{1,0:T(8,128)S(1)}, f32[136,768]{1,0:T(8,128)S(1)}, u32[]{:S(2)}, u32[]{:S(2)}) %collective-permute-start.18) | collective-permute-done | bytes 417824 | tf_op jit(solution)/shard_map/ppermute | solution.py:301
  146.3 9.4 %collective-permute-done.19.refs_2_ = f32[136,768]{1,0:T(8,128)S(1)} collective-permute-done((f32[136,768]{1,0:T(8,128)S(1)}, f32[136,768]{1,0:T(8,128)S(1)}, u32[]{:S(2)}, u32[]{:S(2)}) %collective-permute-start.19) | collective-permute-done | bytes 417824 | tf_op jit(solution)/shard_map/ppermute | solution.py:301
  155.7 2.4 %shard_map.105 = (f32[128,768]{1,0:T(8,128)}, f32[384,384]{1,0:T(8,128)S(1)}, f32[384,384]{1,0:T(8,128)S(1)}) custom-call(f32[136,768]{1,0:T(8,128)S(1)} %get-tuple-element.60.refs_0_, f32[136,768]{1,0:T(8,128)S(1)} %collective-permute-done.18.refs_1_, f32[136,768]{1,0:T(8,128)S(1)} %collective-permute-done.19.refs_2_, ...), custom_call_target="tpu_custom_call" | custom-call | flops 452984832 | bytes 5242880 | tf_op jit(solution)/shard_map/pallas_call | solution.py:277
  158.0 2.0 %collective-permute-done.21 = f32[384,384]{1,0:T(8,128)S(1)} collective-permute-done((f32[384,384]{1,0:T(8,128)S(1)}, f32[384,384]{1,0:T(8,128)S(1)}, u32[]{:S(2)}, u32[]{:S(2)}) %collective-permute-start.21) | collective-permute-done | bytes 589856 | tf_op jit(solution)/shard_map/ppermute | solution.py:304
  160.1 1.6 collective-permute-start.24
  162.2 1.5 collective-permute-start.22
  163.7 4.1 %collective-permute-done.24 = f32[96,384]{1,0:T(8,128)S(1)} collective-permute-done((f32[96,384]{1,0:T(8,128)S(1)}, f32[96,384]{1,0:T(8,128)S(1)}, u32[]{:S(2)}, u32[]{:S(2)}) %collective-permute-start.24) | collective-permute-done | bytes 147488 | tf_op jit(solution)/shard_map/ppermute | solution.py:301
  167.8 2.3 %collective-permute-done.23 = f32[96,384]{1,0:T(8,128)S(1)} collective-permute-done((f32[96,384]{1,0:T(8,128)S(1)}, f32[96,384]{1,0:T(8,128)S(1)}, u32[]{:S(2)}, u32[]{:S(2)}) %collective-permute-start.23) | collective-permute-done | bytes 147488 | tf_op jit(solution)/shard_map/ppermute | solution.py:301
  170.5 0.7 collective-permute-start.26
  171.3 1.0 collective-permute-start.25
  172.3 2.3 %collective-permute-done.27 = f32[24,384]{1,0:T(8,128)S(1)} collective-permute-done((f32[24,384]{1,0:T(8,128)S(1)}, f32[24,384]{1,0:T(8,128)S(1)}, u32[]{:S(2)}, u32[]{:S(2)}) %collective-permute-start.27) | collective-permute-done | bytes 36896 | tf_op jit(solution)/shard_map/ppermute | solution.py:458
  174.6 1.5 collective-permute-done.26
  176.1 0.9 collective-permute-done.25
  177.2 2.0 %collective-permute-start.29 = (f32[24,384]{1,0:T(8,128)S(1)}, f32[24,384]{1,0:T(8,128)S(1)}, u32[]{:S(2)}, u32[]{:S(2)}) collective-permute-start(f32[24,384]{1,0:T(8,128)S(1)} %get-tuple-element.56), channel_id=1, source_target_pairs={{0,16},{2,18},{4,20},{6,22},{8,24},{10,26},{12,28},{14,30},{16,0},... | collective-permute-start | bytes 110600 | tf_op jit(solution)/shard_map/ppermute | solution.py:458
  179.3 1.7 collective-permute-start.30
  180.9 1.9 collective-permute-done.28
  183.4 0.6 collective-permute-start.31
  184.1 1.4 collective-permute-start.32
  185.5 1.4 collective-permute-start.33
  187.0 1.6 collective-permute-done.31
  188.6 0.6 collective-permute-done.32
  189.2 2.3 %collective-permute-done.33 = f32[96,384]{1,0:T(8,128)S(1)} collective-permute-done((f32[96,384]{1,0:T(8,128)S(1)}, f32[96,384]{1,0:T(8,128)S(1)}, u32[]{:S(2)}, u32[]{:S(2)}) %collective-permute-start.33) | collective-permute-done | bytes 147488 | tf_op jit(solution)/shard_map/ppermute | solution.py:301
  191.6 2.0 %collective-permute-done.34 = f32[384,384]{1,0:T(8,128)S(1)} collective-permute-done((f32[384,384]{1,0:T(8,128)S(1)}, f32[384,384]{1,0:T(8,128)S(1)}, u32[]{:S(2)}, u32[]{:S(2)}) %collective-permute-start.34) | collective-permute-done | bytes 589856 | tf_op jit(solution)/shard_map/ppermute | solution.py:304
  193.6 1.1 broadcast_select_fusion
  (104 shorter events, 4.9 us)
Async XLA Ops:
  3.0 7.6 %copy-start.26 = (bf16[256,3072]{1,0:T(8,128)(2,1)S(1)}, bf16[256,3072]{1,0:T(8,128)(2,1)}, u32[]{:S(2)}) copy-start(bf16[256,3072]{1,0:T(8,128)(2,1)} %param.10) | copy-start | bytes 4718596
  3.1 8.5 %copy-start.5 = (bf16[240,768]{1,0:T(8,128)(2,1)}, bf16[240,768]{1,0:T(8,128)(2,1)S(1)}, u32[]{:S(2)}) copy-start(bf16[240,768]{1,0:T(8,128)(2,1)S(1)} %pad_maximum_fusion.7.refs_6_) | copy-start | bytes 1105924
  3.1 11.7 %collective-permute-start.3 = (bf16[240,768]{1,0:T(8,128)(2,1)S(1)}, bf16[240,768]{1,0:T(8,128)(2,1)S(1)}, u32[]{:S(2)}, u32[]{:S(2)}) collective-permute-start(bf16[240,768]{1,0:T(8,128)(2,1)S(1)} %pad_maximum_fusion.7.refs_6_), channel_id=1, source_target_pairs={{8,0},{10,2},{12,4},{14,6},{16,24},{18,26},{20,28},{22,30},{0,8},{... | collective-permute-start | bytes 1105928 | tf_op jit(solution)/shard_map/ppermute | solution.py:340
  6.2 9.3 %collective-permute-start.5 = (bf16[240,768]{1,0:T(8,128)(2,1)S(1)}, bf16[240,768]{1,0:T(8,128)(2,1)S(1)}, u32[]{:S(2)}, u32[]{:S(2)}) collective-permute-start(bf16[240,768]{1,0:T(8,128)(2,1)S(1)} %pad_maximum_fusion.7.refs_6_), channel_id=1, source_target_pairs={{8,16},{10,18},{12,20},{14,22},{16,8},{18,10},{20,12},{22,14},{9,1... | collective-permute-start | bytes 1105928 | tf_op jit(solution)/shard_map/ppermute | solution.py:340
  6.9 12.5 %collective-permute-start.2 = (bf16[240,768]{1,0:T(8,128)(2,1)S(1)}, bf16[240,768]{1,0:T(8,128)(2,1)S(1)}, u32[]{:S(2)}, u32[]{:S(2)}) collective-permute-start(bf16[240,768]{1,0:T(8,128)(2,1)S(1)} %pad_maximum_fusion.6), channel_id=1, source_target_pairs={{0,6},{2,4},{4,2},{6,0},{8,14},{10,12},{12,10},{14,8},{16,22},{18,... | collective-permute-start | bytes 1105928 | tf_op jit(solution)/shard_map/ppermute | solution.py:301
  9.4 16.4 %collective-permute-start.1 = (bf16[240,768]{1,0:T(8,128)(2,1)S(1)}, bf16[240,768]{1,0:T(8,128)(2,1)S(1)}, u32[]{:S(2)}, u32[]{:S(2)}) collective-permute-start(bf16[240,768]{1,0:T(8,128)(2,1)S(1)} %pad_maximum_fusion.5), channel_id=1, source_target_pairs={{0,4},{2,6},{4,0},{6,2},{8,12},{10,14},{12,8},{14,10},{16,20},{18,... | collective-permute-start | bytes 1105928 | tf_op jit(solution)/shard_map/ppermute | solution.py:301
  10.0 6.7 %copy-start.25 = (bf16[256,1536]{1,0:T(8,128)(2,1)S(1)}, bf16[256,1536]{1,0:T(8,128)(2,1)}, u32[]{:S(2)}) copy-start(bf16[256,1536]{1,0:T(8,128)(2,1)} %param.8) | copy-start | bytes 2359300
  10.0 15.9 %collective-permute-start = (bf16[240,768]{1,0:T(8,128)(2,1)S(1)}, bf16[240,768]{1,0:T(8,128)(2,1)S(1)}, u32[]{:S(2)}, u32[]{:S(2)}) collective-permute-start(bf16[240,768]{1,0:T(8,128)(2,1)S(1)} %pad_maximum_fusion.4), channel_id=1, source_target_pairs={{0,2},{2,0},{4,6},{6,4},{8,10},{10,8},{12,14},{14,12},{16,18},{18,... | collective-permute-start | bytes 1105928 | tf_op jit(solution)/shard_map/ppermute | solution.py:301
  14.8 2.3 %copy-start.15 = (bf16[240,768]{1,0:T(8,128)(2,1)}, bf16[240,768]{1,0:T(8,128)(2,1)S(1)}, u32[]{:S(2)}) copy-start(bf16[240,768]{1,0:T(8,128)(2,1)S(1)} %collective-permute-done.3.refs_8_) | copy-start | bytes 1105924
  14.8 11.2 %collective-permute-start.4 = (bf16[240,768]{1,0:T(8,128)(2,1)S(1)}, bf16[240,768]{1,0:T(8,128)(2,1)S(1)}, u32[]{:S(2)}, u32[]{:S(2)}) collective-permute-start(bf16[240,768]{1,0:T(8,128)(2,1)S(1)} %collective-permute-done.3.refs_8_), channel_id=1, source_target_pairs={{8,16},{10,18},{12,20},{14,22},{16,8},{18,10},{20,12},{22,14},{9,1... | collective-permute-start | bytes 1105928 | tf_op jit(solution)/shard_map/ppermute | solution.py:340
  15.5 1.6 copy-start.17
  15.5 13.3 %collective-permute-start.6 = (bf16[240,768]{1,0:T(8,128)(2,1)S(1)}, bf16[240,768]{1,0:T(8,128)(2,1)S(1)}, u32[]{:S(2)}, u32[]{:S(2)}) collective-permute-start(bf16[240,768]{1,0:T(8,128)(2,1)S(1)} %collective-permute-done.5.refs_10_), channel_id=1, source_target_pairs={{8,0},{10,2},{12,4},{14,6},{16,24},{18,26},{20,28},{22,30},{9,1},{... | collective-permute-start | bytes 1105928 | tf_op jit(solution)/shard_map/ppermute | solution.py:340
  26.0 44.2 %copy-start = (bf16[720,768]{1,0:T(8,128)(2,1)}, bf16[720,768]{1,0:T(8,128)(2,1)S(1)}, u32[]{:S(2)}) copy-start(bf16[720,768]{1,0:T(8,128)(2,1)S(1)} %pad_maximum_fusion.3.refs_7_) | copy-start | bytes 3317764
  26.0 44.2 %copy-start.19 = (bf16[240,768]{1,0:T(8,128)(2,1)}, bf16[240,768]{1,0:T(8,128)(2,1)S(1)}, u32[]{:S(2)}) copy-start(bf16[240,768]{1,0:T(8,128)(2,1)S(1)} %collective-permute-done.4.refs_12_) | copy-start | bytes 1105924
  28.7 0.7 copy-start.21
  29.5 35.9 %collective-permute-start.7 = (bf16[256,2304]{1,0:T(8,128)(2,1)S(1)}, bf16[256,2304]{1,0:T(8,128)(2,1)S(1)}, u32[]{:S(2)}, u32[]{:S(2)}) collective-permute-start(bf16[256,2304]{1,0:T(8,128)(2,1)S(1)} %get-tuple-element.29), channel_id=1, source_target_pairs={{0,2},{2,0},{4,6},{6,4},{8,10},{10,8},{12,14},{14,12},{16,18},{18,... | collective-permute-start | bytes 3538952 | tf_op jit(solution)/shard_map/ppermute | solution.py:301
  30.9 34.4 %collective-permute-start.8 = (bf16[256,2304]{1,0:T(8,128)(2,1)S(1)}, bf16[256,2304]{1,0:T(8,128)(2,1)S(1)}, u32[]{:S(2)}, u32[]{:S(2)}) collective-permute-start(bf16[256,2304]{1,0:T(8,128)(2,1)S(1)} %get-tuple-element.30), channel_id=1, source_target_pairs={{0,4},{2,6},{4,0},{6,2},{8,12},{10,14},{12,8},{14,10},{16,20},{18,... | collective-permute-start | bytes 3538952 | tf_op jit(solution)/shard_map/ppermute | solution.py:301
  32.5 32.8 %collective-permute-start.9 = (bf16[720,768]{1,0:T(8,128)(2,1)S(1)}, bf16[720,768]{1,0:T(8,128)(2,1)S(1)}, u32[]{:S(2)}, u32[]{:S(2)}) collective-permute-start(bf16[720,768]{1,0:T(8,128)(2,1)S(1)} %pad_maximum_fusion.3.refs_7_), channel_id=1, source_target_pairs={{8,0},{10,2},{12,4},{14,6},{16,24},{18,26},{20,28},{22,30},{0,8},{... | collective-permute-start | bytes 3317768 | tf_op jit(solution)/shard_map/ppermute | solution.py:340
  33.2 32.1 %collective-permute-start.10 = (bf16[720,768]{1,0:T(8,128)(2,1)S(1)}, bf16[720,768]{1,0:T(8,128)(2,1)S(1)}, u32[]{:S(2)}, u32[]{:S(2)}) collective-permute-start(bf16[720,768]{1,0:T(8,128)(2,1)S(1)} %pad_maximum_fusion.3.refs_7_), channel_id=1, source_target_pairs={{8,16},{10,18},{12,20},{14,22},{16,8},{18,10},{20,12},{22,14},{9,1... | collective-permute-start | bytes 3317768 | tf_op jit(solution)/shard_map/ppermute | solution.py:340
  33.9 30.6 %collective-permute-start.11 = (bf16[240,768]{1,0:T(8,128)(2,1)S(1)}, bf16[240,768]{1,0:T(8,128)(2,1)S(1)}, u32[]{:S(2)}, u32[]{:S(2)}) collective-permute-start(bf16[240,768]{1,0:T(8,128)(2,1)S(1)} %collective-permute-done.4.refs_12_), channel_id=1, source_target_pairs={{8,0},{10,2},{12,4},{14,6},{16,24},{18,26},{20,28},{22,30},{9,1},{... | collective-permute-start | bytes 1105928 | tf_op jit(solution)/shard_map/ppermute | solution.py:340
  64.5 0.8 copy-start.23
  65.3 4.9 %copy-start.9 = (bf16[720,768]{1,0:T(8,128)(2,1)}, bf16[720,768]{1,0:T(8,128)(2,1)S(1)}, u32[]{:S(2)}) copy-start(bf16[720,768]{1,0:T(8,128)(2,1)S(1)} %collective-permute-done.9.refs_9_) | copy-start | bytes 3317764
  65.3 4.9 %copy-start.11 = (bf16[720,768]{1,0:T(8,128)(2,1)}, bf16[720,768]{1,0:T(8,128)(2,1)S(1)}, u32[]{:S(2)}) copy-start(bf16[720,768]{1,0:T(8,128)(2,1)S(1)} %collective-permute-done.10.refs_11_) | copy-start | bytes 3317764
  65.3 29.4 %collective-permute-start.12 = (bf16[256,2304]{1,0:T(8,128)(2,1)S(1)}, bf16[256,2304]{1,0:T(8,128)(2,1)S(1)}, u32[]{:S(2)}, u32[]{:S(2)}) collective-permute-start(bf16[256,2304]{1,0:T(8,128)(2,1)S(1)} %get-tuple-element.34), channel_id=1, source_target_pairs={{0,6},{2,4},{4,2},{6,0},{8,14},{10,12},{12,10},{14,8},{16,22},{18,... | collective-permute-start | bytes 3538952 | tf_op jit(solution)/shard_map/ppermute | solution.py:301
  67.1 7.9 %collective-permute-start.13 = (bf16[720,768]{1,0:T(8,128)(2,1)S(1)}, bf16[720,768]{1,0:T(8,128)(2,1)}, u32[]{:S(2)}, u32[]{:S(2)}) collective-permute-start(bf16[720,768]{1,0:T(8,128)(2,1)S(1)} %collective-permute-done.9.refs_9_), channel_id=1, source_target_pairs={{8,16},{10,18},{12,20},{14,22},{16,8},{18,10},{20,12},{22,14},{9,1... | collective-permute-start | bytes 3317768 | tf_op jit(solution)/shard_map/ppermute | solution.py:340
  68.7 26.0 %collective-permute-start.14 = (bf16[720,768]{1,0:T(8,128)(2,1)S(1)}, bf16[720,768]{1,0:T(8,128)(2,1)S(1)}, u32[]{:S(2)}, u32[]{:S(2)}) collective-permute-start(bf16[720,768]{1,0:T(8,128)(2,1)S(1)} %collective-permute-done.10.refs_11_), channel_id=1, source_target_pairs={{8,0},{10,2},{12,4},{14,6},{16,24},{18,26},{20,28},{22,30},{9,1},{... | collective-permute-start | bytes 3317768 | tf_op jit(solution)/shard_map/ppermute | solution.py:340
  94.8 1.0 copy-start.13
  94.8 1.4 copy-start.27
  95.8 5.8 %collective-permute-start.15 = (bf16[1024,1536]{1,0:T(8,128)(2,1)S(1)}, bf16[1024,1536]{1,0:T(8,128)(2,1)}, u32[]{:S(2)}, u32[]{:S(2)}) collective-permute-start(bf16[1024,1536]{1,0:T(8,128)(2,1)S(1)} %slice_dynamic-update-slice_fusion), channel_id=1, source_target_pairs={{0,1},{1,0},{2,3},{3,2},{4,5},{5,4},{6,7},{7,6},{8,9},{9,8},{10,11... | collective-permute-start | bytes 9437192 | tf_op jit(solution)/shard_map/ppermute | solution.py:304
  96.2 28.6 %collective-permute-start.16 = (bf16[720,768]{1,0:T(8,128)(2,1)}, bf16[720,768]{1,0:T(8,128)(2,1)}, u32[]{:S(2)}, u32[]{:S(2)}) collective-permute-start(bf16[720,768]{1,0:T(8,128)(2,1)} %collective-permute-done.13.refs_13_), channel_id=1, source_target_pairs={{8,0},{10,2},{12,4},{14,6},{16,24},{18,26},{20,28},{22,30},{9,1},{... | collective-permute-start | bytes 3317768 | tf_op jit(solution)/shard_map/ppermute | solution.py:340
  101.5 3.5 %copy-start.10 = (bf16[720,768]{1,0:T(8,128)(2,1)S(1)}, bf16[720,768]{1,0:T(8,128)(2,1)}, u32[]{:S(2)}) copy-start(bf16[720,768]{1,0:T(8,128)(2,1)} %copy-done.9) | copy-start | bytes 3317764
  101.5 3.5 %copy-start.12 = (bf16[720,768]{1,0:T(8,128)(2,1)S(1)}, bf16[720,768]{1,0:T(8,128)(2,1)}, u32[]{:S(2)}) copy-start(bf16[720,768]{1,0:T(8,128)(2,1)} %copy-done.11) | copy-start | bytes 3317764
  101.5 3.6 %copy-start.14 = (bf16[720,768]{1,0:T(8,128)(2,1)S(1)}, bf16[720,768]{1,0:T(8,128)(2,1)}, u32[]{:S(2)}) copy-start(bf16[720,768]{1,0:T(8,128)(2,1)} %copy-done.13) | copy-start | bytes 3317764
  101.6 3.6 %copy-start.20 = (bf16[240,768]{1,0:T(8,128)(2,1)S(1)}, bf16[240,768]{1,0:T(8,128)(2,1)}, u32[]{:S(2)}) copy-start(bf16[240,768]{1,0:T(8,128)(2,1)} %copy-done.19) | copy-start | bytes 1105924
  101.6 3.6 %copy-start.22 = (bf16[240,768]{1,0:T(8,128)(2,1)S(1)}, bf16[240,768]{1,0:T(8,128)(2,1)}, u32[]{:S(2)}) copy-start(bf16[240,768]{1,0:T(8,128)(2,1)} %copy-done.21) | copy-start | bytes 1105924
  104.9 1.2 copy-start.1
  104.9 1.3 copy-start.2
  104.9 1.4 copy-start.4
  104.9 1.5 copy-start.6
  104.9 1.6 copy-start.16
  105.0 1.7 copy-start.18
  106.7 18.1 %copy-start.24 = (bf16[240,768]{1,0:T(8,128)(2,1)S(1)}, bf16[240,768]{1,0:T(8,128)(2,1)}, u32[]{:S(2)}) copy-start(bf16[240,768]{1,0:T(8,128)(2,1)} %copy-done.23) | copy-start | bytes 1105924
  129.7 3.6 %collective-permute-start.17 = (f32[544,768]{1,0:T(8,128)S(1)}, f32[544,768]{1,0:T(8,128)S(1)}, u32[]{:S(2)}, u32[]{:S(2)}) collective-permute-start(f32[544,768]{1,0:T(8,128)S(1)} %get-tuple-element.51), channel_id=1, source_target_pairs={{0,1},{1,0},{2,3},{3,2},{4,5},{5,4},{6,7},{7,6},{8,9},{9,8},{10,11... | collective-permute-start | bytes 5013512 | tf_op jit(solution)/shard_map/ppermute | solution.py:304
  133.6 22.1 %copy-start.3 = (f32[128,768]{1,0:T(8,128)S(1)}, f32[128,768]{1,0:T(8,128)}, u32[]{:S(2)}) copy-start(f32[128,768]{1,0:T(8,128)} %refs_6_.1) | copy-start | bytes 1179652
  133.6 22.1 %copy-start.7 = (bf16[384,384]{1,0:T(8,128)(2,1)S(1)}, bf16[384,384]{1,0:T(8,128)(2,1)}, u32[]{:S(2)}) copy-start(bf16[384,384]{1,0:T(8,128)(2,1)} %refs_4_.1) | copy-start | bytes 884740
  133.6 22.1 %copy-start.8 = (bf16[384,384]{1,0:T(8,128)(2,1)S(1)}, bf16[384,384]{1,0:T(8,128)(2,1)}, u32[]{:S(2)}) copy-start(bf16[384,384]{1,0:T(8,128)(2,1)} %refs_5_.1) | copy-start | bytes 884740
  133.7 12.5 %collective-permute-start.18 = (f32[136,768]{1,0:T(8,128)S(1)}, f32[136,768]{1,0:T(8,128)S(1)}, u32[]{:S(2)}, u32[]{:S(2)}) collective-permute-start(f32[136,768]{1,0:T(8,128)S(1)} %get-tuple-element.59), channel_id=1, source_target_pairs={{0,2},{2,0},{4,6},{6,4},{8,10},{10,8},{12,14},{14,12},{16,18},{18,... | collective-permute-start | bytes 1253384 | tf_op jit(solution)/shard_map/ppermute | solution.py:301
  135.3 20.4 %collective-permute-start.19 = (f32[136,768]{1,0:T(8,128)S(1)}, f32[136,768]{1,0:T(8,128)S(1)}, u32[]{:S(2)}, u32[]{:S(2)}) collective-permute-start(f32[136,768]{1,0:T(8,128)S(1)} %get-tuple-element.58), channel_id=1, source_target_pairs={{0,4},{2,6},{4,0},{6,2},{8,12},{10,14},{12,8},{14,10},{16,20},{18,... | collective-permute-start | bytes 1253384 | tf_op jit(solution)/shard_map/ppermute | solution.py:301
  135.4 20.3 %collective-permute-start.20 = (f32[136,768]{1,0:T(8,128)S(1)}, f32[136,768]{1,0:T(8,128)S(1)}, u32[]{:S(2)}, u32[]{:S(2)}) collective-permute-start(f32[136,768]{1,0:T(8,128)S(1)} %get-tuple-element.57), channel_id=1, source_target_pairs={{0,6},{2,4},{4,2},{6,0},{8,14},{10,12},{12,10},{14,8},{16,22},{18,... | collective-permute-start | bytes 1253384 | tf_op jit(solution)/shard_map/ppermute | solution.py:301
  158.0 2.0 %collective-permute-start.21 = (f32[384,384]{1,0:T(8,128)S(1)}, f32[384,384]{1,0:T(8,128)S(1)}, u32[]{:S(2)}, u32[]{:S(2)}) collective-permute-start(f32[384,384]{1,0:T(8,128)S(1)} %get-tuple-element.54), channel_id=1, source_target_pairs={{0,1},{1,0},{2,3},{3,2},{4,5},{5,4},{6,7},{7,6},{8,9},{9,8},{10,11... | collective-permute-start | bytes 1769480 | tf_op jit(solution)/shard_map/ppermute | solution.py:304
  160.1 7.7 %collective-permute-start.24 = (f32[96,384]{1,0:T(8,128)S(1)}, f32[96,384]{1,0:T(8,128)S(1)}, u32[]{:S(2)}, u32[]{:S(2)}) collective-permute-start(f32[96,384]{1,0:T(8,128)S(1)} %get-tuple-element.75), channel_id=1, source_target_pairs={{0,6},{2,4},{4,2},{6,0},{8,14},{10,12},{12,10},{14,8},{16,22},{18,... | collective-permute-start | bytes 442376 | tf_op jit(solution)/shard_map/ppermute | solution.py:301
  161.7 8.5 %collective-permute-start.23 = (f32[96,384]{1,0:T(8,128)S(1)}, f32[96,384]{1,0:T(8,128)S(1)}, u32[]{:S(2)}, u32[]{:S(2)}) collective-permute-start(f32[96,384]{1,0:T(8,128)S(1)} %get-tuple-element.76), channel_id=1, source_target_pairs={{0,4},{2,6},{4,0},{6,2},{8,12},{10,14},{12,8},{14,10},{16,20},{18,... | collective-permute-start | bytes 442376 | tf_op jit(solution)/shard_map/ppermute | solution.py:301
  162.2 8.0 %collective-permute-start.22 = (f32[96,384]{1,0:T(8,128)S(1)}, f32[96,384]{1,0:T(8,128)S(1)}, u32[]{:S(2)}, u32[]{:S(2)}) collective-permute-start(f32[96,384]{1,0:T(8,128)S(1)} %get-tuple-element.74), channel_id=1, source_target_pairs={{0,2},{2,0},{4,6},{6,4},{8,10},{10,8},{12,14},{14,12},{16,18},{18,... | collective-permute-start | bytes 442376 | tf_op jit(solution)/shard_map/ppermute | solution.py:301
  170.2 4.4 %collective-permute-start.27 = (f32[24,384]{1,0:T(8,128)S(1)}, f32[24,384]{1,0:T(8,128)S(1)}, u32[]{:S(2)}, u32[]{:S(2)}) collective-permute-start(f32[24,384]{1,0:T(8,128)S(1)} %get-tuple-element.82), channel_id=1, source_target_pairs={{0,24},{2,26},{4,28},{6,30},{8,0},{10,2},{12,4},{14,6},{16,8},{18,... | collective-permute-start | bytes 110600 | tf_op jit(solution)/shard_map/ppermute | solution.py:458
  170.5 5.6 %collective-permute-start.26 = (f32[24,384]{1,0:T(8,128)S(1)}, f32[24,384]{1,0:T(8,128)S(1)}, u32[]{:S(2)}, u32[]{:S(2)}) collective-permute-start(f32[24,384]{1,0:T(8,128)S(1)} %get-tuple-element.83), channel_id=1, source_target_pairs={{0,16},{2,18},{4,20},{6,22},{8,24},{10,26},{12,28},{14,30},{16,0},... | collective-permute-start | bytes 110600 | tf_op jit(solution)/shard_map/ppermute | solution.py:458
  171.3 5.8 %collective-permute-start.25 = (f32[24,384]{1,0:T(8,128)S(1)}, f32[24,384]{1,0:T(8,128)S(1)}, u32[]{:S(2)}, u32[]{:S(2)}) collective-permute-start(f32[24,384]{1,0:T(8,128)S(1)} %get-tuple-element.81), channel_id=1, source_target_pairs={{0,8},{2,10},{4,12},{6,14},{8,16},{10,18},{12,20},{14,22},{16,24},... | collective-permute-start | bytes 110600 | tf_op jit(solution)/shard_map/ppermute | solution.py:458
  177.1 5.8 %collective-permute-start.28 = (f32[24,384]{1,0:T(8,128)S(1)}, f32[24,384]{1,0:T(8,128)S(1)}, u32[]{:S(2)}, u32[]{:S(2)}) collective-permute-start(f32[24,384]{1,0:T(8,128)S(1)} %get-tuple-element.56), channel_id=1, source_target_pairs={{0,8},{2,10},{4,12},{6,14},{8,16},{10,18},{12,20},{14,22},{16,24},... | collective-permute-start | bytes 110600 | tf_op jit(solution)/shard_map/ppermute | solution.py:458
  177.2 5.6 %collective-permute-start.29 = (f32[24,384]{1,0:T(8,128)S(1)}, f32[24,384]{1,0:T(8,128)S(1)}, u32[]{:S(2)}, u32[]{:S(2)}) collective-permute-start(f32[24,384]{1,0:T(8,128)S(1)} %get-tuple-element.56), channel_id=1, source_target_pairs={{0,16},{2,18},{4,20},{6,22},{8,24},{10,26},{12,28},{14,30},{16,0},... | collective-permute-start | bytes 110600 | tf_op jit(solution)/shard_map/ppermute | solution.py:458
  179.3 4.2 %collective-permute-start.30 = (f32[24,384]{1,0:T(8,128)S(1)}, f32[24,384]{1,0:T(8,128)S(1)}, u32[]{:S(2)}, u32[]{:S(2)}) collective-permute-start(f32[24,384]{1,0:T(8,128)S(1)} %get-tuple-element.56), channel_id=1, source_target_pairs={{0,24},{2,26},{4,28},{6,30},{8,0},{10,2},{12,4},{14,6},{16,8},{18,... | collective-permute-start | bytes 110600 | tf_op jit(solution)/shard_map/ppermute | solution.py:458
  183.4 5.1 %collective-permute-start.31 = (f32[96,384]{1,0:T(8,128)S(1)}, f32[96,384]{1,0:T(8,128)S(1)}, u32[]{:S(2)}, u32[]{:S(2)}) collective-permute-start(f32[96,384]{1,0:T(8,128)S(1)} %constant_dynamic-update-slice_fusion.4), channel_id=1, source_target_pairs={{0,2},{2,0},{4,6},{6,4},{8,10},{10,8},{12,14},{14,12},{16,18},{18,... | collective-permute-start | bytes 442376 | tf_op jit(solution)/shard_map/ppermute | solution.py:301
  184.1 5.1 %collective-permute-start.32 = (f32[96,384]{1,0:T(8,128)S(1)}, f32[96,384]{1,0:T(8,128)S(1)}, u32[]{:S(2)}, u32[]{:S(2)}) collective-permute-start(f32[96,384]{1,0:T(8,128)S(1)} %constant_dynamic-update-slice_fusion.4), channel_id=1, source_target_pairs={{0,4},{2,6},{4,0},{6,2},{8,12},{10,14},{12,8},{14,10},{16,20},{18,... | collective-permute-start | bytes 442376 | tf_op jit(solution)/shard_map/ppermute | solution.py:301
  185.5 6.0 %collective-permute-start.33 = (f32[96,384]{1,0:T(8,128)S(1)}, f32[96,384]{1,0:T(8,128)S(1)}, u32[]{:S(2)}, u32[]{:S(2)}) collective-permute-start(f32[96,384]{1,0:T(8,128)S(1)} %constant_dynamic-update-slice_fusion.4), channel_id=1, source_target_pairs={{0,6},{2,4},{4,2},{6,0},{8,14},{10,12},{12,10},{14,8},{16,22},{18,... | collective-permute-start | bytes 442376 | tf_op jit(solution)/shard_map/ppermute | solution.py:301
  191.6 2.1 %collective-permute-start.34 = (f32[384,384]{1,0:T(8,128)S(1)}, f32[384,384]{1,0:T(8,128)S(1)}, u32[]{:S(2)}, u32[]{:S(2)}) collective-permute-start(f32[384,384]{1,0:T(8,128)S(1)} %constant_dynamic-update-slice_fusion), channel_id=1, source_target_pairs={{0,1},{1,0},{2,3},{3,2},{4,5},{5,4},{6,7},{7,6},{8,9},{9,8},{10,11... | collective-permute-start | bytes 1769480 | tf_op jit(solution)/shard_map/ppermute | solution.py:304

commit v7 on v6

--- a/solution.py
+++ b/solution.py
@@ -351,13 +351,13 @@
         own_two = step_two(*own_one)
         rest = jnp.concatenate([to_member(own[s], s) for s in range(1, group)], axis=0)
 
-        rest, boxes, own_two = lax.optimization_barrier((rest, boxes, own_two))
         rest_one = step_one(rest)
+        _, boxes, own_two = lax.optimization_barrier((rest, boxes, own_two))
         own_last = line(own_two[0], outward)
         arrived = [to_member(boxes[0], 1), to_member(boxes[1], 2)]
 
-        arrived, boxes, rest_one, own_last = lax.optimization_barrier((arrived, boxes, rest_one, own_last))
         rest_two = step_two(*rest_one)
+        arrived, boxes, _, own_last = lax.optimization_barrier((arrived, boxes, rest_one, own_last))
         arrived.append(to_member(boxes[2], 3))
         heads = context.shape[1]
         part = jnp.concatenate([context] + [v[:, :heads] for v in arrived[:2]] + [jnp.zeros_like(context)], axis=0)

time: 195 us -> 193 us (0.990)
  waiting for transfers between devices: 119 us -> 115 us
    ppermute x10, waiting for transfers between devices: 63.5 us -> 59.6 us  [line(): return lax.ppermute(value, 'wide', pairs)]
    unnamed x56 -> x58, local copies, waits for them, and re-layouts: 4.51 us -> 6.32 us
where the time goes in v7:
time: 193 us
  waiting for transfers between devices  115 us (60%)
  starting transfers between devices  37.4 us (19%)
  Pallas kernels  16.9 us (9%)
  local copies, waits for them, and re-layouts  12.8 us (7%)
  other arithmetic  9 us (5%)
    ppermute x10, waiting for transfers between devices, line(): return lax.ppermute(value, 'wide', pairs)  59.6 us
    ppermute x15, waiting for transfers between devices, to_member(): return lax.ppermute(value, 'wide', pairs) if s else value  38.5 us
    ppermute x15, starting transfers between devices, to_member(): return lax.ppermute(value, 'wide', pairs) if s else value  17.8 us
    ppermute x10, starting transfers between devices, line(): return lax.ppermute(value, 'wide', pairs)  12.7 us
    ppermute x4, waiting for transfers between devices, to_core(): lax.ppermute(value, 'narrow', [(i, i ^ t) for i in range(narrows)])  9.76 us
    pallas_call x1, Pallas kernels, attend(): pl.pallas_call(functools.partial(attend_kernel, rows, planes), grid=(2,),...  9.54 us
    ppermute x6, waiting for transfers between devices, shift(): lax.ppermute(value, 'wide', [(i, (i + k * group) % wides) for i in range(...  7.36 us
    ppermute x6, starting transfers between devices, shift(): lax.ppermute(value, 'wide', [(i, (i + k * group) % wides) for i in range(...  6.74 us
  transfers between devices with their start and end apart: 35, of which 24 were waited for; matrix products, arithmetic and copies ran while one was open for 6% of the time, Pallas kernels for 5%

profile of v7, /device:TPU:0, one launch (start us, length us, event | category | flops | bytes accessed | tf_op | source)
XLA Modules:
  0.0 192.6 jit_solution(7980530893461715249)
XLA Ops:
  0.7 1.0 dynamic-slice_bitcast_fusion
  1.7 1.3 constant_dynamic-slice_fusion.7
  3.1 3.1 %collective-permute-start.3 = (bf16[240,768]{1,0:T(8,128)(2,1)S(1)}, bf16[240,768]{1,0:T(8,128)(2,1)S(1)}, u32[]{:S(2)}, u32[]{:S(2)}) collective-permute-start(bf16[240,768]{1,0:T(8,128)(2,1)S(1)} %pad_maximum_fusion.6.refs_6_), channel_id=1, source_target_pairs={{8,0},{10,2},{12,4},{14,6},{16,24},{18,26},{20,28},{22,30},{0,8},{... | collective-permute-start | bytes 1105928 | tf_op jit(solution)/shard_map/ppermute | solution.py:340
  6.2 0.7 collective-permute-start.5
  6.9 1.6 collective-permute-start
  8.5 1.6 collective-permute-start.1
  10.6 0.9 constant_dynamic-slice_fusion.6
  11.5 3.2 %collective-permute-done.3.refs_8_ = bf16[240,768]{1,0:T(8,128)(2,1)S(1)} collective-permute-done((bf16[240,768]{1,0:T(8,128)(2,1)S(1)}, bf16[240,768]{1,0:T(8,128)(2,1)S(1)}, u32[]{:S(2)}, u32[]{:S(2)}) %collective-permute-start.3) | collective-permute-done | bytes 368672 | tf_op jit(solution)/shard_map/ppermute | solution.py:340
  14.8 0.7 collective-permute-start.4
  15.5 1.3 collective-permute-start.6
  17.0 1.4 collective-permute-done
  18.5 7.7 %collective-permute-done.1 = bf16[240,768]{1,0:T(8,128)(2,1)S(1)} collective-permute-done((bf16[240,768]{1,0:T(8,128)(2,1)S(1)}, bf16[240,768]{1,0:T(8,128)(2,1)S(1)}, u32[]{:S(2)}, u32[]{:S(2)}) %collective-permute-start.1) | collective-permute-done | bytes 368672 | tf_op jit(solution)/shard_map/ppermute | solution.py:301
  26.3 2.4 %collective-permute-done.6.refs_14_ = bf16[240,768]{1,0:T(8,128)(2,1)S(1)} collective-permute-done((bf16[240,768]{1,0:T(8,128)(2,1)S(1)}, bf16[240,768]{1,0:T(8,128)(2,1)S(1)}, u32[]{:S(2)}, u32[]{:S(2)}) %collective-permute-start.6) | collective-permute-done | bytes 368672 | tf_op jit(solution)/shard_map/ppermute | solution.py:340
  28.7 0.8 copy-done.21
  29.5 1.5 collective-permute-start.7
  31.0 1.5 collective-permute-start.8
  32.5 0.7 collective-permute-start.9
  33.2 0.7 collective-permute-start.10
  33.9 1.0 copy-done.7
  35.0 1.3 collective-permute-start.11
  36.3 0.7 copy-done.19
  37.0 27.2 %collective-permute-done.11.refs_4_ = bf16[240,768]{1,0:T(8,128)(2,1)S(1)} collective-permute-done((bf16[240,768]{1,0:T(8,128)(2,1)S(1)}, bf16[240,768]{1,0:T(8,128)(2,1)S(1)}, u32[]{:S(2)}, u32[]{:S(2)}) %collective-permute-start.11) | collective-permute-done | bytes 368672 | tf_op jit(solution)/shard_map/ppermute | solution.py:340
  64.2 0.8 copy-done.23
  65.5 1.6 collective-permute-start.13
  67.1 1.3 collective-permute-start.14
  68.6 0.8 slice.33.refs_4_
  69.4 3.9 %maximum_maximum_fusion = bf16[1024,1536]{1,0:T(8,128)(2,1)S(1)} fusion(bf16[256,1536]{1,0:T(8,128)(2,1)S(1)} %slice.31, bf16[256,1536]{1,0:T(8,128)(2,1)S(1)} %slice.30, bf16[256,1536]{1,0:T(8,128)(2,1)S(1)} %copy-done.25, bf16[1024]{0:T(1024)(128)(2,1)S(1)} %pad.3.clone), kind=kLoop, calls=%fused_computation | loop fusion | flops 12582912 | bytes 5507072 | tf_op jit(solution)/shard_map/concatenate | solution.py:363
  73.4 18.2 %collective-permute-done.14.refs_15_ = bf16[720,768]{1,0:T(8,128)(2,1)S(1)} collective-permute-done((bf16[720,768]{1,0:T(8,128)(2,1)S(1)}, bf16[720,768]{1,0:T(8,128)(2,1)S(1)}, u32[]{:S(2)}, u32[]{:S(2)}) %collective-permute-start.14) | collective-permute-done | bytes 1105952 | tf_op jit(solution)/shard_map/ppermute | solution.py:340
  91.7 0.9 copy-done.13
  93.0 1.3 collective-permute-start.16
  94.3 0.8 dynamic_slice.79
  95.1 1.0 slice.35.refs_5_
  96.2 2.2 %collective-permute-done.15 = bf16[1024,1536]{1,0:T(8,128)(2,1)} collective-permute-done((bf16[1024,1536]{1,0:T(8,128)(2,1)S(1)}, bf16[1024,1536]{1,0:T(8,128)(2,1)}, u32[]{:S(2)}, u32[]{:S(2)}) %collective-permute-start.15) | collective-permute-done | bytes 3145760 | tf_op jit(solution)/shard_map/ppermute | solution.py:304
  98.4 3.3 %dynamic-slice_select_fusion = bf16[4,256,768]{2,1,0:T(8,128)(2,1)S(1)} fusion(bf16[4,256,1536]{2,1,0:T(8,128)(2,1)} %bitcast.5.refs_1_, s32[]{:T(128)S(6)} %select_n.150, bf16[4,256,1536]{2,1,0:T(8,128)(2,1)S(1)} %bitcast.14, pred[]{:T(512)S(6)} %eq.22), kind=kLoop, calls=%fused_computation.1 | loop fusion | flops 786432 | bytes 4718597 | tf_op jit(solution)/shard_map/jit(_where)/select_n | solution.py:377
  102.0 0.8 copy-done
  103.5 9.5 %shard_map.103 = (f32[1024,768]{1,0:T(8,128)S(1)}, bf16[768,768]{1,0:T(8,128)(2,1)S(1)}) custom-call(bf16[4,256,1536]{2,1,0:T(8,128)(2,1)S(1)} %bitcast.15, bf16[4,256,1536]{2,1,0:T(8,128)(2,1)} %bitcast.5.refs_1_, bf16[256,768]{1,0:T(8,128)(2,1)S(1)} %copy-done.2, bf16[256,768]{1,0:T(8,128)(2,1)S(1)} %slice.32.refs_3_, bf16[256,768]{1,0:T(8,128)(2,1)S(1)} %copy-done, ...), custom_call_target="tpu_custom_call" | custom-call | flops 4831838208 | bytes 16777216 | tf_op jit(solution)/shard_map/pallas_call | solution.py:87
  113.1 8.5 %collective-permute-done.16.refs_5_ = bf16[720,768]{1,0:T(8,128)(2,1)} collective-permute-done((bf16[720,768]{1,0:T(8,128)(2,1)}, bf16[720,768]{1,0:T(8,128)(2,1)}, u32[]{:S(2)}, u32[]{:S(2)}) %collective-permute-start.16) | collective-permute-done | bytes 1105952 | tf_op jit(solution)/shard_map/ppermute | solution.py:340
  121.6 5.0 %shard_map.104 = (f32[544,768]{1,0:T(8,128)S(1)}, f32[544,768]{1,0:T(8,128)S(1)}) custom-call(f32[1024,768]{1,0:T(8,128)S(1)} %get-tuple-element.41.refs_0_, bf16[1024,768]{1,0:T(8,128)(2,1)S(1)} %bitcast.16, bf16[1,768]{1,0:T(2,128)(2,1)S(1)} %broadcast_in_dim.13.refs_2_, bf16[768,768]{1,0:T(8,128)(2,1)S(1)} %get-tuple-element.42.refs_3_, ...), custom_call_target="tpu_custom_call" | custom-call | flops 2415919104 | bytes 16777216 | tf_op jit(solution)/shard_map/pallas_call | solution.py:191
  126.7 3.5 %collective-permute-done.17 = f32[544,768]{1,0:T(8,128)S(1)} collective-permute-done((f32[544,768]{1,0:T(8,128)S(1)}, f32[544,768]{1,0:T(8,128)S(1)}, u32[]{:S(2)}, u32[]{:S(2)}) %collective-permute-start.17) | collective-permute-done | bytes 1671200 | tf_op jit(solution)/shard_map/ppermute | solution.py:304
  130.6 1.6 collective-permute-start.18
  132.1 1.5 collective-permute-start.19
  134.1 9.0 %collective-permute-done.18.refs_1_ = f32[136,768]{1,0:T(8,128)S(1)} collective-permute-done((f32[136,768]{1,0:T(8,128)S(1)}, f32[136,768]{1,0:T(8,128)S(1)}, u32[]{:S(2)}, u32[]{:S(2)}) %collective-permute-start.18) | collective-permute-done | bytes 417824 | tf_op jit(solution)/shard_map/ppermute | solution.py:301
  143.1 9.4 %collective-permute-done.19.refs_2_ = f32[136,768]{1,0:T(8,128)S(1)} collective-permute-done((f32[136,768]{1,0:T(8,128)S(1)}, f32[136,768]{1,0:T(8,128)S(1)}, u32[]{:S(2)}, u32[]{:S(2)}) %collective-permute-start.19) | collective-permute-done | bytes 417824 | tf_op jit(solution)/shard_map/ppermute | solution.py:301
  152.5 2.4 %shard_map.105 = (f32[128,768]{1,0:T(8,128)}, f32[384,384]{1,0:T(8,128)S(1)}, f32[384,384]{1,0:T(8,128)S(1)}) custom-call(f32[136,768]{1,0:T(8,128)S(1)} %get-tuple-element.54.refs_0_, f32[136,768]{1,0:T(8,128)S(1)} %collective-permute-done.18.refs_1_, f32[136,768]{1,0:T(8,128)S(1)} %collective-permute-done.19.refs_2_, ...), custom_call_target="tpu_custom_call" | custom-call | flops 452984832 | bytes 5242880 | tf_op jit(solution)/shard_map/pallas_call | solution.py:277
  154.9 2.0 %collective-permute-done.21 = f32[384,384]{1,0:T(8,128)S(1)} collective-permute-done((f32[384,384]{1,0:T(8,128)S(1)}, f32[384,384]{1,0:T(8,128)S(1)}, u32[]{:S(2)}, u32[]{:S(2)}) %collective-permute-start.21) | collective-permute-done | bytes 589856 | tf_op jit(solution)/shard_map/ppermute | solution.py:304
  157.0 1.5 collective-permute-start.24
  158.5 1.2 collective-permute-start.23
  159.7 0.8 collective-permute-start.22
  160.5 4.1 %collective-permute-done.24 = f32[96,384]{1,0:T(8,128)S(1)} collective-permute-done((f32[96,384]{1,0:T(8,128)S(1)}, f32[96,384]{1,0:T(8,128)S(1)}, u32[]{:S(2)}, u32[]{:S(2)}) %collective-permute-start.24) | collective-permute-done | bytes 147488 | tf_op jit(solution)/shard_map/ppermute | solution.py:301
  164.7 2.3 %collective-permute-done.23 = f32[96,384]{1,0:T(8,128)S(1)} collective-permute-done((f32[96,384]{1,0:T(8,128)S(1)}, f32[96,384]{1,0:T(8,128)S(1)}, u32[]{:S(2)}, u32[]{:S(2)}) %collective-permute-start.23) | collective-permute-done | bytes 147488 | tf_op jit(solution)/shard_map/ppermute | solution.py:301
  167.2 2.1 %collective-permute-start.27 = (f32[24,384]{1,0:T(8,128)S(1)}, f32[24,384]{1,0:T(8,128)S(1)}, u32[]{:S(2)}, u32[]{:S(2)}) collective-permute-start(f32[24,384]{1,0:T(8,128)S(1)} %get-tuple-element.76), channel_id=1, source_target_pairs={{0,24},{2,26},{4,28},{6,30},{8,0},{10,2},{12,4},{14,6},{16,8},{18,... | collective-permute-start | bytes 110600 | tf_op jit(solution)/shard_map/ppermute | solution.py:458
  169.9 1.3 collective-permute-done.27
  171.2 3.2 %collective-permute-done.26 = f32[24,384]{1,0:T(8,128)S(1)} collective-permute-done((f32[24,384]{1,0:T(8,128)S(1)}, f32[24,384]{1,0:T(8,128)S(1)}, u32[]{:S(2)}, u32[]{:S(2)}) %collective-permute-start.26) | collective-permute-done | bytes 36896 | tf_op jit(solution)/shard_map/ppermute | solution.py:458
  175.2 1.2 collective-permute-start.29
  176.3 2.8 %collective-permute-start.30 = (f32[24,384]{1,0:T(8,128)S(1)}, f32[24,384]{1,0:T(8,128)S(1)}, u32[]{:S(2)}, u32[]{:S(2)}) collective-permute-start(f32[24,384]{1,0:T(8,128)S(1)} %get-tuple-element.50), channel_id=1, source_target_pairs={{0,24},{2,26},{4,28},{6,30},{8,0},{10,2},{12,4},{14,6},{16,8},{18,... | collective-permute-start | bytes 110600 | tf_op jit(solution)/shard_map/ppermute | solution.py:458
  179.1 1.7 collective-permute-done.28
  181.4 1.1 collective-permute-start.31
  182.5 0.8 collective-permute-start.32
  183.4 1.5 collective-permute-start.33
  185.0 1.7 collective-permute-done.31
  186.7 1.0 collective-permute-done.32
  187.7 1.7 collective-permute-done.33
  189.5 2.0 %collective-permute-done.34 = f32[384,384]{1,0:T(8,128)S(1)} collective-permute-done((f32[384,384]{1,0:T(8,128)S(1)}, f32[384,384]{1,0:T(8,128)S(1)}, u32[]{:S(2)}, u32[]{:S(2)}) %collective-permute-start.34) | collective-permute-done | bytes 589856 | tf_op jit(solution)/shard_map/ppermute | solution.py:304
  191.5 1.1 broadcast_select_fusion
  (106 shorter events, 6.4 us)
Async XLA Ops:
  3.0 7.6 %copy-start.26 = (bf16[256,3072]{1,0:T(8,128)(2,1)S(1)}, bf16[256,3072]{1,0:T(8,128)(2,1)}, u32[]{:S(2)}) copy-start(bf16[256,3072]{1,0:T(8,128)(2,1)} %param.10) | copy-start | bytes 4718596
  3.1 8.5 %copy-start.3 = (bf16[240,768]{1,0:T(8,128)(2,1)}, bf16[240,768]{1,0:T(8,128)(2,1)S(1)}, u32[]{:S(2)}) copy-start(bf16[240,768]{1,0:T(8,128)(2,1)S(1)} %pad_maximum_fusion.6.refs_6_) | copy-start | bytes 1105924
  3.1 11.7 %collective-permute-start.3 = (bf16[240,768]{1,0:T(8,128)(2,1)S(1)}, bf16[240,768]{1,0:T(8,128)(2,1)S(1)}, u32[]{:S(2)}, u32[]{:S(2)}) collective-permute-start(bf16[240,768]{1,0:T(8,128)(2,1)S(1)} %pad_maximum_fusion.6.refs_6_), channel_id=1, source_target_pairs={{8,0},{10,2},{12,4},{14,6},{16,24},{18,26},{20,28},{22,30},{0,8},{... | collective-permute-start | bytes 1105928 | tf_op jit(solution)/shard_map/ppermute | solution.py:340
  6.2 9.3 %collective-permute-start.5 = (bf16[240,768]{1,0:T(8,128)(2,1)S(1)}, bf16[240,768]{1,0:T(8,128)(2,1)S(1)}, u32[]{:S(2)}, u32[]{:S(2)}) collective-permute-start(bf16[240,768]{1,0:T(8,128)(2,1)S(1)} %pad_maximum_fusion.6.refs_6_), channel_id=1, source_target_pairs={{8,16},{10,18},{12,20},{14,22},{16,8},{18,10},{20,12},{22,14},{9,1... | collective-permute-start | bytes 1105928 | tf_op jit(solution)/shard_map/ppermute | solution.py:340
  6.9 11.6 %collective-permute-start = (bf16[240,768]{1,0:T(8,128)(2,1)S(1)}, bf16[240,768]{1,0:T(8,128)(2,1)S(1)}, u32[]{:S(2)}, u32[]{:S(2)}) collective-permute-start(bf16[240,768]{1,0:T(8,128)(2,1)S(1)} %pad_maximum_fusion.3), channel_id=1, source_target_pairs={{0,2},{2,0},{4,6},{6,4},{8,10},{10,8},{12,14},{14,12},{16,18},{18,... | collective-permute-start | bytes 1105928 | tf_op jit(solution)/shard_map/ppermute | solution.py:301
  8.5 17.7 %collective-permute-start.1 = (bf16[240,768]{1,0:T(8,128)(2,1)S(1)}, bf16[240,768]{1,0:T(8,128)(2,1)S(1)}, u32[]{:S(2)}, u32[]{:S(2)}) collective-permute-start(bf16[240,768]{1,0:T(8,128)(2,1)S(1)} %pad_maximum_fusion.4), channel_id=1, source_target_pairs={{0,4},{2,6},{4,0},{6,2},{8,12},{10,14},{12,8},{14,10},{16,20},{18,... | collective-permute-start | bytes 1105928 | tf_op jit(solution)/shard_map/ppermute | solution.py:301
  10.1 6.7 %copy-start.25 = (bf16[256,1536]{1,0:T(8,128)(2,1)S(1)}, bf16[256,1536]{1,0:T(8,128)(2,1)}, u32[]{:S(2)}) copy-start(bf16[256,1536]{1,0:T(8,128)(2,1)} %param.8) | copy-start | bytes 2359300
  10.1 16.1 %collective-permute-start.2 = (bf16[240,768]{1,0:T(8,128)(2,1)S(1)}, bf16[240,768]{1,0:T(8,128)(2,1)S(1)}, u32[]{:S(2)}, u32[]{:S(2)}) collective-permute-start(bf16[240,768]{1,0:T(8,128)(2,1)S(1)} %pad_maximum_fusion.5), channel_id=1, source_target_pairs={{0,6},{2,4},{4,2},{6,0},{8,14},{10,12},{12,10},{14,8},{16,22},{18,... | collective-permute-start | bytes 1105928 | tf_op jit(solution)/shard_map/ppermute | solution.py:301
  14.8 2.3 %copy-start.15 = (bf16[240,768]{1,0:T(8,128)(2,1)}, bf16[240,768]{1,0:T(8,128)(2,1)S(1)}, u32[]{:S(2)}) copy-start(bf16[240,768]{1,0:T(8,128)(2,1)S(1)} %collective-permute-done.3.refs_8_) | copy-start | bytes 1105924
  14.8 11.5 %collective-permute-start.4 = (bf16[240,768]{1,0:T(8,128)(2,1)S(1)}, bf16[240,768]{1,0:T(8,128)(2,1)S(1)}, u32[]{:S(2)}, u32[]{:S(2)}) collective-permute-start(bf16[240,768]{1,0:T(8,128)(2,1)S(1)} %collective-permute-done.3.refs_8_), channel_id=1, source_target_pairs={{8,16},{10,18},{12,20},{14,22},{16,8},{18,10},{20,12},{22,14},{9,1... | collective-permute-start | bytes 1105928 | tf_op jit(solution)/shard_map/ppermute | solution.py:340
  15.5 1.6 copy-start.17
  15.5 13.3 %collective-permute-start.6 = (bf16[240,768]{1,0:T(8,128)(2,1)S(1)}, bf16[240,768]{1,0:T(8,128)(2,1)S(1)}, u32[]{:S(2)}, u32[]{:S(2)}) collective-permute-start(bf16[240,768]{1,0:T(8,128)(2,1)S(1)} %collective-permute-done.5.refs_10_), channel_id=1, source_target_pairs={{8,0},{10,2},{12,4},{14,6},{16,24},{18,26},{20,28},{22,30},{9,1},{... | collective-permute-start | bytes 1105928 | tf_op jit(solution)/shard_map/ppermute | solution.py:340
  28.7 0.8 copy-start.21
  29.5 35.5 %collective-permute-start.7 = (bf16[256,2304]{1,0:T(8,128)(2,1)S(1)}, bf16[256,2304]{1,0:T(8,128)(2,1)S(1)}, u32[]{:S(2)}, u32[]{:S(2)}) collective-permute-start(bf16[256,2304]{1,0:T(8,128)(2,1)S(1)} %get-tuple-element.26), channel_id=1, source_target_pairs={{0,2},{2,0},{4,6},{6,4},{8,10},{10,8},{12,14},{14,12},{16,18},{18,... | collective-permute-start | bytes 3538952 | tf_op jit(solution)/shard_map/ppermute | solution.py:301
  31.0 34.0 %collective-permute-start.8 = (bf16[256,2304]{1,0:T(8,128)(2,1)S(1)}, bf16[256,2304]{1,0:T(8,128)(2,1)S(1)}, u32[]{:S(2)}, u32[]{:S(2)}) collective-permute-start(bf16[256,2304]{1,0:T(8,128)(2,1)S(1)} %get-tuple-element.27), channel_id=1, source_target_pairs={{0,4},{2,6},{4,0},{6,2},{8,12},{10,14},{12,8},{14,10},{16,20},{18,... | collective-permute-start | bytes 3538952 | tf_op jit(solution)/shard_map/ppermute | solution.py:301
  32.5 32.4 %collective-permute-start.9 = (bf16[720,768]{1,0:T(8,128)(2,1)S(1)}, bf16[720,768]{1,0:T(8,128)(2,1)S(1)}, u32[]{:S(2)}, u32[]{:S(2)}) collective-permute-start(bf16[720,768]{1,0:T(8,128)(2,1)S(1)} %constant_dynamic-update-slice_fusion.refs_7_), channel_id=1, source_target_pairs={{8,0},{10,2},{12,4},{14,6},{16,24},{18,26},{20,28},{22,30},{0,8},{... | collective-permute-start | bytes 3317768 | tf_op jit(solution)/shard_map/ppermute | solution.py:340
  33.2 31.7 %collective-permute-start.10 = (bf16[720,768]{1,0:T(8,128)(2,1)S(1)}, bf16[720,768]{1,0:T(8,128)(2,1)S(1)}, u32[]{:S(2)}, u32[]{:S(2)}) collective-permute-start(bf16[720,768]{1,0:T(8,128)(2,1)S(1)} %constant_dynamic-update-slice_fusion.refs_7_), channel_id=1, source_target_pairs={{8,16},{10,18},{12,20},{14,22},{16,8},{18,10},{20,12},{22,14},{9,1... | collective-permute-start | bytes 3317768 | tf_op jit(solution)/shard_map/ppermute | solution.py:340
  33.9 1.0 copy-start.7
  35.0 29.2 %collective-permute-start.11 = (bf16[240,768]{1,0:T(8,128)(2,1)S(1)}, bf16[240,768]{1,0:T(8,128)(2,1)S(1)}, u32[]{:S(2)}, u32[]{:S(2)}) collective-permute-start(bf16[240,768]{1,0:T(8,128)(2,1)S(1)} %collective-permute-done.4.refs_12_), channel_id=1, source_target_pairs={{8,0},{10,2},{12,4},{14,6},{16,24},{18,26},{20,28},{22,30},{9,1},{... | collective-permute-start | bytes 1105928 | tf_op jit(solution)/shard_map/ppermute | solution.py:340
  36.3 0.7 copy-start.19
  64.2 0.8 copy-start.23
  64.9 3.7 %copy-start.9 = (bf16[720,768]{1,0:T(8,128)(2,1)}, bf16[720,768]{1,0:T(8,128)(2,1)S(1)}, u32[]{:S(2)}) copy-start(bf16[720,768]{1,0:T(8,128)(2,1)S(1)} %collective-permute-done.9.refs_9_) | copy-start | bytes 3317764
  64.9 3.7 %copy-start.11 = (bf16[720,768]{1,0:T(8,128)(2,1)}, bf16[720,768]{1,0:T(8,128)(2,1)S(1)}, u32[]{:S(2)}) copy-start(bf16[720,768]{1,0:T(8,128)(2,1)S(1)} %collective-permute-done.10.refs_11_) | copy-start | bytes 3317764
  65.0 26.6 %collective-permute-start.12 = (bf16[256,2304]{1,0:T(8,128)(2,1)S(1)}, bf16[256,2304]{1,0:T(8,128)(2,1)S(1)}, u32[]{:S(2)}, u32[]{:S(2)}) collective-permute-start(bf16[256,2304]{1,0:T(8,128)(2,1)S(1)} %get-tuple-element.30), channel_id=1, source_target_pairs={{0,6},{2,4},{4,2},{6,0},{8,14},{10,12},{12,10},{14,8},{16,22},{18,... | collective-permute-start | bytes 3538952 | tf_op jit(solution)/shard_map/ppermute | solution.py:301
  65.5 7.8 %collective-permute-start.13 = (bf16[720,768]{1,0:T(8,128)(2,1)S(1)}, bf16[720,768]{1,0:T(8,128)(2,1)}, u32[]{:S(2)}, u32[]{:S(2)}) collective-permute-start(bf16[720,768]{1,0:T(8,128)(2,1)S(1)} %collective-permute-done.9.refs_9_), channel_id=1, source_target_pairs={{8,16},{10,18},{12,20},{14,22},{16,8},{18,10},{20,12},{22,14},{9,1... | collective-permute-start | bytes 3317768 | tf_op jit(solution)/shard_map/ppermute | solution.py:340
  67.1 24.5 %collective-permute-start.14 = (bf16[720,768]{1,0:T(8,128)(2,1)S(1)}, bf16[720,768]{1,0:T(8,128)(2,1)S(1)}, u32[]{:S(2)}, u32[]{:S(2)}) collective-permute-start(bf16[720,768]{1,0:T(8,128)(2,1)S(1)} %collective-permute-done.10.refs_11_), channel_id=1, source_target_pairs={{8,0},{10,2},{12,4},{14,6},{16,24},{18,26},{20,28},{22,30},{9,1},{... | collective-permute-start | bytes 3317768 | tf_op jit(solution)/shard_map/ppermute | solution.py:340
  91.6 1.0 copy-start.13
  91.6 1.4 copy-start.27
  92.6 5.8 %collective-permute-start.15 = (bf16[1024,1536]{1,0:T(8,128)(2,1)S(1)}, bf16[1024,1536]{1,0:T(8,128)(2,1)}, u32[]{:S(2)}, u32[]{:S(2)}) collective-permute-start(bf16[1024,1536]{1,0:T(8,128)(2,1)S(1)} %slice_dynamic-update-slice_fusion), channel_id=1, source_target_pairs={{0,1},{1,0},{2,3},{3,2},{4,5},{5,4},{6,7},{7,6},{8,9},{9,8},{10,11... | collective-permute-start | bytes 9437192 | tf_op jit(solution)/shard_map/ppermute | solution.py:304
  93.0 28.6 %collective-permute-start.16 = (bf16[720,768]{1,0:T(8,128)(2,1)}, bf16[720,768]{1,0:T(8,128)(2,1)}, u32[]{:S(2)}, u32[]{:S(2)}) collective-permute-start(bf16[720,768]{1,0:T(8,128)(2,1)} %collective-permute-done.13.refs_13_), channel_id=1, source_target_pairs={{8,0},{10,2},{12,4},{14,6},{16,24},{18,26},{20,28},{22,30},{9,1},{... | collective-permute-start | bytes 3317768 | tf_op jit(solution)/shard_map/ppermute | solution.py:340
  98.4 3.5 %copy-start.10 = (bf16[720,768]{1,0:T(8,128)(2,1)S(1)}, bf16[720,768]{1,0:T(8,128)(2,1)}, u32[]{:S(2)}) copy-start(bf16[720,768]{1,0:T(8,128)(2,1)} %copy-done.9) | copy-start | bytes 3317764
  98.4 3.5 %copy-start.12 = (bf16[720,768]{1,0:T(8,128)(2,1)S(1)}, bf16[720,768]{1,0:T(8,128)(2,1)}, u32[]{:S(2)}) copy-start(bf16[720,768]{1,0:T(8,128)(2,1)} %copy-done.11) | copy-start | bytes 3317764
  98.4 3.6 %copy-start.14 = (bf16[720,768]{1,0:T(8,128)(2,1)S(1)}, bf16[720,768]{1,0:T(8,128)(2,1)}, u32[]{:S(2)}) copy-start(bf16[720,768]{1,0:T(8,128)(2,1)} %copy-done.13) | copy-start | bytes 3317764
  98.4 3.6 %copy-start.20 = (bf16[240,768]{1,0:T(8,128)(2,1)S(1)}, bf16[240,768]{1,0:T(8,128)(2,1)}, u32[]{:S(2)}) copy-start(bf16[240,768]{1,0:T(8,128)(2,1)} %copy-done.19) | copy-start | bytes 1105924
  98.4 3.6 %copy-start.22 = (bf16[240,768]{1,0:T(8,128)(2,1)S(1)}, bf16[240,768]{1,0:T(8,128)(2,1)}, u32[]{:S(2)}) copy-start(bf16[240,768]{1,0:T(8,128)(2,1)} %copy-done.21) | copy-start | bytes 1105924
  101.7 1.0 copy-start
  101.8 1.1 copy-start.2
  101.8 1.2 copy-start.4
  101.8 1.6 copy-start.8
  101.8 1.6 copy-start.16
  101.8 1.7 copy-start.18
  103.5 18.1 %copy-start.24 = (bf16[240,768]{1,0:T(8,128)(2,1)S(1)}, bf16[240,768]{1,0:T(8,128)(2,1)}, u32[]{:S(2)}) copy-start(bf16[240,768]{1,0:T(8,128)(2,1)} %copy-done.23) | copy-start | bytes 1105924
  126.6 3.6 %collective-permute-start.17 = (f32[544,768]{1,0:T(8,128)S(1)}, f32[544,768]{1,0:T(8,128)S(1)}, u32[]{:S(2)}, u32[]{:S(2)}) collective-permute-start(f32[544,768]{1,0:T(8,128)S(1)} %get-tuple-element.45), channel_id=1, source_target_pairs={{0,1},{1,0},{2,3},{3,2},{4,5},{5,4},{6,7},{7,6},{8,9},{9,8},{10,11... | collective-permute-start | bytes 5013512 | tf_op jit(solution)/shard_map/ppermute | solution.py:304
  130.4 22.1 %copy-start.1 = (f32[128,768]{1,0:T(8,128)S(1)}, f32[128,768]{1,0:T(8,128)}, u32[]{:S(2)}) copy-start(f32[128,768]{1,0:T(8,128)} %refs_6_.1) | copy-start | bytes 1179652
  130.4 22.1 %copy-start.5 = (bf16[384,384]{1,0:T(8,128)(2,1)S(1)}, bf16[384,384]{1,0:T(8,128)(2,1)}, u32[]{:S(2)}) copy-start(bf16[384,384]{1,0:T(8,128)(2,1)} %refs_4_.1) | copy-start | bytes 884740
  130.4 22.1 %copy-start.6 = (bf16[384,384]{1,0:T(8,128)(2,1)S(1)}, bf16[384,384]{1,0:T(8,128)(2,1)}, u32[]{:S(2)}) copy-start(bf16[384,384]{1,0:T(8,128)(2,1)} %refs_5_.1) | copy-start | bytes 884740
  130.6 12.5 %collective-permute-start.18 = (f32[136,768]{1,0:T(8,128)S(1)}, f32[136,768]{1,0:T(8,128)S(1)}, u32[]{:S(2)}, u32[]{:S(2)}) collective-permute-start(f32[136,768]{1,0:T(8,128)S(1)} %get-tuple-element.53), channel_id=1, source_target_pairs={{0,2},{2,0},{4,6},{6,4},{8,10},{10,8},{12,14},{14,12},{16,18},{18,... | collective-permute-start | bytes 1253384 | tf_op jit(solution)/shard_map/ppermute | solution.py:301
  132.1 20.4 %collective-permute-start.19 = (f32[136,768]{1,0:T(8,128)S(1)}, f32[136,768]{1,0:T(8,128)S(1)}, u32[]{:S(2)}, u32[]{:S(2)}) collective-permute-start(f32[136,768]{1,0:T(8,128)S(1)} %get-tuple-element.52), channel_id=1, source_target_pairs={{0,4},{2,6},{4,0},{6,2},{8,12},{10,14},{12,8},{14,10},{16,20},{18,... | collective-permute-start | bytes 1253384 | tf_op jit(solution)/shard_map/ppermute | solution.py:301
  133.6 18.8 %collective-permute-start.20 = (f32[136,768]{1,0:T(8,128)S(1)}, f32[136,768]{1,0:T(8,128)S(1)}, u32[]{:S(2)}, u32[]{:S(2)}) collective-permute-start(f32[136,768]{1,0:T(8,128)S(1)} %get-tuple-element.51), channel_id=1, source_target_pairs={{0,6},{2,4},{4,2},{6,0},{8,14},{10,12},{12,10},{14,8},{16,22},{18,... | collective-permute-start | bytes 1253384 | tf_op jit(solution)/shard_map/ppermute | solution.py:301
  154.9 2.0 %collective-permute-start.21 = (f32[384,384]{1,0:T(8,128)S(1)}, f32[384,384]{1,0:T(8,128)S(1)}, u32[]{:S(2)}, u32[]{:S(2)}) collective-permute-start(f32[384,384]{1,0:T(8,128)S(1)} %get-tuple-element.48), channel_id=1, source_target_pairs={{0,1},{1,0},{2,3},{3,2},{4,5},{5,4},{6,7},{7,6},{8,9},{9,8},{10,11... | collective-permute-start | bytes 1769480 | tf_op jit(solution)/shard_map/ppermute | solution.py:304
  157.0 7.7 %collective-permute-start.24 = (f32[96,384]{1,0:T(8,128)S(1)}, f32[96,384]{1,0:T(8,128)S(1)}, u32[]{:S(2)}, u32[]{:S(2)}) collective-permute-start(f32[96,384]{1,0:T(8,128)S(1)} %get-tuple-element.69), channel_id=1, source_target_pairs={{0,6},{2,4},{4,2},{6,0},{8,14},{10,12},{12,10},{14,8},{16,22},{18,... | collective-permute-start | bytes 442376 | tf_op jit(solution)/shard_map/ppermute | solution.py:301
  158.5 8.5 %collective-permute-start.23 = (f32[96,384]{1,0:T(8,128)S(1)}, f32[96,384]{1,0:T(8,128)S(1)}, u32[]{:S(2)}, u32[]{:S(2)}) collective-permute-start(f32[96,384]{1,0:T(8,128)S(1)} %get-tuple-element.70), channel_id=1, source_target_pairs={{0,4},{2,6},{4,0},{6,2},{8,12},{10,14},{12,8},{14,10},{16,20},{18,... | collective-permute-start | bytes 442376 | tf_op jit(solution)/shard_map/ppermute | solution.py:301
  159.7 7.4 %collective-permute-start.22 = (f32[96,384]{1,0:T(8,128)S(1)}, f32[96,384]{1,0:T(8,128)S(1)}, u32[]{:S(2)}, u32[]{:S(2)}) collective-permute-start(f32[96,384]{1,0:T(8,128)S(1)} %get-tuple-element.68), channel_id=1, source_target_pairs={{0,2},{2,0},{4,6},{6,4},{8,10},{10,8},{12,14},{14,12},{16,18},{18,... | collective-permute-start | bytes 442376 | tf_op jit(solution)/shard_map/ppermute | solution.py:301
  167.2 4.0 %collective-permute-start.27 = (f32[24,384]{1,0:T(8,128)S(1)}, f32[24,384]{1,0:T(8,128)S(1)}, u32[]{:S(2)}, u32[]{:S(2)}) collective-permute-start(f32[24,384]{1,0:T(8,128)S(1)} %get-tuple-element.76), channel_id=1, source_target_pairs={{0,24},{2,26},{4,28},{6,30},{8,0},{10,2},{12,4},{14,6},{16,8},{18,... | collective-permute-start | bytes 110600 | tf_op jit(solution)/shard_map/ppermute | solution.py:458
  169.2 5.1 %collective-permute-start.26 = (f32[24,384]{1,0:T(8,128)S(1)}, f32[24,384]{1,0:T(8,128)S(1)}, u32[]{:S(2)}, u32[]{:S(2)}) collective-permute-start(f32[24,384]{1,0:T(8,128)S(1)} %get-tuple-element.77), channel_id=1, source_target_pairs={{0,16},{2,18},{4,20},{6,22},{8,24},{10,26},{12,28},{14,30},{16,0},... | collective-permute-start | bytes 110600 | tf_op jit(solution)/shard_map/ppermute | solution.py:458
  169.2 5.8 %collective-permute-start.25 = (f32[24,384]{1,0:T(8,128)S(1)}, f32[24,384]{1,0:T(8,128)S(1)}, u32[]{:S(2)}, u32[]{:S(2)}) collective-permute-start(f32[24,384]{1,0:T(8,128)S(1)} %get-tuple-element.75), channel_id=1, source_target_pairs={{0,8},{2,10},{4,12},{6,14},{8,16},{10,18},{12,20},{14,22},{16,24},... | collective-permute-start | bytes 110600 | tf_op jit(solution)/shard_map/ppermute | solution.py:458
  175.0 5.8 %collective-permute-start.28 = (f32[24,384]{1,0:T(8,128)S(1)}, f32[24,384]{1,0:T(8,128)S(1)}, u32[]{:S(2)}, u32[]{:S(2)}) collective-permute-start(f32[24,384]{1,0:T(8,128)S(1)} %get-tuple-element.50), channel_id=1, source_target_pairs={{0,8},{2,10},{4,12},{6,14},{8,16},{10,18},{12,20},{14,22},{16,24},... | collective-permute-start | bytes 110600 | tf_op jit(solution)/shard_map/ppermute | solution.py:458
  175.2 5.7 %collective-permute-start.29 = (f32[24,384]{1,0:T(8,128)S(1)}, f32[24,384]{1,0:T(8,128)S(1)}, u32[]{:S(2)}, u32[]{:S(2)}) collective-permute-start(f32[24,384]{1,0:T(8,128)S(1)} %get-tuple-element.50), channel_id=1, source_target_pairs={{0,16},{2,18},{4,20},{6,22},{8,24},{10,26},{12,28},{14,30},{16,0},... | collective-permute-start | bytes 110600 | tf_op jit(solution)/shard_map/ppermute | solution.py:458
  176.3 5.1 %collective-permute-start.30 = (f32[24,384]{1,0:T(8,128)S(1)}, f32[24,384]{1,0:T(8,128)S(1)}, u32[]{:S(2)}, u32[]{:S(2)}) collective-permute-start(f32[24,384]{1,0:T(8,128)S(1)} %get-tuple-element.50), channel_id=1, source_target_pairs={{0,24},{2,26},{4,28},{6,30},{8,0},{10,2},{12,4},{14,6},{16,8},{18,... | collective-permute-start | bytes 110600 | tf_op jit(solution)/shard_map/ppermute | solution.py:458
  181.4 5.2 %collective-permute-start.31 = (f32[96,384]{1,0:T(8,128)S(1)}, f32[96,384]{1,0:T(8,128)S(1)}, u32[]{:S(2)}, u32[]{:S(2)}) collective-permute-start(f32[96,384]{1,0:T(8,128)S(1)} %constant_dynamic-update-slice_fusion.7), channel_id=1, source_target_pairs={{0,2},{2,0},{4,6},{6,4},{8,10},{10,8},{12,14},{14,12},{16,18},{18,... | collective-permute-start | bytes 442376 | tf_op jit(solution)/shard_map/ppermute | solution.py:301
  182.5 5.1 %collective-permute-start.32 = (f32[96,384]{1,0:T(8,128)S(1)}, f32[96,384]{1,0:T(8,128)S(1)}, u32[]{:S(2)}, u32[]{:S(2)}) collective-permute-start(f32[96,384]{1,0:T(8,128)S(1)} %constant_dynamic-update-slice_fusion.7), channel_id=1, source_target_pairs={{0,4},{2,6},{4,0},{6,2},{8,12},{10,14},{12,8},{14,10},{16,20},{18,... | collective-permute-start | bytes 442376 | tf_op jit(solution)/shard_map/ppermute | solution.py:301
  183.4 6.0 %collective-permute-start.33 = (f32[96,384]{1,0:T(8,128)S(1)}, f32[96,384]{1,0:T(8,128)S(1)}, u32[]{:S(2)}, u32[]{:S(2)}) collective-permute-start(f32[96,384]{1,0:T(8,128)S(1)} %constant_dynamic-update-slice_fusion.7), channel_id=1, source_target_pairs={{0,6},{2,4},{4,2},{6,0},{8,14},{10,12},{12,10},{14,8},{16,22},{18,... | collective-permute-start | bytes 442376 | tf_op jit(solution)/shard_map/ppermute | solution.py:301
  189.4 2.1 %collective-permute-start.34 = (f32[384,384]{1,0:T(8,128)S(1)}, f32[384,384]{1,0:T(8,128)S(1)}, u32[]{:S(2)}, u32[]{:S(2)}) collective-permute-start(f32[384,384]{1,0:T(8,128)S(1)} %constant_dynamic-update-slice_fusion.3), channel_id=1, source_target_pairs={{0,1},{1,0},{2,3},{3,2},{4,5},{5,4},{6,7},{7,6},{8,9},{9,8},{10,11... | collective-permute-start | bytes 1769480 | tf_op jit(solution)/shard_map/ppermute | solution.py:304

commit v8 on v7

--- a/solution.py
+++ b/solution.py
@@ -103,7 +103,7 @@
             pltpu.SemaphoreType.DMA((planes, group)),
             pltpu.SemaphoreType.DMA((planes, group)),
         ],
-        compiler_params=pltpu.CompilerParams(vmem_limit_bytes=28 << 20),
+        compiler_params=pltpu.CompilerParams(vmem_limit_bytes=26 << 20),
         cost_estimate=pl.CostEstimate(
             flops=4 * group * tokens * heads * count, bytes_accessed=16 << 20, transcendentals=0
         ),
@@ -333,7 +333,6 @@
 
     if short:
         own = [jnp.concatenate(pair, axis=0) for pair in zip(own, down_own)]
-        boxes = [jnp.concatenate([context, value], axis=1) for value in stay_own[1:]]
 
         def line(value, pairs):
             pairs = [(i * group + m, j * group + m) for i, j in pairs for m in members]
@@ -352,7 +351,8 @@
         rest = jnp.concatenate([to_member(own[s], s) for s in range(1, group)], axis=0)
 
         rest_one = step_one(rest)
-        _, boxes, own_two = lax.optimization_barrier((rest, boxes, own_two))
+        _, context, stay_own, own_two = lax.optimization_barrier((rest, context, stay_own, own_two))
+        boxes = [jnp.concatenate([context, value], axis=1) for value in stay_own[1:]]
         own_last = line(own_two[0], outward)
         arrived = [to_member(boxes[0], 1), to_member(boxes[1], 2)]
 

time: 193 us -> 193 us (level)
    unnamed x58 -> x60, local copies, waits for them, and re-layouts: 6.32 us -> 4.49 us
  transfers between devices with their start and end apart: 35 -> 35, of which waited for: 24 -> 23; matrix products, arithmetic and copies ran while one was open for 6% -> 6% of each run, Pallas kernels for 5% -> 5%
where the time goes in v8:
time: 193 us; the launch traced here: 192 us
  waiting for transfers between devices  115 us (60%)
  starting transfers between devices  38.5 us (20%)
  Pallas kernels  16.9 us (9%)
  local copies, waits for them, and re-layouts  11 us (6%)
  other arithmetic  8.87 us (5%)
    ppermute x10, waiting for transfers between devices, line(): return lax.ppermute(value, 'wide', pairs)  60 us
    ppermute x15, waiting for transfers between devices, to_member(): return lax.ppermute(value, 'wide', pairs) if s else value  38.6 us
    ppermute x15, starting transfers between devices, to_member(): return lax.ppermute(value, 'wide', pairs) if s else value  18.7 us
    ppermute x10, starting transfers between devices, line(): return lax.ppermute(value, 'wide', pairs)  13.5 us
    ppermute x4, waiting for transfers between devices, to_core(): lax.ppermute(value, 'narrow', [(i, i ^ t) for i in range(narrows)])  9.76 us
    pallas_call x1, Pallas kernels, attend(): pl.pallas_call(functools.partial(attend_kernel, rows, planes), grid=(2,),...  9.54 us
    ppermute x6, waiting for transfers between devices, shift(): lax.ppermute(value, 'wide', [(i, (i + k * group) % wides) for i in range(...  7 us
    ppermute x6, starting transfers between devices, shift(): lax.ppermute(value, 'wide', [(i, (i + k * group) % wides) for i in range(...  6.15 us
  transfers between devices with their start and end apart: 35, of which 23 were waited for; matrix products, arithmetic and copies ran while one was open for 6% of the time, Pallas kernels for 5%

profile of v8, /device:TPU:0, one launch (start us, length us, event | category | flops | bytes accessed | tf_op | source)
XLA Modules:
  0.0 192.0 jit_solution(16379721646161149740)
XLA Ops:
  0.7 1.0 dynamic-slice_bitcast_fusion
  1.7 1.3 constant_dynamic-slice_fusion.6
  3.1 3.1 %collective-permute-start.3 = (bf16[240,768]{1,0:T(8,128)(2,1)S(1)}, bf16[240,768]{1,0:T(8,128)(2,1)S(1)}, u32[]{:S(2)}, u32[]{:S(2)}) collective-permute-start(bf16[240,768]{1,0:T(8,128)(2,1)S(1)} %pad_maximum_fusion.4.refs_6_), channel_id=1, source_target_pairs={{8,0},{10,2},{12,4},{14,6},{16,24},{18,26},{20,28},{22,30},{0,8},{... | collective-permute-start | bytes 1105928 | tf_op jit(solution)/shard_map/ppermute | solution.py:339
  6.2 0.7 collective-permute-start.5
  6.9 0.7 copy-done.3
  7.6 1.6 collective-permute-start
  9.2 1.6 collective-permute-start.1
  11.4 3.4 %collective-permute-done.3.refs_8_ = bf16[240,768]{1,0:T(8,128)(2,1)S(1)} collective-permute-done((bf16[240,768]{1,0:T(8,128)(2,1)S(1)}, bf16[240,768]{1,0:T(8,128)(2,1)S(1)}, u32[]{:S(2)}, u32[]{:S(2)}) %collective-permute-start.3) | collective-permute-done | bytes 368672 | tf_op jit(solution)/shard_map/ppermute | solution.py:339
  14.8 0.7 collective-permute-start.4
  15.5 1.3 collective-permute-start.6
  16.8 0.9 constant_dynamic-slice_fusion.7
  17.7 1.5 collective-permute-done
  19.2 7.7 %collective-permute-done.1 = bf16[240,768]{1,0:T(8,128)(2,1)S(1)} collective-permute-done((bf16[240,768]{1,0:T(8,128)(2,1)S(1)}, bf16[240,768]{1,0:T(8,128)(2,1)S(1)}, u32[]{:S(2)}, u32[]{:S(2)}) %collective-permute-start.1) | collective-permute-done | bytes 368672 | tf_op jit(solution)/shard_map/ppermute | solution.py:301
  27.0 1.7 collective-permute-done.6.refs_14_
  29.5 1.6 collective-permute-start.7
  31.0 1.6 collective-permute-start.8
  32.6 1.5 collective-permute-start.9
  34.2 0.7 collective-permute-start.10
  34.9 1.3 collective-permute-start.11
  36.3 28.0 %collective-permute-done.11.refs_4_ = bf16[240,768]{1,0:T(8,128)(2,1)S(1)} collective-permute-done((bf16[240,768]{1,0:T(8,128)(2,1)S(1)}, bf16[240,768]{1,0:T(8,128)(2,1)S(1)}, u32[]{:S(2)}, u32[]{:S(2)}) %collective-permute-start.11) | collective-permute-done | bytes 368672 | tf_op jit(solution)/shard_map/ppermute | solution.py:339
  64.4 1.3 collective-permute-start.12
  65.6 1.7 collective-permute-start.13
  67.3 1.3 collective-permute-start.14
  68.8 0.8 slice.33.refs_4_
  69.5 4.0 %maximum_maximum_fusion = bf16[1024,1536]{1,0:T(8,128)(2,1)S(1)} fusion(bf16[256,1536]{1,0:T(8,128)(2,1)S(1)} %slice.31, bf16[256,1536]{1,0:T(8,128)(2,1)S(1)} %slice.30, bf16[256,1536]{1,0:T(8,128)(2,1)S(1)} %copy-done.25, bf16[1024]{0:T(1024)(128)(2,1)S(1)} %pad.3.clone), kind=kLoop, calls=%fused_computation | loop fusion | flops 12582912 | bytes 5507072 | tf_op jit(solution)/shard_map/concatenate | solution.py:363
  73.5 18.4 %collective-permute-done.14.refs_15_ = bf16[720,768]{1,0:T(8,128)(2,1)S(1)} collective-permute-done((bf16[720,768]{1,0:T(8,128)(2,1)S(1)}, bf16[720,768]{1,0:T(8,128)(2,1)S(1)}, u32[]{:S(2)}, u32[]{:S(2)}) %collective-permute-start.14) | collective-permute-done | bytes 1105952 | tf_op jit(solution)/shard_map/ppermute | solution.py:339
  92.0 0.9 copy-done.13
  93.4 1.3 collective-permute-start.16
  94.7 0.8 dynamic_slice.79
  95.5 1.0 slice.35.refs_5_
  96.5 2.2 %collective-permute-done.15 = bf16[1024,1536]{1,0:T(8,128)(2,1)} collective-permute-done((bf16[1024,1536]{1,0:T(8,128)(2,1)S(1)}, bf16[1024,1536]{1,0:T(8,128)(2,1)}, u32[]{:S(2)}, u32[]{:S(2)}) %collective-permute-start.15) | collective-permute-done | bytes 3145760 | tf_op jit(solution)/shard_map/ppermute | solution.py:304
  98.8 3.3 %dynamic-slice_select_fusion = bf16[4,256,768]{2,1,0:T(8,128)(2,1)S(1)} fusion(bf16[4,256,1536]{2,1,0:T(8,128)(2,1)} %bitcast.5.refs_1_, s32[]{:T(128)S(6)} %select_n.150, bf16[4,256,1536]{2,1,0:T(8,128)(2,1)S(1)} %bitcast.14, pred[]{:T(512)S(6)} %eq.22), kind=kLoop, calls=%fused_computation.1 | loop fusion | flops 786432 | bytes 4718597 | tf_op jit(solution)/shard_map/jit(_where)/select_n | solution.py:377
  102.3 0.8 copy-done
  103.9 9.5 %shard_map.103 = (f32[1024,768]{1,0:T(8,128)S(1)}, bf16[768,768]{1,0:T(8,128)(2,1)S(1)}) custom-call(bf16[4,256,1536]{2,1,0:T(8,128)(2,1)S(1)} %bitcast.15, bf16[4,256,1536]{2,1,0:T(8,128)(2,1)} %bitcast.5.refs_1_, bf16[256,768]{1,0:T(8,128)(2,1)S(1)} %copy-done.2, bf16[256,768]{1,0:T(8,128)(2,1)S(1)} %slice.32.refs_3_, bf16[256,768]{1,0:T(8,128)(2,1)S(1)} %copy-done, ...), custom_call_target="tpu_custom_call" | custom-call | flops 4831838208 | bytes 16777216 | tf_op jit(solution)/shard_map/pallas_call | solution.py:87
  113.4 8.5 %collective-permute-done.16.refs_5_ = bf16[720,768]{1,0:T(8,128)(2,1)} collective-permute-done((bf16[720,768]{1,0:T(8,128)(2,1)}, bf16[720,768]{1,0:T(8,128)(2,1)}, u32[]{:S(2)}, u32[]{:S(2)}) %collective-permute-start.16) | collective-permute-done | bytes 1105952 | tf_op jit(solution)/shard_map/ppermute | solution.py:339
  122.0 5.0 %shard_map.104 = (f32[544,768]{1,0:T(8,128)S(1)}, f32[544,768]{1,0:T(8,128)S(1)}) custom-call(f32[1024,768]{1,0:T(8,128)S(1)} %get-tuple-element.45.refs_0_, bf16[1024,768]{1,0:T(8,128)(2,1)S(1)} %bitcast.16, bf16[1,768]{1,0:T(2,128)(2,1)S(1)} %broadcast_in_dim.13.refs_2_, bf16[768,768]{1,0:T(8,128)(2,1)S(1)} %get-tuple-element.46.refs_3_, ...), custom_call_target="tpu_custom_call" | custom-call | flops 2415919104 | bytes 16777216 | tf_op jit(solution)/shard_map/pallas_call | solution.py:191
  127.0 3.5 %collective-permute-done.17 = f32[544,768]{1,0:T(8,128)S(1)} collective-permute-done((f32[544,768]{1,0:T(8,128)S(1)}, f32[544,768]{1,0:T(8,128)S(1)}, u32[]{:S(2)}, u32[]{:S(2)}) %collective-permute-start.17) | collective-permute-done | bytes 1671200 | tf_op jit(solution)/shard_map/ppermute | solution.py:304
  130.9 1.9 collective-permute-start.18
  133.0 1.4 collective-permute-start.20
  134.5 9.0 %collective-permute-done.18.refs_1_ = f32[136,768]{1,0:T(8,128)S(1)} collective-permute-done((f32[136,768]{1,0:T(8,128)S(1)}, f32[136,768]{1,0:T(8,128)S(1)}, u32[]{:S(2)}, u32[]{:S(2)}) %collective-permute-start.18) | collective-permute-done | bytes 417824 | tf_op jit(solution)/shard_map/ppermute | solution.py:301
  143.5 9.7 %collective-permute-done.19.refs_2_ = f32[136,768]{1,0:T(8,128)S(1)} collective-permute-done((f32[136,768]{1,0:T(8,128)S(1)}, f32[136,768]{1,0:T(8,128)S(1)}, u32[]{:S(2)}, u32[]{:S(2)}) %collective-permute-start.19) | collective-permute-done | bytes 417824 | tf_op jit(solution)/shard_map/ppermute | solution.py:301
  153.2 2.4 %shard_map.105 = (f32[128,768]{1,0:T(8,128)}, f32[384,384]{1,0:T(8,128)S(1)}, f32[384,384]{1,0:T(8,128)S(1)}) custom-call(f32[136,768]{1,0:T(8,128)S(1)} %get-tuple-element.58.refs_0_, f32[136,768]{1,0:T(8,128)S(1)} %collective-permute-done.18.refs_1_, f32[136,768]{1,0:T(8,128)S(1)} %collective-permute-done.19.refs_2_, ...), custom_call_target="tpu_custom_call" | custom-call | flops 452984832 | bytes 5242880 | tf_op jit(solution)/shard_map/pallas_call | solution.py:277
  155.5 2.0 %collective-permute-done.21 = f32[384,384]{1,0:T(8,128)S(1)} collective-permute-done((f32[384,384]{1,0:T(8,128)S(1)}, f32[384,384]{1,0:T(8,128)S(1)}, u32[]{:S(2)}, u32[]{:S(2)}) %collective-permute-start.21) | collective-permute-done | bytes 589856 | tf_op jit(solution)/shard_map/ppermute | solution.py:304
  157.6 1.2 collective-permute-start.24
  158.9 0.7 collective-permute-start.23
  159.5 1.7 collective-permute-start.22
  161.2 4.1 %collective-permute-done.24 = f32[96,384]{1,0:T(8,128)S(1)} collective-permute-done((f32[96,384]{1,0:T(8,128)S(1)}, f32[96,384]{1,0:T(8,128)S(1)}, u32[]{:S(2)}, u32[]{:S(2)}) %collective-permute-start.24) | collective-permute-done | bytes 147488 | tf_op jit(solution)/shard_map/ppermute | solution.py:301
  165.3 2.3 %collective-permute-done.23 = f32[96,384]{1,0:T(8,128)S(1)} collective-permute-done((f32[96,384]{1,0:T(8,128)S(1)}, f32[96,384]{1,0:T(8,128)S(1)}, u32[]{:S(2)}, u32[]{:S(2)}) %collective-permute-start.23) | collective-permute-done | bytes 147488 | tf_op jit(solution)/shard_map/ppermute | solution.py:301
  167.7 1.0 collective-permute-start.27
  168.7 1.0 collective-permute-start.25
  169.8 1.9 %collective-permute-done.27 = f32[24,384]{1,0:T(8,128)S(1)} collective-permute-done((f32[24,384]{1,0:T(8,128)S(1)}, f32[24,384]{1,0:T(8,128)S(1)}, u32[]{:S(2)}, u32[]{:S(2)}) %collective-permute-start.27) | collective-permute-done | bytes 36896 | tf_op jit(solution)/shard_map/ppermute | solution.py:458
  171.7 1.9 %collective-permute-done.26 = f32[24,384]{1,0:T(8,128)S(1)} collective-permute-done((f32[24,384]{1,0:T(8,128)S(1)}, f32[24,384]{1,0:T(8,128)S(1)}, u32[]{:S(2)}, u32[]{:S(2)}) %collective-permute-start.26) | collective-permute-done | bytes 36896 | tf_op jit(solution)/shard_map/ppermute | solution.py:458
  173.6 0.9 collective-permute-done.25
  174.7 2.0 %collective-permute-start.29 = (f32[24,384]{1,0:T(8,128)S(1)}, f32[24,384]{1,0:T(8,128)S(1)}, u32[]{:S(2)}, u32[]{:S(2)}) collective-permute-start(f32[24,384]{1,0:T(8,128)S(1)} %get-tuple-element.54), channel_id=1, source_target_pairs={{0,16},{2,18},{4,20},{6,22},{8,24},{10,26},{12,28},{14,30},{16,0},... | collective-permute-start | bytes 110600 | tf_op jit(solution)/shard_map/ppermute | solution.py:458
  176.7 1.9 collective-permute-start.30
  178.6 1.7 collective-permute-done.28
  180.9 1.0 collective-permute-start.31
  181.9 0.8 collective-permute-start.32
  182.8 1.6 collective-permute-start.33
  184.5 1.6 collective-permute-done.31
  186.1 0.9 collective-permute-done.32
  187.1 1.7 collective-permute-done.33
  188.9 2.0 %collective-permute-done.34 = f32[384,384]{1,0:T(8,128)S(1)} collective-permute-done((f32[384,384]{1,0:T(8,128)S(1)}, f32[384,384]{1,0:T(8,128)S(1)}, u32[]{:S(2)}, u32[]{:S(2)}) %collective-permute-start.34) | collective-permute-done | bytes 589856 | tf_op jit(solution)/shard_map/ppermute | solution.py:304
  190.9 1.1 broadcast_select_fusion
  (110 shorter events, 5.0 us)
Async XLA Ops:
  3.0 13.7 %copy-start.26 = (bf16[256,3072]{1,0:T(8,128)(2,1)S(1)}, bf16[256,3072]{1,0:T(8,128)(2,1)}, u32[]{:S(2)}) copy-start(bf16[256,3072]{1,0:T(8,128)(2,1)} %param.10) | copy-start | bytes 4718596
  3.1 11.7 %collective-permute-start.3 = (bf16[240,768]{1,0:T(8,128)(2,1)S(1)}, bf16[240,768]{1,0:T(8,128)(2,1)S(1)}, u32[]{:S(2)}, u32[]{:S(2)}) collective-permute-start(bf16[240,768]{1,0:T(8,128)(2,1)S(1)} %pad_maximum_fusion.4.refs_6_), channel_id=1, source_target_pairs={{8,0},{10,2},{12,4},{14,6},{16,24},{18,26},{20,28},{22,30},{0,8},{... | collective-permute-start | bytes 1105928 | tf_op jit(solution)/shard_map/ppermute | solution.py:339
  6.2 9.3 %collective-permute-start.5 = (bf16[240,768]{1,0:T(8,128)(2,1)S(1)}, bf16[240,768]{1,0:T(8,128)(2,1)S(1)}, u32[]{:S(2)}, u32[]{:S(2)}) collective-permute-start(bf16[240,768]{1,0:T(8,128)(2,1)S(1)} %pad_maximum_fusion.4.refs_6_), channel_id=1, source_target_pairs={{8,16},{10,18},{12,20},{14,22},{16,8},{18,10},{20,12},{22,14},{9,1... | collective-permute-start | bytes 1105928 | tf_op jit(solution)/shard_map/ppermute | solution.py:339
  6.8 0.7 copy-start.3
  7.6 11.6 %collective-permute-start = (bf16[240,768]{1,0:T(8,128)(2,1)S(1)}, bf16[240,768]{1,0:T(8,128)(2,1)S(1)}, u32[]{:S(2)}, u32[]{:S(2)}) collective-permute-start(bf16[240,768]{1,0:T(8,128)(2,1)S(1)} %pad_maximum_fusion.1), channel_id=1, source_target_pairs={{0,2},{2,0},{4,6},{6,4},{8,10},{10,8},{12,14},{14,12},{16,18},{18,... | collective-permute-start | bytes 1105928 | tf_op jit(solution)/shard_map/ppermute | solution.py:301
  9.2 17.7 %collective-permute-start.1 = (bf16[240,768]{1,0:T(8,128)(2,1)S(1)}, bf16[240,768]{1,0:T(8,128)(2,1)S(1)}, u32[]{:S(2)}, u32[]{:S(2)}) collective-permute-start(bf16[240,768]{1,0:T(8,128)(2,1)S(1)} %pad_maximum_fusion.2), channel_id=1, source_target_pairs={{0,4},{2,6},{4,0},{6,2},{8,12},{10,14},{12,8},{14,10},{16,20},{18,... | collective-permute-start | bytes 1105928 | tf_op jit(solution)/shard_map/ppermute | solution.py:301
  10.8 16.2 %collective-permute-start.2 = (bf16[240,768]{1,0:T(8,128)(2,1)S(1)}, bf16[240,768]{1,0:T(8,128)(2,1)S(1)}, u32[]{:S(2)}, u32[]{:S(2)}) collective-permute-start(bf16[240,768]{1,0:T(8,128)(2,1)S(1)} %pad_maximum_fusion.3), channel_id=1, source_target_pairs={{0,6},{2,4},{4,2},{6,0},{8,14},{10,12},{12,10},{14,8},{16,22},{18,... | collective-permute-start | bytes 1105928 | tf_op jit(solution)/shard_map/ppermute | solution.py:301
  14.7 2.9 %copy-start.15 = (bf16[240,768]{1,0:T(8,128)(2,1)}, bf16[240,768]{1,0:T(8,128)(2,1)S(1)}, u32[]{:S(2)}) copy-start(bf16[240,768]{1,0:T(8,128)(2,1)S(1)} %collective-permute-done.3.refs_8_) | copy-start | bytes 1105924
  14.8 12.3 %collective-permute-start.4 = (bf16[240,768]{1,0:T(8,128)(2,1)S(1)}, bf16[240,768]{1,0:T(8,128)(2,1)S(1)}, u32[]{:S(2)}, u32[]{:S(2)}) collective-permute-start(bf16[240,768]{1,0:T(8,128)(2,1)S(1)} %collective-permute-done.3.refs_8_), channel_id=1, source_target_pairs={{8,16},{10,18},{12,20},{14,22},{16,8},{18,10},{20,12},{22,14},{9,1... | collective-permute-start | bytes 1105928 | tf_op jit(solution)/shard_map/ppermute | solution.py:339
  15.4 2.2 %copy-start.17 = (bf16[240,768]{1,0:T(8,128)(2,1)}, bf16[240,768]{1,0:T(8,128)(2,1)S(1)}, u32[]{:S(2)}) copy-start(bf16[240,768]{1,0:T(8,128)(2,1)S(1)} %collective-permute-done.5.refs_10_) | copy-start | bytes 1105924
  15.5 13.3 %collective-permute-start.6 = (bf16[240,768]{1,0:T(8,128)(2,1)S(1)}, bf16[240,768]{1,0:T(8,128)(2,1)S(1)}, u32[]{:S(2)}, u32[]{:S(2)}) collective-permute-start(bf16[240,768]{1,0:T(8,128)(2,1)S(1)} %collective-permute-done.5.refs_10_), channel_id=1, source_target_pairs={{8,0},{10,2},{12,4},{14,6},{16,24},{18,26},{20,28},{22,30},{9,1},{... | collective-permute-start | bytes 1105928 | tf_op jit(solution)/shard_map/ppermute | solution.py:339
  17.7 11.0 %copy-start.25 = (bf16[256,1536]{1,0:T(8,128)(2,1)S(1)}, bf16[256,1536]{1,0:T(8,128)(2,1)}, u32[]{:S(2)}) copy-start(bf16[256,1536]{1,0:T(8,128)(2,1)} %param.8) | copy-start | bytes 2359300
  27.0 7.2 %copy-start.7 = (bf16[720,768]{1,0:T(8,128)(2,1)}, bf16[720,768]{1,0:T(8,128)(2,1)S(1)}, u32[]{:S(2)}) copy-start(bf16[720,768]{1,0:T(8,128)(2,1)S(1)} %constant_dynamic-update-slice_fusion.refs_7_) | copy-start | bytes 3317764
  27.0 7.9 %copy-start.19 = (bf16[240,768]{1,0:T(8,128)(2,1)}, bf16[240,768]{1,0:T(8,128)(2,1)S(1)}, u32[]{:S(2)}) copy-start(bf16[240,768]{1,0:T(8,128)(2,1)S(1)} %collective-permute-done.4.refs_12_) | copy-start | bytes 1105924
  28.7 0.7 copy-start.21
  29.5 34.9 %collective-permute-start.7 = (bf16[256,2304]{1,0:T(8,128)(2,1)S(1)}, bf16[256,2304]{1,0:T(8,128)(2,1)S(1)}, u32[]{:S(2)}, u32[]{:S(2)}) collective-permute-start(bf16[256,2304]{1,0:T(8,128)(2,1)S(1)} %constant_dynamic-update-slice_fusion.3), channel_id=1, source_target_pairs={{0,2},{2,0},{4,6},{6,4},{8,10},{10,8},{12,14},{14,12},{16,18},{18,... | collective-permute-start | bytes 3538952 | tf_op jit(solution)/shard_map/ppermute | solution.py:301
  31.0 33.3 %collective-permute-start.8 = (bf16[256,2304]{1,0:T(8,128)(2,1)S(1)}, bf16[256,2304]{1,0:T(8,128)(2,1)S(1)}, u32[]{:S(2)}, u32[]{:S(2)}) collective-permute-start(bf16[256,2304]{1,0:T(8,128)(2,1)S(1)} %constant_dynamic-update-slice_fusion.5), channel_id=1, source_target_pairs={{0,4},{2,6},{4,0},{6,2},{8,12},{10,14},{12,8},{14,10},{16,20},{18,... | collective-permute-start | bytes 3538952 | tf_op jit(solution)/shard_map/ppermute | solution.py:301
  32.6 31.7 %collective-permute-start.9 = (bf16[720,768]{1,0:T(8,128)(2,1)S(1)}, bf16[720,768]{1,0:T(8,128)(2,1)S(1)}, u32[]{:S(2)}, u32[]{:S(2)}) collective-permute-start(bf16[720,768]{1,0:T(8,128)(2,1)S(1)} %constant_dynamic-update-slice_fusion.refs_7_), channel_id=1, source_target_pairs={{8,0},{10,2},{12,4},{14,6},{16,24},{18,26},{20,28},{22,30},{0,8},{... | collective-permute-start | bytes 3317768 | tf_op jit(solution)/shard_map/ppermute | solution.py:339
  34.2 30.1 %collective-permute-start.10 = (bf16[720,768]{1,0:T(8,128)(2,1)S(1)}, bf16[720,768]{1,0:T(8,128)(2,1)S(1)}, u32[]{:S(2)}, u32[]{:S(2)}) collective-permute-start(bf16[720,768]{1,0:T(8,128)(2,1)S(1)} %constant_dynamic-update-slice_fusion.refs_7_), channel_id=1, source_target_pairs={{8,16},{10,18},{12,20},{14,22},{16,8},{18,10},{20,12},{22,14},{9,1... | collective-permute-start | bytes 3317768 | tf_op jit(solution)/shard_map/ppermute | solution.py:339
  34.9 29.4 %collective-permute-start.11 = (bf16[240,768]{1,0:T(8,128)(2,1)S(1)}, bf16[240,768]{1,0:T(8,128)(2,1)S(1)}, u32[]{:S(2)}, u32[]{:S(2)}) collective-permute-start(bf16[240,768]{1,0:T(8,128)(2,1)S(1)} %collective-permute-done.4.refs_12_), channel_id=1, source_target_pairs={{8,0},{10,2},{12,4},{14,6},{16,24},{18,26},{20,28},{22,30},{9,1},{... | collective-permute-start | bytes 1105928 | tf_op jit(solution)/shard_map/ppermute | solution.py:339
  64.3 4.4 %copy-start.23 = (bf16[240,768]{1,0:T(8,128)(2,1)}, bf16[240,768]{1,0:T(8,128)(2,1)S(1)}, u32[]{:S(2)}) copy-start(bf16[240,768]{1,0:T(8,128)(2,1)S(1)} %collective-permute-done.11.refs_4_) | copy-start | bytes 1105924
  64.3 4.4 %copy-start.9 = (bf16[720,768]{1,0:T(8,128)(2,1)}, bf16[720,768]{1,0:T(8,128)(2,1)S(1)}, u32[]{:S(2)}) copy-start(bf16[720,768]{1,0:T(8,128)(2,1)S(1)} %collective-permute-done.9.refs_9_) | copy-start | bytes 3317764
  64.3 4.4 %copy-start.11 = (bf16[720,768]{1,0:T(8,128)(2,1)}, bf16[720,768]{1,0:T(8,128)(2,1)S(1)}, u32[]{:S(2)}) copy-start(bf16[720,768]{1,0:T(8,128)(2,1)S(1)} %collective-permute-done.10.refs_11_) | copy-start | bytes 3317764
  64.4 27.6 %collective-permute-start.12 = (bf16[256,2304]{1,0:T(8,128)(2,1)S(1)}, bf16[256,2304]{1,0:T(8,128)(2,1)S(1)}, u32[]{:S(2)}, u32[]{:S(2)}) collective-permute-start(bf16[256,2304]{1,0:T(8,128)(2,1)S(1)} %pad_maximum_fusion), channel_id=1, source_target_pairs={{0,6},{2,4},{4,2},{6,0},{8,14},{10,12},{12,10},{14,8},{16,22},{18,... | collective-permute-start | bytes 3538952 | tf_op jit(solution)/shard_map/ppermute | solution.py:301
  65.6 7.9 %collective-permute-start.13 = (bf16[720,768]{1,0:T(8,128)(2,1)S(1)}, bf16[720,768]{1,0:T(8,128)(2,1)}, u32[]{:S(2)}, u32[]{:S(2)}) collective-permute-start(bf16[720,768]{1,0:T(8,128)(2,1)S(1)} %collective-permute-done.9.refs_9_), channel_id=1, source_target_pairs={{8,16},{10,18},{12,20},{14,22},{16,8},{18,10},{20,12},{22,14},{9,1... | collective-permute-start | bytes 3317768 | tf_op jit(solution)/shard_map/ppermute | solution.py:339
  67.3 24.7 %collective-permute-start.14 = (bf16[720,768]{1,0:T(8,128)(2,1)S(1)}, bf16[720,768]{1,0:T(8,128)(2,1)S(1)}, u32[]{:S(2)}, u32[]{:S(2)}) collective-permute-start(bf16[720,768]{1,0:T(8,128)(2,1)S(1)} %collective-permute-done.10.refs_11_), channel_id=1, source_target_pairs={{8,0},{10,2},{12,4},{14,6},{16,24},{18,26},{20,28},{22,30},{9,1},{... | collective-permute-start | bytes 3317768 | tf_op jit(solution)/shard_map/ppermute | solution.py:339
  92.0 1.0 copy-start.13
  92.0 1.4 copy-start.27
  92.9 5.8 %collective-permute-start.15 = (bf16[1024,1536]{1,0:T(8,128)(2,1)S(1)}, bf16[1024,1536]{1,0:T(8,128)(2,1)}, u32[]{:S(2)}, u32[]{:S(2)}) collective-permute-start(bf16[1024,1536]{1,0:T(8,128)(2,1)S(1)} %slice_dynamic-update-slice_fusion), channel_id=1, source_target_pairs={{0,1},{1,0},{2,3},{3,2},{4,5},{5,4},{6,7},{7,6},{8,9},{9,8},{10,11... | collective-permute-start | bytes 9437192 | tf_op jit(solution)/shard_map/ppermute | solution.py:304
  93.4 28.6 %collective-permute-start.16 = (bf16[720,768]{1,0:T(8,128)(2,1)}, bf16[720,768]{1,0:T(8,128)(2,1)}, u32[]{:S(2)}, u32[]{:S(2)}) collective-permute-start(bf16[720,768]{1,0:T(8,128)(2,1)} %collective-permute-done.13.refs_13_), channel_id=1, source_target_pairs={{8,0},{10,2},{12,4},{14,6},{16,24},{18,26},{20,28},{22,30},{9,1},{... | collective-permute-start | bytes 3317768 | tf_op jit(solution)/shard_map/ppermute | solution.py:339
  98.7 3.5 %copy-start.10 = (bf16[720,768]{1,0:T(8,128)(2,1)S(1)}, bf16[720,768]{1,0:T(8,128)(2,1)}, u32[]{:S(2)}) copy-start(bf16[720,768]{1,0:T(8,128)(2,1)} %copy-done.9) | copy-start | bytes 3317764
  98.7 3.6 %copy-start.12 = (bf16[720,768]{1,0:T(8,128)(2,1)S(1)}, bf16[720,768]{1,0:T(8,128)(2,1)}, u32[]{:S(2)}) copy-start(bf16[720,768]{1,0:T(8,128)(2,1)} %copy-done.11) | copy-start | bytes 3317764
  98.7 3.6 %copy-start.14 = (bf16[720,768]{1,0:T(8,128)(2,1)S(1)}, bf16[720,768]{1,0:T(8,128)(2,1)}, u32[]{:S(2)}) copy-start(bf16[720,768]{1,0:T(8,128)(2,1)} %copy-done.13) | copy-start | bytes 3317764
  98.7 3.6 %copy-start.20 = (bf16[240,768]{1,0:T(8,128)(2,1)S(1)}, bf16[240,768]{1,0:T(8,128)(2,1)}, u32[]{:S(2)}) copy-start(bf16[240,768]{1,0:T(8,128)(2,1)} %copy-done.19) | copy-start | bytes 1105924
  98.8 3.6 %copy-start.22 = (bf16[240,768]{1,0:T(8,128)(2,1)S(1)}, bf16[240,768]{1,0:T(8,128)(2,1)}, u32[]{:S(2)}) copy-start(bf16[240,768]{1,0:T(8,128)(2,1)} %copy-done.21) | copy-start | bytes 1105924
  102.1 1.0 copy-start
  102.1 1.1 copy-start.2
  102.1 1.2 copy-start.4
  102.1 1.6 copy-start.8
  102.1 1.6 copy-start.16
  102.2 1.7 copy-start.18
  103.9 18.1 %copy-start.24 = (bf16[240,768]{1,0:T(8,128)(2,1)S(1)}, bf16[240,768]{1,0:T(8,128)(2,1)}, u32[]{:S(2)}) copy-start(bf16[240,768]{1,0:T(8,128)(2,1)} %copy-done.23) | copy-start | bytes 1105924
  126.9 3.6 %collective-permute-start.17 = (f32[544,768]{1,0:T(8,128)S(1)}, f32[544,768]{1,0:T(8,128)S(1)}, u32[]{:S(2)}, u32[]{:S(2)}) collective-permute-start(f32[544,768]{1,0:T(8,128)S(1)} %get-tuple-element.49), channel_id=1, source_target_pairs={{0,1},{1,0},{2,3},{3,2},{4,5},{5,4},{6,7},{7,6},{8,9},{9,8},{10,11... | collective-permute-start | bytes 5013512 | tf_op jit(solution)/shard_map/ppermute | solution.py:304
  130.8 22.4 %copy-start.1 = (f32[128,768]{1,0:T(8,128)S(1)}, f32[128,768]{1,0:T(8,128)}, u32[]{:S(2)}) copy-start(f32[128,768]{1,0:T(8,128)} %refs_6_.1) | copy-start | bytes 1179652
  130.8 22.4 %copy-start.5 = (bf16[384,384]{1,0:T(8,128)(2,1)S(1)}, bf16[384,384]{1,0:T(8,128)(2,1)}, u32[]{:S(2)}) copy-start(bf16[384,384]{1,0:T(8,128)(2,1)} %refs_4_.1) | copy-start | bytes 884740
  130.8 22.4 %copy-start.6 = (bf16[384,384]{1,0:T(8,128)(2,1)S(1)}, bf16[384,384]{1,0:T(8,128)(2,1)}, u32[]{:S(2)}) copy-start(bf16[384,384]{1,0:T(8,128)(2,1)} %refs_5_.1) | copy-start | bytes 884740
  130.9 12.5 %collective-permute-start.18 = (f32[136,768]{1,0:T(8,128)S(1)}, f32[136,768]{1,0:T(8,128)S(1)}, u32[]{:S(2)}, u32[]{:S(2)}) collective-permute-start(f32[136,768]{1,0:T(8,128)S(1)} %get-tuple-element.57), channel_id=1, source_target_pairs={{0,2},{2,0},{4,6},{6,4},{8,10},{10,8},{12,14},{14,12},{16,18},{18,... | collective-permute-start | bytes 1253384 | tf_op jit(solution)/shard_map/ppermute | solution.py:301
  132.8 20.4 %collective-permute-start.19 = (f32[136,768]{1,0:T(8,128)S(1)}, f32[136,768]{1,0:T(8,128)S(1)}, u32[]{:S(2)}, u32[]{:S(2)}) collective-permute-start(f32[136,768]{1,0:T(8,128)S(1)} %get-tuple-element.56), channel_id=1, source_target_pairs={{0,4},{2,6},{4,0},{6,2},{8,12},{10,14},{12,8},{14,10},{16,20},{18,... | collective-permute-start | bytes 1253384 | tf_op jit(solution)/shard_map/ppermute | solution.py:301
  133.0 20.1 %collective-permute-start.20 = (f32[136,768]{1,0:T(8,128)S(1)}, f32[136,768]{1,0:T(8,128)S(1)}, u32[]{:S(2)}, u32[]{:S(2)}) collective-permute-start(f32[136,768]{1,0:T(8,128)S(1)} %get-tuple-element.55), channel_id=1, source_target_pairs={{0,6},{2,4},{4,2},{6,0},{8,14},{10,12},{12,10},{14,8},{16,22},{18,... | collective-permute-start | bytes 1253384 | tf_op jit(solution)/shard_map/ppermute | solution.py:301
  155.5 2.0 %collective-permute-start.21 = (f32[384,384]{1,0:T(8,128)S(1)}, f32[384,384]{1,0:T(8,128)S(1)}, u32[]{:S(2)}, u32[]{:S(2)}) collective-permute-start(f32[384,384]{1,0:T(8,128)S(1)} %get-tuple-element.52), channel_id=1, source_target_pairs={{0,1},{1,0},{2,3},{3,2},{4,5},{5,4},{6,7},{7,6},{8,9},{9,8},{10,11... | collective-permute-start | bytes 1769480 | tf_op jit(solution)/shard_map/ppermute | solution.py:304
  157.6 7.7 %collective-permute-start.24 = (f32[96,384]{1,0:T(8,128)S(1)}, f32[96,384]{1,0:T(8,128)S(1)}, u32[]{:S(2)}, u32[]{:S(2)}) collective-permute-start(f32[96,384]{1,0:T(8,128)S(1)} %get-tuple-element.70), channel_id=1, source_target_pairs={{0,6},{2,4},{4,2},{6,0},{8,14},{10,12},{12,10},{14,8},{16,22},{18,... | collective-permute-start | bytes 442376 | tf_op jit(solution)/shard_map/ppermute | solution.py:301
  158.9 8.8 %collective-permute-start.23 = (f32[96,384]{1,0:T(8,128)S(1)}, f32[96,384]{1,0:T(8,128)S(1)}, u32[]{:S(2)}, u32[]{:S(2)}) collective-permute-start(f32[96,384]{1,0:T(8,128)S(1)} %get-tuple-element.71), channel_id=1, source_target_pairs={{0,4},{2,6},{4,0},{6,2},{8,12},{10,14},{12,8},{14,10},{16,20},{18,... | collective-permute-start | bytes 442376 | tf_op jit(solution)/shard_map/ppermute | solution.py:301
  159.5 8.1 %collective-permute-start.22 = (f32[96,384]{1,0:T(8,128)S(1)}, f32[96,384]{1,0:T(8,128)S(1)}, u32[]{:S(2)}, u32[]{:S(2)}) collective-permute-start(f32[96,384]{1,0:T(8,128)S(1)} %get-tuple-element.69), channel_id=1, source_target_pairs={{0,2},{2,0},{4,6},{6,4},{8,10},{10,8},{12,14},{14,12},{16,18},{18,... | collective-permute-start | bytes 442376 | tf_op jit(solution)/shard_map/ppermute | solution.py:301
  167.7 4.0 %collective-permute-start.27 = (f32[24,384]{1,0:T(8,128)S(1)}, f32[24,384]{1,0:T(8,128)S(1)}, u32[]{:S(2)}, u32[]{:S(2)}) collective-permute-start(f32[24,384]{1,0:T(8,128)S(1)} %get-tuple-element.77), channel_id=1, source_target_pairs={{0,24},{2,26},{4,28},{6,30},{8,0},{10,2},{12,4},{14,6},{16,8},{18,... | collective-permute-start | bytes 110600 | tf_op jit(solution)/shard_map/ppermute | solution.py:458
  168.7 4.9 %collective-permute-start.26 = (f32[24,384]{1,0:T(8,128)S(1)}, f32[24,384]{1,0:T(8,128)S(1)}, u32[]{:S(2)}, u32[]{:S(2)}) collective-permute-start(f32[24,384]{1,0:T(8,128)S(1)} %get-tuple-element.78), channel_id=1, source_target_pairs={{0,16},{2,18},{4,20},{6,22},{8,24},{10,26},{12,28},{14,30},{16,0},... | collective-permute-start | bytes 110600 | tf_op jit(solution)/shard_map/ppermute | solution.py:458
  168.7 5.8 %collective-permute-start.25 = (f32[24,384]{1,0:T(8,128)S(1)}, f32[24,384]{1,0:T(8,128)S(1)}, u32[]{:S(2)}, u32[]{:S(2)}) collective-permute-start(f32[24,384]{1,0:T(8,128)S(1)} %get-tuple-element.76), channel_id=1, source_target_pairs={{0,8},{2,10},{4,12},{6,14},{8,16},{10,18},{12,20},{14,22},{16,24},... | collective-permute-start | bytes 110600 | tf_op jit(solution)/shard_map/ppermute | solution.py:458
  174.5 5.8 %collective-permute-start.28 = (f32[24,384]{1,0:T(8,128)S(1)}, f32[24,384]{1,0:T(8,128)S(1)}, u32[]{:S(2)}, u32[]{:S(2)}) collective-permute-start(f32[24,384]{1,0:T(8,128)S(1)} %get-tuple-element.54), channel_id=1, source_target_pairs={{0,8},{2,10},{4,12},{6,14},{8,16},{10,18},{12,20},{14,22},{16,24},... | collective-permute-start | bytes 110600 | tf_op jit(solution)/shard_map/ppermute | solution.py:458
  174.7 5.6 %collective-permute-start.29 = (f32[24,384]{1,0:T(8,128)S(1)}, f32[24,384]{1,0:T(8,128)S(1)}, u32[]{:S(2)}, u32[]{:S(2)}) collective-permute-start(f32[24,384]{1,0:T(8,128)S(1)} %get-tuple-element.54), channel_id=1, source_target_pairs={{0,16},{2,18},{4,20},{6,22},{8,24},{10,26},{12,28},{14,30},{16,0},... | collective-permute-start | bytes 110600 | tf_op jit(solution)/shard_map/ppermute | solution.py:458
  176.7 4.2 %collective-permute-start.30 = (f32[24,384]{1,0:T(8,128)S(1)}, f32[24,384]{1,0:T(8,128)S(1)}, u32[]{:S(2)}, u32[]{:S(2)}) collective-permute-start(f32[24,384]{1,0:T(8,128)S(1)} %get-tuple-element.54), channel_id=1, source_target_pairs={{0,24},{2,26},{4,28},{6,30},{8,0},{10,2},{12,4},{14,6},{16,8},{18,... | collective-permute-start | bytes 110600 | tf_op jit(solution)/shard_map/ppermute | solution.py:458
  180.9 5.2 %collective-permute-start.31 = (f32[96,384]{1,0:T(8,128)S(1)}, f32[96,384]{1,0:T(8,128)S(1)}, u32[]{:S(2)}, u32[]{:S(2)}) collective-permute-start(f32[96,384]{1,0:T(8,128)S(1)} %constant_dynamic-update-slice_fusion.11), channel_id=1, source_target_pairs={{0,2},{2,0},{4,6},{6,4},{8,10},{10,8},{12,14},{14,12},{16,18},{18,... | collective-permute-start | bytes 442376 | tf_op jit(solution)/shard_map/ppermute | solution.py:301
  181.9 5.1 %collective-permute-start.32 = (f32[96,384]{1,0:T(8,128)S(1)}, f32[96,384]{1,0:T(8,128)S(1)}, u32[]{:S(2)}, u32[]{:S(2)}) collective-permute-start(f32[96,384]{1,0:T(8,128)S(1)} %constant_dynamic-update-slice_fusion.11), channel_id=1, source_target_pairs={{0,4},{2,6},{4,0},{6,2},{8,12},{10,14},{12,8},{14,10},{16,20},{18,... | collective-permute-start | bytes 442376 | tf_op jit(solution)/shard_map/ppermute | solution.py:301
  182.8 6.0 %collective-permute-start.33 = (f32[96,384]{1,0:T(8,128)S(1)}, f32[96,384]{1,0:T(8,128)S(1)}, u32[]{:S(2)}, u32[]{:S(2)}) collective-permute-start(f32[96,384]{1,0:T(8,128)S(1)} %constant_dynamic-update-slice_fusion.11), channel_id=1, source_target_pairs={{0,6},{2,4},{4,2},{6,0},{8,14},{10,12},{12,10},{14,8},{16,22},{18,... | collective-permute-start | bytes 442376 | tf_op jit(solution)/shard_map/ppermute | solution.py:301
  188.8 2.1 %collective-permute-start.34 = (f32[384,384]{1,0:T(8,128)S(1)}, f32[384,384]{1,0:T(8,128)S(1)}, u32[]{:S(2)}, u32[]{:S(2)}) collective-permute-start(f32[384,384]{1,0:T(8,128)S(1)} %constant_dynamic-update-slice_fusion.7), channel_id=1, source_target_pairs={{0,1},{1,0},{2,3},{3,2},{4,5},{5,4},{6,7},{7,6},{8,9},{9,8},{10,11... | collective-permute-start | bytes 1769480 | tf_op jit(solution)/shard_map/ppermute | solution.py:304

commit v9 on v8

--- a/solution.py
+++ b/solution.py
@@ -319,7 +319,7 @@
         return total
 
     own = [block(out_weight, member ^ s, features, 1) for s in members]
-    down_own = [block(side_down.T, member ^ s, features, 1) for s in members]
+    down_own = [block(side_down, member ^ s, features, 0).T for s in members]
     stay_own = [block(residual, member ^ s, features, 1) for s in members]
     gain = block(ln_gain, member, features, 0)[None, :]
     columns = down_own[0].shape[0]

time: 193 us -> 193 us (level)
    dynamic_slice x6 -> x5, local copies, waits for them, and re-layouts: 4.09 us -> 3.07 us  [block(): return lax.dynamic_slice_in_dim(value, index * size, size, axis)]
where the time goes in v9:
time: 193 us; the launch traced here: 192 us
  waiting for transfers between devices  115 us (60%)
  starting transfers between devices  38.5 us (20%)
  Pallas kernels  16.9 us (9%)
  local copies, waits for them, and re-layouts  11 us (6%)
  other arithmetic  8.87 us (5%)
    ppermute x10, waiting for transfers between devices, line(): return lax.ppermute(value, 'wide', pairs)  60 us
    ppermute x15, waiting for transfers between devices, to_member(): return lax.ppermute(value, 'wide', pairs) if s else value  38.6 us
    ppermute x15, starting transfers between devices, to_member(): return lax.ppermute(value, 'wide', pairs) if s else value  18.7 us
    ppermute x10, starting transfers between devices, line(): return lax.ppermute(value, 'wide', pairs)  13.5 us
    ppermute x4, waiting for transfers between devices, to_core(): lax.ppermute(value, 'narrow', [(i, i ^ t) for i in range(narrows)])  9.76 us
    pallas_call x1, Pallas kernels, attend(): pl.pallas_call(functools.partial(attend_kernel, rows, planes), grid=(2,),...  9.54 us
    ppermute x6, waiting for transfers between devices, shift(): lax.ppermute(value, 'wide', [(i, (i + k * group) % wides) for i in range(...  7 us
    ppermute x6, starting transfers between devices, shift(): lax.ppermute(value, 'wide', [(i, (i + k * group) % wides) for i in range(...  6.15 us
  transfers between devices with their start and end apart: 35, of which 23 were waited for; matrix products, arithmetic and copies ran while one was open for 6% of the time, Pallas kernels for 5%

profile of v9, /device:TPU:0, one launch (start us, length us, event | category | flops | bytes accessed | tf_op | source)
XLA Modules:
  0.0 192.0 jit_solution(16379721646161149740)
XLA Ops:
  0.7 1.0 dynamic-slice_bitcast_fusion
  1.7 1.3 constant_dynamic-slice_fusion.6
  3.1 3.1 %collective-permute-start.3 = (bf16[240,768]{1,0:T(8,128)(2,1)S(1)}, bf16[240,768]{1,0:T(8,128)(2,1)S(1)}, u32[]{:S(2)}, u32[]{:S(2)}) collective-permute-start(bf16[240,768]{1,0:T(8,128)(2,1)S(1)} %pad_maximum_fusion.4.refs_6_), channel_id=1, source_target_pairs={{8,0},{10,2},{12,4},{14,6},{16,24},{18,26},{20,28},{22,30},{0,8},{... | collective-permute-start | bytes 1105928 | tf_op jit(solution)/shard_map/ppermute | solution.py:339
  6.2 0.7 collective-permute-start.5
  6.9 0.7 copy-done.3
  7.6 1.6 collective-permute-start
  9.2 1.6 collective-permute-start.1
  11.4 3.4 %collective-permute-done.3.refs_8_ = bf16[240,768]{1,0:T(8,128)(2,1)S(1)} collective-permute-done((bf16[240,768]{1,0:T(8,128)(2,1)S(1)}, bf16[240,768]{1,0:T(8,128)(2,1)S(1)}, u32[]{:S(2)}, u32[]{:S(2)}) %collective-permute-start.3) | collective-permute-done | bytes 368672 | tf_op jit(solution)/shard_map/ppermute | solution.py:339
  14.8 0.7 collective-permute-start.4
  15.5 1.3 collective-permute-start.6
  16.8 0.9 constant_dynamic-slice_fusion.7
  17.7 1.5 collective-permute-done
  19.2 7.7 %collective-permute-done.1 = bf16[240,768]{1,0:T(8,128)(2,1)S(1)} collective-permute-done((bf16[240,768]{1,0:T(8,128)(2,1)S(1)}, bf16[240,768]{1,0:T(8,128)(2,1)S(1)}, u32[]{:S(2)}, u32[]{:S(2)}) %collective-permute-start.1) | collective-permute-done | bytes 368672 | tf_op jit(solution)/shard_map/ppermute | solution.py:301
  27.0 1.7 collective-permute-done.6.refs_14_
  29.5 1.6 collective-permute-start.7
  31.0 1.6 collective-permute-start.8
  32.6 1.5 collective-permute-start.9
  34.2 0.7 collective-permute-start.10
  34.9 1.3 collective-permute-start.11
  36.3 28.0 %collective-permute-done.11.refs_4_ = bf16[240,768]{1,0:T(8,128)(2,1)S(1)} collective-permute-done((bf16[240,768]{1,0:T(8,128)(2,1)S(1)}, bf16[240,768]{1,0:T(8,128)(2,1)S(1)}, u32[]{:S(2)}, u32[]{:S(2)}) %collective-permute-start.11) | collective-permute-done | bytes 368672 | tf_op jit(solution)/shard_map/ppermute | solution.py:339
  64.4 1.3 collective-permute-start.12
  65.6 1.7 collective-permute-start.13
  67.3 1.3 collective-permute-start.14
  68.8 0.8 slice.33.refs_4_
  69.5 4.0 %maximum_maximum_fusion = bf16[1024,1536]{1,0:T(8,128)(2,1)S(1)} fusion(bf16[256,1536]{1,0:T(8,128)(2,1)S(1)} %slice.31, bf16[256,1536]{1,0:T(8,128)(2,1)S(1)} %slice.30, bf16[256,1536]{1,0:T(8,128)(2,1)S(1)} %copy-done.25, bf16[1024]{0:T(1024)(128)(2,1)S(1)} %pad.3.clone), kind=kLoop, calls=%fused_computation | loop fusion | flops 12582912 | bytes 5507072 | tf_op jit(solution)/shard_map/concatenate | solution.py:363
  73.5 18.4 %collective-permute-done.14.refs_15_ = bf16[720,768]{1,0:T(8,128)(2,1)S(1)} collective-permute-done((bf16[720,768]{1,0:T(8,128)(2,1)S(1)}, bf16[720,768]{1,0:T(8,128)(2,1)S(1)}, u32[]{:S(2)}, u32[]{:S(2)}) %collective-permute-start.14) | collective-permute-done | bytes 1105952 | tf_op jit(solution)/shard_map/ppermute | solution.py:339
  92.0 0.9 copy-done.13
  93.4 1.3 collective-permute-start.16
  94.7 0.8 dynamic_slice.79
  95.5 1.0 slice.35.refs_5_
  96.5 2.2 %collective-permute-done.15 = bf16[1024,1536]{1,0:T(8,128)(2,1)} collective-permute-done((bf16[1024,1536]{1,0:T(8,128)(2,1)S(1)}, bf16[1024,1536]{1,0:T(8,128)(2,1)}, u32[]{:S(2)}, u32[]{:S(2)}) %collective-permute-start.15) | collective-permute-done | bytes 3145760 | tf_op jit(solution)/shard_map/ppermute | solution.py:304
  98.8 3.3 %dynamic-slice_select_fusion = bf16[4,256,768]{2,1,0:T(8,128)(2,1)S(1)} fusion(bf16[4,256,1536]{2,1,0:T(8,128)(2,1)} %bitcast.5.refs_1_, s32[]{:T(128)S(6)} %select_n.150, bf16[4,256,1536]{2,1,0:T(8,128)(2,1)S(1)} %bitcast.14, pred[]{:T(512)S(6)} %eq.22), kind=kLoop, calls=%fused_computation.1 | loop fusion | flops 786432 | bytes 4718597 | tf_op jit(solution)/shard_map/jit(_where)/select_n | solution.py:377
  102.3 0.8 copy-done
  103.9 9.5 %shard_map.103 = (f32[1024,768]{1,0:T(8,128)S(1)}, bf16[768,768]{1,0:T(8,128)(2,1)S(1)}) custom-call(bf16[4,256,1536]{2,1,0:T(8,128)(2,1)S(1)} %bitcast.15, bf16[4,256,1536]{2,1,0:T(8,128)(2,1)} %bitcast.5.refs_1_, bf16[256,768]{1,0:T(8,128)(2,1)S(1)} %copy-done.2, bf16[256,768]{1,0:T(8,128)(2,1)S(1)} %slice.32.refs_3_, bf16[256,768]{1,0:T(8,128)(2,1)S(1)} %copy-done, ...), custom_call_target="tpu_custom_call" | custom-call | flops 4831838208 | bytes 16777216 | tf_op jit(solution)/shard_map/pallas_call | solution.py:87
  113.4 8.5 %collective-permute-done.16.refs_5_ = bf16[720,768]{1,0:T(8,128)(2,1)} collective-permute-done((bf16[720,768]{1,0:T(8,128)(2,1)}, bf16[720,768]{1,0:T(8,128)(2,1)}, u32[]{:S(2)}, u32[]{:S(2)}) %collective-permute-start.16) | collective-permute-done | bytes 1105952 | tf_op jit(solution)/shard_map/ppermute | solution.py:339
  122.0 5.0 %shard_map.104 = (f32[544,768]{1,0:T(8,128)S(1)}, f32[544,768]{1,0:T(8,128)S(1)}) custom-call(f32[1024,768]{1,0:T(8,128)S(1)} %get-tuple-element.45.refs_0_, bf16[1024,768]{1,0:T(8,128)(2,1)S(1)} %bitcast.16, bf16[1,768]{1,0:T(2,128)(2,1)S(1)} %broadcast_in_dim.13.refs_2_, bf16[768,768]{1,0:T(8,128)(2,1)S(1)} %get-tuple-element.46.refs_3_, ...), custom_call_target="tpu_custom_call" | custom-call | flops 2415919104 | bytes 16777216 | tf_op jit(solution)/shard_map/pallas_call | solution.py:191
  127.0 3.5 %collective-permute-done.17 = f32[544,768]{1,0:T(8,128)S(1)} collective-permute-done((f32[544,768]{1,0:T(8,128)S(1)}, f32[544,768]{1,0:T(8,128)S(1)}, u32[]{:S(2)}, u32[]{:S(2)}) %collective-permute-start.17) | collective-permute-done | bytes 1671200 | tf_op jit(solution)/shard_map/ppermute | solution.py:304
  130.9 1.9 collective-permute-start.18
  133.0 1.4 collective-permute-start.20
  134.5 9.0 %collective-permute-done.18.refs_1_ = f32[136,768]{1,0:T(8,128)S(1)} collective-permute-done((f32[136,768]{1,0:T(8,128)S(1)}, f32[136,768]{1,0:T(8,128)S(1)}, u32[]{:S(2)}, u32[]{:S(2)}) %collective-permute-start.18) | collective-permute-done | bytes 417824 | tf_op jit(solution)/shard_map/ppermute | solution.py:301
  143.5 9.7 %collective-permute-done.19.refs_2_ = f32[136,768]{1,0:T(8,128)S(1)} collective-permute-done((f32[136,768]{1,0:T(8,128)S(1)}, f32[136,768]{1,0:T(8,128)S(1)}, u32[]{:S(2)}, u32[]{:S(2)}) %collective-permute-start.19) | collective-permute-done | bytes 417824 | tf_op jit(solution)/shard_map/ppermute | solution.py:301
  153.2 2.4 %shard_map.105 = (f32[128,768]{1,0:T(8,128)}, f32[384,384]{1,0:T(8,128)S(1)}, f32[384,384]{1,0:T(8,128)S(1)}) custom-call(f32[136,768]{1,0:T(8,128)S(1)} %get-tuple-element.58.refs_0_, f32[136,768]{1,0:T(8,128)S(1)} %collective-permute-done.18.refs_1_, f32[136,768]{1,0:T(8,128)S(1)} %collective-permute-done.19.refs_2_, ...), custom_call_target="tpu_custom_call" | custom-call | flops 452984832 | bytes 5242880 | tf_op jit(solution)/shard_map/pallas_call | solution.py:277
  155.5 2.0 %collective-permute-done.21 = f32[384,384]{1,0:T(8,128)S(1)} collective-permute-done((f32[384,384]{1,0:T(8,128)S(1)}, f32[384,384]{1,0:T(8,128)S(1)}, u32[]{:S(2)}, u32[]{:S(2)}) %collective-permute-start.21) | collective-permute-done | bytes 589856 | tf_op jit(solution)/shard_map/ppermute | solution.py:304
  157.6 1.2 collective-permute-start.24
  158.9 0.7 collective-permute-start.23
  159.5 1.7 collective-permute-start.22
  161.2 4.1 %collective-permute-done.24 = f32[96,384]{1,0:T(8,128)S(1)} collective-permute-done((f32[96,384]{1,0:T(8,128)S(1)}, f32[96,384]{1,0:T(8,128)S(1)}, u32[]{:S(2)}, u32[]{:S(2)}) %collective-permute-start.24) | collective-permute-done | bytes 147488 | tf_op jit(solution)/shard_map/ppermute | solution.py:301
  165.3 2.3 %collective-permute-done.23 = f32[96,384]{1,0:T(8,128)S(1)} collective-permute-done((f32[96,384]{1,0:T(8,128)S(1)}, f32[96,384]{1,0:T(8,128)S(1)}, u32[]{:S(2)}, u32[]{:S(2)}) %collective-permute-start.23) | collective-permute-done | bytes 147488 | tf_op jit(solution)/shard_map/ppermute | solution.py:301
  167.7 1.0 collective-permute-start.27
  168.7 1.0 collective-permute-start.25
  169.8 1.9 %collective-permute-done.27 = f32[24,384]{1,0:T(8,128)S(1)} collective-permute-done((f32[24,384]{1,0:T(8,128)S(1)}, f32[24,384]{1,0:T(8,128)S(1)}, u32[]{:S(2)}, u32[]{:S(2)}) %collective-permute-start.27) | collective-permute-done | bytes 36896 | tf_op jit(solution)/shard_map/ppermute | solution.py:458
  171.7 1.9 %collective-permute-done.26 = f32[24,384]{1,0:T(8,128)S(1)} collective-permute-done((f32[24,384]{1,0:T(8,128)S(1)}, f32[24,384]{1,0:T(8,128)S(1)}, u32[]{:S(2)}, u32[]{:S(2)}) %collective-permute-start.26) | collective-permute-done | bytes 36896 | tf_op jit(solution)/shard_map/ppermute | solution.py:458
  173.6 0.9 collective-permute-done.25
  174.7 2.0 %collective-permute-start.29 = (f32[24,384]{1,0:T(8,128)S(1)}, f32[24,384]{1,0:T(8,128)S(1)}, u32[]{:S(2)}, u32[]{:S(2)}) collective-permute-start(f32[24,384]{1,0:T(8,128)S(1)} %get-tuple-element.54), channel_id=1, source_target_pairs={{0,16},{2,18},{4,20},{6,22},{8,24},{10,26},{12,28},{14,30},{16,0},... | collective-permute-start | bytes 110600 | tf_op jit(solution)/shard_map/ppermute | solution.py:458
  176.7 1.9 collective-permute-start.30
  178.6 1.7 collective-permute-done.28
  180.9 1.0 collective-permute-start.31
  181.9 0.8 collective-permute-start.32
  182.8 1.6 collective-permute-start.33
  184.5 1.6 collective-permute-done.31
  186.1 0.9 collective-permute-done.32
  187.1 1.7 collective-permute-done.33
  188.9 2.0 %collective-permute-done.34 = f32[384,384]{1,0:T(8,128)S(1)} collective-permute-done((f32[384,384]{1,0:T(8,128)S(1)}, f32[384,384]{1,0:T(8,128)S(1)}, u32[]{:S(2)}, u32[]{:S(2)}) %collective-permute-start.34) | collective-permute-done | bytes 589856 | tf_op jit(solution)/shard_map/ppermute | solution.py:304
  190.9 1.1 broadcast_select_fusion
  (110 shorter events, 5.0 us)
Async XLA Ops:
  3.0 13.7 %copy-start.26 = (bf16[256,3072]{1,0:T(8,128)(2,1)S(1)}, bf16[256,3072]{1,0:T(8,128)(2,1)}, u32[]{:S(2)}) copy-start(bf16[256,3072]{1,0:T(8,128)(2,1)} %param.10) | copy-start | bytes 4718596
  3.1 11.7 %collective-permute-start.3 = (bf16[240,768]{1,0:T(8,128)(2,1)S(1)}, bf16[240,768]{1,0:T(8,128)(2,1)S(1)}, u32[]{:S(2)}, u32[]{:S(2)}) collective-permute-start(bf16[240,768]{1,0:T(8,128)(2,1)S(1)} %pad_maximum_fusion.4.refs_6_), channel_id=1, source_target_pairs={{8,0},{10,2},{12,4},{14,6},{16,24},{18,26},{20,28},{22,30},{0,8},{... | collective-permute-start | bytes 1105928 | tf_op jit(solution)/shard_map/ppermute | solution.py:339
  6.2 9.3 %collective-permute-start.5 = (bf16[240,768]{1,0:T(8,128)(2,1)S(1)}, bf16[240,768]{1,0:T(8,128)(2,1)S(1)}, u32[]{:S(2)}, u32[]{:S(2)}) collective-permute-start(bf16[240,768]{1,0:T(8,128)(2,1)S(1)} %pad_maximum_fusion.4.refs_6_), channel_id=1, source_target_pairs={{8,16},{10,18},{12,20},{14,22},{16,8},{18,10},{20,12},{22,14},{9,1... | collective-permute-start | bytes 1105928 | tf_op jit(solution)/shard_map/ppermute | solution.py:339
  6.8 0.7 copy-start.3
  7.6 11.6 %collective-permute-start = (bf16[240,768]{1,0:T(8,128)(2,1)S(1)}, bf16[240,768]{1,0:T(8,128)(2,1)S(1)}, u32[]{:S(2)}, u32[]{:S(2)}) collective-permute-start(bf16[240,768]{1,0:T(8,128)(2,1)S(1)} %pad_maximum_fusion.1), channel_id=1, source_target_pairs={{0,2},{2,0},{4,6},{6,4},{8,10},{10,8},{12,14},{14,12},{16,18},{18,... | collective-permute-start | bytes 1105928 | tf_op jit(solution)/shard_map/ppermute | solution.py:301
  9.2 17.7 %collective-permute-start.1 = (bf16[240,768]{1,0:T(8,128)(2,1)S(1)}, bf16[240,768]{1,0:T(8,128)(2,1)S(1)}, u32[]{:S(2)}, u32[]{:S(2)}) collective-permute-start(bf16[240,768]{1,0:T(8,128)(2,1)S(1)} %pad_maximum_fusion.2), channel_id=1, source_target_pairs={{0,4},{2,6},{4,0},{6,2},{8,12},{10,14},{12,8},{14,10},{16,20},{18,... | collective-permute-start | bytes 1105928 | tf_op jit(solution)/shard_map/ppermute | solution.py:301
  10.8 16.2 %collective-permute-start.2 = (bf16[240,768]{1,0:T(8,128)(2,1)S(1)}, bf16[240,768]{1,0:T(8,128)(2,1)S(1)}, u32[]{:S(2)}, u32[]{:S(2)}) collective-permute-start(bf16[240,768]{1,0:T(8,128)(2,1)S(1)} %pad_maximum_fusion.3), channel_id=1, source_target_pairs={{0,6},{2,4},{4,2},{6,0},{8,14},{10,12},{12,10},{14,8},{16,22},{18,... | collective-permute-start | bytes 1105928 | tf_op jit(solution)/shard_map/ppermute | solution.py:301
  14.7 2.9 %copy-start.15 = (bf16[240,768]{1,0:T(8,128)(2,1)}, bf16[240,768]{1,0:T(8,128)(2,1)S(1)}, u32[]{:S(2)}) copy-start(bf16[240,768]{1,0:T(8,128)(2,1)S(1)} %collective-permute-done.3.refs_8_) | copy-start | bytes 1105924
  14.8 12.3 %collective-permute-start.4 = (bf16[240,768]{1,0:T(8,128)(2,1)S(1)}, bf16[240,768]{1,0:T(8,128)(2,1)S(1)}, u32[]{:S(2)}, u32[]{:S(2)}) collective-permute-start(bf16[240,768]{1,0:T(8,128)(2,1)S(1)} %collective-permute-done.3.refs_8_), channel_id=1, source_target_pairs={{8,16},{10,18},{12,20},{14,22},{16,8},{18,10},{20,12},{22,14},{9,1... | collective-permute-start | bytes 1105928 | tf_op jit(solution)/shard_map/ppermute | solution.py:339
  15.4 2.2 %copy-start.17 = (bf16[240,768]{1,0:T(8,128)(2,1)}, bf16[240,768]{1,0:T(8,128)(2,1)S(1)}, u32[]{:S(2)}) copy-start(bf16[240,768]{1,0:T(8,128)(2,1)S(1)} %collective-permute-done.5.refs_10_) | copy-start | bytes 1105924
  15.5 13.3 %collective-permute-start.6 = (bf16[240,768]{1,0:T(8,128)(2,1)S(1)}, bf16[240,768]{1,0:T(8,128)(2,1)S(1)}, u32[]{:S(2)}, u32[]{:S(2)}) collective-permute-start(bf16[240,768]{1,0:T(8,128)(2,1)S(1)} %collective-permute-done.5.refs_10_), channel_id=1, source_target_pairs={{8,0},{10,2},{12,4},{14,6},{16,24},{18,26},{20,28},{22,30},{9,1},{... | collective-permute-start | bytes 1105928 | tf_op jit(solution)/shard_map/ppermute | solution.py:339
  17.7 11.0 %copy-start.25 = (bf16[256,1536]{1,0:T(8,128)(2,1)S(1)}, bf16[256,1536]{1,0:T(8,128)(2,1)}, u32[]{:S(2)}) copy-start(bf16[256,1536]{1,0:T(8,128)(2,1)} %param.8) | copy-start | bytes 2359300
  27.0 7.2 %copy-start.7 = (bf16[720,768]{1,0:T(8,128)(2,1)}, bf16[720,768]{1,0:T(8,128)(2,1)S(1)}, u32[]{:S(2)}) copy-start(bf16[720,768]{1,0:T(8,128)(2,1)S(1)} %constant_dynamic-update-slice_fusion.refs_7_) | copy-start | bytes 3317764
  27.0 7.9 %copy-start.19 = (bf16[240,768]{1,0:T(8,128)(2,1)}, bf16[240,768]{1,0:T(8,128)(2,1)S(1)}, u32[]{:S(2)}) copy-start(bf16[240,768]{1,0:T(8,128)(2,1)S(1)} %collective-permute-done.4.refs_12_) | copy-start | bytes 1105924
  28.7 0.7 copy-start.21
  29.5 34.9 %collective-permute-start.7 = (bf16[256,2304]{1,0:T(8,128)(2,1)S(1)}, bf16[256,2304]{1,0:T(8,128)(2,1)S(1)}, u32[]{:S(2)}, u32[]{:S(2)}) collective-permute-start(bf16[256,2304]{1,0:T(8,128)(2,1)S(1)} %constant_dynamic-update-slice_fusion.3), channel_id=1, source_target_pairs={{0,2},{2,0},{4,6},{6,4},{8,10},{10,8},{12,14},{14,12},{16,18},{18,... | collective-permute-start | bytes 3538952 | tf_op jit(solution)/shard_map/ppermute | solution.py:301
  31.0 33.3 %collective-permute-start.8 = (bf16[256,2304]{1,0:T(8,128)(2,1)S(1)}, bf16[256,2304]{1,0:T(8,128)(2,1)S(1)}, u32[]{:S(2)}, u32[]{:S(2)}) collective-permute-start(bf16[256,2304]{1,0:T(8,128)(2,1)S(1)} %constant_dynamic-update-slice_fusion.5), channel_id=1, source_target_pairs={{0,4},{2,6},{4,0},{6,2},{8,12},{10,14},{12,8},{14,10},{16,20},{18,... | collective-permute-start | bytes 3538952 | tf_op jit(solution)/shard_map/ppermute | solution.py:301
  32.6 31.7 %collective-permute-start.9 = (bf16[720,768]{1,0:T(8,128)(2,1)S(1)}, bf16[720,768]{1,0:T(8,128)(2,1)S(1)}, u32[]{:S(2)}, u32[]{:S(2)}) collective-permute-start(bf16[720,768]{1,0:T(8,128)(2,1)S(1)} %constant_dynamic-update-slice_fusion.refs_7_), channel_id=1, source_target_pairs={{8,0},{10,2},{12,4},{14,6},{16,24},{18,26},{20,28},{22,30},{0,8},{... | collective-permute-start | bytes 3317768 | tf_op jit(solution)/shard_map/ppermute | solution.py:339
  34.2 30.1 %collective-permute-start.10 = (bf16[720,768]{1,0:T(8,128)(2,1)S(1)}, bf16[720,768]{1,0:T(8,128)(2,1)S(1)}, u32[]{:S(2)}, u32[]{:S(2)}) collective-permute-start(bf16[720,768]{1,0:T(8,128)(2,1)S(1)} %constant_dynamic-update-slice_fusion.refs_7_), channel_id=1, source_target_pairs={{8,16},{10,18},{12,20},{14,22},{16,8},{18,10},{20,12},{22,14},{9,1... | collective-permute-start | bytes 3317768 | tf_op jit(solution)/shard_map/ppermute | solution.py:339
  34.9 29.4 %collective-permute-start.11 = (bf16[240,768]{1,0:T(8,128)(2,1)S(1)}, bf16[240,768]{1,0:T(8,128)(2,1)S(1)}, u32[]{:S(2)}, u32[]{:S(2)}) collective-permute-start(bf16[240,768]{1,0:T(8,128)(2,1)S(1)} %collective-permute-done.4.refs_12_), channel_id=1, source_target_pairs={{8,0},{10,2},{12,4},{14,6},{16,24},{18,26},{20,28},{22,30},{9,1},{... | collective-permute-start | bytes 1105928 | tf_op jit(solution)/shard_map/ppermute | solution.py:339
  64.3 4.4 %copy-start.23 = (bf16[240,768]{1,0:T(8,128)(2,1)}, bf16[240,768]{1,0:T(8,128)(2,1)S(1)}, u32[]{:S(2)}) copy-start(bf16[240,768]{1,0:T(8,128)(2,1)S(1)} %collective-permute-done.11.refs_4_) | copy-start | bytes 1105924
  64.3 4.4 %copy-start.9 = (bf16[720,768]{1,0:T(8,128)(2,1)}, bf16[720,768]{1,0:T(8,128)(2,1)S(1)}, u32[]{:S(2)}) copy-start(bf16[720,768]{1,0:T(8,128)(2,1)S(1)} %collective-permute-done.9.refs_9_) | copy-start | bytes 3317764
  64.3 4.4 %copy-start.11 = (bf16[720,768]{1,0:T(8,128)(2,1)}, bf16[720,768]{1,0:T(8,128)(2,1)S(1)}, u32[]{:S(2)}) copy-start(bf16[720,768]{1,0:T(8,128)(2,1)S(1)} %collective-permute-done.10.refs_11_) | copy-start | bytes 3317764
  64.4 27.6 %collective-permute-start.12 = (bf16[256,2304]{1,0:T(8,128)(2,1)S(1)}, bf16[256,2304]{1,0:T(8,128)(2,1)S(1)}, u32[]{:S(2)}, u32[]{:S(2)}) collective-permute-start(bf16[256,2304]{1,0:T(8,128)(2,1)S(1)} %pad_maximum_fusion), channel_id=1, source_target_pairs={{0,6},{2,4},{4,2},{6,0},{8,14},{10,12},{12,10},{14,8},{16,22},{18,... | collective-permute-start | bytes 3538952 | tf_op jit(solution)/shard_map/ppermute | solution.py:301
  65.6 7.9 %collective-permute-start.13 = (bf16[720,768]{1,0:T(8,128)(2,1)S(1)}, bf16[720,768]{1,0:T(8,128)(2,1)}, u32[]{:S(2)}, u32[]{:S(2)}) collective-permute-start(bf16[720,768]{1,0:T(8,128)(2,1)S(1)} %collective-permute-done.9.refs_9_), channel_id=1, source_target_pairs={{8,16},{10,18},{12,20},{14,22},{16,8},{18,10},{20,12},{22,14},{9,1... | collective-permute-start | bytes 3317768 | tf_op jit(solution)/shard_map/ppermute | solution.py:339
  67.3 24.7 %collective-permute-start.14 = (bf16[720,768]{1,0:T(8,128)(2,1)S(1)}, bf16[720,768]{1,0:T(8,128)(2,1)S(1)}, u32[]{:S(2)}, u32[]{:S(2)}) collective-permute-start(bf16[720,768]{1,0:T(8,128)(2,1)S(1)} %collective-permute-done.10.refs_11_), channel_id=1, source_target_pairs={{8,0},{10,2},{12,4},{14,6},{16,24},{18,26},{20,28},{22,30},{9,1},{... | collective-permute-start | bytes 3317768 | tf_op jit(solution)/shard_map/ppermute | solution.py:339
  92.0 1.0 copy-start.13
  92.0 1.4 copy-start.27
  92.9 5.8 %collective-permute-start.15 = (bf16[1024,1536]{1,0:T(8,128)(2,1)S(1)}, bf16[1024,1536]{1,0:T(8,128)(2,1)}, u32[]{:S(2)}, u32[]{:S(2)}) collective-permute-start(bf16[1024,1536]{1,0:T(8,128)(2,1)S(1)} %slice_dynamic-update-slice_fusion), channel_id=1, source_target_pairs={{0,1},{1,0},{2,3},{3,2},{4,5},{5,4},{6,7},{7,6},{8,9},{9,8},{10,11... | collective-permute-start | bytes 9437192 | tf_op jit(solution)/shard_map/ppermute | solution.py:304
  93.4 28.6 %collective-permute-start.16 = (bf16[720,768]{1,0:T(8,128)(2,1)}, bf16[720,768]{1,0:T(8,128)(2,1)}, u32[]{:S(2)}, u32[]{:S(2)}) collective-permute-start(bf16[720,768]{1,0:T(8,128)(2,1)} %collective-permute-done.13.refs_13_), channel_id=1, source_target_pairs={{8,0},{10,2},{12,4},{14,6},{16,24},{18,26},{20,28},{22,30},{9,1},{... | collective-permute-start | bytes 3317768 | tf_op jit(solution)/shard_map/ppermute | solution.py:339
  98.7 3.5 %copy-start.10 = (bf16[720,768]{1,0:T(8,128)(2,1)S(1)}, bf16[720,768]{1,0:T(8,128)(2,1)}, u32[]{:S(2)}) copy-start(bf16[720,768]{1,0:T(8,128)(2,1)} %copy-done.9) | copy-start | bytes 3317764
  98.7 3.6 %copy-start.12 = (bf16[720,768]{1,0:T(8,128)(2,1)S(1)}, bf16[720,768]{1,0:T(8,128)(2,1)}, u32[]{:S(2)}) copy-start(bf16[720,768]{1,0:T(8,128)(2,1)} %copy-done.11) | copy-start | bytes 3317764
  98.7 3.6 %copy-start.14 = (bf16[720,768]{1,0:T(8,128)(2,1)S(1)}, bf16[720,768]{1,0:T(8,128)(2,1)}, u32[]{:S(2)}) copy-start(bf16[720,768]{1,0:T(8,128)(2,1)} %copy-done.13) | copy-start | bytes 3317764
  98.7 3.6 %copy-start.20 = (bf16[240,768]{1,0:T(8,128)(2,1)S(1)}, bf16[240,768]{1,0:T(8,128)(2,1)}, u32[]{:S(2)}) copy-start(bf16[240,768]{1,0:T(8,128)(2,1)} %copy-done.19) | copy-start | bytes 1105924
  98.8 3.6 %copy-start.22 = (bf16[240,768]{1,0:T(8,128)(2,1)S(1)}, bf16[240,768]{1,0:T(8,128)(2,1)}, u32[]{:S(2)}) copy-start(bf16[240,768]{1,0:T(8,128)(2,1)} %copy-done.21) | copy-start | bytes 1105924
  102.1 1.0 copy-start
  102.1 1.1 copy-start.2
  102.1 1.2 copy-start.4
  102.1 1.6 copy-start.8
  102.1 1.6 copy-start.16
  102.2 1.7 copy-start.18
  103.9 18.1 %copy-start.24 = (bf16[240,768]{1,0:T(8,128)(2,1)S(1)}, bf16[240,768]{1,0:T(8,128)(2,1)}, u32[]{:S(2)}) copy-start(bf16[240,768]{1,0:T(8,128)(2,1)} %copy-done.23) | copy-start | bytes 1105924
  126.9 3.6 %collective-permute-start.17 = (f32[544,768]{1,0:T(8,128)S(1)}, f32[544,768]{1,0:T(8,128)S(1)}, u32[]{:S(2)}, u32[]{:S(2)}) collective-permute-start(f32[544,768]{1,0:T(8,128)S(1)} %get-tuple-element.49), channel_id=1, source_target_pairs={{0,1},{1,0},{2,3},{3,2},{4,5},{5,4},{6,7},{7,6},{8,9},{9,8},{10,11... | collective-permute-start | bytes 5013512 | tf_op jit(solution)/shard_map/ppermute | solution.py:304
  130.8 22.4 %copy-start.1 = (f32[128,768]{1,0:T(8,128)S(1)}, f32[128,768]{1,0:T(8,128)}, u32[]{:S(2)}) copy-start(f32[128,768]{1,0:T(8,128)} %refs_6_.1) | copy-start | bytes 1179652
  130.8 22.4 %copy-start.5 = (bf16[384,384]{1,0:T(8,128)(2,1)S(1)}, bf16[384,384]{1,0:T(8,128)(2,1)}, u32[]{:S(2)}) copy-start(bf16[384,384]{1,0:T(8,128)(2,1)} %refs_4_.1) | copy-start | bytes 884740
  130.8 22.4 %copy-start.6 = (bf16[384,384]{1,0:T(8,128)(2,1)S(1)}, bf16[384,384]{1,0:T(8,128)(2,1)}, u32[]{:S(2)}) copy-start(bf16[384,384]{1,0:T(8,128)(2,1)} %refs_5_.1) | copy-start | bytes 884740
  130.9 12.5 %collective-permute-start.18 = (f32[136,768]{1,0:T(8,128)S(1)}, f32[136,768]{1,0:T(8,128)S(1)}, u32[]{:S(2)}, u32[]{:S(2)}) collective-permute-start(f32[136,768]{1,0:T(8,128)S(1)} %get-tuple-element.57), channel_id=1, source_target_pairs={{0,2},{2,0},{4,6},{6,4},{8,10},{10,8},{12,14},{14,12},{16,18},{18,... | collective-permute-start | bytes 1253384 | tf_op jit(solution)/shard_map/ppermute | solution.py:301
  132.8 20.4 %collective-permute-start.19 = (f32[136,768]{1,0:T(8,128)S(1)}, f32[136,768]{1,0:T(8,128)S(1)}, u32[]{:S(2)}, u32[]{:S(2)}) collective-permute-start(f32[136,768]{1,0:T(8,128)S(1)} %get-tuple-element.56), channel_id=1, source_target_pairs={{0,4},{2,6},{4,0},{6,2},{8,12},{10,14},{12,8},{14,10},{16,20},{18,... | collective-permute-start | bytes 1253384 | tf_op jit(solution)/shard_map/ppermute | solution.py:301
  133.0 20.1 %collective-permute-start.20 = (f32[136,768]{1,0:T(8,128)S(1)}, f32[136,768]{1,0:T(8,128)S(1)}, u32[]{:S(2)}, u32[]{:S(2)}) collective-permute-start(f32[136,768]{1,0:T(8,128)S(1)} %get-tuple-element.55), channel_id=1, source_target_pairs={{0,6},{2,4},{4,2},{6,0},{8,14},{10,12},{12,10},{14,8},{16,22},{18,... | collective-permute-start | bytes 1253384 | tf_op jit(solution)/shard_map/ppermute | solution.py:301
  155.5 2.0 %collective-permute-start.21 = (f32[384,384]{1,0:T(8,128)S(1)}, f32[384,384]{1,0:T(8,128)S(1)}, u32[]{:S(2)}, u32[]{:S(2)}) collective-permute-start(f32[384,384]{1,0:T(8,128)S(1)} %get-tuple-element.52), channel_id=1, source_target_pairs={{0,1},{1,0},{2,3},{3,2},{4,5},{5,4},{6,7},{7,6},{8,9},{9,8},{10,11... | collective-permute-start | bytes 1769480 | tf_op jit(solution)/shard_map/ppermute | solution.py:304
  157.6 7.7 %collective-permute-start.24 = (f32[96,384]{1,0:T(8,128)S(1)}, f32[96,384]{1,0:T(8,128)S(1)}, u32[]{:S(2)}, u32[]{:S(2)}) collective-permute-start(f32[96,384]{1,0:T(8,128)S(1)} %get-tuple-element.70), channel_id=1, source_target_pairs={{0,6},{2,4},{4,2},{6,0},{8,14},{10,12},{12,10},{14,8},{16,22},{18,... | collective-permute-start | bytes 442376 | tf_op jit(solution)/shard_map/ppermute | solution.py:301
  158.9 8.8 %collective-permute-start.23 = (f32[96,384]{1,0:T(8,128)S(1)}, f32[96,384]{1,0:T(8,128)S(1)}, u32[]{:S(2)}, u32[]{:S(2)}) collective-permute-start(f32[96,384]{1,0:T(8,128)S(1)} %get-tuple-element.71), channel_id=1, source_target_pairs={{0,4},{2,6},{4,0},{6,2},{8,12},{10,14},{12,8},{14,10},{16,20},{18,... | collective-permute-start | bytes 442376 | tf_op jit(solution)/shard_map/ppermute | solution.py:301
  159.5 8.1 %collective-permute-start.22 = (f32[96,384]{1,0:T(8,128)S(1)}, f32[96,384]{1,0:T(8,128)S(1)}, u32[]{:S(2)}, u32[]{:S(2)}) collective-permute-start(f32[96,384]{1,0:T(8,128)S(1)} %get-tuple-element.69), channel_id=1, source_target_pairs={{0,2},{2,0},{4,6},{6,4},{8,10},{10,8},{12,14},{14,12},{16,18},{18,... | collective-permute-start | bytes 442376 | tf_op jit(solution)/shard_map/ppermute | solution.py:301
  167.7 4.0 %collective-permute-start.27 = (f32[24,384]{1,0:T(8,128)S(1)}, f32[24,384]{1,0:T(8,128)S(1)}, u32[]{:S(2)}, u32[]{:S(2)}) collective-permute-start(f32[24,384]{1,0:T(8,128)S(1)} %get-tuple-element.77), channel_id=1, source_target_pairs={{0,24},{2,26},{4,28},{6,30},{8,0},{10,2},{12,4},{14,6},{16,8},{18,... | collective-permute-start | bytes 110600 | tf_op jit(solution)/shard_map/ppermute | solution.py:458
  168.7 4.9 %collective-permute-start.26 = (f32[24,384]{1,0:T(8,128)S(1)}, f32[24,384]{1,0:T(8,128)S(1)}, u32[]{:S(2)}, u32[]{:S(2)}) collective-permute-start(f32[24,384]{1,0:T(8,128)S(1)} %get-tuple-element.78), channel_id=1, source_target_pairs={{0,16},{2,18},{4,20},{6,22},{8,24},{10,26},{12,28},{14,30},{16,0},... | collective-permute-start | bytes 110600 | tf_op jit(solution)/shard_map/ppermute | solution.py:458
  168.7 5.8 %collective-permute-start.25 = (f32[24,384]{1,0:T(8,128)S(1)}, f32[24,384]{1,0:T(8,128)S(1)}, u32[]{:S(2)}, u32[]{:S(2)}) collective-permute-start(f32[24,384]{1,0:T(8,128)S(1)} %get-tuple-element.76), channel_id=1, source_target_pairs={{0,8},{2,10},{4,12},{6,14},{8,16},{10,18},{12,20},{14,22},{16,24},... | collective-permute-start | bytes 110600 | tf_op jit(solution)/shard_map/ppermute | solution.py:458
  174.5 5.8 %collective-permute-start.28 = (f32[24,384]{1,0:T(8,128)S(1)}, f32[24,384]{1,0:T(8,128)S(1)}, u32[]{:S(2)}, u32[]{:S(2)}) collective-permute-start(f32[24,384]{1,0:T(8,128)S(1)} %get-tuple-element.54), channel_id=1, source_target_pairs={{0,8},{2,10},{4,12},{6,14},{8,16},{10,18},{12,20},{14,22},{16,24},... | collective-permute-start | bytes 110600 | tf_op jit(solution)/shard_map/ppermute | solution.py:458
  174.7 5.6 %collective-permute-start.29 = (f32[24,384]{1,0:T(8,128)S(1)}, f32[24,384]{1,0:T(8,128)S(1)}, u32[]{:S(2)}, u32[]{:S(2)}) collective-permute-start(f32[24,384]{1,0:T(8,128)S(1)} %get-tuple-element.54), channel_id=1, source_target_pairs={{0,16},{2,18},{4,20},{6,22},{8,24},{10,26},{12,28},{14,30},{16,0},... | collective-permute-start | bytes 110600 | tf_op jit(solution)/shard_map/ppermute | solution.py:458
  176.7 4.2 %collective-permute-start.30 = (f32[24,384]{1,0:T(8,128)S(1)}, f32[24,384]{1,0:T(8,128)S(1)}, u32[]{:S(2)}, u32[]{:S(2)}) collective-permute-start(f32[24,384]{1,0:T(8,128)S(1)} %get-tuple-element.54), channel_id=1, source_target_pairs={{0,24},{2,26},{4,28},{6,30},{8,0},{10,2},{12,4},{14,6},{16,8},{18,... | collective-permute-start | bytes 110600 | tf_op jit(solution)/shard_map/ppermute | solution.py:458
  180.9 5.2 %collective-permute-start.31 = (f32[96,384]{1,0:T(8,128)S(1)}, f32[96,384]{1,0:T(8,128)S(1)}, u32[]{:S(2)}, u32[]{:S(2)}) collective-permute-start(f32[96,384]{1,0:T(8,128)S(1)} %constant_dynamic-update-slice_fusion.11), channel_id=1, source_target_pairs={{0,2},{2,0},{4,6},{6,4},{8,10},{10,8},{12,14},{14,12},{16,18},{18,... | collective-permute-start | bytes 442376 | tf_op jit(solution)/shard_map/ppermute | solution.py:301
  181.9 5.1 %collective-permute-start.32 = (f32[96,384]{1,0:T(8,128)S(1)}, f32[96,384]{1,0:T(8,128)S(1)}, u32[]{:S(2)}, u32[]{:S(2)}) collective-permute-start(f32[96,384]{1,0:T(8,128)S(1)} %constant_dynamic-update-slice_fusion.11), channel_id=1, source_target_pairs={{0,4},{2,6},{4,0},{6,2},{8,12},{10,14},{12,8},{14,10},{16,20},{18,... | collective-permute-start | bytes 442376 | tf_op jit(solution)/shard_map/ppermute | solution.py:301
  182.8 6.0 %collective-permute-start.33 = (f32[96,384]{1,0:T(8,128)S(1)}, f32[96,384]{1,0:T(8,128)S(1)}, u32[]{:S(2)}, u32[]{:S(2)}) collective-permute-start(f32[96,384]{1,0:T(8,128)S(1)} %constant_dynamic-update-slice_fusion.11), channel_id=1, source_target_pairs={{0,6},{2,4},{4,2},{6,0},{8,14},{10,12},{12,10},{14,8},{16,22},{18,... | collective-permute-start | bytes 442376 | tf_op jit(solution)/shard_map/ppermute | solution.py:301
  188.8 2.1 %collective-permute-start.34 = (f32[384,384]{1,0:T(8,128)S(1)}, f32[384,384]{1,0:T(8,128)S(1)}, u32[]{:S(2)}, u32[]{:S(2)}) collective-permute-start(f32[384,384]{1,0:T(8,128)S(1)} %constant_dynamic-update-slice_fusion.7), channel_id=1, source_target_pairs={{0,1},{1,0},{2,3},{3,2},{4,5},{5,4},{6,7},{7,6},{8,9},{9,8},{10,11... | collective-permute-start | bytes 1769480 | tf_op jit(solution)/shard_map/ppermute | solution.py:304
